TPU v7x, 32 devices: a whole 2x2x4 slice. The times are simulated.
32 devices in a mesh: groups: 2 (over y), fsdp: 4 (over z), dp: 4 (over x, core).
Axes of the slice: x: 2, y: 2, z: 4, core: 2. Of those that a mesh axis runs over, the one named last changes fastest.
Arguments:
- output_gradient: bfloat16 [6144, 4096], P(('groups', 'dp'), 'fsdp'), parts along dimension 0, may hold values from -6 to 6
- hidden: bfloat16 [6144, 16384], P(('groups', 'dp'), 'fsdp'), parts along dimension 0, may hold values from -6 to 6
- frozen_down_weight: bfloat16 [16384, 4096], P('fsdp', 'dp'), may hold values from -0.09375 to 0.09375
- adapter_first_factors: bfloat16 [64, 16384, 64], P(('groups', 'dp'), 'fsdp'), parts along dimension 0, may hold values from -0.046875 to 0.046875
- adapter_second_factors: bfloat16 [64, 64, 4096], P(('groups', 'dp'), None, 'fsdp'), parts along dimension 0, may hold values from -0.09375 to 0.09375
- island_live_rows: int32 [24], P(('groups', 'dp')), parts along dimension 0, may hold values from 33 to 256, as said below
- island_adapter_ids: int32 [24], P(('groups', 'dp')), parts along dimension 0, may hold values from 0 to 31
- owner_slot_adapters: int32 [64], P('groups'), parts along dimension 0, may hold values from 0 to 31, each once
Outputs:
- grad_hidden: bfloat16 [6144, 16384], P(('groups', 'dp'), 'fsdp'), parts along dimension 0
- grad_a: float32 [64, 16384, 64], P(('groups', 'dp'), 'fsdp'), parts along dimension 0
- grad_b: float32 [64, 64, 4096], P(('groups', 'dp'), None, 'fsdp'), parts along dimension 0
There are 2 independent parts, one for each index of `groups`. A program takes and returns all parts, laid end to end along the dimension named above; an argument that names none is the same for every part. Nothing has to cross between parts.
Inputs may be any that keep to these rules, and one draw needn't show every extreme that they name: `island_live_rows`: at least one block in every draw has all 256 rows live. `owner_slot_adapters`: slot j belongs to index j // (32 / 4) of dp.
All inputs are finite; a program needn't handle non-finite values.
Results may differ from a plain program's by a relative error of at most 0.0029.
Values may be sent and summed in bfloat16 or wider, within the bound.
No kernel may reach another device: no remote copies, remote signals or barrier semaphores. Data moves between devices by JAX's collectives and lax.ppermute only.
A program may use at most 320 MiB of HBM per device.

v0:
```python
import functools

import jax
import jax.numpy as jnp
from jax import lax
from jax.experimental import pallas as pl
from jax.experimental.pallas import tpu as pltpu
from jax.sharding import PartitionSpec as P

adapter_scale = 2.0
factor_gradient = 0.0625
vmem_bytes = 60 * 1024 * 1024
bf16, f32, i32 = jnp.bfloat16, jnp.float32, jnp.int32


def behind(value, *after):
    if not after:
        return value
    return lax.optimization_barrier((value, *after))[0]


def params(cost):
    return dict(
        compiler_params=pltpu.CompilerParams(vmem_limit_bytes=vmem_bytes),
        cost_estimate=pl.CostEstimate(flops=cost[0], bytes_accessed=cost[1], transcendentals=0),
    )


def pick_kernel(pieces, index_ref, source_ref, *refs):
    a_refs, b_refs, out_ref = refs[:pieces], refs[pieces : 2 * pieces], refs[-1]
    source = source_ref[pl.program_id(0)]
    a, b = a_refs[0][0], b_refs[0][0]
    for r in range(1, pieces):
        a = jnp.where(source == r, a_refs[r][0], a)
        b = jnp.where(source == r, b_refs[r][0], b)
    ff = a.shape[1]
    out_ref[0, :, :ff] = a
    out_ref[0, :, ff:] = b


def factor_specs(pieces, count, rank, width):
    return [
        pl.BlockSpec(
            (1, rank, width), lambda i, index, source, r=r: (index[r * count + i], 0, 0)
        )
        for r in range(pieces)
    ]


def pick(index, source, a_pieces, b_pieces):
    count, pieces = source.shape[0], len(a_pieces)
    _, rank, ff = a_pieces[0].shape
    d = b_pieces[0].shape[2]
    return pl.pallas_call(
        functools.partial(pick_kernel, pieces),
        grid_spec=pltpu.PrefetchScalarGridSpec(
            num_scalar_prefetch=2,
            grid=(count,),
            in_specs=factor_specs(pieces, count, rank, ff) + factor_specs(pieces, count, rank, d),
            out_specs=pl.BlockSpec((1, rank, ff + d), lambda i, index, source: (i, 0, 0)),
        ),
        out_shape=jax.ShapeDtypeStruct((count, rank, ff + d), bf16),
        **params((0, 2 * (pieces + 1) * count * rank * (ff + d))),
    )(index, source, *a_pieces, *b_pieces)


def project_kernel(pieces, index_ref, source_ref, *refs):
    a_refs, b_refs = refs[:pieces], refs[pieces : 2 * pieces]
    far_ref, hid_ref, grad_ref, part_ref, block_ref, grad_a_ref, grad_b_ref = refs[
        2 * pieces : 2 * pieces + 7
    ]
    zeros, zero_sem = refs[2 * pieces + 7 :]
    step = pl.program_id(0)
    source = source_ref[step]
    ff = hid_ref.shape[1]
    d = grad_ref.shape[1]

    fills = []
    for slot in range(grad_a_ref.shape[0]):
        fills.append(pltpu.make_async_copy(zeros, grad_a_ref.at[slot], zero_sem.at[2 * slot]))
        fills.append(
            pltpu.make_async_copy(
                zeros.at[:, pl.ds(0, d)], grad_b_ref.at[slot], zero_sem.at[2 * slot + 1]
            )
        )

    @pl.when(step == 0)
    def _():
        zeros[...] = jnp.zeros_like(zeros)
        for fill in fills:
            fill.start()

    a, b = far_ref[0, :, :ff], far_ref[0, :, ff:]
    for r in range(pieces):
        a = jnp.where(source == r, a_refs[r][0], a)
        b = jnp.where(source == r, b_refs[r][0], b)
    block_ref[0] = a
    over_last = (((1,), (1,)), ((), ()))
    rank = a.shape[0]
    part_ref[0, :, :rank] = lax.dot_general(
        hid_ref[...], a, over_last, preferred_element_type=f32
    )
    part_ref[0, :, rank:] = lax.dot_general(
        grad_ref[...], b, over_last, preferred_element_type=f32
    )

    @pl.when(step == pl.num_programs(0) - 1)
    def _():
        for fill in fills:
            fill.wait()


def project(index, source, a_pieces, b_pieces, far, hidden, grad):
    count, pieces = source.shape[0], len(a_pieces)
    local, rank, ff = a_pieces[0].shape
    d = b_pieces[0].shape[2]
    rows = hidden.shape[0]
    height = rows // count
    own = lambda i, index, source: (i, 0)
    own3 = lambda i, index, source: (i, 0, 0)
    return pl.pallas_call(
        functools.partial(project_kernel, pieces),
        grid_spec=pltpu.PrefetchScalarGridSpec(
            num_scalar_prefetch=2,
            grid=(count,),
            in_specs=factor_specs(pieces, count, rank, ff)
            + factor_specs(pieces, count, rank, d)
            + [
                pl.BlockSpec((1, rank, ff + d), own3),
                pl.BlockSpec((height, ff), own),
                pl.BlockSpec((height, d), own),
            ],
            out_specs=[
                pl.BlockSpec((1, height, 2 * rank), own3),
                pl.BlockSpec((1, rank, ff), own3),
                pl.BlockSpec(memory_space=pl.ANY),
                pl.BlockSpec(memory_space=pl.ANY),
            ],
            scratch_shapes=[
                pltpu.VMEM((rank, ff), f32),
                pltpu.SemaphoreType.DMA((2 * local,)),
            ],
        ),
        out_shape=[
            jax.ShapeDtypeStruct((count, height, 2 * rank), f32),
            jax.ShapeDtypeStruct((count, rank, ff), bf16),
            jax.ShapeDtypeStruct((local, rank, ff), f32),
            jax.ShapeDtypeStruct((local, rank, d), f32),
        ],
        **params((2 * rows * rank * (ff + d), 2 * (rows + (pieces + 2) * count * rank) * (ff + d))),
    )(index, source, *a_pieces, *b_pieces, far, hidden, grad)


def terms_kernel(live_ref, here_ref, there_ref, hid_ref, grad_ref, terms_ref, coef_ref):
    ff = hid_ref.shape[1]
    rank = coef_ref.shape[2]
    total = here_ref[0] + there_ref[0]
    valid = lax.broadcasted_iota(i32, total.shape, 0) < live_ref[pl.program_id(0)]
    total = jnp.where(valid, total, 0.0)
    low = total[:, :rank].astype(bf16)
    coef = (adapter_scale * total[:, rank:]).astype(bf16)
    coef_ref[0] = coef
    over_rows = (((0,), (0,)), ((), ()))
    terms_ref[0, :, :ff] = (
        factor_gradient
        * lax.dot_general(coef, hid_ref[...], over_rows, preferred_element_type=f32)
    ).astype(bf16)
    terms_ref[0, :, ff:] = (
        factor_gradient
        * adapter_scale
        * lax.dot_general(low, grad_ref[...], over_rows, preferred_element_type=f32)
    ).astype(bf16)


def block_terms(live, here, there, hidden, grad):
    count, height, both = here.shape
    rank = both // 2
    rows, ff = hidden.shape
    d = grad.shape[1]
    own = lambda i, live: (i, 0)
    own3 = lambda i, live: (i, 0, 0)
    return pl.pallas_call(
        terms_kernel,
        grid_spec=pltpu.PrefetchScalarGridSpec(
            num_scalar_prefetch=1,
            grid=(count,),
            in_specs=[
                pl.BlockSpec((1, height, both), own3),
                pl.BlockSpec((1, height, both), own3),
                pl.BlockSpec((height, ff), own),
                pl.BlockSpec((height, d), own),
            ],
            out_specs=[
                pl.BlockSpec((1, rank, ff + d), own3),
                pl.BlockSpec((1, height, rank), own3),
            ],
        ),
        out_shape=[
            jax.ShapeDtypeStruct((count, rank, ff + d), bf16),
            jax.ShapeDtypeStruct((count, height, rank), bf16),
        ],
        **params((2 * rows * rank * (ff + d), 2 * (rows + count * rank) * (ff + d))),
    )(live, here, there, hidden, grad)


def base_kernel(n_dp, tiles, n_chunks, blocks, scalars_ref, kept_ref, *refs):
    near = n_dp // 2
    near_refs = refs[:near]
    far_refs = refs[near : near + n_chunks * near]
    coef_ref, block_ref = refs[near + n_chunks * near : near + n_chunks * near + 2]
    out_ref, token_ref, kept, weight, factor, result = refs[-10:-4]
    kept_sem, in_sem, factor_sem, out_sem = refs[-4:]
    _, tile, depth = weight.shape
    deep = depth // n_dp
    height = coef_ref.shape[1]
    steps = len(tiles)
    rows = pl.ds(blocks[0] * height, len(blocks) * height)
    token_ref[...] = jnp.zeros_like(token_ref)

    def lanes(r):
        return pl.ds(pl.multiple_of(scalars_ref[steps + r] * deep, deep), deep)

    def span(j):
        return pl.ds(pl.multiple_of(scalars_ref[j] * tile, tile), tile)

    def loads(j, slot, r):
        if r < near:
            return [
                pltpu.make_async_copy(
                    near_refs[r].at[span(j), :], weight.at[slot, :, lanes(r)], in_sem.at[slot, r, 0]
                )
            ]
        copies, low = [], 0
        for k, (chunk, start, size) in enumerate(tiles[j]):
            copies.append(
                pltpu.make_async_copy(
                    far_refs[chunk * near + r - near].at[pl.ds(start, size)],
                    weight.at[slot, pl.ds(low, size), lanes(r)],
                    in_sem.at[slot, r, k],
                )
            )
            low += size
        return copies

    def factors(j, slot):
        return pltpu.make_async_copy(
            block_ref.at[:, :, span(j)], factor.at[slot], factor_sem.at[slot]
        )

    def columns(r):
        return pltpu.make_async_copy(kept_ref.at[:, lanes(r)], kept.at[:, lanes(r)], kept_sem.at[r])

    def store(j, slot):
        return pltpu.make_async_copy(result.at[slot], out_ref.at[rows, span(j)], out_sem.at[slot])

    def load(j, slot):
        for r in range(n_dp):
            for copy in loads(j, slot, r):
                copy.start()
        factors(j, slot).start()

    over_last = (((1,), (1,)), ((), ()))

    def finish(slot, total):
        for k, b in enumerate(blocks):
            extra = jnp.dot(coef_ref[b], factor[slot, b], preferred_element_type=f32)
            here = total[k * height : (k + 1) * height] + extra
            valid = lax.broadcasted_iota(i32, here.shape, 0) < scalars_ref[steps + n_dp + b]
            result[slot, k * height : (k + 1) * height, :] = jnp.where(valid, here, 0.0).astype(
                bf16
            )

    for r in range(n_dp):
        columns(r).start()
        for copy in loads(0, 0, r):
            copy.start()
    factors(0, 0).start()
    if steps > 1:
        load(1, 1)
    total = None
    for r in range(n_dp):
        columns(r).wait()
        for copy in loads(0, 0, r):
            copy.wait()
        part = lax.dot_general(
            kept[:, lanes(r)], weight[0, :, lanes(r)], over_last, preferred_element_type=f32
        )
        total = part if total is None else total + part
    factors(0, 0).wait()
    finish(0, total)
    store(0, 0).start()

    @pl.loop(1, steps)
    def _(step):
        slot = lax.rem(step, 2)
        for j in range(1, steps):

            @pl.when(step == j)
            def _():
                if j + 1 < steps:
                    load(j + 1, (j + 1) % 2)
                for r in range(n_dp):
                    for copy in loads(j, j % 2, r):
                        copy.wait()
                factors(j, j % 2).wait()
                if j >= 2:
                    store(j - 2, j % 2).wait()

        finish(
            slot,
            lax.dot_general(kept[...], weight[slot], over_last, preferred_element_type=f32),
        )
        for j in range(1, steps):
            pl.when(step == j)(lambda j=j: store(j, j % 2).start())

    for j in range(max(steps - 2, 0), steps):
        store(j, j % 2).wait()


def base(places, scalars, kept, near, chunks, tiles, tile, coef, block_a, blocks, held, token):
    rows, depth = kept.shape
    count, rank, ff = block_a.shape
    top = len(near)
    anywhere = pl.BlockSpec(memory_space=pl.ANY)
    operands = [kept] + [near[r] for r in range(top)]
    for piece in chunks:
        operands += [piece[r] for r in range(top, 2 * top)]
    in_specs = [anywhere] * len(operands)
    in_specs += [pl.BlockSpec(coef.shape, lambda i, s: (0, 0, 0)), anywhere]
    operands += [coef, block_a]
    aliases = {}
    if held is not None:
        in_specs += [anywhere, anywhere]
        operands += [token, held]
        aliases = {len(operands): 0}
    most = max(len(segments) for segments in tiles)
    span = tile * len(tiles)
    return pl.pallas_call(
        functools.partial(base_kernel, 2 * top, tiles, len(chunks), blocks),
        grid_spec=pltpu.PrefetchScalarGridSpec(
            num_scalar_prefetch=1,
            grid=(1,),
            in_specs=in_specs,
            out_specs=[anywhere, pl.BlockSpec((8, 128), lambda i, s: (0, 0))],
            scratch_shapes=[
                pltpu.VMEM((rows, depth), bf16),
                pltpu.VMEM((2, tile, depth), bf16),
                pltpu.VMEM((2, count, rank, tile), bf16),
                pltpu.VMEM((2, rows, tile), bf16),
                pltpu.SemaphoreType.DMA((2 * top,)),
                pltpu.SemaphoreType.DMA((2, 2 * top, most)),
                pltpu.SemaphoreType.DMA((2,)),
                pltpu.SemaphoreType.DMA((2,)),
            ],
        ),
        out_shape=[
            jax.ShapeDtypeStruct((rows // len(blocks) * count, ff), bf16),
            jax.ShapeDtypeStruct((8, 128), f32),
        ],
        input_output_aliases=aliases,
        **params((2 * rows * depth * span, 2 * (rows * depth + (rows + depth) * span))),
    )(jnp.concatenate([jnp.stack(places).astype(i32), scalars]), *operands)


def add_kernel(pieces, count, slots_ref, *refs):
    term_refs = refs[:pieces]
    a_ref, b_ref, terms, a, b, term_sem, a_sem, b_sem = refs[pieces + 2 :]
    local, _, ff = a.shape

    def load(k):
        return pltpu.make_async_copy(
            term_refs[k // count].at[k % count], terms.at[k], term_sem.at[k]
        )

    def whole(slot, inward):
        pairs = [(a_ref.at[slot], a.at[slot]), (b_ref.at[slot], b.at[slot])]
        return [
            pltpu.make_async_copy(*(pair if inward else pair[::-1]), sem.at[slot])
            for pair, sem in zip(pairs, (a_sem, b_sem))
        ]

    wanted = [slots_ref[k] for k in range(pieces * count)]
    owned = [(slot >= 0) & (slot < local) for slot in wanted]
    hit = []
    for j in range(local):
        any_here = wanted[0] == j
        for slot in wanted[1:]:
            any_here = any_here | (slot == j)
        hit.append(any_here)

    def start(copies):
        for copy in copies:
            copy.start()

    def wait(copies):
        for copy in copies:
            copy.wait()

    for j in range(local):
        pl.when(hit[j])(lambda j=j: start(whole(j, True)))
    for k in range(pieces * count):
        pl.when(owned[k])(lambda k=k: start([load(k)]))
    for j in range(local):
        pl.when(hit[j])(lambda j=j: wait(whole(j, True)))

    def add(k):
        wait([load(k)])
        a[wanted[k]] += terms[k, :, :ff].astype(f32)
        b[wanted[k]] += terms[k, :, ff:].astype(f32)

    for k in range(pieces * count):
        pl.when(owned[k])(lambda k=k: add(k))
    for j in range(local):
        pl.when(hit[j])(lambda j=j: start(whole(j, False)))
    for j in range(local):
        pl.when(hit[j])(lambda j=j: wait(whole(j, False)))


def add_terms(slots, pieces, grad_a, grad_b):
    count, rank, both = pieces[0].shape
    anywhere = pl.BlockSpec(memory_space=pl.ANY)
    n = len(pieces)
    local = grad_a.shape[0]
    return pl.pallas_call(
        functools.partial(add_kernel, n, count),
        grid_spec=pltpu.PrefetchScalarGridSpec(
            num_scalar_prefetch=1,
            grid=(1,),
            in_specs=[anywhere] * (n + 2),
            out_specs=[anywhere] * 2,
            scratch_shapes=[
                pltpu.VMEM((n * count, rank, both), bf16),
                pltpu.VMEM(grad_a.shape, f32),
                pltpu.VMEM(grad_b.shape, f32),
                pltpu.SemaphoreType.DMA((n * count,)),
                pltpu.SemaphoreType.DMA((local,)),
                pltpu.SemaphoreType.DMA((local,)),
            ],
        ),
        out_shape=[
            jax.ShapeDtypeStruct(grad_a.shape, f32),
            jax.ShapeDtypeStruct(grad_b.shape, f32),
        ],
        input_output_aliases={n + 1: 0, n + 2: 1},
        **params((0, n * count * 10 * rank * both)),
    )(slots, *pieces, grad_a, grad_b)


def on_device(
    n_groups,
    n_fsdp,
    n_dp,
    output_gradient,
    hidden,
    frozen_down_weight,
    adapter_first_factors,
    adapter_second_factors,
    island_live_rows,
    island_adapter_ids,
    owner_slot_adapters,
):
    rows, ff = hidden.shape
    d = output_gradient.shape[1]
    count = island_live_rows.shape[0]
    local = adapter_first_factors.shape[0]
    n_slots = owner_slot_adapters.shape[0]
    top = n_dp // 2
    me = lax.axis_index("dp")
    group = lax.axis_index("groups")

    def swap(value, bit, axis="dp", size=n_dp):
        return lax.ppermute(value, axis, [(i, i ^ bit) for i in range(size)])

    def spread(held):
        held = dict(held)
        bit = top // 2
        while bit:
            for r in list(held):
                held[r ^ bit] = swap(held[r], bit)
            bit //= 2
        return held

    match = island_adapter_ids[:, None] == owner_slot_adapters[None, :]
    slots = jnp.sum(jnp.where(match, jnp.arange(n_slots, dtype=i32)[None, :], 0), axis=1)
    far_slots = swap(slots, top)

    cut = (2 * count + 2) // 3
    row_parts = [range(cut), range(cut, count)] if cut < count else [range(count)]
    height = rows // count
    kept = []

    def gather(*after):
        k = len(kept)
        if k < len(row_parts):
            part = row_parts[k]
            mine = output_gradient[part[0] * height : (part[-1] + 1) * height]
            kept.append(lax.all_gather(behind(mine, *after), "fsdp", axis=1, tiled=True))

    gather()

    share = ff // n_groups
    if share % 2048 == 0:
        unit, tile = share // 8, share // 4
        sizes = [unit, 2 * unit, 3 * unit, 2 * unit]
    else:
        tile = share
        sizes = [share]
    parts = [(sum(sizes[:j]), size) for j, size in enumerate(sizes)]

    crossed = []
    turned = []

    def flat(*pieces):
        return [v for piece in pieces for v in piece.values()]

    def cross(*after):
        j = len(crossed)
        if j < len(parts):
            start, size = parts[j]
            piece = lax.dynamic_slice_in_dim(
                frozen_down_weight, group * share + start, size, axis=0
            )
            crossed.append({top: swap(behind(piece, *after), top)})

    def turn(*after):
        j = len(turned)
        if j < len(parts):
            piece = behind(crossed[j][top], *after)
            turned.append([])
            for shift in range(1, n_groups):
                ring = [(i, (i + shift) % n_groups) for i in range(n_groups)]
                turned[j].append({top: lax.ppermute(piece, "groups", ring)})

    def fill(chunks, *after):
        for piece in chunks:
            piece.update(spread({top: behind(piece[top], *after)}))

    cross()

    first = jnp.swapaxes(adapter_first_factors, 1, 2)
    a_near = spread({0: first})
    b_near = spread({0: adapter_second_factors})
    near = sorted(a_near)
    a_near = [a_near[r] for r in near]
    b_near = [b_near[r] for r in near]
    def places(wanted):
        owner = wanted // local
        index = jnp.concatenate([wanted % local] * len(near))
        return index, jnp.where((owner ^ me) < top, owner ^ me, len(near))

    picked = pick(*places(behind(far_slots, *flat(*crossed))), a_near, b_near)
    far = swap(picked, top)
    whole = spread({0: behind(frozen_down_weight, picked)})
    both_slots = spread({0: jnp.concatenate([slots, far_slots])})
    turn()

    ready = behind(slots, *flat(whole, both_slots, *turned[0]))
    part, block_a, grad_a, grad_b = project(
        *places(ready), a_near, b_near, far, hidden, output_gradient
    )
    cross(far, *flat(*turned[0]))
    fill(crossed[:1], far)
    fill(turned[0], far)
    sums = [part]
    bit = 1
    while bit < n_fsdp:
        sums.append(swap(sums[-1], bit, "fsdp", n_fsdp))
        if 2 * bit < n_fsdp:
            sums.append(sums[-2] + sums[-1])
        bit *= 2
    total, other = sums[-2:]
    past = [sums[2], *flat(*crossed[:2], *turned[0])]
    cross(*past)
    turn(*past)
    fill(crossed[1:2], *past)
    gather(other)
    past = [other, *flat(*crossed[:3], *sum(turned, []))]
    cross(*past)
    turn(*past)
    fill(crossed[2:3], *past)
    for pieces in turned[1:2]:
        fill(pieces, *past)
    terms, coef = block_terms(island_live_rows, total, other, hidden, output_gradient)
    far_terms = swap(terms, top)
    near_terms = spread({0: behind(terms, *flat(*crossed[:3]))})

    relative = [both_slots[r][:count] for r in near] + [both_slots[r][count:] for r in near]
    relative = jnp.concatenate(relative) - me * local
    edge = count * len(near)
    grad_a, grad_b = add_terms(
        relative[:edge], [near_terms[r] for r in near], grad_a, grad_b
    )

    scalars = jnp.concatenate([jnp.stack([me ^ r for r in range(n_dp)]).astype(i32), island_live_rows])
    grad_hidden = token = None

    def multiply(k, *where):
        nonlocal grad_hidden, token
        chunks, tiles, places = [], [], []
        for shift, t in where:
            start = lax.rem(group + n_groups - shift, n_groups) * share
            places.append(start // tile + t)
            tiles.append([])
            for j, (first, size) in enumerate(parts):
                low, high = max(first, t * tile), min(first + size, (t + 1) * tile)
                if low < high:
                    if (shift, j) not in chunks:
                        chunks.append((shift, j))
                    tiles[-1].append((chunks.index((shift, j)), low - first, high - low))
        pieces = [turned[j][shift - 1] if shift else crossed[j] for shift, j in chunks]
        grad_hidden, token = base(
            places, scalars, kept[k], whole, pieces, tiles, tile, coef, block_a,
            list(row_parts[k]), grad_hidden, token,
        )

    last = share // tile - 1
    others = range(1, n_groups)
    if last:
        multiply(0, *[(0, t) for t in range(last)], *[(g, 0) for g in others])
        past = [token, *flat(*crossed)]
        turn(*past)
        fill(crossed[3:], *past)
        for pieces in turned[2:3]:
            fill(pieces, *flat(*crossed))
        multiply(0, (0, last), *[(g, t) for g in others for t in range(1, last)])
        for k in range(1, len(row_parts)):
            multiply(
                k, *[(0, t) for t in range(last + 1)], *[(g, t) for g in others for t in range(last)]
            )
        for pieces in turned[3:]:
            fill(pieces, token)
        early = token
        for k in range(len(row_parts)):
            multiply(k, *[(g, last) for g in others])
    else:
        for k in range(len(row_parts)):
            multiply(k, *[(g, 0) for g in range(n_groups)])
        early = token

    all_far = spread({top: behind(far_terms, early)})
    grad_a, grad_b = add_terms(
        relative[edge:], [all_far[r + top] for r in near], grad_a, grad_b
    )
    return grad_hidden, jnp.swapaxes(grad_a, 1, 2), grad_b


def solution(mesh):
    placed = (
        P(("groups", "dp"), "fsdp"),
        P(("groups", "dp"), "fsdp"),
        P("fsdp", "dp"),
        P(("groups", "dp"), "fsdp", None),
        P(("groups", "dp"), None, "fsdp"),
        P(("groups", "dp")),
        P(("groups", "dp")),
        P("groups"),
    )
    sizes = [mesh.shape[name] for name in ("groups", "fsdp", "dp")]
    return jax.shard_map(
        functools.partial(on_device, *sizes),
        mesh=mesh,
        in_specs=placed,
        out_specs=(
            P(("groups", "dp"), "fsdp"),
            P(("groups", "dp"), "fsdp", None),
            P(("groups", "dp"), None, "fsdp"),
        ),
        check_vma=False,
    )
```

profile of v0, /device:TPU:11, one launch (start us, length us, event | category | flops | bytes accessed | tf_op | source)
XLA Modules:
  0.0 285.9 jit_solution(17825427297644374546)
XLA Ops:
  7.2 0.7 collective-permute-start.2
  8.0 1.1 constant_dynamic-slice_fusion.3
  9.1 0.3 collective-permute-start.1
  9.4 0.9 select_reduce_fusion
  10.3 1.3 collective-permute-start
  11.6 10.7 %collective-permute-done = s32[3]{0:T(128)S(1)} collective-permute-done((s32[3]{0:T(128)S(1)}, s32[3]{0:T(128)S(1)}, u32[]{:S(2)}, u32[]{:S(2)}) %collective-permute-start) | collective-permute-done | bytes 44 | tf_op jit(solution)/shard_map/ppermute | solution.py:472
  22.3 0.6 compare_select_fusion.1
  22.8 0.6 pad_add_fusion.index_ref
  23.4 1.0 copy-done.6
  24.4 4.9 %shard_map.103 = bf16[3,64,5120]{2,1,0:T(8,128)(2,1)} custom-call(s32[6]{0:T(128)} %pad_add_fusion.index_ref, s32[3]{0:T(128)} %get-tuple-element.83.source_ref, bf16[8,64,4096]{2,1,0:T(8,128)(2,1)} %bitcast.16, bf16[8,64,4096]{2,1,0:T(8,128)(2,1)} %collective-permute-done.2.refs_1_, bf16[8,64,1024]{2,1,0:T(8,128)(2,1)} %refs_2_.3, ...), custom_call_target="tpu_custom_call" | custom-call | bytes 5898240 | tf_op jit(solution)/shard_map/pallas_call | solution.py:54
  29.3 1.3 collective-permute-start.4
  30.6 1.0 slice.19
  31.7 0.3 collective-permute-start.7
  32.0 1.2 collective-permute-start.6
  33.2 3.1 %constant_dynamic-slice_fusion.1 = (bf16[512,1024]{1,0:T(8,128)(2,1)}, bf16[512,1024]{1,0:T(8,128)(2,1)}) fusion(bf16[4096,1024]{1,0:T(8,128)(2,1)} %refs_0_.4, s32[]{:T(128)S(6)} %select_n.73, s32[]{:T(128)S(6)} %select_n.72), kind=kLoop, calls=%fused_computation.14 | loop fusion | bytes 4194312 | tf_op jit(solution)/shard_map/dynamic_slice | solution.py:520
  36.3 9.1 %collective-permute-done.6.refs_8_.refs_10_ = bf16[256,1024]{1,0:T(8,128)(2,1)S(1)} collective-permute-done((bf16[256,1024]{1,0:T(8,128)(2,1)S(1)}, bf16[256,1024]{1,0:T(8,128)(2,1)S(1)}, u32[]{:S(2)}, u32[]{:S(2)}) %collective-permute-start.6) | collective-permute-done | bytes 524320 | tf_op jit(solution)/shard_map/ppermute | solution.py:532
  45.4 31.2 %collective-permute-done.7.refs_4_ = bf16[3,64,5120]{2,1,0:T(8,128)(2,1)} collective-permute-done((bf16[3,64,5120]{2,1,0:T(8,128)(2,1)}, bf16[3,64,5120]{2,1,0:T(8,128)(2,1)}, u32[]{:S(2)}, u32[]{:S(2)}) %collective-permute-start.7) | collective-permute-done | bytes 1966112 | tf_op jit(solution)/shard_map/ppermute | solution.py:472
  76.5 0.3 collective-permute-start.11
  76.9 1.1 collective-permute-start.5
  78.0 0.4 collective-permute-start.12
  78.4 0.3 collective-permute-done.5
  78.7 0.6 compare_select_fusion
  79.3 0.6 pad_add_fusion.2.index_ref
  79.9 11.8 %shard_map.104 = (f32[3,256,128]{2,1,0:T(8,128)}, bf16[3,64,4096]{2,1,0:T(8,128)(2,1)}, f32[8,64,4096]{2,1,0:T(8,128)}, f32[8,64,1024]{2,1,0:T(8,128)}) custom-call(s32[6]{0:T(128)} %pad_add_fusion.2.index_ref, s32[3]{0:T(128)} %get-tuple-element.81.source_ref, bf16[8,64,4096]{2,1,0:T(8,128)(2,1)} %bitcast.17, ...), custom_call_target="tpu_custom_call" | custom-call | flops 503316480 | bytes 15728640 | tf_op jit(solution)/shard_map/pallas_call | solution.py:121
  91.8 1.6 constant_dynamic-slice_fusion
  93.4 24.3 %collective-permute-done.8 = f32[3,256,128]{2,1,0:T(8,128)} collective-permute-done((f32[3,256,128]{2,1,0:T(8,128)}, f32[3,256,128]{2,1,0:T(8,128)}, u32[]{:S(2)}, u32[]{:S(2)}) %collective-permute-start.8) | collective-permute-done | bytes 393248 | tf_op jit(solution)/shard_map/ppermute | solution.py:472
  117.7 1.0 add.93.here_ref
  118.8 0.8 copy-done.12
  119.6 0.2 copy-done.13
  119.8 0.3 collective-permute-start.14
  120.1 0.7 collective-permute-start.13
  120.7 1.2 collective-permute-start.15
  121.9 3.1 %collective-permute-start.9 = (f32[3,256,128]{2,1,0:T(8,128)S(1)}, f32[3,256,128]{2,1,0:T(8,128)S(1)}, u32[]{:S(2)}, u32[]{:S(2)}) collective-permute-start(f32[3,256,128]{2,1,0:T(8,128)S(1)} %add.93.here_ref), channel_id=1, source_target_pairs={{0,8},{4,12},{8,0},{12,4},{1,9},{5,13},{9,1},{13,5},{2,10},{6,14},... | collective-permute-start | bytes 1179656 | tf_op jit(solution)/shard_map/ppermute | solution.py:472
  125.1 16.3 %collective-permute-done.9.there_ref = f32[3,256,128]{2,1,0:T(8,128)S(1)} collective-permute-done((f32[3,256,128]{2,1,0:T(8,128)S(1)}, f32[3,256,128]{2,1,0:T(8,128)S(1)}, u32[]{:S(2)}, u32[]{:S(2)}) %collective-permute-start.9) | collective-permute-done | bytes 393248 | tf_op jit(solution)/shard_map/ppermute | solution.py:472
  141.3 4.3 %collective-permute-done.15.refs_10_.refs_4_.refs_12_ = bf16[512,1024]{1,0:T(8,128)(2,1)S(1)} collective-permute-done((bf16[512,1024]{1,0:T(8,128)(2,1)S(1)}, bf16[512,1024]{1,0:T(8,128)(2,1)S(1)}, u32[]{:S(2)}, u32[]{:S(2)}) %collective-permute-start.15) | collective-permute-done | bytes 1048608 | tf_op jit(solution)/shard_map/ppermute | solution.py:532
  145.6 9.8 %collective-permute-done.14.refs_6_ = bf16[768,1024]{1,0:T(8,128)(2,1)} collective-permute-done((bf16[768,1024]{1,0:T(8,128)(2,1)S(1)}, bf16[768,1024]{1,0:T(8,128)(2,1)}, u32[]{:S(2)}, u32[]{:S(2)}) %collective-permute-start.14) | collective-permute-done | bytes 1572896 | tf_op jit(solution)/shard_map/ppermute | solution.py:472
  155.5 1.2 collective-permute-start.17
  156.8 0.3 collective-permute-start.16
  157.1 0.6 concatenate.35.scalars_ref
  157.6 7.0 %shard_map.105 = (bf16[3,64,5120]{2,1,0:T(8,128)(2,1)}, bf16[3,256,64]{2,1,0:T(8,128)(2,1)}) custom-call(s32[3]{0:T(128)} %live_ref.1, f32[3,256,128]{2,1,0:T(8,128)} %copy-done.14, f32[3,256,128]{2,1,0:T(8,128)} %copy-done.15, bf16[768,4096]{1,0:T(8,128)(2,1)} %hid_ref.1, bf16[768,1024]{1,0:T(8,128)(2,1)} %grad_ref.1), custom_call_target="tpu_custom_call" | custom-call | flops 503316480 | bytes 9830400 | tf_op jit(solution)/shard_map/pallas_call | solution.py:182
  164.7 1.3 collective-permute-start.21
  165.9 1.0 copy-done.2
  166.9 17.2 %shard_map.106 = (bf16[768,4096]{1,0:T(8,128)(2,1)}, f32[8,128]{1,0:T(8,128)}) custom-call(s32[11]{0:T(128)} %concatenate.35.scalars_ref, bf16[512,4096]{1,0:T(8,128)(2,1)} %all-gather.5.cloned.1.call-done.kept_ref, bf16[4096,1024]{1,0:T(8,128)(2,1)} %refs_0_.4, bf16[4096,1024]{1,0:T(8,128)(2,1)} %collective-permute-done.4.refs_1_, ...), custom_call_target="tpu_custom_call" | custom-call | flops 8589934592 | bytes 23068672 | tf_op jit(solution)/shard_map/pallas_call | solution.py:338
  184.1 1.1 collective-permute-start.20
  185.2 1.9 slice.18
  187.1 13.2 %collective-permute-done.21.refs_6_.refs_14_ = bf16[768,1024]{1,0:T(8,128)(2,1)} collective-permute-done((bf16[768,1024]{1,0:T(8,128)(2,1)}, bf16[768,1024]{1,0:T(8,128)(2,1)}, u32[]{:S(2)}, u32[]{:S(2)}) %collective-permute-start.21) | collective-permute-done | bytes 1572896 | tf_op jit(solution)/shard_map/ppermute | solution.py:532
  200.3 1.6 collective-permute-start.22
  201.9 1.2 collective-permute-start.24
  203.1 0.6 concatenate.37.scalars_ref
  203.7 0.6 concatenate.36.scalars_ref
  204.3 1.2 collective-permute-start.19
  205.5 0.6 collective-permute-start.26
  206.1 1.2 copy-done.3
  207.3 14.5 %shard_map.107 = (bf16[768,4096]{1,0:T(8,128)(2,1)}, f32[8,128]{1,0:T(8,128)}) custom-call(s32[10]{0:T(128)} %concatenate.37.scalars_ref, bf16[512,4096]{1,0:T(8,128)(2,1)} %all-gather.5.cloned.1.call-done.kept_ref, bf16[4096,1024]{1,0:T(8,128)(2,1)} %refs_0_.4, bf16[4096,1024]{1,0:T(8,128)(2,1)} %collective-permute-done.4.refs_1_, ...), custom_call_target="tpu_custom_call", output_to_operand_aliasing={{0}: (13, {})} | custom-call | flops 6442450944 | bytes 18350080 | tf_op jit(solution)/shard_map/pallas_call | solution.py:338
  221.8 10.0 %all-gather.3.cloned.1.call-done.kept_ref = bf16[256,4096]{1,0:T(8,128)(2,1)} async-done(((bf16[256,1024]{1,0:T(8,128)(2,1)}), bf16[256,4096]{1,0:T(8,128)(2,1)}) %all-gather.3.cloned.1.call-update) | async-done | bytes 2097168 | tf_op jit(solution)/shard_map/all_gather | solution.py:497
  231.7 18.8 %shard_map.108 = (bf16[768,4096]{1,0:T(8,128)(2,1)}, f32[8,128]{1,0:T(8,128)}) custom-call(s32[14]{0:T(128)} %concatenate.36.scalars_ref, bf16[256,4096]{1,0:T(8,128)(2,1)} %all-gather.3.cloned.1.call-done.kept_ref, bf16[4096,1024]{1,0:T(8,128)(2,1)} %refs_0_.4, bf16[4096,1024]{1,0:T(8,128)(2,1)} %collective-permute-done.4.refs_1_, ...), custom_call_target="tpu_custom_call", output_to_operand_aliasing={{0}: (21, {})} | custom-call | flops 7516192768 | bytes 33292288 | tf_op jit(solution)/shard_map/pallas_call | solution.py:338
  250.5 1.0 collective-permute-start.25
  251.6 0.8 concatenate.31.scalars_ref
  252.6 0.6 fusion
  253.2 5.9 %shard_map.111 = (f32[8,64,4096]{2,1,0:T(8,128)}, f32[8,64,1024]{2,1,0:T(8,128)}) custom-call(s32[6]{0:T(128)} %get-tuple-element.77.slots_ref, bf16[3,64,5120]{2,1,0:T(8,128)(2,1)} %get-tuple-element.68.refs_0_, bf16[3,64,5120]{2,1,0:T(8,128)(2,1)} %collective-permute-done.26.refs_1_, ...), custom_call_target="tpu_custom_call", output_to_operand_aliasing={{0}: (3, {}), {1}: (4, {})} | custom-call | bytes 19660800 | tf_op jit(solution)/shard_map/pallas_call | solution.py:424
  259.1 1.0 copy-done.8
  260.1 8.0 %shard_map.109 = (bf16[768,4096]{1,0:T(8,128)(2,1)}, f32[8,128]{1,0:T(8,128)}) custom-call(s32[8]{0:T(128)} %concatenate.31.scalars_ref, bf16[512,4096]{1,0:T(8,128)(2,1)} %all-gather.5.cloned.1.call-done.kept_ref, bf16[4096,1024]{1,0:T(8,128)(2,1)} %refs_0_.4, bf16[4096,1024]{1,0:T(8,128)(2,1)} %collective-permute-done.4.refs_1_, ...), custom_call_target="tpu_custom_call", output_to_operand_aliasing={{0}: (9, {})} | custom-call | flops 2147483648 | bytes 8912896 | tf_op jit(solution)/shard_map/pallas_call | solution.py:338
  268.1 6.4 %shard_map.110 = (bf16[768,4096]{1,0:T(8,128)(2,1)}, f32[8,128]{1,0:T(8,128)}) custom-call(s32[8]{0:T(128)} %concatenate.31.scalars_ref, bf16[256,4096]{1,0:T(8,128)(2,1)} %all-gather.3.cloned.1.call-done.kept_ref, bf16[4096,1024]{1,0:T(8,128)(2,1)} %refs_0_.4, bf16[4096,1024]{1,0:T(8,128)(2,1)} %collective-permute-done.4.refs_1_, ...), custom_call_target="tpu_custom_call", output_to_operand_aliasing={{0}: (9, {})} | custom-call | flops 1073741824 | bytes 6553600 | tf_op jit(solution)/shard_map/pallas_call | solution.py:338
  274.5 4.6 %shard_map.112 = (f32[8,64,4096]{2,1,0:T(8,128)}, f32[8,64,1024]{2,1,0:T(8,128)}) custom-call(s32[6]{0:T(128)} %get-tuple-element.78.slots_ref, bf16[3,64,5120]{2,1,0:T(8,128)(2,1)} %collective-permute-done.24.refs_0_, bf16[3,64,5120]{2,1,0:T(8,128)(2,1)} %collective-permute-done.25.refs_1_, ...), custom_call_target="tpu_custom_call", output_to_operand_aliasing={{0}: (3, {}), {1}: (4, {})} | custom-call | bytes 19660800 | tf_op jit(solution)/shard_map/pallas_call | solution.py:424
  (63 shorter events, 0.8 us)
Async XLA Ops:
  7.2 158.8 %all-gather.5.cloned.1.call-start = ((), (), s32[]{:S(2)}) async-start(), calls=%async_computation.1 | async-start | bytes 5242880 | tf_op jit(solution)/shard_map/all_gather | solution.py:497
  7.2 16.2 %collective-permute-start.2 = (bf16[8,64,4096]{2,1,0:T(8,128)(2,1)}, bf16[8,64,4096]{2,1,0:T(8,128)(2,1)}, u32[]{:S(2)}, u32[]{:S(2)}) collective-permute-start(bf16[8,64,4096]{2,1,0:T(8,128)(2,1)} %bitcast.15), channel_id=1, source_target_pairs={{0,1},{1,0},{2,3},{3,2},{4,5},{5,4},{6,7},{7,6},{8,9},{9,8},{10,11... | collective-permute-start | bytes 12582920 | tf_op jit(solution)/shard_map/ppermute | solution.py:472
  8.0 15.5 %collective-permute-start.3 = (bf16[8,64,1024]{2,1,0:T(8,128)(2,1)}, bf16[8,64,1024]{2,1,0:T(8,128)(2,1)S(1)}, u32[]{:S(2)}, u32[]{:S(2)}) collective-permute-start(bf16[8,64,1024]{2,1,0:T(8,128)(2,1)} %refs_2_.3), channel_id=1, source_target_pairs={{0,1},{1,0},{2,3},{3,2},{4,5},{5,4},{6,7},{7,6},{8,9},{9,8},{10,11... | collective-permute-start | bytes 3145736 | tf_op jit(solution)/shard_map/ppermute | solution.py:472
  9.1 13.1 %collective-permute-start.1 = (bf16[256,1024]{1,0:T(8,128)(2,1)S(1)}, bf16[256,1024]{1,0:T(8,128)(2,1)S(1)}, u32[]{:S(2)}, u32[]{:S(2)}) collective-permute-start(bf16[256,1024]{1,0:T(8,128)(2,1)S(1)} %constant_dynamic-slice_fusion.3), channel_id=1, source_target_pairs={{0,2},{1,3},{2,0},{3,1},{4,6},{5,7},{6,4},{7,5},{8,10},{9,11},{10,... | collective-permute-start | bytes 1572872 | tf_op jit(solution)/shard_map/ppermute | solution.py:472
  10.3 12.0 %collective-permute-start = (s32[3]{0:T(128)S(1)}, s32[3]{0:T(128)S(1)}, u32[]{:S(2)}, u32[]{:S(2)}) collective-permute-start(s32[3]{0:T(128)S(1)} %select_reduce_fusion), channel_id=1, source_target_pairs={{0,2},{1,3},{2,0},{3,1},{4,6},{5,7},{6,4},{7,5},{8,10},{9,11},{10,... | collective-permute-start | bytes 44 | tf_op jit(solution)/shard_map/ppermute | solution.py:472
  22.3 9.8 %copy-start.9 = (bf16[256,1024]{1,0:T(8,128)(2,1)}, bf16[256,1024]{1,0:T(8,128)(2,1)S(1)}, u32[]{:S(2)}) copy-start(bf16[256,1024]{1,0:T(8,128)(2,1)S(1)} %collective-permute-done.1.refs_2_) | copy-start | bytes 1572868
  23.4 1.0 copy-start.6
  24.4 6.2 %copy-start = (bf16[768,1024]{1,0:T(8,128)(2,1)S(1)}, bf16[768,1024]{1,0:T(8,128)(2,1)}, u32[]{:S(2)}) copy-start(bf16[768,1024]{1,0:T(8,128)(2,1)} %grad_ref.1) | copy-start | bytes 4718596
  29.3 49.5 %collective-permute-start.4 = (bf16[4096,1024]{1,0:T(8,128)(2,1)}, bf16[4096,1024]{1,0:T(8,128)(2,1)}, u32[]{:S(2)}, u32[]{:S(2)}) collective-permute-start(bf16[4096,1024]{1,0:T(8,128)(2,1)} %refs_0_.4), channel_id=1, source_target_pairs={{0,1},{1,0},{2,3},{3,2},{4,5},{5,4},{6,7},{7,6},{8,9},{9,8},{10,11... | collective-permute-start | bytes 25165832 | tf_op jit(solution)/shard_map/ppermute | solution.py:472
  31.6 200.1 %all-gather.3.cloned.1.call-start = ((), (), s32[]{:S(2)}) async-start(), calls=%async_computation | async-start | bytes 2621440 | tf_op jit(solution)/shard_map/all_gather | solution.py:497
  31.7 44.8 %collective-permute-start.7 = (bf16[3,64,5120]{2,1,0:T(8,128)(2,1)}, bf16[3,64,5120]{2,1,0:T(8,128)(2,1)}, u32[]{:S(2)}, u32[]{:S(2)}) collective-permute-start(bf16[3,64,5120]{2,1,0:T(8,128)(2,1)} %shard_map.103), channel_id=1, source_target_pairs={{0,2},{1,3},{2,0},{3,1},{4,6},{5,7},{6,4},{7,5},{8,10},{9,11},{10,... | collective-permute-start | bytes 5898248 | tf_op jit(solution)/shard_map/ppermute | solution.py:472
  32.0 13.3 %collective-permute-start.6 = (bf16[256,1024]{1,0:T(8,128)(2,1)S(1)}, bf16[256,1024]{1,0:T(8,128)(2,1)S(1)}, u32[]{:S(2)}, u32[]{:S(2)}) collective-permute-start(bf16[256,1024]{1,0:T(8,128)(2,1)S(1)} %collective-permute-done.1.refs_2_), channel_id=1, source_target_pairs={{0,16},{16,0},{1,17},{17,1},{2,18},{18,2},{3,19},{19,3},{4,20},{20... | collective-permute-start | bytes 1572872 | tf_op jit(solution)/shard_map/ppermute | solution.py:532
  33.2 44.7 %copy-start.10 = (bf16[256,1024]{1,0:T(8,128)(2,1)S(1)}, bf16[256,1024]{1,0:T(8,128)(2,1)}, u32[]{:S(2)}) copy-start(bf16[256,1024]{1,0:T(8,128)(2,1)} %copy-done.9) | copy-start | bytes 1572868
  45.4 46.3 %copy-start.11 = (bf16[256,1024]{1,0:T(8,128)(2,1)}, bf16[256,1024]{1,0:T(8,128)(2,1)S(1)}, u32[]{:S(2)}) copy-start(bf16[256,1024]{1,0:T(8,128)(2,1)S(1)} %collective-permute-done.6.refs_8_.refs_10_) | copy-start | bytes 1572868
  76.5 42.3 %collective-permute-start.11 = (bf16[512,1024]{1,0:T(8,128)(2,1)}, bf16[512,1024]{1,0:T(8,128)(2,1)S(1)}, u32[]{:S(2)}, u32[]{:S(2)}) collective-permute-start(bf16[512,1024]{1,0:T(8,128)(2,1)} %get-tuple-element.45), channel_id=1, source_target_pairs={{0,2},{1,3},{2,0},{3,1},{4,6},{5,7},{6,4},{7,5},{8,10},{9,11},{10,... | collective-permute-start | bytes 3145736 | tf_op jit(solution)/shard_map/ppermute | solution.py:472
  76.9 1.9 collective-permute-start.5
  77.9 40.8 %collective-permute-start.10 = (bf16[256,1024]{1,0:T(8,128)(2,1)S(1)}, bf16[256,1024]{1,0:T(8,128)(2,1)S(1)}, u32[]{:S(2)}, u32[]{:S(2)}) collective-permute-start(bf16[256,1024]{1,0:T(8,128)(2,1)S(1)} %copy-done.10), channel_id=1, source_target_pairs={{0,1},{1,0},{2,3},{3,2},{4,5},{5,4},{6,7},{7,6},{8,9},{9,8},{10,11... | collective-permute-start | bytes 1572872 | tf_op jit(solution)/shard_map/ppermute | solution.py:472
  78.0 40.8 %collective-permute-start.12 = (bf16[256,1024]{1,0:T(8,128)(2,1)S(1)}, bf16[256,1024]{1,0:T(8,128)(2,1)S(1)}, u32[]{:S(2)}, u32[]{:S(2)}) collective-permute-start(bf16[256,1024]{1,0:T(8,128)(2,1)S(1)} %collective-permute-done.6.refs_8_.refs_10_), channel_id=1, source_target_pairs={{0,1},{1,0},{2,3},{3,2},{4,5},{5,4},{6,7},{7,6},{8,9},{9,8},{10,11... | collective-permute-start | bytes 1572872 | tf_op jit(solution)/shard_map/ppermute | solution.py:472
  91.7 26.0 %collective-permute-start.8 = (f32[3,256,128]{2,1,0:T(8,128)}, f32[3,256,128]{2,1,0:T(8,128)}, u32[]{:S(2)}, u32[]{:S(2)}) collective-permute-start(f32[3,256,128]{2,1,0:T(8,128)} %get-tuple-element.42), channel_id=1, source_target_pairs={{0,4},{4,0},{8,12},{12,8},{1,5},{5,1},{9,13},{13,9},{2,6},{6,2},{1... | collective-permute-start | bytes 1179656 | tf_op jit(solution)/shard_map/ppermute | solution.py:472
  91.8 25.9 %copy-start.16 = (f32[3,256,128]{2,1,0:T(8,128)S(1)}, f32[3,256,128]{2,1,0:T(8,128)}, u32[]{:S(2)}) copy-start(f32[3,256,128]{2,1,0:T(8,128)} %get-tuple-element.42) | copy-start | bytes 1179652
  91.8 65.3 %copy-start.17 = (s32[3]{0:T(128)S(1)}, s32[3]{0:T(128)}, u32[]{:S(2)}) copy-start(s32[3]{0:T(128)} %live_ref.1) | copy-start | bytes 40
  118.7 38.9 %copy-start.14 = (f32[3,256,128]{2,1,0:T(8,128)}, f32[3,256,128]{2,1,0:T(8,128)S(1)}, u32[]{:S(2)}) copy-start(f32[3,256,128]{2,1,0:T(8,128)S(1)} %add.93.here_ref) | copy-start | bytes 1179652
  118.8 0.9 copy-start.12
  118.8 1.0 copy-start.13
  119.8 44.9 %copy-start.4 = (bf16[512,1024]{1,0:T(8,128)(2,1)}, bf16[512,1024]{1,0:T(8,128)(2,1)S(1)}, u32[]{:S(2)}) copy-start(bf16[512,1024]{1,0:T(8,128)(2,1)S(1)} %collective-permute-done.11.refs_4_) | copy-start | bytes 3145732
  119.8 35.7 %collective-permute-start.14 = (bf16[768,1024]{1,0:T(8,128)(2,1)S(1)}, bf16[768,1024]{1,0:T(8,128)(2,1)}, u32[]{:S(2)}, u32[]{:S(2)}) collective-permute-start(bf16[768,1024]{1,0:T(8,128)(2,1)S(1)} %constant_dynamic-slice_fusion), channel_id=1, source_target_pairs={{0,2},{1,3},{2,0},{3,1},{4,6},{5,7},{6,4},{7,5},{8,10},{9,11},{10,... | collective-permute-start | bytes 4718600 | tf_op jit(solution)/shard_map/ppermute | solution.py:472
  120.1 21.3 %collective-permute-start.13 = (bf16[512,1024]{1,0:T(8,128)(2,1)S(1)}, bf16[512,1024]{1,0:T(8,128)(2,1)S(1)}, u32[]{:S(2)}, u32[]{:S(2)}) collective-permute-start(bf16[512,1024]{1,0:T(8,128)(2,1)S(1)} %collective-permute-done.11.refs_4_), channel_id=1, source_target_pairs={{0,1},{1,0},{2,3},{3,2},{4,5},{5,4},{6,7},{7,6},{8,9},{9,8},{10,11... | collective-permute-start | bytes 3145736 | tf_op jit(solution)/shard_map/ppermute | solution.py:472
  120.7 24.9 %collective-permute-start.15 = (bf16[512,1024]{1,0:T(8,128)(2,1)S(1)}, bf16[512,1024]{1,0:T(8,128)(2,1)S(1)}, u32[]{:S(2)}, u32[]{:S(2)}) collective-permute-start(bf16[512,1024]{1,0:T(8,128)(2,1)S(1)} %collective-permute-done.11.refs_4_), channel_id=1, source_target_pairs={{0,16},{16,0},{1,17},{17,1},{2,18},{18,2},{3,19},{19,3},{4,20},{20... | collective-permute-start | bytes 3145736 | tf_op jit(solution)/shard_map/ppermute | solution.py:532
  121.9 19.4 %collective-permute-start.9 = (f32[3,256,128]{2,1,0:T(8,128)S(1)}, f32[3,256,128]{2,1,0:T(8,128)S(1)}, u32[]{:S(2)}, u32[]{:S(2)}) collective-permute-start(f32[3,256,128]{2,1,0:T(8,128)S(1)} %add.93.here_ref), channel_id=1, source_target_pairs={{0,8},{4,12},{8,0},{12,4},{1,9},{5,13},{9,1},{13,5},{2,10},{6,14},... | collective-permute-start | bytes 1179656 | tf_op jit(solution)/shard_map/ppermute | solution.py:472
  141.3 14.2 %copy-start.15 = (f32[3,256,128]{2,1,0:T(8,128)}, f32[3,256,128]{2,1,0:T(8,128)S(1)}, u32[]{:S(2)}) copy-start(f32[3,256,128]{2,1,0:T(8,128)S(1)} %collective-permute-done.9.there_ref) | copy-start | bytes 1179652
  141.3 14.2 %copy-start.5 = (bf16[512,1024]{1,0:T(8,128)(2,1)}, bf16[512,1024]{1,0:T(8,128)(2,1)S(1)}, u32[]{:S(2)}) copy-start(bf16[512,1024]{1,0:T(8,128)(2,1)S(1)} %collective-permute-done.13.refs_5_) | copy-start | bytes 3145732
  145.6 19.0 %copy-start.1 = (bf16[512,1024]{1,0:T(8,128)(2,1)}, bf16[512,1024]{1,0:T(8,128)(2,1)S(1)}, u32[]{:S(2)}) copy-start(bf16[512,1024]{1,0:T(8,128)(2,1)S(1)} %collective-permute-done.15.refs_10_.refs_4_.refs_12_) | copy-start | bytes 3145732
  155.5 10.4 %collective-permute-start.17 = (bf16[768,1024]{1,0:T(8,128)(2,1)}, bf16[768,1024]{1,0:T(8,128)(2,1)}, u32[]{:S(2)}, u32[]{:S(2)}) collective-permute-start(bf16[768,1024]{1,0:T(8,128)(2,1)} %collective-permute-done.14.refs_6_), channel_id=1, source_target_pairs={{0,1},{1,0},{2,3},{3,2},{4,5},{5,4},{6,7},{7,6},{8,9},{9,8},{10,11... | collective-permute-start | bytes 4718600 | tf_op jit(solution)/shard_map/ppermute | solution.py:472
  156.7 9.2 %collective-permute-start.18 = (bf16[512,1024]{1,0:T(8,128)(2,1)S(1)}, bf16[512,1024]{1,0:T(8,128)(2,1)S(1)}, u32[]{:S(2)}, u32[]{:S(2)}) collective-permute-start(bf16[512,1024]{1,0:T(8,128)(2,1)S(1)} %collective-permute-done.15.refs_10_.refs_4_.refs_12_), channel_id=1, source_target_pairs={{0,1},{1,0},{2,3},{3,2},{4,5},{5,4},{6,7},{7,6},{8,9},{9,8},{10,11... | collective-permute-start | bytes 3145736 | tf_op jit(solution)/shard_map/ppermute | solution.py:472
  156.8 27.3 %collective-permute-start.16 = (bf16[512,1024]{1,0:T(8,128)(2,1)}, bf16[512,1024]{1,0:T(8,128)(2,1)}, u32[]{:S(2)}, u32[]{:S(2)}) collective-permute-start(bf16[512,1024]{1,0:T(8,128)(2,1)} %get-tuple-element.49), channel_id=1, source_target_pairs={{0,2},{1,3},{2,0},{3,1},{4,6},{5,7},{6,4},{7,5},{8,10},{9,11},{10,... | collective-permute-start | bytes 3145736 | tf_op jit(solution)/shard_map/ppermute | solution.py:472
  164.7 35.6 %collective-permute-start.21 = (bf16[768,1024]{1,0:T(8,128)(2,1)}, bf16[768,1024]{1,0:T(8,128)(2,1)}, u32[]{:S(2)}, u32[]{:S(2)}) collective-permute-start(bf16[768,1024]{1,0:T(8,128)(2,1)} %collective-permute-done.14.refs_6_), channel_id=1, source_target_pairs={{0,16},{16,0},{1,17},{17,1},{2,18},{18,2},{3,19},{19,3},{4,20},{20... | collective-permute-start | bytes 4718600 | tf_op jit(solution)/shard_map/ppermute | solution.py:532
  165.9 1.0 copy-start.2
  166.9 36.1 %copy-start.18 = (s32[3]{0:T(128)S(1)}, s32[3]{0:T(128)}, u32[]{:S(2)}) copy-start(s32[3]{0:T(128)} %live_ref.1) | copy-start | bytes 40
  184.1 16.1 %collective-permute-start.20 = (bf16[512,1024]{1,0:T(8,128)(2,1)}, bf16[512,1024]{1,0:T(8,128)(2,1)}, u32[]{:S(2)}, u32[]{:S(2)}) collective-permute-start(bf16[512,1024]{1,0:T(8,128)(2,1)} %collective-permute-done.16.refs_2_.refs_8_), channel_id=1, source_target_pairs={{0,1},{1,0},{2,3},{3,2},{4,5},{5,4},{6,7},{7,6},{8,9},{9,8},{10,11... | collective-permute-start | bytes 3145736 | tf_op jit(solution)/shard_map/ppermute | solution.py:472
  200.3 5.8 %collective-permute-start.22 = (bf16[768,1024]{1,0:T(8,128)(2,1)}, bf16[768,1024]{1,0:T(8,128)(2,1)S(1)}, u32[]{:S(2)}, u32[]{:S(2)}) collective-permute-start(bf16[768,1024]{1,0:T(8,128)(2,1)} %collective-permute-done.21.refs_6_.refs_14_), channel_id=1, source_target_pairs={{0,1},{1,0},{2,3},{3,2},{4,5},{5,4},{6,7},{7,6},{8,9},{9,8},{10,11... | collective-permute-start | bytes 4718600 | tf_op jit(solution)/shard_map/ppermute | solution.py:472
  201.9 48.6 %collective-permute-start.24 = (bf16[3,64,5120]{2,1,0:T(8,128)(2,1)}, bf16[3,64,5120]{2,1,0:T(8,128)(2,1)}, u32[]{:S(2)}, u32[]{:S(2)}) collective-permute-start(bf16[3,64,5120]{2,1,0:T(8,128)(2,1)} %get-tuple-element.68.refs_0_), channel_id=1, source_target_pairs={{0,2},{1,3},{2,0},{3,1},{4,6},{5,7},{6,4},{7,5},{8,10},{9,11},{10,... | collective-permute-start | bytes 5898248 | tf_op jit(solution)/shard_map/ppermute | solution.py:472
  204.3 47.2 %collective-permute-start.19 = (bf16[512,1024]{1,0:T(8,128)(2,1)}, bf16[512,1024]{1,0:T(8,128)(2,1)S(1)}, u32[]{:S(2)}, u32[]{:S(2)}) collective-permute-start(bf16[512,1024]{1,0:T(8,128)(2,1)} %collective-permute-done.16.refs_2_.refs_8_), channel_id=1, source_target_pairs={{0,16},{16,0},{1,17},{17,1},{2,18},{18,2},{3,19},{19,3},{4,20},{20... | collective-permute-start | bytes 3145736 | tf_op jit(solution)/shard_map/ppermute | solution.py:532
  205.5 47.7 %collective-permute-start.26 = (bf16[3,64,5120]{2,1,0:T(8,128)(2,1)}, bf16[3,64,5120]{2,1,0:T(8,128)(2,1)}, u32[]{:S(2)}, u32[]{:S(2)}) collective-permute-start(bf16[3,64,5120]{2,1,0:T(8,128)(2,1)} %get-tuple-element.68.refs_0_), channel_id=1, source_target_pairs={{0,1},{1,0},{2,3},{3,2},{4,5},{5,4},{6,7},{7,6},{8,9},{9,8},{10,11... | collective-permute-start | bytes 5898248 | tf_op jit(solution)/shard_map/ppermute | solution.py:472
  206.1 1.2 copy-start.3
  250.5 24.0 %collective-permute-start.25 = (bf16[3,64,5120]{2,1,0:T(8,128)(2,1)}, bf16[3,64,5120]{2,1,0:T(8,128)(2,1)}, u32[]{:S(2)}, u32[]{:S(2)}) collective-permute-start(bf16[3,64,5120]{2,1,0:T(8,128)(2,1)} %collective-permute-done.24.refs_0_), channel_id=1, source_target_pairs={{0,1},{1,0},{2,3},{3,2},{4,5},{5,4},{6,7},{7,6},{8,9},{9,8},{10,11... | collective-permute-start | bytes 5898248 | tf_op jit(solution)/shard_map/ppermute | solution.py:472
  251.5 7.6 %copy-start.7 = (bf16[512,1024]{1,0:T(8,128)(2,1)}, bf16[512,1024]{1,0:T(8,128)(2,1)S(1)}, u32[]{:S(2)}) copy-start(bf16[512,1024]{1,0:T(8,128)(2,1)S(1)} %collective-permute-done.19.refs_2_) | copy-start | bytes 3145732
  251.5 7.6 %collective-permute-start.23 = (bf16[512,1024]{1,0:T(8,128)(2,1)S(1)}, bf16[512,1024]{1,0:T(8,128)(2,1)S(1)}, u32[]{:S(2)}, u32[]{:S(2)}) collective-permute-start(bf16[512,1024]{1,0:T(8,128)(2,1)S(1)} %collective-permute-done.19.refs_2_), channel_id=1, source_target_pairs={{0,1},{1,0},{2,3},{3,2},{4,5},{5,4},{6,7},{7,6},{8,9},{9,8},{10,11... | collective-permute-start | bytes 3145736 | tf_op jit(solution)/shard_map/ppermute | solution.py:472
  259.1 1.0 copy-start.8
Sparse Core Ops, SparseCore 0:
  31.8 87.2 all-gather.4
  187.2 44.4 all-gather.2
where the time goes:
time: 288 us; the launch traced here: 286 us
  waiting for transfers between devices  129 us (45%)
  Pallas kernels  98.9 us (34%)
  starting transfers between devices  22 us (8%)
  local copies, waits for them, and re-layouts  17.1 us (6%)
  between operations  14.3 us (5%)
  other arithmetic  4.35 us (2%)
    ppermute x23, waiting for transfers between devices, swap(): return lax.ppermute(value, axis, [(i, i ^ bit) for i in range(size)])  92.7 us
    pallas_call x5, Pallas kernels, base(): pl.pallas_call(functools.partial(base_kernel, 2 * top, tiles, len(chunks)...  64.9 us
    ppermute x4, waiting for transfers between devices, turn(): turned[j].append({top: lax.ppermute(piece, 'groups', ring)})  26.5 us
    ppermute x23, starting transfers between devices, swap(): return lax.ppermute(value, axis, [(i, i ^ bit) for i in range(size)])  17.1 us
    pallas_call x1, Pallas kernels, project(): pl.pallas_call(functools.partial(project_kernel, pieces), grid_spec=pltpu...  11.8 us
    pallas_call x2, Pallas kernels, add_terms(): pl.pallas_call(functools.partial(add_kernel, n, count), grid_spec=pltpu.P...  10.4 us
    all_gather x2, waiting for transfers between devices, gather(): lax.all_gather(behind(mine, *after), 'fsdp', axis=1, tiled=True)  9.97 us
    pallas_call x1, Pallas kernels, block_terms(): pl.pallas_call(terms_kernel, grid_spec=pltpu.PrefetchScalarGridSpec(num_s...  7.01 us
  transfers between devices with their start and end apart: 29, of which 10 were waited for; matrix products, arithmetic and copies ran while one was open for 6% of the time, Pallas kernels for 31%

commit v1 on v0

--- a/solution.py
+++ b/solution.py
@@ -201,6 +201,37 @@
         ],
         **params((2 * rows * rank * (ff + d), 2 * (rows + count * rank) * (ff + d))),
     )(live, here, there, hidden, grad)
+
+
+def join_kernel(n, *refs):
+    at_ref, piece_refs, (out_ref, sem) = refs[0], refs[1 : 1 + n], refs[1 + n :]
+    deep = piece_refs[0].shape[1]
+
+    def copy(k):
+        lanes = pl.ds(pl.multiple_of(at_ref[k] * deep, deep), deep)
+        return pltpu.make_async_copy(piece_refs[k], out_ref.at[:, lanes], sem.at[k])
+
+    for k in range(n):
+        pl.when(at_ref[k] >= 0)(lambda k=k: copy(k).start())
+    for k in range(n):
+        pl.when(at_ref[k] >= 0)(lambda k=k: copy(k).wait())
+
+
+def join(at, pieces, parts):
+    rows, deep = pieces[0].shape
+    anywhere = pl.BlockSpec(memory_space=pl.ANY)
+    return pl.pallas_call(
+        functools.partial(join_kernel, len(pieces)),
+        grid_spec=pltpu.PrefetchScalarGridSpec(
+            num_scalar_prefetch=1,
+            grid=(1,),
+            in_specs=[anywhere] * len(pieces),
+            out_specs=anywhere,
+            scratch_shapes=[pltpu.SemaphoreType.DMA((len(pieces),))],
+        ),
+        out_shape=jax.ShapeDtypeStruct((rows, parts * deep), bf16),
+        **params((0, 4 * rows * parts * deep)),
+    )(at, *pieces)
 
 
 def base_kernel(n_dp, tiles, n_chunks, blocks, scalars_ref, kept_ref, *refs):
@@ -358,7 +389,7 @@
             jax.ShapeDtypeStruct((8, 128), f32),
         ],
         input_output_aliases=aliases,
-        **params((2 * rows * depth * span, 2 * (rows * depth + (rows + depth) * span))),
+        **params((1, 1)),
     )(jnp.concatenate([jnp.stack(places).astype(i32), scalars]), *operands)
 
 
@@ -442,7 +473,7 @@
             jax.ShapeDtypeStruct(grad_b.shape, f32),
         ],
         input_output_aliases={n + 1: 0, n + 2: 1},
-        **params((0, n * count * 10 * rank * both)),
+        **params((1, 1)),
     )(slots, *pieces, grad_a, grad_b)
 
 
@@ -484,24 +515,29 @@
     slots = jnp.sum(jnp.where(match, jnp.arange(n_slots, dtype=i32)[None, :], 0), axis=1)
     far_slots = swap(slots, top)
 
-    cut = (2 * count + 2) // 3
-    row_parts = [range(cut), range(cut, count)] if cut < count else [range(count)]
-    height = rows // count
-    kept = []
-
-    def gather(*after):
-        k = len(kept)
-        if k < len(row_parts):
-            part = row_parts[k]
-            mine = output_gradient[part[0] * height : (part[-1] + 1) * height]
-            kept.append(lax.all_gather(behind(mine, *after), "fsdp", axis=1, tiled=True))
-
-    gather()
+    place = lax.axis_index("fsdp")
+    line = n_fsdp <= 4
+    pieces_of_kept, at = [output_gradient], [place]
+
+    def hop(*after):
+        k = len(pieces_of_kept) // 2
+        if not line or k + 1 >= n_fsdp:
+            return []
+        right = [(i, i + 1) for i in range(n_fsdp - 1)]
+        left = [(i + 1, i) for i in range(n_fsdp - 1)]
+        ends = pieces_of_kept[-2:] if k else pieces_of_kept * 2
+        for piece, pairs in zip(ends, (right, left)):
+            pieces_of_kept.append(lax.ppermute(behind(piece, *after), "fsdp", pairs))
+        at.append(place - k - 1)
+        at.append(jnp.where(place + k + 1 < n_fsdp, place + k + 1, -1))
+        return pieces_of_kept[-2:]
+
+    first_hop = hop()
 
     share = ff // n_groups
     if share % 2048 == 0:
         unit, tile = share // 8, share // 4
-        sizes = [unit, 2 * unit, 3 * unit, 2 * unit]
+        sizes = [3 * unit, 3 * unit, 2 * unit]
     else:
         tile = share
         sizes = [share]
@@ -535,7 +571,7 @@
         for piece in chunks:
             piece.update(spread({top: behind(piece[top], *after)}))
 
-    cross()
+    cross(far_slots)
 
     first = jnp.swapaxes(adapter_first_factors, 1, 2)
     a_near = spread({0: first})
@@ -548,19 +584,21 @@
         index = jnp.concatenate([wanted % local] * len(near))
         return index, jnp.where((owner ^ me) < top, owner ^ me, len(near))
 
-    picked = pick(*places(behind(far_slots, *flat(*crossed))), a_near, b_near)
-    far = swap(picked, top)
-    whole = spread({0: behind(frozen_down_weight, picked)})
-    both_slots = spread({0: jnp.concatenate([slots, far_slots])})
-    turn()
-
-    ready = behind(slots, *flat(whole, both_slots, *turned[0]))
+    picked = pick(*places(far_slots), a_near, b_near)
+    both_slots = spread({0: behind(jnp.concatenate([slots, far_slots]), picked)})
+    past = [picked, *first_hop, *flat(both_slots, *crossed)]
+    far = swap(behind(picked, *past[1:]), top)
+    whole = spread({0: behind(frozen_down_weight, *past)})
+    turn(*past)
+    past = [far, *hop(*past), *flat(*turned[0])]
+
+    ready = behind(slots, *flat(whole, both_slots), *past)
     part, block_a, grad_a, grad_b = project(
         *places(ready), a_near, b_near, far, hidden, output_gradient
     )
-    cross(far, *flat(*turned[0]))
-    fill(crossed[:1], far)
-    fill(turned[0], far)
+    cross(*past)
+    fill(crossed[:1], *past)
+    third_hop = hop(*past)
     sums = [part]
     bit = 1
     while bit < n_fsdp:
@@ -569,20 +607,23 @@
             sums.append(sums[-2] + sums[-1])
         bit *= 2
     total, other = sums[-2:]
-    past = [sums[2], *flat(*crossed[:2], *turned[0])]
+    past = [sums[2], *flat(*crossed), *third_hop]
     cross(*past)
     turn(*past)
     fill(crossed[1:2], *past)
-    gather(other)
-    past = [other, *flat(*crossed[:3], *sum(turned, []))]
-    cross(*past)
+    fill(turned[0], *past)
+    past = [other, *flat(*crossed)]
+    fill(crossed[2:], *past)
+    terms, coef = block_terms(island_live_rows, total, other, hidden, output_gradient)
+    far_terms = swap(terms, top)
+    near_terms = spread({0: behind(terms, *past)})
     turn(*past)
-    fill(crossed[2:3], *past)
     for pieces in turned[1:2]:
         fill(pieces, *past)
-    terms, coef = block_terms(island_live_rows, total, other, hidden, output_gradient)
-    far_terms = swap(terms, top)
-    near_terms = spread({0: behind(terms, *flat(*crossed[:3]))})
+    if line:
+        kept = join(jnp.stack(at).astype(i32), pieces_of_kept, n_fsdp)
+    else:
+        kept = lax.all_gather(output_gradient, "fsdp", axis=1, tiled=True)
 
     relative = [both_slots[r][:count] for r in near] + [both_slots[r][count:] for r in near]
     relative = jnp.concatenate(relative) - me * local
@@ -594,7 +635,7 @@
     scalars = jnp.concatenate([jnp.stack([me ^ r for r in range(n_dp)]).astype(i32), island_live_rows])
     grad_hidden = token = None
 
-    def multiply(k, *where):
+    def multiply(*where):
         nonlocal grad_hidden, token
         chunks, tiles, places = [], [], []
         for shift, t in where:
@@ -609,32 +650,20 @@
                     tiles[-1].append((chunks.index((shift, j)), low - first, high - low))
         pieces = [turned[j][shift - 1] if shift else crossed[j] for shift, j in chunks]
         grad_hidden, token = base(
-            places, scalars, kept[k], whole, pieces, tiles, tile, coef, block_a,
-            list(row_parts[k]), grad_hidden, token,
+            places, scalars, kept, whole, pieces, tiles, tile, coef, block_a, list(range(count)),
+            grad_hidden, token,
         )
 
-    last = share // tile - 1
     others = range(1, n_groups)
-    if last:
-        multiply(0, *[(0, t) for t in range(last)], *[(g, 0) for g in others])
-        past = [token, *flat(*crossed)]
-        turn(*past)
-        fill(crossed[3:], *past)
-        for pieces in turned[2:3]:
-            fill(pieces, *flat(*crossed))
-        multiply(0, (0, last), *[(g, t) for g in others for t in range(1, last)])
-        for k in range(1, len(row_parts)):
-            multiply(
-                k, *[(0, t) for t in range(last + 1)], *[(g, t) for g in others for t in range(last)]
-            )
-        for pieces in turned[3:]:
+    if share > tile:
+        multiply((0, 0), (0, 1), (0, 2))
+        multiply((0, 3), *[(g, t) for g in others for t in range(3)])
+        for pieces in turned[2:]:
             fill(pieces, token)
         early = token
-        for k in range(len(row_parts)):
-            multiply(k, *[(g, last) for g in others])
+        multiply(*[(g, 3) for g in others])
     else:
-        for k in range(len(row_parts)):
-            multiply(k, *[(g, 0) for g in range(n_groups)])
+        multiply(*[(g, 0) for g in range(n_groups)])
         early = token
 
     all_far = spread({top: behind(far_terms, early)})

time: 288 us -> 444 us (1.54)
  Pallas kernels: 98.9 us -> 267 us
  starting transfers between devices: 22 us -> 40.2 us
  waiting for transfers between devices: 129 us -> 114 us
  between operations: 14.3 us -> 1.02 us
  local copies, waits for them, and re-layouts: 17.1 us -> 12.2 us
    pallas_call x0 -> x1, Pallas kernels: none -> 192 us  [join(): pl.pallas_call(functools.partial(join_kernel, len(pieces)), grid_spec=plt...]
    ppermute x23 -> x20, waiting for transfers between devices: 92.7 us -> 57.4 us  [swap(): return lax.ppermute(value, axis, [(i, i ^ bit) for i in range(size)])]
    ppermute x0 -> x6, waiting for transfers between devices: none -> 23.5 us  [hop(): pieces_of_kept.append(lax.ppermute(behind(piece, *after), 'fsdp', pairs))]
    ppermute x0 -> x6, starting transfers between devices: none -> 17 us  [hop(): pieces_of_kept.append(lax.ppermute(behind(piece, *after), 'fsdp', pairs))]
    pallas_call x5 -> x3, Pallas kernels: 64.9 us -> 49.7 us  [base(): pl.pallas_call(functools.partial(base_kernel, 2 * top, tiles, len(chunks)...]
    all_gather x2 -> x0, waiting for transfers between devices: 9.97 us -> none  [gather(): lax.all_gather(behind(mine, *after), 'fsdp', axis=1, tiled=True)]
    pallas_call x2, Pallas kernels: 10.4 us -> 2.02 us  [add_terms(): pl.pallas_call(functools.partial(add_kernel, n, count), grid_spec=pltpu.P...]
    ppermute x4 -> x3, waiting for transfers between devices: 26.5 us -> 33 us  [turn(): turned[j].append({top: lax.ppermute(piece, 'groups', ring)})]
  transfers between devices with their start and end apart: 29 -> 29, of which waited for: 10 -> 12; matrix products, arithmetic and copies ran while one was open for 6% -> 3% of each run, Pallas kernels for 31% -> 61%
where the time goes in v1:
time: 444 us; the launch traced here: 438 us
  Pallas kernels  267 us (60%)
  waiting for transfers between devices  114 us (26%)
  starting transfers between devices  40.2 us (9%)
  local copies, waits for them, and re-layouts  12.2 us (3%)
    pallas_call x1, Pallas kernels, join(): pl.pallas_call(functools.partial(join_kernel, len(pieces)), grid_spec=plt...  192 us
    ppermute x20, waiting for transfers between devices, swap(): return lax.ppermute(value, axis, [(i, i ^ bit) for i in range(size)])  57.4 us
    pallas_call x3, Pallas kernels, base(): pl.pallas_call(functools.partial(base_kernel, 2 * top, tiles, len(chunks)...  49.7 us
    ppermute x3, waiting for transfers between devices, turn(): turned[j].append({top: lax.ppermute(piece, 'groups', ring)})  33 us
    ppermute x6, waiting for transfers between devices, hop(): pieces_of_kept.append(lax.ppermute(behind(piece, *after), 'fsdp', pairs))  23.5 us
    ppermute x20, starting transfers between devices, swap(): return lax.ppermute(value, axis, [(i, i ^ bit) for i in range(size)])  19.5 us
    ppermute x6, starting transfers between devices, hop(): pieces_of_kept.append(lax.ppermute(behind(piece, *after), 'fsdp', pairs))  17 us
    pallas_call x1, Pallas kernels, project(): pl.pallas_call(functools.partial(project_kernel, pieces), grid_spec=pltpu...  11.7 us
  transfers between devices with their start and end apart: 29, of which 12 were waited for; matrix products, arithmetic and copies ran while one was open for 3% of the time, Pallas kernels for 61%

profile of v1, /device:TPU:11, one launch (start us, length us, event | category | flops | bytes accessed | tf_op | source)
XLA Modules:
  0.0 438.3 jit_solution(13506557652724675627)
XLA Ops:
  0.6 0.7 collective-permute-start.3
  1.4 3.2 collective-permute-start
  4.6 3.2 collective-permute-start.1
  7.8 0.9 select_reduce_fusion
  8.7 0.3 collective-permute-start.2
  9.0 3.9 constant_dynamic-slice_fusion
  12.9 1.2 collective-permute-start.6
  14.1 1.1 collective-permute-start.4
  15.3 0.5 compare_select_fusion.1
  15.8 0.7 pad_add_fusion.index_ref
  16.5 1.0 collective-permute-done.4.refs_3_
  17.6 1.0 copy-done.1
  18.6 3.8 shard_map.103
  22.3 1.4 collective-permute-start.5
  23.7 15.9 %collective-permute-done.refs_2_ = bf16[768,1024]{1,0:T(8,128)(2,1)} collective-permute-done((bf16[768,1024]{1,0:T(8,128)(2,1)}, bf16[768,1024]{1,0:T(8,128)(2,1)}, u32[]{:S(2)}, u32[]{:S(2)}) %collective-permute-start) | collective-permute-done | bytes 1572896 | tf_op jit(solution)/shard_map/ppermute | solution.py:530
  39.6 2.9 collective-permute-done.1.refs_3_
  42.5 5.8 %collective-permute-done.6.refs_2_ = bf16[768,1024]{1,0:T(8,128)(2,1)} collective-permute-done((bf16[768,1024]{1,0:T(8,128)(2,1)}, bf16[768,1024]{1,0:T(8,128)(2,1)}, u32[]{:S(2)}, u32[]{:S(2)}) %collective-permute-start.6) | collective-permute-done | bytes 1572896 | tf_op jit(solution)/shard_map/ppermute | solution.py:503
  48.3 1.8 collective-permute-start.13
  50.1 1.2 collective-permute-start.9
  51.3 1.2 collective-permute-start.10
  52.5 1.9 collective-permute-start.8
  54.4 3.4 collective-permute-start.7
  57.8 29.5 %collective-permute-done.10.refs_4_ = bf16[768,1024]{1,0:T(8,128)(2,1)S(1)} collective-permute-done((bf16[768,1024]{1,0:T(8,128)(2,1)}, bf16[768,1024]{1,0:T(8,128)(2,1)S(1)}, u32[]{:S(2)}, u32[]{:S(2)}) %collective-permute-start.10) | collective-permute-done | bytes 1572896 | tf_op jit(solution)/shard_map/ppermute | solution.py:568
  87.3 2.8 collective-permute-done.8.refs_5_
  90.1 1.9 collective-permute-done.7.refs_4_
  92.0 2.7 collective-permute-done.9.refs_4_
  94.7 1.2 collective-permute-start.16
  95.9 1.1 collective-permute-start.15
  97.0 1.9 collective-permute-start.12
  98.9 3.4 collective-permute-start.11
  102.3 0.5 compare_select_fusion
  102.8 0.6 pad_add_fusion.2.index_ref
  103.5 11.7 %shard_map.105 = (f32[3,256,128]{2,1,0:T(8,128)}, bf16[3,64,4096]{2,1,0:T(8,128)(2,1)}, f32[8,64,4096]{2,1,0:T(8,128)}, f32[8,64,1024]{2,1,0:T(8,128)}) custom-call(s32[6]{0:T(128)} %pad_add_fusion.2.index_ref, s32[3]{0:T(128)} %get-tuple-element.83.source_ref, bf16[8,64,4096]{2,1,0:T(8,128)(2,1)} %bitcast.24, ...), custom_call_target="tpu_custom_call" | custom-call | flops 503316480 | bytes 15728640 | tf_op jit(solution)/shard_map/pallas_call | solution.py:121
  115.2 1.2 collective-permute-start.14
  116.4 29.1 %collective-permute-done.14 = f32[3,256,128]{2,1,0:T(8,128)S(1)} collective-permute-done((f32[3,256,128]{2,1,0:T(8,128)}, f32[3,256,128]{2,1,0:T(8,128)S(1)}, u32[]{:S(2)}, u32[]{:S(2)}) %collective-permute-start.14) | collective-permute-done | bytes 393248 | tf_op jit(solution)/shard_map/ppermute | solution.py:503
  145.5 1.0 add.104.here_ref
  146.6 0.8 collective-permute-start.19
  147.4 1.3 collective-permute-start.23
  148.7 2.3 constant_dynamic-slice_fusion.1
  150.9 0.3 collective-permute-start.17
  151.2 2.9 collective-permute-start.18
  154.1 16.3 %collective-permute-done.18.there_ref = f32[3,256,128]{2,1,0:T(8,128)S(1)} collective-permute-done((f32[3,256,128]{2,1,0:T(8,128)S(1)}, f32[3,256,128]{2,1,0:T(8,128)S(1)}, u32[]{:S(2)}, u32[]{:S(2)}) %collective-permute-start.18) | collective-permute-done | bytes 393248 | tf_op jit(solution)/shard_map/ppermute | solution.py:503
  170.4 0.8 copy-done.7
  171.2 7.0 %shard_map.106 = (bf16[3,64,5120]{2,1,0:T(8,128)(2,1)}, bf16[3,256,64]{2,1,0:T(8,128)(2,1)}) custom-call(s32[3]{0:T(128)} %live_ref.1, f32[3,256,128]{2,1,0:T(8,128)} %copy-done.5, f32[3,256,128]{2,1,0:T(8,128)} %copy-done.7, bf16[768,4096]{1,0:T(8,128)(2,1)} %hid_ref.1, bf16[768,1024]{1,0:T(8,128)(2,1)} %grad_ref.1), custom_call_target="tpu_custom_call" | custom-call | flops 503316480 | bytes 9830400 | tf_op jit(solution)/shard_map/pallas_call | solution.py:182
  178.2 1.2 collective-permute-start.26
  179.4 0.8 collective-permute-start.22
  180.2 3.5 collective-permute-done.23.refs_6_
  183.7 0.8 collective-permute-start.24
  184.6 1.2 collective-permute-start.20
  185.8 0.6 concatenate.30.scalars_ref
  186.4 0.7 concatenate.29.scalars_ref
  187.1 0.6 stack.72.refs_0_
  187.7 192.4 %shard_map.104.kept_ref = bf16[768,4096]{1,0:T(8,128)(2,1)} custom-call(s32[7]{0:T(128)} %stack.72.refs_0_, bf16[768,1024]{1,0:T(8,128)(2,1)} %grad_ref.1, bf16[768,1024]{1,0:T(8,128)(2,1)} %collective-permute-done.refs_2_, bf16[768,1024]{1,0:T(8,128)(2,1)} %collective-permute-done.1.refs_3_, bf16[768,1024]{1,0:T(8,128)(2,1)} %collective-permute-done.7.refs_4_, ...), custom_call_target="tpu_custom_call" | custom-call | bytes 12582912 | tf_op jit(solution)/shard_map/pallas_call | solution.py:223
  380.1 18.3 %shard_map.107 = (bf16[768,4096]{1,0:T(8,128)(2,1)}, f32[8,128]{1,0:T(8,128)}) custom-call(s32[10]{0:T(128)} %concatenate.30.scalars_ref, bf16[768,4096]{1,0:T(8,128)(2,1)} %shard_map.104.kept_ref, bf16[4096,1024]{1,0:T(8,128)(2,1)} %refs_0_.2, bf16[4096,1024]{1,0:T(8,128)(2,1)} %collective-permute-done.13.refs_1_, ...), custom_call_target="tpu_custom_call" | custom-call | flops 1 | bytes 1 | tf_op jit(solution)/shard_map/pallas_call | solution.py:369
  398.5 0.8 collective-permute-start.28
  399.4 21.8 %shard_map.108 = (bf16[768,4096]{1,0:T(8,128)(2,1)}, f32[8,128]{1,0:T(8,128)}) custom-call(s32[11]{0:T(128)} %concatenate.29.scalars_ref, bf16[768,4096]{1,0:T(8,128)(2,1)} %shard_map.104.kept_ref, bf16[4096,1024]{1,0:T(8,128)(2,1)} %refs_0_.2, bf16[4096,1024]{1,0:T(8,128)(2,1)} %collective-permute-done.13.refs_1_, ...), custom_call_target="tpu_custom_call", output_to_operand_aliasing={{0}: (13, {})} | custom-call | flops 1 | bytes 1 | tf_op jit(solution)/shard_map/pallas_call | solution.py:369
  421.3 0.5 collective-permute-start.25
  421.8 0.6 concatenate.25.scalars_ref
  422.6 0.6 fusion
  423.2 1.0 shard_map.110
  424.2 2.4 collective-permute-done.25.refs_3_
  426.6 1.0 copy-done.6
  427.6 9.5 %shard_map.109 = (bf16[768,4096]{1,0:T(8,128)(2,1)}, f32[8,128]{1,0:T(8,128)}) custom-call(s32[8]{0:T(128)} %concatenate.25.scalars_ref, bf16[768,4096]{1,0:T(8,128)(2,1)} %shard_map.104.kept_ref, bf16[4096,1024]{1,0:T(8,128)(2,1)} %refs_0_.2, bf16[4096,1024]{1,0:T(8,128)(2,1)} %collective-permute-done.13.refs_1_, ...), custom_call_target="tpu_custom_call", output_to_operand_aliasing={{0}: (9, {})} | custom-call | flops 1 | bytes 1 | tf_op jit(solution)/shard_map/pallas_call | solution.py:369
  437.1 1.0 shard_map.111
  (38 shorter events, 0.5 us)
Async XLA Ops:
  0.6 16.9 %collective-permute-start.3 = (bf16[8,64,4096]{2,1,0:T(8,128)(2,1)}, bf16[8,64,4096]{2,1,0:T(8,128)(2,1)}, u32[]{:S(2)}, u32[]{:S(2)}) collective-permute-start(bf16[8,64,4096]{2,1,0:T(8,128)(2,1)} %bitcast.22), channel_id=1, source_target_pairs={{0,1},{1,0},{2,3},{3,2},{4,5},{5,4},{6,7},{7,6},{8,9},{9,8},{10,11... | collective-permute-start | bytes 12582920 | tf_op jit(solution)/shard_map/ppermute | solution.py:503
  1.4 38.2 %collective-permute-start = (bf16[768,1024]{1,0:T(8,128)(2,1)}, bf16[768,1024]{1,0:T(8,128)(2,1)}, u32[]{:S(2)}, u32[]{:S(2)}) collective-permute-start(bf16[768,1024]{1,0:T(8,128)(2,1)} %grad_ref.1), channel_id=1, source_target_pairs={{0,4},{4,8},{8,12},{1,5},{5,9},{9,13},{2,6},{6,10},{10,14},{3,7},{... | collective-permute-start | bytes 4718600 | tf_op jit(solution)/shard_map/ppermute | solution.py:530
  4.6 37.9 %collective-permute-start.1 = (bf16[768,1024]{1,0:T(8,128)(2,1)}, bf16[768,1024]{1,0:T(8,128)(2,1)}, u32[]{:S(2)}, u32[]{:S(2)}) collective-permute-start(bf16[768,1024]{1,0:T(8,128)(2,1)} %grad_ref.1), channel_id=1, source_target_pairs={{4,0},{8,4},{12,8},{5,1},{9,5},{13,9},{6,2},{10,6},{14,10},{7,3},{... | collective-permute-start | bytes 4718600 | tf_op jit(solution)/shard_map/ppermute | solution.py:530
  8.7 4.3 collective-permute-start.2
  9.0 5.2 %copy-start = (bf16[8,64,1024]{2,1,0:T(8,128)(2,1)S(1)}, bf16[8,64,1024]{2,1,0:T(8,128)(2,1)}, u32[]{:S(2)}) copy-start(bf16[8,64,1024]{2,1,0:T(8,128)(2,1)} %refs_2_.3) | copy-start | bytes 3145732
  12.9 35.4 %collective-permute-start.6 = (bf16[768,1024]{1,0:T(8,128)(2,1)}, bf16[768,1024]{1,0:T(8,128)(2,1)}, u32[]{:S(2)}, u32[]{:S(2)}) collective-permute-start(bf16[768,1024]{1,0:T(8,128)(2,1)} %get-tuple-element.40), channel_id=1, source_target_pairs={{0,2},{1,3},{2,0},{3,1},{4,6},{5,7},{6,4},{7,5},{8,10},{9,11},{10,... | collective-permute-start | bytes 4718600 | tf_op jit(solution)/shard_map/ppermute | solution.py:503
  14.1 3.4 collective-permute-start.4
  17.6 1.0 copy-start.1
  22.3 26.0 %collective-permute-start.5 = (s32[6]{0:T(128)S(1)}, s32[6]{0:T(128)S(1)}, u32[]{:S(2)}, u32[]{:S(2)}) collective-permute-start(s32[6]{0:T(128)S(1)} %pad_add_fusion.1), channel_id=1, source_target_pairs={{0,1},{1,0},{2,3},{3,2},{4,5},{5,4},{6,7},{7,6},{8,9},{9,8},{10,11... | collective-permute-start | bytes 80 | tf_op jit(solution)/shard_map/ppermute | solution.py:503
  48.3 54.0 %collective-permute-start.13 = (bf16[4096,1024]{1,0:T(8,128)(2,1)}, bf16[4096,1024]{1,0:T(8,128)(2,1)}, u32[]{:S(2)}, u32[]{:S(2)}) collective-permute-start(bf16[4096,1024]{1,0:T(8,128)(2,1)} %refs_0_.2), channel_id=1, source_target_pairs={{0,1},{1,0},{2,3},{3,2},{4,5},{5,4},{6,7},{7,6},{8,9},{9,8},{10,11... | collective-permute-start | bytes 25165832 | tf_op jit(solution)/shard_map/ppermute | solution.py:503
  50.1 44.7 %collective-permute-start.9 = (bf16[3,64,5120]{2,1,0:T(8,128)(2,1)}, bf16[3,64,5120]{2,1,0:T(8,128)(2,1)S(1)}, u32[]{:S(2)}, u32[]{:S(2)}) collective-permute-start(bf16[3,64,5120]{2,1,0:T(8,128)(2,1)} %shard_map.103), channel_id=1, source_target_pairs={{0,2},{1,3},{2,0},{3,1},{4,6},{5,7},{6,4},{7,5},{8,10},{9,11},{10,... | collective-permute-start | bytes 5898248 | tf_op jit(solution)/shard_map/ppermute | solution.py:503
  51.3 36.0 %collective-permute-start.10 = (bf16[768,1024]{1,0:T(8,128)(2,1)}, bf16[768,1024]{1,0:T(8,128)(2,1)S(1)}, u32[]{:S(2)}, u32[]{:S(2)}) collective-permute-start(bf16[768,1024]{1,0:T(8,128)(2,1)} %collective-permute-done.6.refs_2_), channel_id=1, source_target_pairs={{0,16},{16,0},{1,17},{17,1},{2,18},{18,2},{3,19},{19,3},{4,20},{20... | collective-permute-start | bytes 4718600 | tf_op jit(solution)/shard_map/ppermute | solution.py:568
  52.5 37.6 %collective-permute-start.8 = (bf16[768,1024]{1,0:T(8,128)(2,1)}, bf16[768,1024]{1,0:T(8,128)(2,1)}, u32[]{:S(2)}, u32[]{:S(2)}) collective-permute-start(bf16[768,1024]{1,0:T(8,128)(2,1)} %collective-permute-done.1.refs_3_), channel_id=1, source_target_pairs={{4,0},{8,4},{12,8},{5,1},{9,5},{13,9},{6,2},{10,6},{14,10},{7,3},{... | collective-permute-start | bytes 4718600 | tf_op jit(solution)/shard_map/ppermute | solution.py:530
  54.4 37.6 %collective-permute-start.7 = (bf16[768,1024]{1,0:T(8,128)(2,1)}, bf16[768,1024]{1,0:T(8,128)(2,1)}, u32[]{:S(2)}, u32[]{:S(2)}) collective-permute-start(bf16[768,1024]{1,0:T(8,128)(2,1)} %collective-permute-done.refs_2_), channel_id=1, source_target_pairs={{0,4},{4,8},{8,12},{1,5},{5,9},{9,13},{2,6},{6,10},{10,14},{3,7},{... | collective-permute-start | bytes 4718600 | tf_op jit(solution)/shard_map/ppermute | solution.py:530
  87.3 92.1 %copy-start.4 = (bf16[768,1024]{1,0:T(8,128)(2,1)}, bf16[768,1024]{1,0:T(8,128)(2,1)S(1)}, u32[]{:S(2)}) copy-start(bf16[768,1024]{1,0:T(8,128)(2,1)S(1)} %collective-permute-done.10.refs_4_) | copy-start | bytes 4718596
  94.7 8.8 %copy-start.3 = (bf16[3,64,5120]{2,1,0:T(8,128)(2,1)}, bf16[3,64,5120]{2,1,0:T(8,128)(2,1)S(1)}, u32[]{:S(2)}) copy-start(bf16[3,64,5120]{2,1,0:T(8,128)(2,1)S(1)} %collective-permute-done.9.refs_4_) | copy-start | bytes 5898244
  94.7 51.8 %collective-permute-start.16 = (bf16[768,1024]{1,0:T(8,128)(2,1)}, bf16[768,1024]{1,0:T(8,128)(2,1)}, u32[]{:S(2)}, u32[]{:S(2)}) collective-permute-start(bf16[768,1024]{1,0:T(8,128)(2,1)} %get-tuple-element.51), channel_id=1, source_target_pairs={{0,2},{1,3},{2,0},{3,1},{4,6},{5,7},{6,4},{7,5},{8,10},{9,11},{10,... | collective-permute-start | bytes 4718600 | tf_op jit(solution)/shard_map/ppermute | solution.py:503
  95.9 50.6 %collective-permute-start.15 = (bf16[768,1024]{1,0:T(8,128)(2,1)}, bf16[768,1024]{1,0:T(8,128)(2,1)}, u32[]{:S(2)}, u32[]{:S(2)}) collective-permute-start(bf16[768,1024]{1,0:T(8,128)(2,1)} %collective-permute-done.6.refs_2_), channel_id=1, source_target_pairs={{0,1},{1,0},{2,3},{3,2},{4,5},{5,4},{6,7},{7,6},{8,9},{9,8},{10,11... | collective-permute-start | bytes 4718600 | tf_op jit(solution)/shard_map/ppermute | solution.py:503
  97.0 49.5 %collective-permute-start.12 = (bf16[768,1024]{1,0:T(8,128)(2,1)}, bf16[768,1024]{1,0:T(8,128)(2,1)}, u32[]{:S(2)}, u32[]{:S(2)}) collective-permute-start(bf16[768,1024]{1,0:T(8,128)(2,1)} %collective-permute-done.8.refs_5_), channel_id=1, source_target_pairs={{4,0},{8,4},{12,8},{5,1},{9,5},{13,9},{6,2},{10,6},{14,10},{7,3},{... | collective-permute-start | bytes 4718600 | tf_op jit(solution)/shard_map/ppermute | solution.py:530
  98.9 47.6 %collective-permute-start.11 = (bf16[768,1024]{1,0:T(8,128)(2,1)}, bf16[768,1024]{1,0:T(8,128)(2,1)}, u32[]{:S(2)}, u32[]{:S(2)}) collective-permute-start(bf16[768,1024]{1,0:T(8,128)(2,1)} %collective-permute-done.7.refs_4_), channel_id=1, source_target_pairs={{0,4},{4,8},{8,12},{1,5},{5,9},{9,13},{2,6},{6,10},{10,14},{3,7},{... | collective-permute-start | bytes 4718600 | tf_op jit(solution)/shard_map/ppermute | solution.py:530
  115.2 30.3 %collective-permute-start.14 = (f32[3,256,128]{2,1,0:T(8,128)}, f32[3,256,128]{2,1,0:T(8,128)S(1)}, u32[]{:S(2)}, u32[]{:S(2)}) collective-permute-start(f32[3,256,128]{2,1,0:T(8,128)} %get-tuple-element.49), channel_id=1, source_target_pairs={{0,4},{4,0},{8,12},{12,8},{1,5},{5,1},{9,13},{13,9},{2,6},{6,2},{1... | collective-permute-start | bytes 1179656 | tf_op jit(solution)/shard_map/ppermute | solution.py:503
  146.5 23.9 %copy-start.5 = (f32[3,256,128]{2,1,0:T(8,128)}, f32[3,256,128]{2,1,0:T(8,128)S(1)}, u32[]{:S(2)}) copy-start(f32[3,256,128]{2,1,0:T(8,128)S(1)} %add.104.here_ref) | copy-start | bytes 1179652
  146.6 33.6 %collective-permute-start.19 = (bf16[768,1024]{1,0:T(8,128)(2,1)}, bf16[768,1024]{1,0:T(8,128)(2,1)}, u32[]{:S(2)}, u32[]{:S(2)}) collective-permute-start(bf16[768,1024]{1,0:T(8,128)(2,1)} %collective-permute-done.16.refs_4_), channel_id=1, source_target_pairs={{0,1},{1,0},{2,3},{3,2},{4,5},{5,4},{6,7},{7,6},{8,9},{9,8},{10,11... | collective-permute-start | bytes 4718600 | tf_op jit(solution)/shard_map/ppermute | solution.py:503
  147.4 36.3 %collective-permute-start.23 = (bf16[768,1024]{1,0:T(8,128)(2,1)}, bf16[768,1024]{1,0:T(8,128)(2,1)}, u32[]{:S(2)}, u32[]{:S(2)}) collective-permute-start(bf16[768,1024]{1,0:T(8,128)(2,1)} %collective-permute-done.16.refs_4_), channel_id=1, source_target_pairs={{0,16},{16,0},{1,17},{17,1},{2,18},{18,2},{3,19},{19,3},{4,20},{20... | collective-permute-start | bytes 4718600 | tf_op jit(solution)/shard_map/ppermute | solution.py:568
  150.9 34.9 %copy-start.8 = (s32[3]{0:T(128)S(1)}, s32[3]{0:T(128)}, u32[]{:S(2)}) copy-start(s32[3]{0:T(128)} %live_ref.1) | copy-start | bytes 40
  150.9 29.3 %collective-permute-start.17 = (bf16[512,1024]{1,0:T(8,128)(2,1)}, bf16[512,1024]{1,0:T(8,128)(2,1)}, u32[]{:S(2)}, u32[]{:S(2)}) collective-permute-start(bf16[512,1024]{1,0:T(8,128)(2,1)} %constant_dynamic-slice_fusion.1), channel_id=1, source_target_pairs={{0,2},{1,3},{2,0},{3,1},{4,6},{5,7},{6,4},{7,5},{8,10},{9,11},{10,... | collective-permute-start | bytes 3145736 | tf_op jit(solution)/shard_map/ppermute | solution.py:503
  151.2 19.2 %collective-permute-start.18 = (f32[3,256,128]{2,1,0:T(8,128)S(1)}, f32[3,256,128]{2,1,0:T(8,128)S(1)}, u32[]{:S(2)}, u32[]{:S(2)}) collective-permute-start(f32[3,256,128]{2,1,0:T(8,128)S(1)} %add.104.here_ref), channel_id=1, source_target_pairs={{0,8},{4,12},{8,0},{12,4},{1,9},{5,13},{9,1},{13,5},{2,10},{6,14},... | collective-permute-start | bytes 1179656 | tf_op jit(solution)/shard_map/ppermute | solution.py:503
  170.4 0.8 copy-start.7
  178.2 243.0 %collective-permute-start.26 = (bf16[3,64,5120]{2,1,0:T(8,128)(2,1)}, bf16[3,64,5120]{2,1,0:T(8,128)(2,1)S(1)}, u32[]{:S(2)}, u32[]{:S(2)}) collective-permute-start(bf16[3,64,5120]{2,1,0:T(8,128)(2,1)} %get-tuple-element.68.refs_0_), channel_id=1, source_target_pairs={{0,2},{1,3},{2,0},{3,1},{4,6},{5,7},{6,4},{7,5},{8,10},{9,11},{10,... | collective-permute-start | bytes 5898248 | tf_op jit(solution)/shard_map/ppermute | solution.py:503
  179.4 219.1 %collective-permute-start.22 = (bf16[768,1024]{1,0:T(8,128)(2,1)S(1)}, bf16[768,1024]{1,0:T(8,128)(2,1)}, u32[]{:S(2)}, u32[]{:S(2)}) collective-permute-start(bf16[768,1024]{1,0:T(8,128)(2,1)S(1)} %collective-permute-done.10.refs_4_), channel_id=1, source_target_pairs={{0,1},{1,0},{2,3},{3,2},{4,5},{5,4},{6,7},{7,6},{8,9},{9,8},{10,11... | collective-permute-start | bytes 4718600 | tf_op jit(solution)/shard_map/ppermute | solution.py:503
  183.7 215.7 %collective-permute-start.24 = (bf16[768,1024]{1,0:T(8,128)(2,1)}, bf16[768,1024]{1,0:T(8,128)(2,1)}, u32[]{:S(2)}, u32[]{:S(2)}) collective-permute-start(bf16[768,1024]{1,0:T(8,128)(2,1)} %collective-permute-done.23.refs_6_), channel_id=1, source_target_pairs={{0,1},{1,0},{2,3},{3,2},{4,5},{5,4},{6,7},{7,6},{8,9},{9,8},{10,11... | collective-permute-start | bytes 4718600 | tf_op jit(solution)/shard_map/ppermute | solution.py:503
  184.6 214.8 %collective-permute-start.21 = (bf16[512,1024]{1,0:T(8,128)(2,1)}, bf16[512,1024]{1,0:T(8,128)(2,1)}, u32[]{:S(2)}, u32[]{:S(2)}) collective-permute-start(bf16[512,1024]{1,0:T(8,128)(2,1)} %collective-permute-done.17.refs_2_), channel_id=1, source_target_pairs={{0,1},{1,0},{2,3},{3,2},{4,5},{5,4},{6,7},{7,6},{8,9},{9,8},{10,11... | collective-permute-start | bytes 3145736 | tf_op jit(solution)/shard_map/ppermute | solution.py:503
  184.6 236.7 %collective-permute-start.20 = (bf16[512,1024]{1,0:T(8,128)(2,1)}, bf16[512,1024]{1,0:T(8,128)(2,1)}, u32[]{:S(2)}, u32[]{:S(2)}) collective-permute-start(bf16[512,1024]{1,0:T(8,128)(2,1)} %collective-permute-done.17.refs_2_), channel_id=1, source_target_pairs={{0,16},{16,0},{1,17},{17,1},{2,18},{18,2},{3,19},{19,3},{4,20},{20... | collective-permute-start | bytes 3145736 | tf_op jit(solution)/shard_map/ppermute | solution.py:568
  398.5 24.7 %collective-permute-start.28 = (bf16[3,64,5120]{2,1,0:T(8,128)(2,1)}, bf16[3,64,5120]{2,1,0:T(8,128)(2,1)}, u32[]{:S(2)}, u32[]{:S(2)}) collective-permute-start(bf16[3,64,5120]{2,1,0:T(8,128)(2,1)} %get-tuple-element.68.refs_0_), channel_id=1, source_target_pairs={{0,1},{1,0},{2,3},{3,2},{4,5},{5,4},{6,7},{7,6},{8,9},{9,8},{10,11... | collective-permute-start | bytes 5898248 | tf_op jit(solution)/shard_map/ppermute | solution.py:503
  421.2 3.0 copy-start.2
  421.2 15.9 %collective-permute-start.27 = (bf16[3,64,5120]{2,1,0:T(8,128)(2,1)S(1)}, bf16[3,64,5120]{2,1,0:T(8,128)(2,1)}, u32[]{:S(2)}, u32[]{:S(2)}) collective-permute-start(bf16[3,64,5120]{2,1,0:T(8,128)(2,1)S(1)} %collective-permute-done.26.refs_0_), channel_id=1, source_target_pairs={{0,1},{1,0},{2,3},{3,2},{4,5},{5,4},{6,7},{7,6},{8,9},{9,8},{10,11... | collective-permute-start | bytes 5898248 | tf_op jit(solution)/shard_map/ppermute | solution.py:503
  421.3 5.3 %collective-permute-start.25 = (bf16[512,1024]{1,0:T(8,128)(2,1)}, bf16[512,1024]{1,0:T(8,128)(2,1)S(1)}, u32[]{:S(2)}, u32[]{:S(2)}) collective-permute-start(bf16[512,1024]{1,0:T(8,128)(2,1)} %collective-permute-done.20.refs_2_), channel_id=1, source_target_pairs={{0,1},{1,0},{2,3},{3,2},{4,5},{5,4},{6,7},{7,6},{8,9},{9,8},{10,11... | collective-permute-start | bytes 3145736 | tf_op jit(solution)/shard_map/ppermute | solution.py:503
  426.6 1.0 copy-start.6

commit v2 on v1

--- a/solution.py
+++ b/solution.py
@@ -203,39 +203,9 @@
     )(live, here, there, hidden, grad)
 
 
-def join_kernel(n, *refs):
-    at_ref, piece_refs, (out_ref, sem) = refs[0], refs[1 : 1 + n], refs[1 + n :]
-    deep = piece_refs[0].shape[1]
-
-    def copy(k):
-        lanes = pl.ds(pl.multiple_of(at_ref[k] * deep, deep), deep)
-        return pltpu.make_async_copy(piece_refs[k], out_ref.at[:, lanes], sem.at[k])
-
-    for k in range(n):
-        pl.when(at_ref[k] >= 0)(lambda k=k: copy(k).start())
-    for k in range(n):
-        pl.when(at_ref[k] >= 0)(lambda k=k: copy(k).wait())
-
-
-def join(at, pieces, parts):
-    rows, deep = pieces[0].shape
-    anywhere = pl.BlockSpec(memory_space=pl.ANY)
-    return pl.pallas_call(
-        functools.partial(join_kernel, len(pieces)),
-        grid_spec=pltpu.PrefetchScalarGridSpec(
-            num_scalar_prefetch=1,
-            grid=(1,),
-            in_specs=[anywhere] * len(pieces),
-            out_specs=anywhere,
-            scratch_shapes=[pltpu.SemaphoreType.DMA((len(pieces),))],
-        ),
-        out_shape=jax.ShapeDtypeStruct((rows, parts * deep), bf16),
-        **params((0, 4 * rows * parts * deep)),
-    )(at, *pieces)
-
-
-def base_kernel(n_dp, tiles, n_chunks, blocks, scalars_ref, kept_ref, *refs):
+def base_kernel(n_dp, tiles, n_chunks, n_kept, count, scalars_ref, *refs):
     near = n_dp // 2
+    kept_refs, refs = refs[:n_kept], refs[n_kept:]
     near_refs = refs[:near]
     far_refs = refs[near : near + n_chunks * near]
     coef_ref, block_ref = refs[near + n_chunks * near : near + n_chunks * near + 2]
@@ -245,7 +215,6 @@
     deep = depth // n_dp
     height = coef_ref.shape[1]
     steps = len(tiles)
-    rows = pl.ds(blocks[0] * height, len(blocks) * height)
     token_ref[...] = jnp.zeros_like(token_ref)
 
     def lanes(r):
@@ -278,11 +247,15 @@
             block_ref.at[:, :, span(j)], factor.at[slot], factor_sem.at[slot]
         )
 
-    def columns(r):
-        return pltpu.make_async_copy(kept_ref.at[:, lanes(r)], kept.at[:, lanes(r)], kept_sem.at[r])
+    at = [scalars_ref[steps + n_dp + count + k] for k in range(n_kept)]
+
+    def columns(k):
+        wide = kept_refs[k].shape[1]
+        place = pl.ds(pl.multiple_of(at[k] * wide, wide), wide)
+        return pltpu.make_async_copy(kept_refs[k], kept.at[:, place], kept_sem.at[k])
 
     def store(j, slot):
-        return pltpu.make_async_copy(result.at[slot], out_ref.at[rows, span(j)], out_sem.at[slot])
+        return pltpu.make_async_copy(result.at[slot], out_ref.at[:, span(j)], out_sem.at[slot])
 
     def load(j, slot):
         for r in range(n_dp):
@@ -293,24 +266,31 @@
     over_last = (((1,), (1,)), ((), ()))
 
     def finish(slot, total):
-        for k, b in enumerate(blocks):
+        for b in range(count):
             extra = jnp.dot(coef_ref[b], factor[slot, b], preferred_element_type=f32)
-            here = total[k * height : (k + 1) * height] + extra
+            here = total[b * height : (b + 1) * height] + extra
             valid = lax.broadcasted_iota(i32, here.shape, 0) < scalars_ref[steps + n_dp + b]
-            result[slot, k * height : (k + 1) * height, :] = jnp.where(valid, here, 0.0).astype(
+            result[slot, b * height : (b + 1) * height, :] = jnp.where(valid, here, 0.0).astype(
                 bf16
             )
 
+    for k in range(n_kept):
+        pl.when(at[k] >= 0)(lambda k=k: columns(k).start())
     for r in range(n_dp):
-        columns(r).start()
         for copy in loads(0, 0, r):
             copy.start()
     factors(0, 0).start()
     if steps > 1:
         load(1, 1)
+    matching = kept_refs[0].shape[1] == deep
+    if not matching:
+        for k in range(n_kept):
+            pl.when(at[k] >= 0)(lambda k=k: columns(k).wait())
     total = None
     for r in range(n_dp):
-        columns(r).wait()
+        if matching:
+            for k in range(n_kept):
+                pl.when(at[k] == scalars_ref[steps + r])(lambda k=k: columns(k).wait())
         for copy in loads(0, 0, r):
             copy.wait()
         part = lax.dot_general(
@@ -348,12 +328,13 @@
         store(j, j % 2).wait()
 
 
-def base(places, scalars, kept, near, chunks, tiles, tile, coef, block_a, blocks, held, token):
-    rows, depth = kept.shape
+def base(places, scalars, kept, near, chunks, tiles, tile, coef, block_a, held, token):
+    rows = kept[0].shape[0]
     count, rank, ff = block_a.shape
     top = len(near)
+    depth = 2 * top * near[0].shape[1]
     anywhere = pl.BlockSpec(memory_space=pl.ANY)
-    operands = [kept] + [near[r] for r in range(top)]
+    operands = [*kept, *[near[r] for r in range(top)]]
     for piece in chunks:
         operands += [piece[r] for r in range(top, 2 * top)]
     in_specs = [anywhere] * len(operands)
@@ -367,7 +348,7 @@
     most = max(len(segments) for segments in tiles)
     span = tile * len(tiles)
     return pl.pallas_call(
-        functools.partial(base_kernel, 2 * top, tiles, len(chunks), blocks),
+        functools.partial(base_kernel, 2 * top, tiles, len(chunks), len(kept), count),
         grid_spec=pltpu.PrefetchScalarGridSpec(
             num_scalar_prefetch=1,
             grid=(1,),
@@ -378,14 +359,14 @@
                 pltpu.VMEM((2, tile, depth), bf16),
                 pltpu.VMEM((2, count, rank, tile), bf16),
                 pltpu.VMEM((2, rows, tile), bf16),
-                pltpu.SemaphoreType.DMA((2 * top,)),
+                pltpu.SemaphoreType.DMA((len(kept),)),
                 pltpu.SemaphoreType.DMA((2, 2 * top, most)),
                 pltpu.SemaphoreType.DMA((2,)),
                 pltpu.SemaphoreType.DMA((2,)),
             ],
         ),
         out_shape=[
-            jax.ShapeDtypeStruct((rows // len(blocks) * count, ff), bf16),
+            jax.ShapeDtypeStruct((rows, ff), bf16),
             jax.ShapeDtypeStruct((8, 128), f32),
         ],
         input_output_aliases=aliases,
@@ -395,7 +376,7 @@
 
 def add_kernel(pieces, count, slots_ref, *refs):
     term_refs = refs[:pieces]
-    a_ref, b_ref, terms, a, b, term_sem, a_sem, b_sem = refs[pieces + 2 :]
+    a_ref, b_ref, terms, a, b, term_sem, a_sem, b_sem = refs[pieces + 3 :]
     local, _, ff = a.shape
 
     def load(k):
@@ -447,7 +428,7 @@
         pl.when(hit[j])(lambda j=j: wait(whole(j, False)))
 
 
-def add_terms(slots, pieces, grad_a, grad_b):
+def add_terms(slots, pieces, grad_a, grad_b, token):
     count, rank, both = pieces[0].shape
     anywhere = pl.BlockSpec(memory_space=pl.ANY)
     n = len(pieces)
@@ -457,7 +438,7 @@
         grid_spec=pltpu.PrefetchScalarGridSpec(
             num_scalar_prefetch=1,
             grid=(1,),
-            in_specs=[anywhere] * (n + 2),
+            in_specs=[anywhere] * (n + 3),
             out_specs=[anywhere] * 2,
             scratch_shapes=[
                 pltpu.VMEM((n * count, rank, both), bf16),
@@ -472,9 +453,9 @@
             jax.ShapeDtypeStruct(grad_a.shape, f32),
             jax.ShapeDtypeStruct(grad_b.shape, f32),
         ],
-        input_output_aliases={n + 1: 0, n + 2: 1},
+        input_output_aliases={n + 2: 0, n + 3: 1},
         **params((1, 1)),
-    )(slots, *pieces, grad_a, grad_b)
+    )(slots, *pieces, token, grad_a, grad_b)
 
 
 def on_device(
@@ -537,7 +518,7 @@
     share = ff // n_groups
     if share % 2048 == 0:
         unit, tile = share // 8, share // 4
-        sizes = [3 * unit, 3 * unit, 2 * unit]
+        sizes = [2 * unit] * 4
     else:
         tile = share
         sizes = [share]
@@ -596,9 +577,9 @@
     part, block_a, grad_a, grad_b = project(
         *places(ready), a_near, b_near, far, hidden, output_gradient
     )
+    third_hop = hop(*past)
     cross(*past)
-    fill(crossed[:1], *past)
-    third_hop = hop(*past)
+    cross(*past)
     sums = [part]
     bit = 1
     while bit < n_fsdp:
@@ -607,32 +588,35 @@
             sums.append(sums[-2] + sums[-1])
         bit *= 2
     total, other = sums[-2:]
-    past = [sums[2], *flat(*crossed), *third_hop]
+    turn(part)
+    past = [sums[2], *flat(*crossed[:3], *sum(turned[:2], [])), *third_hop]
     cross(*past)
     turn(*past)
-    fill(crossed[1:2], *past)
-    fill(turned[0], *past)
-    past = [other, *flat(*crossed)]
-    fill(crossed[2:], *past)
+    fill(crossed[:2], *past)
+    past = [other, *flat(*crossed, *sum(turned, []))]
     terms, coef = block_terms(island_live_rows, total, other, hidden, output_gradient)
     far_terms = swap(terms, top)
+    turn(*past)
+    fill(crossed[2:3], *past)
+    for pieces in turned[:2]:
+        fill(pieces, *past)
     near_terms = spread({0: behind(terms, *past)})
-    turn(*past)
-    for pieces in turned[1:2]:
-        fill(pieces, *past)
     if line:
-        kept = join(jnp.stack(at).astype(i32), pieces_of_kept, n_fsdp)
+        at = jnp.stack(at).astype(i32)
     else:
-        kept = lax.all_gather(output_gradient, "fsdp", axis=1, tiled=True)
+        pieces_of_kept = [lax.all_gather(output_gradient, "fsdp", axis=1, tiled=True)]
+        at = jnp.zeros((1,), i32)
 
     relative = [both_slots[r][:count] for r in near] + [both_slots[r][count:] for r in near]
     relative = jnp.concatenate(relative) - me * local
     edge = count * len(near)
     grad_a, grad_b = add_terms(
-        relative[:edge], [near_terms[r] for r in near], grad_a, grad_b
-    )
-
-    scalars = jnp.concatenate([jnp.stack([me ^ r for r in range(n_dp)]).astype(i32), island_live_rows])
+        relative[:edge], [near_terms[r] for r in near], grad_a, grad_b, coef[0, :8]
+    )
+
+    scalars = jnp.concatenate(
+        [jnp.stack([me ^ r for r in range(n_dp)]).astype(i32), island_live_rows, at]
+    )
     grad_hidden = token = None
 
     def multiply(*where):
@@ -650,25 +634,24 @@
                     tiles[-1].append((chunks.index((shift, j)), low - first, high - low))
         pieces = [turned[j][shift - 1] if shift else crossed[j] for shift, j in chunks]
         grad_hidden, token = base(
-            places, scalars, kept, whole, pieces, tiles, tile, coef, block_a, list(range(count)),
+            places, scalars, pieces_of_kept, whole, pieces, tiles, tile, coef, block_a,
             grad_hidden, token,
         )
 
     others = range(1, n_groups)
     if share > tile:
-        multiply((0, 0), (0, 1), (0, 2))
-        multiply((0, 3), *[(g, t) for g in others for t in range(3)])
+        multiply((0, 0), (0, 1), (0, 2), *[(g, t) for g in others for t in range(2)])
+        fill(crossed[3:], token)
         for pieces in turned[2:]:
             fill(pieces, token)
-        early = token
-        multiply(*[(g, 3) for g in others])
+        scalars = behind(scalars, grad_b)
+        multiply((0, 3), *[(g, t) for g in others for t in range(2, 4)])
     else:
         multiply(*[(g, 0) for g in range(n_groups)])
-        early = token
-
-    all_far = spread({top: behind(far_terms, early)})
+
+    all_far = spread({top: behind(far_terms, token)})
     grad_a, grad_b = add_terms(
-        relative[edge:], [all_far[r + top] for r in near], grad_a, grad_b
+        relative[edge:], [all_far[r + top] for r in near], grad_a, grad_b, token
     )
     return grad_hidden, jnp.swapaxes(grad_a, 1, 2), grad_b
 

time: 444 us -> 246 us (0.55)
  Pallas kernels: 267 us -> 77.5 us
    pallas_call x1 -> x0, Pallas kernels: 192 us -> none  [join(): pl.pallas_call(functools.partial(join_kernel, len(pieces)), grid_spec=plt...]
    ppermute x20 -> x23, waiting for transfers between devices: 57.4 us -> 72.9 us  [swap(): return lax.ppermute(value, axis, [(i, i ^ bit) for i in range(size)])]
    ppermute x6, waiting for transfers between devices: 23.5 us -> 14.2 us  [hop(): pieces_of_kept.append(lax.ppermute(behind(piece, *after), 'fsdp', pairs))]
    ppermute x3 -> x4, waiting for transfers between devices: 33 us -> 23.7 us  [turn(): turned[j].append({top: lax.ppermute(piece, 'groups', ring)})]
    pallas_call x2, Pallas kernels: 2.02 us -> 8.45 us  [add_terms(): pl.pallas_call(functools.partial(add_kernel, n, count), grid_spec=pltpu.P...]
    ppermute x20 -> x23, starting transfers between devices: 19.5 us -> 15.4 us  [swap(): return lax.ppermute(value, axis, [(i, i ^ bit) for i in range(size)])]
    pallas_call x3 -> x2, Pallas kernels: 49.7 us -> 46 us  [base(): pl.pallas_call(functools.partial(base_kernel, 2 * top, tiles, len(chunks)...]
  transfers between devices with their start and end apart: 29 -> 33, of which waited for: 12 -> 13; matrix products, arithmetic and copies ran while one was open for 3% -> 5% of each run, Pallas kernels for 61% -> 30%
where the time goes in v2:
time: 246 us; the launch traced here: 241 us
  waiting for transfers between devices  111 us (45%)
  Pallas kernels  77.5 us (32%)
  starting transfers between devices  38.6 us (16%)
  local copies, waits for them, and re-layouts  8.24 us (3%)
  other arithmetic  5.05 us (2%)
    ppermute x23, waiting for transfers between devices, swap(): return lax.ppermute(value, axis, [(i, i ^ bit) for i in range(size)])  72.9 us
    pallas_call x2, Pallas kernels, base(): pl.pallas_call(functools.partial(base_kernel, 2 * top, tiles, len(chunks)...  46 us
    ppermute x4, waiting for transfers between devices, turn(): turned[j].append({top: lax.ppermute(piece, 'groups', ring)})  23.7 us
    ppermute x6, starting transfers between devices, hop(): pieces_of_kept.append(lax.ppermute(behind(piece, *after), 'fsdp', pairs))  18.2 us
    ppermute x23, starting transfers between devices, swap(): return lax.ppermute(value, axis, [(i, i ^ bit) for i in range(size)])  15.4 us
    ppermute x6, waiting for transfers between devices, hop(): pieces_of_kept.append(lax.ppermute(behind(piece, *after), 'fsdp', pairs))  14.2 us
    pallas_call x1, Pallas kernels, project(): pl.pallas_call(functools.partial(project_kernel, pieces), grid_spec=pltpu...  11.2 us
    pallas_call x2, Pallas kernels, add_terms(): pl.pallas_call(functools.partial(add_kernel, n, count), grid_spec=pltpu.P...  8.45 us
  transfers between devices with their start and end apart: 33, of which 13 were waited for; matrix products, arithmetic and copies ran while one was open for 5% of the time, Pallas kernels for 30%

profile of v2, /device:TPU:11, one launch (start us, length us, event | category | flops | bytes accessed | tf_op | source)
XLA Modules:
  0.0 241.2 jit_solution(18282782505677709060)
XLA Ops:
  0.6 0.7 collective-permute-start.1
  1.4 3.2 %collective-permute-start.4 = (bf16[768,1024]{1,0:T(8,128)(2,1)}, bf16[768,1024]{1,0:T(8,128)(2,1)S(1)}, u32[]{:S(2)}, u32[]{:S(2)}) collective-permute-start(bf16[768,1024]{1,0:T(8,128)(2,1)} %refs_0_.3), channel_id=1, source_target_pairs={{0,4},{4,8},{8,12},{1,5},{5,9},{9,13},{2,6},{6,10},{10,14},{3,7},{... | collective-permute-start | bytes 4718600 | tf_op jit(solution)/shard_map/ppermute | solution.py:511
  4.6 2.2 collective-permute-start.5
  6.8 0.9 select_reduce_fusion
  7.6 0.3 collective-permute-start
  7.9 0.9 collective-permute-start.2
  8.8 4.3 %constant_dynamic-slice_fusion = (bf16[512,1024]{1,0:T(8,128)(2,1)}, bf16[512,1024]{1,0:T(8,128)(2,1)}, bf16[512,1024]{1,0:T(8,128)(2,1)}, bf16[512,1024]{1,0:T(8,128)(2,1)}) fusion(bf16[4096,1024]{1,0:T(8,128)(2,1)} %refs_7_.1, s32[]{:T(128)S(6)} %select_n.80, s32[]{:T(128)S(6)} %select_n.78, s32[]{:T(128)S(6)} %select_n.74, s32[]{:T(128)S(6)} %select_n.79), kind=kLoop, calls=%fused_computation.14 | loop fusion | bytes 8388624 | tf_op jit(solution)/shard_map/dynamic_slice | solution.py:537
  13.1 1.2 collective-permute-start.6
  14.3 0.6 compare_select_fusion.1
  14.9 0.6 pad_add_fusion.1.index_ref
  15.5 4.8 %shard_map.103 = bf16[3,64,5120]{2,1,0:T(8,128)(2,1)} custom-call(s32[6]{0:T(128)} %pad_add_fusion.1.index_ref, s32[3]{0:T(128)} %get-tuple-element.97.source_ref, bf16[8,64,4096]{2,1,0:T(8,128)(2,1)} %bitcast.25, bf16[8,64,4096]{2,1,0:T(8,128)(2,1)} %collective-permute-done.1.refs_1_, bf16[8,64,1024]{2,1,0:T(8,128)(2,1)} %refs_2_.3, ...), custom_call_target="tpu_custom_call" | custom-call | bytes 5898240 | tf_op jit(solution)/shard_map/pallas_call | solution.py:54
  20.3 0.3 collective-permute-start.3
  20.6 17.6 %collective-permute-done.6.refs_9_ = bf16[512,1024]{1,0:T(8,128)(2,1)} collective-permute-done((bf16[512,1024]{1,0:T(8,128)(2,1)}, bf16[512,1024]{1,0:T(8,128)(2,1)}, u32[]{:S(2)}, u32[]{:S(2)}) %collective-permute-start.6) | collective-permute-done | bytes 1048608 | tf_op jit(solution)/shard_map/ppermute | solution.py:484
  38.2 1.3 collective-permute-done.4.refs_1_
  39.5 2.9 %collective-permute-done.5.refs_2_ = bf16[768,1024]{1,0:T(8,128)(2,1)S(1)} collective-permute-done((bf16[768,1024]{1,0:T(8,128)(2,1)}, bf16[768,1024]{1,0:T(8,128)(2,1)S(1)}, u32[]{:S(2)}, u32[]{:S(2)}) %collective-permute-start.5) | collective-permute-done | bytes 1572896 | tf_op jit(solution)/shard_map/ppermute | solution.py:511
  42.4 1.1 collective-permute-start.7
  43.5 0.3 collective-permute-start.8
  43.8 3.2 %collective-permute-start.9 = (bf16[768,1024]{1,0:T(8,128)(2,1)S(1)}, bf16[768,1024]{1,0:T(8,128)(2,1)}, u32[]{:S(2)}, u32[]{:S(2)}) collective-permute-start(bf16[768,1024]{1,0:T(8,128)(2,1)S(1)} %collective-permute-done.4.refs_1_), channel_id=1, source_target_pairs={{0,4},{4,8},{8,12},{1,5},{5,9},{9,13},{2,6},{6,10},{10,14},{3,7},{... | collective-permute-start | bytes 4718600 | tf_op jit(solution)/shard_map/ppermute | solution.py:511
  47.0 3.2 %collective-permute-start.10 = (bf16[768,1024]{1,0:T(8,128)(2,1)S(1)}, bf16[768,1024]{1,0:T(8,128)(2,1)}, u32[]{:S(2)}, u32[]{:S(2)}) collective-permute-start(bf16[768,1024]{1,0:T(8,128)(2,1)S(1)} %collective-permute-done.5.refs_2_), channel_id=1, source_target_pairs={{4,0},{8,4},{12,8},{5,1},{9,5},{13,9},{6,2},{10,6},{14,10},{7,3},{... | collective-permute-start | bytes 4718600 | tf_op jit(solution)/shard_map/ppermute | solution.py:511
  50.2 1.3 collective-permute-start.11
  51.5 22.8 %collective-permute-done.11.refs_15_ = bf16[512,1024]{1,0:T(8,128)(2,1)S(1)} collective-permute-done((bf16[512,1024]{1,0:T(8,128)(2,1)}, bf16[512,1024]{1,0:T(8,128)(2,1)S(1)}, u32[]{:S(2)}, u32[]{:S(2)}) %collective-permute-start.11) | collective-permute-done | bytes 1048608 | tf_op jit(solution)/shard_map/ppermute | solution.py:549
  74.3 7.1 %collective-permute-done.9.refs_3_ = bf16[768,1024]{1,0:T(8,128)(2,1)} collective-permute-done((bf16[768,1024]{1,0:T(8,128)(2,1)S(1)}, bf16[768,1024]{1,0:T(8,128)(2,1)}, u32[]{:S(2)}, u32[]{:S(2)}) %collective-permute-start.9) | collective-permute-done | bytes 1572896 | tf_op jit(solution)/shard_map/ppermute | solution.py:511
  81.4 2.9 %collective-permute-done.10.refs_4_ = bf16[768,1024]{1,0:T(8,128)(2,1)} collective-permute-done((bf16[768,1024]{1,0:T(8,128)(2,1)S(1)}, bf16[768,1024]{1,0:T(8,128)(2,1)}, u32[]{:S(2)}, u32[]{:S(2)}) %collective-permute-start.10) | collective-permute-done | bytes 1572896 | tf_op jit(solution)/shard_map/ppermute | solution.py:511
  84.3 3.9 %collective-permute-done.8.refs_4_ = bf16[3,64,5120]{2,1,0:T(8,128)(2,1)} collective-permute-done((bf16[3,64,5120]{2,1,0:T(8,128)(2,1)}, bf16[3,64,5120]{2,1,0:T(8,128)(2,1)}, u32[]{:S(2)}, u32[]{:S(2)}) %collective-permute-start.8) | collective-permute-done | bytes 1966112 | tf_op jit(solution)/shard_map/ppermute | solution.py:484
  88.2 0.3 collective-permute-start.14
  88.4 3.2 %collective-permute-start.17 = (bf16[768,1024]{1,0:T(8,128)(2,1)}, bf16[768,1024]{1,0:T(8,128)(2,1)}, u32[]{:S(2)}, u32[]{:S(2)}) collective-permute-start(bf16[768,1024]{1,0:T(8,128)(2,1)} %collective-permute-done.9.refs_3_), channel_id=1, source_target_pairs={{0,4},{4,8},{8,12},{1,5},{5,9},{9,13},{2,6},{6,10},{10,14},{3,7},{... | collective-permute-start | bytes 4718600 | tf_op jit(solution)/shard_map/ppermute | solution.py:511
  91.6 3.3 %collective-permute-start.18 = (bf16[768,1024]{1,0:T(8,128)(2,1)}, bf16[768,1024]{1,0:T(8,128)(2,1)}, u32[]{:S(2)}, u32[]{:S(2)}) collective-permute-start(bf16[768,1024]{1,0:T(8,128)(2,1)} %collective-permute-done.10.refs_4_), channel_id=1, source_target_pairs={{4,0},{8,4},{12,8},{5,1},{9,5},{13,9},{6,2},{10,6},{14,10},{7,3},{... | collective-permute-start | bytes 4718600 | tf_op jit(solution)/shard_map/ppermute | solution.py:511
  94.9 1.3 collective-permute-start.15
  96.2 0.6 compare_select_fusion
  96.8 0.6 pad_add_fusion.2.index_ref
  97.4 11.2 %shard_map.104 = (f32[3,256,128]{2,1,0:T(8,128)}, bf16[3,64,4096]{2,1,0:T(8,128)(2,1)}, f32[8,64,4096]{2,1,0:T(8,128)}, f32[8,64,1024]{2,1,0:T(8,128)}) custom-call(s32[6]{0:T(128)} %pad_add_fusion.2.index_ref, s32[3]{0:T(128)} %get-tuple-element.91.source_ref, bf16[8,64,4096]{2,1,0:T(8,128)(2,1)} %bitcast.26, ...), custom_call_target="tpu_custom_call" | custom-call | flops 503316480 | bytes 15728640 | tf_op jit(solution)/shard_map/pallas_call | solution.py:121
  108.6 3.7 %collective-permute-done.14.refs_11_ = bf16[512,1024]{1,0:T(8,128)(2,1)} collective-permute-done((bf16[512,1024]{1,0:T(8,128)(2,1)}, bf16[512,1024]{1,0:T(8,128)(2,1)}, u32[]{:S(2)}, u32[]{:S(2)}) %collective-permute-start.14) | collective-permute-done | bytes 1048608 | tf_op jit(solution)/shard_map/ppermute | solution.py:484
  112.3 1.2 collective-permute-start.16
  113.6 0.3 collective-permute-start.12
  113.8 22.1 %collective-permute-done.12 = f32[3,256,128]{2,1,0:T(8,128)S(1)} collective-permute-done((f32[3,256,128]{2,1,0:T(8,128)}, f32[3,256,128]{2,1,0:T(8,128)S(1)}, u32[]{:S(2)}, u32[]{:S(2)}) %collective-permute-start.12) | collective-permute-done | bytes 393248 | tf_op jit(solution)/shard_map/ppermute | solution.py:484
  135.9 1.0 add.113.here_ref
  137.0 2.4 collective-permute-start.19
  139.5 1.2 collective-permute-start.21
  140.7 1.2 collective-permute-start.22
  141.9 16.0 %collective-permute-done.13.there_ref = f32[3,256,128]{2,1,0:T(8,128)S(1)} collective-permute-done((f32[3,256,128]{2,1,0:T(8,128)S(1)}, f32[3,256,128]{2,1,0:T(8,128)S(1)}, u32[]{:S(2)}, u32[]{:S(2)}) %collective-permute-start.13) | collective-permute-done | bytes 393248 | tf_op jit(solution)/shard_map/ppermute | solution.py:484
  158.0 6.0 %collective-permute-done.21.refs_9_ = bf16[512,1024]{1,0:T(8,128)(2,1)S(1)} collective-permute-done((bf16[512,1024]{1,0:T(8,128)(2,1)}, bf16[512,1024]{1,0:T(8,128)(2,1)S(1)}, u32[]{:S(2)}, u32[]{:S(2)}) %collective-permute-start.21) | collective-permute-done | bytes 1048608 | tf_op jit(solution)/shard_map/ppermute | solution.py:484
  164.0 0.9 collective-permute-done.22.refs_11_
  164.9 1.6 collective-permute-start.24
  166.5 0.5 collective-permute-start.26
  167.0 1.2 collective-permute-start.29
  168.2 7.0 %shard_map.105 = (bf16[3,64,5120]{2,1,0:T(8,128)(2,1)}, bf16[3,256,64]{2,1,0:T(8,128)(2,1)}) custom-call(s32[3]{0:T(128)} %live_ref.1, f32[3,256,128]{2,1,0:T(8,128)} %copy-done.4, f32[3,256,128]{2,1,0:T(8,128)} %copy-done.10, bf16[768,4096]{1,0:T(8,128)(2,1)} %hid_ref.1, bf16[768,1024]{1,0:T(8,128)(2,1)} %refs_0_.3), custom_call_target="tpu_custom_call" | custom-call | flops 503316480 | bytes 9830400 | tf_op jit(solution)/shard_map/pallas_call | solution.py:182
  175.3 0.3 collective-permute-start.23
  175.6 0.3 collective-permute-start.31
  175.9 0.1 concatenate.22
  176.0 0.6 concatenate.28.scalars_ref
  176.6 26.8 %shard_map.107 = (bf16[768,4096]{1,0:T(8,128)(2,1)}, f32[8,128]{1,0:T(8,128)}) custom-call(s32[19]{0:T(128)} %concatenate.28.scalars_ref, bf16[768,1024]{1,0:T(8,128)(2,1)} %refs_0_.3, bf16[768,1024]{1,0:T(8,128)(2,1)} %copy-done, bf16[768,1024]{1,0:T(8,128)(2,1)} %copy-done.1, bf16[768,1024]{1,0:T(8,128)(2,1)} %collective-permute-done.9.refs_3_, ...), custom_call_target="tpu_custom_call" | custom-call | flops 1 | bytes 1 | tf_op jit(solution)/shard_map/pallas_call | solution.py:350
  203.3 0.3 collective-permute-start.27
  203.6 0.3 collective-permute-start.28
  203.9 0.3 collective-permute-start.30
  204.3 0.1 add_subtract_fusion
  204.4 0.6 fusion
  205.0 1.2 slice_bitcast_fusion.refs_2_
  206.2 3.7 %shard_map.106 = (f32[8,64,4096]{2,1,0:T(8,128)}, f32[8,64,1024]{2,1,0:T(8,128)}) custom-call(s32[6]{0:T(128)} %get-tuple-element.90.slots_ref, bf16[3,64,5120]{2,1,0:T(8,128)(2,1)} %get-tuple-element.63.refs_0_, bf16[3,64,5120]{2,1,0:T(8,128)(2,1)} %collective-permute-done.23.refs_1_, ...), custom_call_target="tpu_custom_call", output_to_operand_aliasing={{0}: (4, {}), {1}: (5, {})} | custom-call | flops 1 | bytes 1 | tf_op jit(solution)/shard_map/pallas_call | solution.py:436
  209.9 0.7 pad_add_fusion.3.scalars_ref
  210.6 19.3 %shard_map.108 = (bf16[768,4096]{1,0:T(8,128)(2,1)}, f32[8,128]{1,0:T(8,128)}) custom-call(s32[17]{0:T(128)} %pad_add_fusion.3.scalars_ref, bf16[768,1024]{1,0:T(8,128)(2,1)} %refs_0_.3, bf16[768,1024]{1,0:T(8,128)(2,1)} %copy-done, bf16[768,1024]{1,0:T(8,128)(2,1)} %copy-done.1, ...), custom_call_target="tpu_custom_call", output_to_operand_aliasing={{0}: (19, {})} | custom-call | flops 1 | bytes 1 | tf_op jit(solution)/shard_map/pallas_call | solution.py:350
  229.9 1.5 collective-permute-start.32
  231.4 3.6 %collective-permute-done.32.refs_1_ = bf16[3,64,5120]{2,1,0:T(8,128)(2,1)S(1)} collective-permute-done((bf16[3,64,5120]{2,1,0:T(8,128)(2,1)S(1)}, bf16[3,64,5120]{2,1,0:T(8,128)(2,1)S(1)}, u32[]{:S(2)}, u32[]{:S(2)}) %collective-permute-start.32) | collective-permute-done | bytes 1966112 | tf_op jit(solution)/shard_map/ppermute | solution.py:484
  235.0 1.3 copy-done.3
  236.3 4.7 %shard_map.109 = (f32[8,64,4096]{2,1,0:T(8,128)}, f32[8,64,1024]{2,1,0:T(8,128)}) custom-call(s32[6]{0:T(128)} %get-tuple-element.89.slots_ref, bf16[3,64,5120]{2,1,0:T(8,128)(2,1)} %copy-done.2, bf16[3,64,5120]{2,1,0:T(8,128)(2,1)} %copy-done.3, f32[8,128]{1,0:T(8,128)} %get-tuple-element.80.refs_2_, ...), custom_call_target="tpu_custom_call", output_to_operand_aliasing={{0}: (4, {}), {1}: (5, {})} | custom-call | flops 1 | bytes 1 | tf_op jit(solution)/shard_map/pallas_call | solution.py:436
  (49 shorter events, 0.4 us)
Async XLA Ops:
  0.6 14.9 %collective-permute-start.1 = (bf16[8,64,4096]{2,1,0:T(8,128)(2,1)}, bf16[8,64,4096]{2,1,0:T(8,128)(2,1)}, u32[]{:S(2)}, u32[]{:S(2)}) collective-permute-start(bf16[8,64,4096]{2,1,0:T(8,128)(2,1)} %bitcast.24), channel_id=1, source_target_pairs={{0,1},{1,0},{2,3},{3,2},{4,5},{5,4},{6,7},{7,6},{8,9},{9,8},{10,11... | collective-permute-start | bytes 12582920 | tf_op jit(solution)/shard_map/ppermute | solution.py:484
  1.4 38.1 %collective-permute-start.4 = (bf16[768,1024]{1,0:T(8,128)(2,1)}, bf16[768,1024]{1,0:T(8,128)(2,1)S(1)}, u32[]{:S(2)}, u32[]{:S(2)}) collective-permute-start(bf16[768,1024]{1,0:T(8,128)(2,1)} %refs_0_.3), channel_id=1, source_target_pairs={{0,4},{4,8},{8,12},{1,5},{5,9},{9,13},{2,6},{6,10},{10,14},{3,7},{... | collective-permute-start | bytes 4718600 | tf_op jit(solution)/shard_map/ppermute | solution.py:511
  4.6 37.8 %collective-permute-start.5 = (bf16[768,1024]{1,0:T(8,128)(2,1)}, bf16[768,1024]{1,0:T(8,128)(2,1)S(1)}, u32[]{:S(2)}, u32[]{:S(2)}) collective-permute-start(bf16[768,1024]{1,0:T(8,128)(2,1)} %refs_0_.3), channel_id=1, source_target_pairs={{4,0},{8,4},{12,8},{5,1},{9,5},{13,9},{6,2},{10,6},{14,10},{7,3},{... | collective-permute-start | bytes 4718600 | tf_op jit(solution)/shard_map/ppermute | solution.py:511
  7.6 5.4 %collective-permute-start = (s32[3]{0:T(128)S(1)}, s32[3]{0:T(128)S(1)}, u32[]{:S(2)}, u32[]{:S(2)}) collective-permute-start(s32[3]{0:T(128)S(1)} %select_reduce_fusion), channel_id=1, source_target_pairs={{0,2},{1,3},{2,0},{3,1},{4,6},{5,7},{6,4},{7,5},{8,10},{9,11},{10,... | collective-permute-start | bytes 44 | tf_op jit(solution)/shard_map/ppermute | solution.py:484
  7.9 7.6 %collective-permute-start.2 = (bf16[8,64,1024]{2,1,0:T(8,128)(2,1)}, bf16[8,64,1024]{2,1,0:T(8,128)(2,1)}, u32[]{:S(2)}, u32[]{:S(2)}) collective-permute-start(bf16[8,64,1024]{2,1,0:T(8,128)(2,1)} %refs_2_.3), channel_id=1, source_target_pairs={{0,1},{1,0},{2,3},{3,2},{4,5},{5,4},{6,7},{7,6},{8,9},{9,8},{10,11... | collective-permute-start | bytes 3145736 | tf_op jit(solution)/shard_map/ppermute | solution.py:484
  13.1 25.1 %collective-permute-start.6 = (bf16[512,1024]{1,0:T(8,128)(2,1)}, bf16[512,1024]{1,0:T(8,128)(2,1)}, u32[]{:S(2)}, u32[]{:S(2)}) collective-permute-start(bf16[512,1024]{1,0:T(8,128)(2,1)} %get-tuple-element.45), channel_id=1, source_target_pairs={{0,2},{1,3},{2,0},{3,1},{4,6},{5,7},{6,4},{7,5},{8,10},{9,11},{10,... | collective-permute-start | bytes 3145736 | tf_op jit(solution)/shard_map/ppermute | solution.py:484
  20.3 22.1 %collective-permute-start.3 = (s32[6]{0:T(128)S(1)}, s32[6]{0:T(128)S(1)}, u32[]{:S(2)}, u32[]{:S(2)}) collective-permute-start(s32[6]{0:T(128)S(1)} %pad_add_fusion), channel_id=1, source_target_pairs={{0,1},{1,0},{2,3},{3,2},{4,5},{5,4},{6,7},{7,6},{8,9},{9,8},{10,11... | collective-permute-start | bytes 80 | tf_op jit(solution)/shard_map/ppermute | solution.py:484
  39.5 69.2 %copy-start = (bf16[768,1024]{1,0:T(8,128)(2,1)}, bf16[768,1024]{1,0:T(8,128)(2,1)S(1)}, u32[]{:S(2)}) copy-start(bf16[768,1024]{1,0:T(8,128)(2,1)S(1)} %collective-permute-done.4.refs_1_) | copy-start | bytes 4718596
  42.4 66.3 %copy-start.1 = (bf16[768,1024]{1,0:T(8,128)(2,1)}, bf16[768,1024]{1,0:T(8,128)(2,1)S(1)}, u32[]{:S(2)}) copy-start(bf16[768,1024]{1,0:T(8,128)(2,1)S(1)} %collective-permute-done.5.refs_2_) | copy-start | bytes 4718596
  42.4 53.8 %collective-permute-start.7 = (bf16[4096,1024]{1,0:T(8,128)(2,1)}, bf16[4096,1024]{1,0:T(8,128)(2,1)}, u32[]{:S(2)}, u32[]{:S(2)}) collective-permute-start(bf16[4096,1024]{1,0:T(8,128)(2,1)} %refs_7_.1), channel_id=1, source_target_pairs={{0,1},{1,0},{2,3},{3,2},{4,5},{5,4},{6,7},{7,6},{8,9},{9,8},{10,11... | collective-permute-start | bytes 25165832 | tf_op jit(solution)/shard_map/ppermute | solution.py:484
  43.5 44.7 %collective-permute-start.8 = (bf16[3,64,5120]{2,1,0:T(8,128)(2,1)}, bf16[3,64,5120]{2,1,0:T(8,128)(2,1)}, u32[]{:S(2)}, u32[]{:S(2)}) collective-permute-start(bf16[3,64,5120]{2,1,0:T(8,128)(2,1)} %shard_map.103), channel_id=1, source_target_pairs={{0,2},{1,3},{2,0},{3,1},{4,6},{5,7},{6,4},{7,5},{8,10},{9,11},{10,... | collective-permute-start | bytes 5898248 | tf_op jit(solution)/shard_map/ppermute | solution.py:484
  43.8 37.6 %collective-permute-start.9 = (bf16[768,1024]{1,0:T(8,128)(2,1)S(1)}, bf16[768,1024]{1,0:T(8,128)(2,1)}, u32[]{:S(2)}, u32[]{:S(2)}) collective-permute-start(bf16[768,1024]{1,0:T(8,128)(2,1)S(1)} %collective-permute-done.4.refs_1_), channel_id=1, source_target_pairs={{0,4},{4,8},{8,12},{1,5},{5,9},{9,13},{2,6},{6,10},{10,14},{3,7},{... | collective-permute-start | bytes 4718600 | tf_op jit(solution)/shard_map/ppermute | solution.py:511
  47.0 37.3 %collective-permute-start.10 = (bf16[768,1024]{1,0:T(8,128)(2,1)S(1)}, bf16[768,1024]{1,0:T(8,128)(2,1)}, u32[]{:S(2)}, u32[]{:S(2)}) collective-permute-start(bf16[768,1024]{1,0:T(8,128)(2,1)S(1)} %collective-permute-done.5.refs_2_), channel_id=1, source_target_pairs={{4,0},{8,4},{12,8},{5,1},{9,5},{13,9},{6,2},{10,6},{14,10},{7,3},{... | collective-permute-start | bytes 4718600 | tf_op jit(solution)/shard_map/ppermute | solution.py:511
  50.2 24.1 %collective-permute-start.11 = (bf16[512,1024]{1,0:T(8,128)(2,1)}, bf16[512,1024]{1,0:T(8,128)(2,1)S(1)}, u32[]{:S(2)}, u32[]{:S(2)}) collective-permute-start(bf16[512,1024]{1,0:T(8,128)(2,1)} %collective-permute-done.6.refs_9_), channel_id=1, source_target_pairs={{0,16},{16,0},{1,17},{17,1},{2,18},{18,2},{3,19},{19,3},{4,20},{20... | collective-permute-start | bytes 3145736 | tf_op jit(solution)/shard_map/ppermute | solution.py:549
  74.3 10.0 %copy-start.7 = (bf16[512,1024]{1,0:T(8,128)(2,1)}, bf16[512,1024]{1,0:T(8,128)(2,1)S(1)}, u32[]{:S(2)}) copy-start(bf16[512,1024]{1,0:T(8,128)(2,1)S(1)} %collective-permute-done.11.refs_15_) | copy-start | bytes 3145732
  88.2 24.1 %collective-permute-start.14 = (bf16[512,1024]{1,0:T(8,128)(2,1)}, bf16[512,1024]{1,0:T(8,128)(2,1)}, u32[]{:S(2)}, u32[]{:S(2)}) collective-permute-start(bf16[512,1024]{1,0:T(8,128)(2,1)} %get-tuple-element.54), channel_id=1, source_target_pairs={{0,2},{1,3},{2,0},{3,1},{4,6},{5,7},{6,4},{7,5},{8,10},{9,11},{10,... | collective-permute-start | bytes 3145736 | tf_op jit(solution)/shard_map/ppermute | solution.py:484
  88.4 48.5 %collective-permute-start.17 = (bf16[768,1024]{1,0:T(8,128)(2,1)}, bf16[768,1024]{1,0:T(8,128)(2,1)}, u32[]{:S(2)}, u32[]{:S(2)}) collective-permute-start(bf16[768,1024]{1,0:T(8,128)(2,1)} %collective-permute-done.9.refs_3_), channel_id=1, source_target_pairs={{0,4},{4,8},{8,12},{1,5},{5,9},{9,13},{2,6},{6,10},{10,14},{3,7},{... | collective-permute-start | bytes 4718600 | tf_op jit(solution)/shard_map/ppermute | solution.py:511
  91.6 45.3 %collective-permute-start.18 = (bf16[768,1024]{1,0:T(8,128)(2,1)}, bf16[768,1024]{1,0:T(8,128)(2,1)}, u32[]{:S(2)}, u32[]{:S(2)}) collective-permute-start(bf16[768,1024]{1,0:T(8,128)(2,1)} %collective-permute-done.10.refs_4_), channel_id=1, source_target_pairs={{4,0},{8,4},{12,8},{5,1},{9,5},{13,9},{6,2},{10,6},{14,10},{7,3},{... | collective-permute-start | bytes 4718600 | tf_op jit(solution)/shard_map/ppermute | solution.py:511
  94.9 42.0 %collective-permute-start.15 = (bf16[512,1024]{1,0:T(8,128)(2,1)}, bf16[512,1024]{1,0:T(8,128)(2,1)}, u32[]{:S(2)}, u32[]{:S(2)}) collective-permute-start(bf16[512,1024]{1,0:T(8,128)(2,1)} %get-tuple-element.55), channel_id=1, source_target_pairs={{0,2},{1,3},{2,0},{3,1},{4,6},{5,7},{6,4},{7,5},{8,10},{9,11},{10,... | collective-permute-start | bytes 3145736 | tf_op jit(solution)/shard_map/ppermute | solution.py:484
  112.3 24.7 %collective-permute-start.16 = (bf16[512,1024]{1,0:T(8,128)(2,1)}, bf16[512,1024]{1,0:T(8,128)(2,1)}, u32[]{:S(2)}, u32[]{:S(2)}) collective-permute-start(bf16[512,1024]{1,0:T(8,128)(2,1)} %collective-permute-done.14.refs_11_), channel_id=1, source_target_pairs={{0,16},{16,0},{1,17},{17,1},{2,18},{18,2},{3,19},{19,3},{4,20},{20... | collective-permute-start | bytes 3145736 | tf_op jit(solution)/shard_map/ppermute | solution.py:549
  113.6 22.3 %collective-permute-start.12 = (f32[3,256,128]{2,1,0:T(8,128)}, f32[3,256,128]{2,1,0:T(8,128)S(1)}, u32[]{:S(2)}, u32[]{:S(2)}) collective-permute-start(f32[3,256,128]{2,1,0:T(8,128)} %get-tuple-element.52), channel_id=1, source_target_pairs={{0,4},{4,0},{8,12},{12,8},{1,5},{5,1},{9,13},{13,9},{2,6},{6,2},{1... | collective-permute-start | bytes 1179656 | tf_op jit(solution)/shard_map/ppermute | solution.py:484
  136.9 31.3 %copy-start.4 = (f32[3,256,128]{2,1,0:T(8,128)}, f32[3,256,128]{2,1,0:T(8,128)S(1)}, u32[]{:S(2)}) copy-start(f32[3,256,128]{2,1,0:T(8,128)S(1)} %add.113.here_ref) | copy-start | bytes 1179652
  137.0 21.0 %collective-permute-start.19 = (bf16[512,1024]{1,0:T(8,128)(2,1)}, bf16[512,1024]{1,0:T(8,128)(2,1)S(1)}, u32[]{:S(2)}, u32[]{:S(2)}) collective-permute-start(bf16[512,1024]{1,0:T(8,128)(2,1)} %collective-permute-done.6.refs_9_), channel_id=1, source_target_pairs={{0,1},{1,0},{2,3},{3,2},{4,5},{5,4},{6,7},{7,6},{8,9},{9,8},{10,11... | collective-permute-start | bytes 3145736 | tf_op jit(solution)/shard_map/ppermute | solution.py:484
  139.4 18.6 %collective-permute-start.20 = (bf16[512,1024]{1,0:T(8,128)(2,1)}, bf16[512,1024]{1,0:T(8,128)(2,1)S(1)}, u32[]{:S(2)}, u32[]{:S(2)}) collective-permute-start(bf16[512,1024]{1,0:T(8,128)(2,1)} %collective-permute-done.14.refs_11_), channel_id=1, source_target_pairs={{0,1},{1,0},{2,3},{3,2},{4,5},{5,4},{6,7},{7,6},{8,9},{9,8},{10,11... | collective-permute-start | bytes 3145736 | tf_op jit(solution)/shard_map/ppermute | solution.py:484
  139.5 36.4 %copy-start.11 = (s32[3]{0:T(128)S(1)}, s32[3]{0:T(128)}, u32[]{:S(2)}) copy-start(s32[3]{0:T(128)} %live_ref.1) | copy-start | bytes 40
  139.5 24.5 %collective-permute-start.21 = (bf16[512,1024]{1,0:T(8,128)(2,1)}, bf16[512,1024]{1,0:T(8,128)(2,1)S(1)}, u32[]{:S(2)}, u32[]{:S(2)}) collective-permute-start(bf16[512,1024]{1,0:T(8,128)(2,1)} %get-tuple-element.61), channel_id=1, source_target_pairs={{0,2},{1,3},{2,0},{3,1},{4,6},{5,7},{6,4},{7,5},{8,10},{9,11},{10,... | collective-permute-start | bytes 3145736 | tf_op jit(solution)/shard_map/ppermute | solution.py:484
  140.7 24.2 %collective-permute-start.22 = (bf16[512,1024]{1,0:T(8,128)(2,1)}, bf16[512,1024]{1,0:T(8,128)(2,1)S(1)}, u32[]{:S(2)}, u32[]{:S(2)}) collective-permute-start(bf16[512,1024]{1,0:T(8,128)(2,1)} %collective-permute-done.15.refs_13_), channel_id=1, source_target_pairs={{0,16},{16,0},{1,17},{17,1},{2,18},{18,2},{3,19},{19,3},{4,20},{20... | collective-permute-start | bytes 3145736 | tf_op jit(solution)/shard_map/ppermute | solution.py:549
  141.9 16.0 %collective-permute-start.13 = (f32[3,256,128]{2,1,0:T(8,128)S(1)}, f32[3,256,128]{2,1,0:T(8,128)S(1)}, u32[]{:S(2)}, u32[]{:S(2)}) collective-permute-start(f32[3,256,128]{2,1,0:T(8,128)S(1)} %add.113.here_ref), channel_id=1, source_target_pairs={{0,8},{4,12},{8,0},{12,4},{1,9},{5,13},{9,1},{13,5},{2,10},{6,14},... | collective-permute-start | bytes 1179656 | tf_op jit(solution)/shard_map/ppermute | solution.py:484
  158.0 10.3 %copy-start.10 = (f32[3,256,128]{2,1,0:T(8,128)}, f32[3,256,128]{2,1,0:T(8,128)S(1)}, u32[]{:S(2)}) copy-start(f32[3,256,128]{2,1,0:T(8,128)S(1)} %collective-permute-done.13.there_ref) | copy-start | bytes 1179652
  158.0 8.5 %copy-start.8 = (bf16[512,1024]{1,0:T(8,128)(2,1)}, bf16[512,1024]{1,0:T(8,128)(2,1)S(1)}, u32[]{:S(2)}) copy-start(bf16[512,1024]{1,0:T(8,128)(2,1)S(1)} %collective-permute-done.19.refs_10_) | copy-start | bytes 3145732
  158.0 9.0 %copy-start.9 = (bf16[512,1024]{1,0:T(8,128)(2,1)}, bf16[512,1024]{1,0:T(8,128)(2,1)S(1)}, u32[]{:S(2)}) copy-start(bf16[512,1024]{1,0:T(8,128)(2,1)S(1)} %collective-permute-done.20.refs_12_) | copy-start | bytes 3145732
  164.0 39.3 %copy-start.5 = (bf16[512,1024]{1,0:T(8,128)(2,1)}, bf16[512,1024]{1,0:T(8,128)(2,1)S(1)}, u32[]{:S(2)}) copy-start(bf16[512,1024]{1,0:T(8,128)(2,1)S(1)} %collective-permute-done.21.refs_9_) | copy-start | bytes 3145732
  164.9 10.7 %copy-start.6 = (bf16[512,1024]{1,0:T(8,128)(2,1)}, bf16[512,1024]{1,0:T(8,128)(2,1)S(1)}, u32[]{:S(2)}) copy-start(bf16[512,1024]{1,0:T(8,128)(2,1)S(1)} %collective-permute-done.22.refs_11_) | copy-start | bytes 3145732
  164.9 10.7 %collective-permute-start.24 = (bf16[512,1024]{1,0:T(8,128)(2,1)}, bf16[512,1024]{1,0:T(8,128)(2,1)}, u32[]{:S(2)}, u32[]{:S(2)}) collective-permute-start(bf16[512,1024]{1,0:T(8,128)(2,1)} %collective-permute-done.15.refs_13_), channel_id=1, source_target_pairs={{0,1},{1,0},{2,3},{3,2},{4,5},{5,4},{6,7},{7,6},{8,9},{9,8},{10,11... | collective-permute-start | bytes 3145736 | tf_op jit(solution)/shard_map/ppermute | solution.py:484
  166.5 10.1 %collective-permute-start.25 = (bf16[512,1024]{1,0:T(8,128)(2,1)}, bf16[512,1024]{1,0:T(8,128)(2,1)}, u32[]{:S(2)}, u32[]{:S(2)}) collective-permute-start(bf16[512,1024]{1,0:T(8,128)(2,1)} %copy-done.7), channel_id=1, source_target_pairs={{0,1},{1,0},{2,3},{3,2},{4,5},{5,4},{6,7},{7,6},{8,9},{9,8},{10,11... | collective-permute-start | bytes 3145736 | tf_op jit(solution)/shard_map/ppermute | solution.py:484
  166.5 10.1 %collective-permute-start.26 = (bf16[512,1024]{1,0:T(8,128)(2,1)}, bf16[512,1024]{1,0:T(8,128)(2,1)}, u32[]{:S(2)}, u32[]{:S(2)}) collective-permute-start(bf16[512,1024]{1,0:T(8,128)(2,1)} %collective-permute-done.16.refs_17_), channel_id=1, source_target_pairs={{0,1},{1,0},{2,3},{3,2},{4,5},{5,4},{6,7},{7,6},{8,9},{9,8},{10,11... | collective-permute-start | bytes 3145736 | tf_op jit(solution)/shard_map/ppermute | solution.py:484
  167.0 36.9 %collective-permute-start.29 = (bf16[512,1024]{1,0:T(8,128)(2,1)S(1)}, bf16[512,1024]{1,0:T(8,128)(2,1)}, u32[]{:S(2)}, u32[]{:S(2)}) collective-permute-start(bf16[512,1024]{1,0:T(8,128)(2,1)S(1)} %collective-permute-done.21.refs_9_), channel_id=1, source_target_pairs={{0,16},{16,0},{1,17},{17,1},{2,18},{18,2},{3,19},{19,3},{4,20},{20... | collective-permute-start | bytes 3145736 | tf_op jit(solution)/shard_map/ppermute | solution.py:549
  175.3 31.0 %collective-permute-start.23 = (bf16[3,64,5120]{2,1,0:T(8,128)(2,1)}, bf16[3,64,5120]{2,1,0:T(8,128)(2,1)}, u32[]{:S(2)}, u32[]{:S(2)}) collective-permute-start(bf16[3,64,5120]{2,1,0:T(8,128)(2,1)} %get-tuple-element.63.refs_0_), channel_id=1, source_target_pairs={{0,1},{1,0},{2,3},{3,2},{4,5},{5,4},{6,7},{7,6},{8,9},{9,8},{10,11... | collective-permute-start | bytes 5898248 | tf_op jit(solution)/shard_map/ppermute | solution.py:484
  175.6 54.3 %collective-permute-start.31 = (bf16[3,64,5120]{2,1,0:T(8,128)(2,1)}, bf16[3,64,5120]{2,1,0:T(8,128)(2,1)S(1)}, u32[]{:S(2)}, u32[]{:S(2)}) collective-permute-start(bf16[3,64,5120]{2,1,0:T(8,128)(2,1)} %get-tuple-element.63.refs_0_), channel_id=1, source_target_pairs={{0,2},{1,3},{2,0},{3,1},{4,6},{5,7},{6,4},{7,5},{8,10},{9,11},{10,... | collective-permute-start | bytes 5898248 | tf_op jit(solution)/shard_map/ppermute | solution.py:484
  203.3 7.3 %collective-permute-start.27 = (bf16[512,1024]{1,0:T(8,128)(2,1)S(1)}, bf16[512,1024]{1,0:T(8,128)(2,1)}, u32[]{:S(2)}, u32[]{:S(2)}) collective-permute-start(bf16[512,1024]{1,0:T(8,128)(2,1)S(1)} %collective-permute-done.21.refs_9_), channel_id=1, source_target_pairs={{0,1},{1,0},{2,3},{3,2},{4,5},{5,4},{6,7},{7,6},{8,9},{9,8},{10,11... | collective-permute-start | bytes 3145736 | tf_op jit(solution)/shard_map/ppermute | solution.py:484
  203.6 7.0 %collective-permute-start.28 = (bf16[512,1024]{1,0:T(8,128)(2,1)}, bf16[512,1024]{1,0:T(8,128)(2,1)}, u32[]{:S(2)}, u32[]{:S(2)}) collective-permute-start(bf16[512,1024]{1,0:T(8,128)(2,1)} %copy-done.6), channel_id=1, source_target_pairs={{0,1},{1,0},{2,3},{3,2},{4,5},{5,4},{6,7},{7,6},{8,9},{9,8},{10,11... | collective-permute-start | bytes 3145736 | tf_op jit(solution)/shard_map/ppermute | solution.py:484
  203.9 6.7 %collective-permute-start.30 = (bf16[512,1024]{1,0:T(8,128)(2,1)}, bf16[512,1024]{1,0:T(8,128)(2,1)}, u32[]{:S(2)}, u32[]{:S(2)}) collective-permute-start(bf16[512,1024]{1,0:T(8,128)(2,1)} %collective-permute-done.29.refs_13_), channel_id=1, source_target_pairs={{0,1},{1,0},{2,3},{3,2},{4,5},{5,4},{6,7},{7,6},{8,9},{9,8},{10,11... | collective-permute-start | bytes 3145736 | tf_op jit(solution)/shard_map/ppermute | solution.py:484
  229.9 5.1 %copy-start.2 = (bf16[3,64,5120]{2,1,0:T(8,128)(2,1)}, bf16[3,64,5120]{2,1,0:T(8,128)(2,1)S(1)}, u32[]{:S(2)}) copy-start(bf16[3,64,5120]{2,1,0:T(8,128)(2,1)S(1)} %collective-permute-done.31.refs_0_) | copy-start | bytes 5898244
  229.9 5.1 %collective-permute-start.32 = (bf16[3,64,5120]{2,1,0:T(8,128)(2,1)S(1)}, bf16[3,64,5120]{2,1,0:T(8,128)(2,1)S(1)}, u32[]{:S(2)}, u32[]{:S(2)}) collective-permute-start(bf16[3,64,5120]{2,1,0:T(8,128)(2,1)S(1)} %collective-permute-done.31.refs_0_), channel_id=1, source_target_pairs={{0,1},{1,0},{2,3},{3,2},{4,5},{5,4},{6,7},{7,6},{8,9},{9,8},{10,11... | collective-permute-start | bytes 5898248 | tf_op jit(solution)/shard_map/ppermute | solution.py:484
  235.0 1.3 copy-start.3

commit v3 on v2

--- a/solution.py
+++ b/solution.py
@@ -151,8 +151,9 @@
     )(index, source, *a_pieces, *b_pieces, far, hidden, grad)
 
 
-def terms_kernel(live_ref, here_ref, there_ref, hid_ref, grad_ref, terms_ref, coef_ref):
+def terms_kernel(live_ref, here_ref, there_ref, hid_ref, grad_ref, low_ref, high_ref, coef_ref):
     ff = hid_ref.shape[1]
+    cut = low_ref.shape[2]
     rank = coef_ref.shape[2]
     total = here_ref[0] + there_ref[0]
     valid = lax.broadcasted_iota(i32, total.shape, 0) < live_ref[pl.program_id(0)]
@@ -161,11 +162,13 @@
     coef = (adapter_scale * total[:, rank:]).astype(bf16)
     coef_ref[0] = coef
     over_rows = (((0,), (0,)), ((), ()))
-    terms_ref[0, :, :ff] = (
+    term_a = (
         factor_gradient
         * lax.dot_general(coef, hid_ref[...], over_rows, preferred_element_type=f32)
     ).astype(bf16)
-    terms_ref[0, :, ff:] = (
+    low_ref[0] = term_a[:, :cut]
+    high_ref[0, :, : ff - cut] = term_a[:, cut:]
+    high_ref[0, :, ff - cut :] = (
         factor_gradient
         * adapter_scale
         * lax.dot_general(low, grad_ref[...], over_rows, preferred_element_type=f32)
@@ -177,6 +180,7 @@
     rank = both // 2
     rows, ff = hidden.shape
     d = grad.shape[1]
+    cut = (ff + d) // 384 * 128
     own = lambda i, live: (i, 0)
     own3 = lambda i, live: (i, 0, 0)
     return pl.pallas_call(
@@ -191,12 +195,14 @@
                 pl.BlockSpec((height, d), own),
             ],
             out_specs=[
-                pl.BlockSpec((1, rank, ff + d), own3),
+                pl.BlockSpec((1, rank, cut), own3),
+                pl.BlockSpec((1, rank, ff + d - cut), own3),
                 pl.BlockSpec((1, height, rank), own3),
             ],
         ),
         out_shape=[
-            jax.ShapeDtypeStruct((count, rank, ff + d), bf16),
+            jax.ShapeDtypeStruct((count, rank, cut), bf16),
+            jax.ShapeDtypeStruct((count, rank, ff + d - cut), bf16),
             jax.ShapeDtypeStruct((count, height, rank), bf16),
         ],
         **params((2 * rows * rank * (ff + d), 2 * (rows + count * rank) * (ff + d))),
@@ -375,14 +381,22 @@
 
 
 def add_kernel(pieces, count, slots_ref, *refs):
-    term_refs = refs[:pieces]
-    a_ref, b_ref, terms, a, b, term_sem, a_sem, b_sem = refs[pieces + 3 :]
+    term_refs = refs[: 2 * pieces]
+    a_ref, b_ref, terms, a, b, term_sem, a_sem, b_sem = refs[2 * pieces + 3 :]
     local, _, ff = a.shape
+    both = terms.shape[2]
+    cut = term_refs[0].shape[2]
 
     def load(k):
-        return pltpu.make_async_copy(
-            term_refs[k // count].at[k % count], terms.at[k], term_sem.at[k]
-        )
+        lanes = (pl.ds(0, cut), pl.ds(cut, both - cut))
+        return [
+            pltpu.make_async_copy(
+                term_refs[k // count * 2 + part].at[k % count],
+                terms.at[k, :, lanes[part]],
+                term_sem.at[k, part],
+            )
+            for part in range(2)
+        ]
 
     def whole(slot, inward):
         pairs = [(a_ref.at[slot], a.at[slot]), (b_ref.at[slot], b.at[slot])]
@@ -411,12 +425,12 @@
     for j in range(local):
         pl.when(hit[j])(lambda j=j: start(whole(j, True)))
     for k in range(pieces * count):
-        pl.when(owned[k])(lambda k=k: start([load(k)]))
+        pl.when(owned[k])(lambda k=k: start(load(k)))
     for j in range(local):
         pl.when(hit[j])(lambda j=j: wait(whole(j, True)))
 
     def add(k):
-        wait([load(k)])
+        wait(load(k))
         a[wanted[k]] += terms[k, :, :ff].astype(f32)
         b[wanted[k]] += terms[k, :, ff:].astype(f32)
 
@@ -429,22 +443,23 @@
 
 
 def add_terms(slots, pieces, grad_a, grad_b, token):
-    count, rank, both = pieces[0].shape
+    count, rank, _ = pieces[0].shape
+    both = pieces[0].shape[2] + pieces[1].shape[2]
     anywhere = pl.BlockSpec(memory_space=pl.ANY)
-    n = len(pieces)
+    n = len(pieces) // 2
     local = grad_a.shape[0]
     return pl.pallas_call(
         functools.partial(add_kernel, n, count),
         grid_spec=pltpu.PrefetchScalarGridSpec(
             num_scalar_prefetch=1,
             grid=(1,),
-            in_specs=[anywhere] * (n + 3),
+            in_specs=[anywhere] * (2 * n + 3),
             out_specs=[anywhere] * 2,
             scratch_shapes=[
                 pltpu.VMEM((n * count, rank, both), bf16),
                 pltpu.VMEM(grad_a.shape, f32),
                 pltpu.VMEM(grad_b.shape, f32),
-                pltpu.SemaphoreType.DMA((n * count,)),
+                pltpu.SemaphoreType.DMA((n * count, 2)),
                 pltpu.SemaphoreType.DMA((local,)),
                 pltpu.SemaphoreType.DMA((local,)),
             ],
@@ -453,7 +468,7 @@
             jax.ShapeDtypeStruct(grad_a.shape, f32),
             jax.ShapeDtypeStruct(grad_b.shape, f32),
         ],
-        input_output_aliases={n + 2: 0, n + 3: 1},
+        input_output_aliases={2 * n + 2: 0, 2 * n + 3: 1},
         **params((1, 1)),
     )(slots, *pieces, token, grad_a, grad_b)
 
@@ -577,7 +592,6 @@
     part, block_a, grad_a, grad_b = project(
         *places(ready), a_near, b_near, far, hidden, output_gradient
     )
-    third_hop = hop(*past)
     cross(*past)
     cross(*past)
     sums = [part]
@@ -588,19 +602,25 @@
             sums.append(sums[-2] + sums[-1])
         bit *= 2
     total, other = sums[-2:]
-    turn(part)
-    past = [sums[2], *flat(*crossed[:3], *sum(turned[:2], [])), *third_hop]
+    past = [sums[2], *flat(*crossed[1:2])]
+    turn(*past)
+    fill(crossed[:1], *past)
+    fill(turned[0], *past)
+    past = [other, *flat(*crossed, *sum(turned, []))]
+    third_hop = hop(*past)
     cross(*past)
     turn(*past)
-    fill(crossed[:2], *past)
-    past = [other, *flat(*crossed, *sum(turned, []))]
-    terms, coef = block_terms(island_live_rows, total, other, hidden, output_gradient)
-    far_terms = swap(terms, top)
+    low_terms, high_terms, coef = block_terms(
+        island_live_rows, total, other, hidden, output_gradient
+    )
+    far_low = swap(behind(low_terms, *flat(*crossed)), top)
+    past = flat(*crossed[3:])
+    fill(crossed[1:], *past)
+    for pieces in turned[1:3]:
+        fill(pieces, *past)
+    past = [far_low, *third_hop, *flat(*crossed, *sum(turned, []))]
+    far_high = swap(behind(high_terms, *past), top)
     turn(*past)
-    fill(crossed[2:3], *past)
-    for pieces in turned[:2]:
-        fill(pieces, *past)
-    near_terms = spread({0: behind(terms, *past)})
     if line:
         at = jnp.stack(at).astype(i32)
     else:
@@ -609,10 +629,6 @@
 
     relative = [both_slots[r][:count] for r in near] + [both_slots[r][count:] for r in near]
     relative = jnp.concatenate(relative) - me * local
-    edge = count * len(near)
-    grad_a, grad_b = add_terms(
-        relative[:edge], [near_terms[r] for r in near], grad_a, grad_b, coef[0, :8]
-    )
 
     scalars = jnp.concatenate(
         [jnp.stack([me ^ r for r in range(n_dp)]).astype(i32), island_live_rows, at]
@@ -640,19 +656,21 @@
 
     others = range(1, n_groups)
     if share > tile:
-        multiply((0, 0), (0, 1), (0, 2), *[(g, t) for g in others for t in range(2)])
-        fill(crossed[3:], token)
-        for pieces in turned[2:]:
-            fill(pieces, token)
-        scalars = behind(scalars, grad_b)
-        multiply((0, 3), *[(g, t) for g in others for t in range(2, 4)])
+        multiply(*[(0, t) for t in range(4)], *[(g, t) for g in others for t in range(3)])
+        past = [token, far_high]
+        for pieces in turned[3:]:
+            fill(pieces, *past)
+        multiply(*[(g, 3) for g in others])
     else:
         multiply(*[(g, 0) for g in range(n_groups)])
 
-    all_far = spread({top: behind(far_terms, token)})
-    grad_a, grad_b = add_terms(
-        relative[edge:], [all_far[r + top] for r in near], grad_a, grad_b, token
-    )
+    near_low = spread({0: behind(low_terms, *past)})
+    near_high = spread({0: behind(high_terms, *past)})
+    all_low = spread({top: behind(far_low, token)})
+    all_high = spread({top: behind(far_high, token)})
+    terms = [p for r in near for p in (near_low[r], near_high[r])]
+    terms += [p for r in near for p in (all_low[r + top], all_high[r + top])]
+    grad_a, grad_b = add_terms(relative, terms, grad_a, grad_b, token)
     return grad_hidden, jnp.swapaxes(grad_a, 1, 2), grad_b
 
 

time: 246 us -> 256 us (1.041); the launches traced: 241 us -> 254 us
  starting transfers between devices: 38.6 us -> 45.9 us
  waiting for transfers between devices: 111 us -> 117 us
    ppermute x23 -> x26, starting transfers between devices: 15.4 us -> 24.6 us  [swap(): return lax.ppermute(value, axis, [(i, i ^ bit) for i in range(size)])]
    ppermute x6, waiting for transfers between devices: 14.2 us -> 20.5 us  [hop(): pieces_of_kept.append(lax.ppermute(behind(piece, *after), 'fsdp', pairs))]
    ppermute x4, waiting for transfers between devices: 23.7 us -> 30 us  [turn(): turned[j].append({top: lax.ppermute(piece, 'groups', ring)})]
    ppermute x23 -> x26, waiting for transfers between devices: 72.9 us -> 66.7 us  [swap(): return lax.ppermute(value, axis, [(i, i ^ bit) for i in range(size)])]
    pallas_call x2 -> x1, Pallas kernels: 8.45 us -> 7.43 us  [add_terms(): pl.pallas_call(functools.partial(add_kernel, n, count), grid_spec=pltpu.P...]
  transfers between devices with their start and end apart: 33 -> 36, of which waited for: 13 -> 20; matrix products, arithmetic and copies ran while one was open for 5% -> 4% of each run, Pallas kernels for 30% -> 27%
where the time goes in v3:
time: 256 us; the launch traced here: 254 us
  waiting for transfers between devices  117 us (46%)
  Pallas kernels  75.8 us (30%)
  starting transfers between devices  45.9 us (18%)
  local copies, waits for them, and re-layouts  9.26 us (4%)
  other arithmetic  4.92 us (2%)
    ppermute x26, waiting for transfers between devices, swap(): return lax.ppermute(value, axis, [(i, i ^ bit) for i in range(size)])  66.7 us
    pallas_call x2, Pallas kernels, base(): pl.pallas_call(functools.partial(base_kernel, 2 * top, tiles, len(chunks)...  45 us
    ppermute x4, waiting for transfers between devices, turn(): turned[j].append({top: lax.ppermute(piece, 'groups', ring)})  30 us
    ppermute x26, starting transfers between devices, swap(): return lax.ppermute(value, axis, [(i, i ^ bit) for i in range(size)])  24.6 us
    ppermute x6, waiting for transfers between devices, hop(): pieces_of_kept.append(lax.ppermute(behind(piece, *after), 'fsdp', pairs))  20.5 us
    ppermute x6, starting transfers between devices, hop(): pieces_of_kept.append(lax.ppermute(behind(piece, *after), 'fsdp', pairs))  16.3 us
    pallas_call x1, Pallas kernels, project(): pl.pallas_call(functools.partial(project_kernel, pieces), grid_spec=pltpu...  11.7 us
    pallas_call x1, Pallas kernels, add_terms(): pl.pallas_call(functools.partial(add_kernel, n, count), grid_spec=pltpu.P...  7.43 us
  transfers between devices with their start and end apart: 36, of which 20 were waited for; matrix products, arithmetic and copies ran while one was open for 4% of the time, Pallas kernels for 27%

profile of v3, /device:TPU:11, one launch (start us, length us, event | category | flops | bytes accessed | tf_op | source)
XLA Modules:
  0.0 254.2 jit_solution(16511620467052195762)
XLA Ops:
  0.6 0.7 collective-permute-start.3
  1.4 3.2 %collective-permute-start = (bf16[768,1024]{1,0:T(8,128)(2,1)}, bf16[768,1024]{1,0:T(8,128)(2,1)S(1)}, u32[]{:S(2)}, u32[]{:S(2)}) collective-permute-start(bf16[768,1024]{1,0:T(8,128)(2,1)} %refs_0_.3), channel_id=1, source_target_pairs={{0,4},{4,8},{8,12},{1,5},{5,9},{9,13},{2,6},{6,10},{10,14},{3,7},{... | collective-permute-start | bytes 4718600 | tf_op jit(solution)/shard_map/ppermute | solution.py:526
  4.6 2.2 collective-permute-start.1
  6.8 0.9 select_reduce_fusion
  7.9 0.9 collective-permute-start.4
  8.8 4.3 %constant_dynamic-slice_fusion = (bf16[512,1024]{1,0:T(8,128)(2,1)}, bf16[512,1024]{1,0:T(8,128)(2,1)}, bf16[512,1024]{1,0:T(8,128)(2,1)}, bf16[512,1024]{1,0:T(8,128)(2,1)}) fusion(bf16[4096,1024]{1,0:T(8,128)(2,1)} %refs_7_.1, s32[]{:T(128)S(6)} %select_n.79, s32[]{:T(128)S(6)} %select_n.77, s32[]{:T(128)S(6)} %select_n.73, s32[]{:T(128)S(6)} %select_n.78), kind=kLoop, calls=%fused_computation.13 | loop fusion | bytes 8388624 | tf_op jit(solution)/shard_map/dynamic_slice | solution.py:552
  13.1 1.2 collective-permute-start.6
  14.3 0.5 compare_select_fusion.1
  14.8 0.6 pad_add_fusion.index_ref
  15.5 4.8 %shard_map.103 = bf16[3,64,5120]{2,1,0:T(8,128)(2,1)} custom-call(s32[6]{0:T(128)} %pad_add_fusion.index_ref, s32[3]{0:T(128)} %get-tuple-element.99.source_ref, bf16[8,64,4096]{2,1,0:T(8,128)(2,1)} %bitcast.22, bf16[8,64,4096]{2,1,0:T(8,128)(2,1)} %collective-permute-done.3.refs_1_, bf16[8,64,1024]{2,1,0:T(8,128)(2,1)} %refs_2_.3, ...), custom_call_target="tpu_custom_call" | custom-call | bytes 5898240 | tf_op jit(solution)/shard_map/pallas_call | solution.py:54
  20.6 17.6 %collective-permute-done.6.refs_9_ = bf16[512,1024]{1,0:T(8,128)(2,1)} collective-permute-done((bf16[512,1024]{1,0:T(8,128)(2,1)}, bf16[512,1024]{1,0:T(8,128)(2,1)}, u32[]{:S(2)}, u32[]{:S(2)}) %collective-permute-start.6) | collective-permute-done | bytes 1048608 | tf_op jit(solution)/shard_map/ppermute | solution.py:499
  38.2 1.3 collective-permute-done.refs_1_
  39.5 2.9 %collective-permute-done.1.refs_2_ = bf16[768,1024]{1,0:T(8,128)(2,1)S(1)} collective-permute-done((bf16[768,1024]{1,0:T(8,128)(2,1)}, bf16[768,1024]{1,0:T(8,128)(2,1)S(1)}, u32[]{:S(2)}, u32[]{:S(2)}) %collective-permute-start.1) | collective-permute-done | bytes 1572896 | tf_op jit(solution)/shard_map/ppermute | solution.py:526
  42.4 1.1 collective-permute-start.9
  43.8 3.2 %collective-permute-start.7 = (bf16[768,1024]{1,0:T(8,128)(2,1)S(1)}, bf16[768,1024]{1,0:T(8,128)(2,1)S(1)}, u32[]{:S(2)}, u32[]{:S(2)}) collective-permute-start(bf16[768,1024]{1,0:T(8,128)(2,1)S(1)} %collective-permute-done.refs_1_), channel_id=1, source_target_pairs={{0,4},{4,8},{8,12},{1,5},{5,9},{9,13},{2,6},{6,10},{10,14},{3,7},{... | collective-permute-start | bytes 4718600 | tf_op jit(solution)/shard_map/ppermute | solution.py:526
  47.0 2.2 collective-permute-start.8
  49.1 1.3 collective-permute-start.11
  50.4 22.7 %collective-permute-done.11.refs_17_ = bf16[512,1024]{1,0:T(8,128)(2,1)S(1)} collective-permute-done((bf16[512,1024]{1,0:T(8,128)(2,1)}, bf16[512,1024]{1,0:T(8,128)(2,1)S(1)}, u32[]{:S(2)}, u32[]{:S(2)}) %collective-permute-start.11) | collective-permute-done | bytes 1048608 | tf_op jit(solution)/shard_map/ppermute | solution.py:564
  73.2 8.1 %collective-permute-done.7.refs_3_ = bf16[768,1024]{1,0:T(8,128)(2,1)S(1)} collective-permute-done((bf16[768,1024]{1,0:T(8,128)(2,1)S(1)}, bf16[768,1024]{1,0:T(8,128)(2,1)S(1)}, u32[]{:S(2)}, u32[]{:S(2)}) %collective-permute-start.7) | collective-permute-done | bytes 1572896 | tf_op jit(solution)/shard_map/ppermute | solution.py:526
  81.3 2.9 %collective-permute-done.8.refs_4_ = bf16[768,1024]{1,0:T(8,128)(2,1)S(1)} collective-permute-done((bf16[768,1024]{1,0:T(8,128)(2,1)S(1)}, bf16[768,1024]{1,0:T(8,128)(2,1)S(1)}, u32[]{:S(2)}, u32[]{:S(2)}) %collective-permute-start.8) | collective-permute-done | bytes 1572896 | tf_op jit(solution)/shard_map/ppermute | solution.py:526
  84.2 3.9 %collective-permute-done.10.refs_4_ = bf16[3,64,5120]{2,1,0:T(8,128)(2,1)S(1)} collective-permute-done((bf16[3,64,5120]{2,1,0:T(8,128)(2,1)}, bf16[3,64,5120]{2,1,0:T(8,128)(2,1)S(1)}, u32[]{:S(2)}, u32[]{:S(2)}) %collective-permute-start.10) | collective-permute-done | bytes 1966112 | tf_op jit(solution)/shard_map/ppermute | solution.py:499
  88.1 1.3 copy-done.6
  89.6 0.6 compare_select_fusion
  90.2 0.6 pad_add_fusion.2.index_ref
  90.8 11.7 %shard_map.104 = (f32[3,256,128]{2,1,0:T(8,128)}, bf16[3,64,4096]{2,1,0:T(8,128)(2,1)}, f32[8,64,4096]{2,1,0:T(8,128)}, f32[8,64,1024]{2,1,0:T(8,128)}) custom-call(s32[6]{0:T(128)} %pad_add_fusion.2.index_ref, s32[3]{0:T(128)} %get-tuple-element.97.source_ref, bf16[8,64,4096]{2,1,0:T(8,128)(2,1)} %bitcast.23, ...), custom_call_target="tpu_custom_call" | custom-call | flops 503316480 | bytes 15728640 | tf_op jit(solution)/shard_map/pallas_call | solution.py:121
  102.5 0.3 collective-permute-start.12
  102.8 1.2 collective-permute-start.16
  104.0 8.3 %collective-permute-done.12 = f32[3,256,128]{2,1,0:T(8,128)S(1)} collective-permute-done((f32[3,256,128]{2,1,0:T(8,128)}, f32[3,256,128]{2,1,0:T(8,128)S(1)}, u32[]{:S(2)}, u32[]{:S(2)}) %collective-permute-start.12) | collective-permute-done | bytes 393248 | tf_op jit(solution)/shard_map/ppermute | solution.py:499
  112.3 1.0 add.110.here_ref
  113.5 3.1 %collective-permute-start.15 = (bf16[512,1024]{1,0:T(8,128)(2,1)}, bf16[512,1024]{1,0:T(8,128)(2,1)S(1)}, u32[]{:S(2)}, u32[]{:S(2)}) collective-permute-start(bf16[512,1024]{1,0:T(8,128)(2,1)} %collective-permute-done.6.refs_9_), channel_id=1, source_target_pairs={{0,1},{1,0},{2,3},{3,2},{4,5},{5,4},{6,7},{7,6},{8,9},{9,8},{10,11... | collective-permute-start | bytes 3145736 | tf_op jit(solution)/shard_map/ppermute | solution.py:499
  116.6 1.2 collective-permute-start.18
  117.9 0.4 collective-permute-start.13
  118.2 17.7 %collective-permute-done.16.refs_13_ = bf16[512,1024]{1,0:T(8,128)(2,1)} collective-permute-done((bf16[512,1024]{1,0:T(8,128)(2,1)}, bf16[512,1024]{1,0:T(8,128)(2,1)}, u32[]{:S(2)}, u32[]{:S(2)}) %collective-permute-start.16) | collective-permute-done | bytes 1048608 | tf_op jit(solution)/shard_map/ppermute | solution.py:499
  136.0 5.0 %collective-permute-done.18.refs_19_ = bf16[512,1024]{1,0:T(8,128)(2,1)S(1)} collective-permute-done((bf16[512,1024]{1,0:T(8,128)(2,1)}, bf16[512,1024]{1,0:T(8,128)(2,1)S(1)}, u32[]{:S(2)}, u32[]{:S(2)}) %collective-permute-start.18) | collective-permute-done | bytes 1048608 | tf_op jit(solution)/shard_map/ppermute | solution.py:564
  141.3 3.2 %collective-permute-start.19 = (bf16[768,1024]{1,0:T(8,128)(2,1)}, bf16[768,1024]{1,0:T(8,128)(2,1)S(1)}, u32[]{:S(2)}, u32[]{:S(2)}) collective-permute-start(bf16[768,1024]{1,0:T(8,128)(2,1)} %copy-done.2), channel_id=1, source_target_pairs={{0,4},{4,8},{8,12},{1,5},{5,9},{9,13},{2,6},{6,10},{10,14},{3,7},{... | collective-permute-start | bytes 4718600 | tf_op jit(solution)/shard_map/ppermute | solution.py:526
  144.5 2.4 collective-permute-start.20
  146.9 1.3 collective-permute-start.27
  148.2 6.9 %shard_map.105 = (bf16[3,64,1664]{2,1,0:T(8,128)(2,1)}, bf16[3,64,3456]{2,1,0:T(8,128)(2,1)}, bf16[3,256,64]{2,1,0:T(8,128)(2,1)}) custom-call(s32[3]{0:T(128)} %live_ref.1, f32[3,256,128]{2,1,0:T(8,128)} %copy-done.7, f32[3,256,128]{2,1,0:T(8,128)} %copy-done.16, bf16[768,4096]{1,0:T(8,128)(2,1)} %hid_ref.1, bf16[768,1024]{1,0:T(8,128)(2,1)} %refs_0_.3), custom_call_target="tpu_custom_call" | custom-call | flops 503316480 | bytes 9830400 | tf_op jit(solution)/shard_map/pallas_call | solution.py:186
  155.1 9.5 %collective-permute-done.21.refs_15_ = bf16[512,1024]{1,0:T(8,128)(2,1)} collective-permute-done((bf16[512,1024]{1,0:T(8,128)(2,1)}, bf16[512,1024]{1,0:T(8,128)(2,1)}, u32[]{:S(2)}, u32[]{:S(2)}) %collective-permute-start.21) | collective-permute-done | bytes 1048608 | tf_op jit(solution)/shard_map/ppermute | solution.py:499
  164.9 2.6 %collective-permute-start.23 = (bf16[512,1024]{1,0:T(8,128)(2,1)}, bf16[512,1024]{1,0:T(8,128)(2,1)}, u32[]{:S(2)}, u32[]{:S(2)}) collective-permute-start(bf16[512,1024]{1,0:T(8,128)(2,1)} %collective-permute-done.14.refs_11_), channel_id=1, source_target_pairs={{0,1},{1,0},{2,3},{3,2},{4,5},{5,4},{6,7},{7,6},{8,9},{9,8},{10,11... | collective-permute-start | bytes 3145736 | tf_op jit(solution)/shard_map/ppermute | solution.py:499
  167.5 2.2 collective-permute-done.27.refs_21_
  169.7 3.1 %collective-permute-start.24 = (bf16[512,1024]{1,0:T(8,128)(2,1)}, bf16[512,1024]{1,0:T(8,128)(2,1)}, u32[]{:S(2)}, u32[]{:S(2)}) collective-permute-start(bf16[512,1024]{1,0:T(8,128)(2,1)} %collective-permute-done.16.refs_13_), channel_id=1, source_target_pairs={{0,1},{1,0},{2,3},{3,2},{4,5},{5,4},{6,7},{7,6},{8,9},{9,8},{10,11... | collective-permute-start | bytes 3145736 | tf_op jit(solution)/shard_map/ppermute | solution.py:499
  172.8 4.9 %collective-permute-done.19.refs_5_ = bf16[768,1024]{1,0:T(8,128)(2,1)S(1)} collective-permute-done((bf16[768,1024]{1,0:T(8,128)(2,1)}, bf16[768,1024]{1,0:T(8,128)(2,1)S(1)}, u32[]{:S(2)}, u32[]{:S(2)}) %collective-permute-start.19) | collective-permute-done | bytes 1572896 | tf_op jit(solution)/shard_map/ppermute | solution.py:526
  177.7 2.5 collective-permute-start.25
  180.2 0.5 collective-permute-done.20.refs_6_
  180.7 2.7 %collective-permute-start.26 = (bf16[512,1024]{1,0:T(8,128)(2,1)}, bf16[512,1024]{1,0:T(8,128)(2,1)}, u32[]{:S(2)}, u32[]{:S(2)}) collective-permute-start(bf16[512,1024]{1,0:T(8,128)(2,1)} %copy-done.13), channel_id=1, source_target_pairs={{0,1},{1,0},{2,3},{3,2},{4,5},{5,4},{6,7},{7,6},{8,9},{9,8},{10,11... | collective-permute-start | bytes 3145736 | tf_op jit(solution)/shard_map/ppermute | solution.py:499
  183.5 2.5 %collective-permute-done.26.refs_20_ = bf16[512,1024]{1,0:T(8,128)(2,1)} collective-permute-done((bf16[512,1024]{1,0:T(8,128)(2,1)}, bf16[512,1024]{1,0:T(8,128)(2,1)}, u32[]{:S(2)}, u32[]{:S(2)}) %collective-permute-start.26) | collective-permute-done | bytes 1048608 | tf_op jit(solution)/shard_map/ppermute | solution.py:499
  186.1 1.5 collective-permute-done.28.refs_22_
  187.6 1.2 collective-permute-start.30
  188.8 1.2 collective-permute-start.29
  190.0 0.6 concatenate.25.scalars_ref
  190.7 34.4 %shard_map.106 = (bf16[768,4096]{1,0:T(8,128)(2,1)}, f32[8,128]{1,0:T(8,128)}) custom-call(s32[21]{0:T(128)} %concatenate.25.scalars_ref, bf16[768,1024]{1,0:T(8,128)(2,1)} %refs_0_.3, bf16[768,1024]{1,0:T(8,128)(2,1)} %copy-done, bf16[768,1024]{1,0:T(8,128)(2,1)} %copy-done.1, bf16[768,1024]{1,0:T(8,128)(2,1)} %copy-done.2, bf16[768,1024]{1,0:T(8,128)(2,1)} %copy-done.3, ...), custom_call_target="tpu_custom_call" | custom-call | flops 1 | bytes 1 | tf_op jit(solution)/shard_map/pallas_call | solution.py:356
  225.1 0.8 collective-permute-start.31
  225.9 0.6 concatenate.21.scalars_ref
  226.5 1.9 collective-permute-done.31.refs_10_
  228.4 1.0 copy-done.14
  229.4 10.6 %shard_map.107 = (bf16[768,4096]{1,0:T(8,128)(2,1)}, f32[8,128]{1,0:T(8,128)}) custom-call(s32[15]{0:T(128)} %concatenate.21.scalars_ref, bf16[768,1024]{1,0:T(8,128)(2,1)} %refs_0_.3, bf16[768,1024]{1,0:T(8,128)(2,1)} %copy-done, bf16[768,1024]{1,0:T(8,128)(2,1)} %copy-done.1, bf16[768,1024]{1,0:T(8,128)(2,1)} %copy-done.2, ...), custom_call_target="tpu_custom_call", output_to_operand_aliasing={{0}: (15, {})} | custom-call | flops 1 | bytes 1 | tf_op jit(solution)/shard_map/pallas_call | solution.py:356
  240.0 0.4 collective-permute-start.35
  240.6 0.4 collective-permute-start.34
  241.1 0.7 add_subtract_fusion.slots_ref
  241.8 3.3 %collective-permute-done.32.refs_2_ = bf16[3,64,1664]{2,1,0:T(8,128)(2,1)} collective-permute-done((bf16[3,64,1664]{2,1,0:T(8,128)(2,1)S(1)}, bf16[3,64,1664]{2,1,0:T(8,128)(2,1)}, u32[]{:S(2)}, u32[]{:S(2)}) %collective-permute-start.32) | collective-permute-done | bytes 639008 | tf_op jit(solution)/shard_map/ppermute | solution.py:499
  245.3 0.9 copy-done.8
  246.2 0.4 copy-done.9
  246.6 7.4 %shard_map.108 = (f32[8,64,4096]{2,1,0:T(8,128)}, f32[8,64,1024]{2,1,0:T(8,128)}) custom-call(s32[12]{0:T(128)} %add_subtract_fusion.slots_ref, bf16[3,64,1664]{2,1,0:T(8,128)(2,1)} %get-tuple-element.80.refs_0_, bf16[3,64,3456]{2,1,0:T(8,128)(2,1)} %get-tuple-element.81.refs_1_, ...), custom_call_target="tpu_custom_call", output_to_operand_aliasing={{0}: (10, {}), {1}: (11, {})} | custom-call | flops 1 | bytes 1 | tf_op jit(solution)/shard_map/pallas_call | solution.py:451
  (63 shorter events, 2.5 us)
Async XLA Ops:
  0.6 14.9 %collective-permute-start.3 = (bf16[8,64,4096]{2,1,0:T(8,128)(2,1)}, bf16[8,64,4096]{2,1,0:T(8,128)(2,1)}, u32[]{:S(2)}, u32[]{:S(2)}) collective-permute-start(bf16[8,64,4096]{2,1,0:T(8,128)(2,1)} %bitcast.21), channel_id=1, source_target_pairs={{0,1},{1,0},{2,3},{3,2},{4,5},{5,4},{6,7},{7,6},{8,9},{9,8},{10,11... | collective-permute-start | bytes 12582920 | tf_op jit(solution)/shard_map/ppermute | solution.py:499
  1.4 38.1 %collective-permute-start = (bf16[768,1024]{1,0:T(8,128)(2,1)}, bf16[768,1024]{1,0:T(8,128)(2,1)S(1)}, u32[]{:S(2)}, u32[]{:S(2)}) collective-permute-start(bf16[768,1024]{1,0:T(8,128)(2,1)} %refs_0_.3), channel_id=1, source_target_pairs={{0,4},{4,8},{8,12},{1,5},{5,9},{9,13},{2,6},{6,10},{10,14},{3,7},{... | collective-permute-start | bytes 4718600 | tf_op jit(solution)/shard_map/ppermute | solution.py:526
  4.6 37.8 %collective-permute-start.1 = (bf16[768,1024]{1,0:T(8,128)(2,1)}, bf16[768,1024]{1,0:T(8,128)(2,1)S(1)}, u32[]{:S(2)}, u32[]{:S(2)}) collective-permute-start(bf16[768,1024]{1,0:T(8,128)(2,1)} %refs_0_.3), channel_id=1, source_target_pairs={{4,0},{8,4},{12,8},{5,1},{9,5},{13,9},{6,2},{10,6},{14,10},{7,3},{... | collective-permute-start | bytes 4718600 | tf_op jit(solution)/shard_map/ppermute | solution.py:526
  7.6 5.5 %collective-permute-start.2 = (s32[3]{0:T(128)S(1)}, s32[3]{0:T(128)S(1)}, u32[]{:S(2)}, u32[]{:S(2)}) collective-permute-start(s32[3]{0:T(128)S(1)} %select_reduce_fusion), channel_id=1, source_target_pairs={{0,2},{1,3},{2,0},{3,1},{4,6},{5,7},{6,4},{7,5},{8,10},{9,11},{10,... | collective-permute-start | bytes 44 | tf_op jit(solution)/shard_map/ppermute | solution.py:499
  7.9 7.6 %collective-permute-start.4 = (bf16[8,64,1024]{2,1,0:T(8,128)(2,1)}, bf16[8,64,1024]{2,1,0:T(8,128)(2,1)}, u32[]{:S(2)}, u32[]{:S(2)}) collective-permute-start(bf16[8,64,1024]{2,1,0:T(8,128)(2,1)} %refs_2_.3), channel_id=1, source_target_pairs={{0,1},{1,0},{2,3},{3,2},{4,5},{5,4},{6,7},{7,6},{8,9},{9,8},{10,11... | collective-permute-start | bytes 3145736 | tf_op jit(solution)/shard_map/ppermute | solution.py:499
  13.1 25.1 %collective-permute-start.6 = (bf16[512,1024]{1,0:T(8,128)(2,1)}, bf16[512,1024]{1,0:T(8,128)(2,1)}, u32[]{:S(2)}, u32[]{:S(2)}) collective-permute-start(bf16[512,1024]{1,0:T(8,128)(2,1)} %get-tuple-element.47), channel_id=1, source_target_pairs={{0,2},{1,3},{2,0},{3,1},{4,6},{5,7},{6,4},{7,5},{8,10},{9,11},{10,... | collective-permute-start | bytes 3145736 | tf_op jit(solution)/shard_map/ppermute | solution.py:499
  20.3 22.1 %collective-permute-start.5 = (s32[6]{0:T(128)S(1)}, s32[6]{0:T(128)S(1)}, u32[]{:S(2)}, u32[]{:S(2)}) collective-permute-start(s32[6]{0:T(128)S(1)} %pad_add_fusion.1), channel_id=1, source_target_pairs={{0,1},{1,0},{2,3},{3,2},{4,5},{5,4},{6,7},{7,6},{8,9},{9,8},{10,11... | collective-permute-start | bytes 80 | tf_op jit(solution)/shard_map/ppermute | solution.py:499
  39.5 63.0 %copy-start = (bf16[768,1024]{1,0:T(8,128)(2,1)}, bf16[768,1024]{1,0:T(8,128)(2,1)S(1)}, u32[]{:S(2)}) copy-start(bf16[768,1024]{1,0:T(8,128)(2,1)S(1)} %collective-permute-done.refs_1_) | copy-start | bytes 4718596
  42.4 60.1 %copy-start.1 = (bf16[768,1024]{1,0:T(8,128)(2,1)}, bf16[768,1024]{1,0:T(8,128)(2,1)S(1)}, u32[]{:S(2)}) copy-start(bf16[768,1024]{1,0:T(8,128)(2,1)S(1)} %collective-permute-done.1.refs_2_) | copy-start | bytes 4718596
  42.4 47.3 %collective-permute-start.9 = (bf16[4096,1024]{1,0:T(8,128)(2,1)}, bf16[4096,1024]{1,0:T(8,128)(2,1)}, u32[]{:S(2)}, u32[]{:S(2)}) collective-permute-start(bf16[4096,1024]{1,0:T(8,128)(2,1)} %refs_7_.1), channel_id=1, source_target_pairs={{0,1},{1,0},{2,3},{3,2},{4,5},{5,4},{6,7},{7,6},{8,9},{9,8},{10,11... | collective-permute-start | bytes 25165832 | tf_op jit(solution)/shard_map/ppermute | solution.py:499
  43.5 44.6 %collective-permute-start.10 = (bf16[3,64,5120]{2,1,0:T(8,128)(2,1)}, bf16[3,64,5120]{2,1,0:T(8,128)(2,1)S(1)}, u32[]{:S(2)}, u32[]{:S(2)}) collective-permute-start(bf16[3,64,5120]{2,1,0:T(8,128)(2,1)} %shard_map.103), channel_id=1, source_target_pairs={{0,2},{1,3},{2,0},{3,1},{4,6},{5,7},{6,4},{7,5},{8,10},{9,11},{10,... | collective-permute-start | bytes 5898248 | tf_op jit(solution)/shard_map/ppermute | solution.py:499
  43.8 37.5 %collective-permute-start.7 = (bf16[768,1024]{1,0:T(8,128)(2,1)S(1)}, bf16[768,1024]{1,0:T(8,128)(2,1)S(1)}, u32[]{:S(2)}, u32[]{:S(2)}) collective-permute-start(bf16[768,1024]{1,0:T(8,128)(2,1)S(1)} %collective-permute-done.refs_1_), channel_id=1, source_target_pairs={{0,4},{4,8},{8,12},{1,5},{5,9},{9,13},{2,6},{6,10},{10,14},{3,7},{... | collective-permute-start | bytes 4718600 | tf_op jit(solution)/shard_map/ppermute | solution.py:526
  47.0 37.2 %collective-permute-start.8 = (bf16[768,1024]{1,0:T(8,128)(2,1)S(1)}, bf16[768,1024]{1,0:T(8,128)(2,1)S(1)}, u32[]{:S(2)}, u32[]{:S(2)}) collective-permute-start(bf16[768,1024]{1,0:T(8,128)(2,1)S(1)} %collective-permute-done.1.refs_2_), channel_id=1, source_target_pairs={{4,0},{8,4},{12,8},{5,1},{9,5},{13,9},{6,2},{10,6},{14,10},{7,3},{... | collective-permute-start | bytes 4718600 | tf_op jit(solution)/shard_map/ppermute | solution.py:526
  49.1 24.0 %collective-permute-start.11 = (bf16[512,1024]{1,0:T(8,128)(2,1)}, bf16[512,1024]{1,0:T(8,128)(2,1)S(1)}, u32[]{:S(2)}, u32[]{:S(2)}) collective-permute-start(bf16[512,1024]{1,0:T(8,128)(2,1)} %collective-permute-done.6.refs_9_), channel_id=1, source_target_pairs={{0,16},{16,0},{1,17},{17,1},{2,18},{18,2},{3,19},{19,3},{4,20},{20... | collective-permute-start | bytes 3145736 | tf_op jit(solution)/shard_map/ppermute | solution.py:564
  73.2 16.4 %copy-start.10 = (bf16[512,1024]{1,0:T(8,128)(2,1)}, bf16[512,1024]{1,0:T(8,128)(2,1)S(1)}, u32[]{:S(2)}) copy-start(bf16[512,1024]{1,0:T(8,128)(2,1)S(1)} %collective-permute-done.11.refs_17_) | copy-start | bytes 3145732
  81.3 2.9 %copy-start.2 = (bf16[768,1024]{1,0:T(8,128)(2,1)}, bf16[768,1024]{1,0:T(8,128)(2,1)S(1)}, u32[]{:S(2)}) copy-start(bf16[768,1024]{1,0:T(8,128)(2,1)S(1)} %collective-permute-done.7.refs_3_) | copy-start | bytes 4718596
  84.2 3.9 %copy-start.3 = (bf16[768,1024]{1,0:T(8,128)(2,1)}, bf16[768,1024]{1,0:T(8,128)(2,1)S(1)}, u32[]{:S(2)}) copy-start(bf16[768,1024]{1,0:T(8,128)(2,1)S(1)} %collective-permute-done.8.refs_4_) | copy-start | bytes 4718596
  88.1 1.3 copy-start.6
  89.4 24.1 %collective-permute-start.14 = (bf16[512,1024]{1,0:T(8,128)(2,1)}, bf16[512,1024]{1,0:T(8,128)(2,1)}, u32[]{:S(2)}, u32[]{:S(2)}) collective-permute-start(bf16[512,1024]{1,0:T(8,128)(2,1)} %get-tuple-element.55), channel_id=1, source_target_pairs={{0,2},{1,3},{2,0},{3,1},{4,6},{5,7},{6,4},{7,5},{8,10},{9,11},{10,... | collective-permute-start | bytes 3145736 | tf_op jit(solution)/shard_map/ppermute | solution.py:499
  102.5 9.8 %collective-permute-start.12 = (f32[3,256,128]{2,1,0:T(8,128)}, f32[3,256,128]{2,1,0:T(8,128)S(1)}, u32[]{:S(2)}, u32[]{:S(2)}) collective-permute-start(f32[3,256,128]{2,1,0:T(8,128)} %get-tuple-element.54), channel_id=1, source_target_pairs={{0,4},{4,0},{8,12},{12,8},{1,5},{5,1},{9,13},{13,9},{2,6},{6,2},{1... | collective-permute-start | bytes 1179656 | tf_op jit(solution)/shard_map/ppermute | solution.py:499
  102.8 33.2 %collective-permute-start.16 = (bf16[512,1024]{1,0:T(8,128)(2,1)}, bf16[512,1024]{1,0:T(8,128)(2,1)}, u32[]{:S(2)}, u32[]{:S(2)}) collective-permute-start(bf16[512,1024]{1,0:T(8,128)(2,1)} %get-tuple-element.57), channel_id=1, source_target_pairs={{0,2},{1,3},{2,0},{3,1},{4,6},{5,7},{6,4},{7,5},{8,10},{9,11},{10,... | collective-permute-start | bytes 3145736 | tf_op jit(solution)/shard_map/ppermute | solution.py:499
  113.3 34.8 %copy-start.7 = (f32[3,256,128]{2,1,0:T(8,128)}, f32[3,256,128]{2,1,0:T(8,128)S(1)}, u32[]{:S(2)}) copy-start(f32[3,256,128]{2,1,0:T(8,128)S(1)} %add.110.here_ref) | copy-start | bytes 1179652
  113.5 22.5 %collective-permute-start.15 = (bf16[512,1024]{1,0:T(8,128)(2,1)}, bf16[512,1024]{1,0:T(8,128)(2,1)S(1)}, u32[]{:S(2)}, u32[]{:S(2)}) collective-permute-start(bf16[512,1024]{1,0:T(8,128)(2,1)} %collective-permute-done.6.refs_9_), channel_id=1, source_target_pairs={{0,1},{1,0},{2,3},{3,2},{4,5},{5,4},{6,7},{7,6},{8,9},{9,8},{10,11... | collective-permute-start | bytes 3145736 | tf_op jit(solution)/shard_map/ppermute | solution.py:499
  116.6 19.4 %collective-permute-start.17 = (bf16[512,1024]{1,0:T(8,128)(2,1)}, bf16[512,1024]{1,0:T(8,128)(2,1)S(1)}, u32[]{:S(2)}, u32[]{:S(2)}) collective-permute-start(bf16[512,1024]{1,0:T(8,128)(2,1)} %copy-done.10), channel_id=1, source_target_pairs={{0,1},{1,0},{2,3},{3,2},{4,5},{5,4},{6,7},{7,6},{8,9},{9,8},{10,11... | collective-permute-start | bytes 3145736 | tf_op jit(solution)/shard_map/ppermute | solution.py:499
  116.6 24.4 %collective-permute-start.18 = (bf16[512,1024]{1,0:T(8,128)(2,1)}, bf16[512,1024]{1,0:T(8,128)(2,1)S(1)}, u32[]{:S(2)}, u32[]{:S(2)}) collective-permute-start(bf16[512,1024]{1,0:T(8,128)(2,1)} %collective-permute-done.14.refs_11_), channel_id=1, source_target_pairs={{0,16},{16,0},{1,17},{17,1},{2,18},{18,2},{3,19},{19,3},{4,20},{20... | collective-permute-start | bytes 3145736 | tf_op jit(solution)/shard_map/ppermute | solution.py:564
  117.9 18.1 %collective-permute-start.13 = (f32[3,256,128]{2,1,0:T(8,128)S(1)}, f32[3,256,128]{2,1,0:T(8,128)S(1)}, u32[]{:S(2)}, u32[]{:S(2)}) collective-permute-start(f32[3,256,128]{2,1,0:T(8,128)S(1)} %add.110.here_ref), channel_id=1, source_target_pairs={{0,8},{4,12},{8,0},{12,4},{1,9},{5,13},{9,1},{13,5},{2,10},{6,14},... | collective-permute-start | bytes 1179656 | tf_op jit(solution)/shard_map/ppermute | solution.py:499
  136.0 12.2 %copy-start.16 = (f32[3,256,128]{2,1,0:T(8,128)}, f32[3,256,128]{2,1,0:T(8,128)S(1)}, u32[]{:S(2)}) copy-start(f32[3,256,128]{2,1,0:T(8,128)S(1)} %collective-permute-done.13.there_ref) | copy-start | bytes 1179652
  136.0 5.3 %copy-start.11 = (bf16[512,1024]{1,0:T(8,128)(2,1)}, bf16[512,1024]{1,0:T(8,128)(2,1)S(1)}, u32[]{:S(2)}) copy-start(bf16[512,1024]{1,0:T(8,128)(2,1)S(1)} %collective-permute-done.15.refs_10_) | copy-start | bytes 3145732
  136.0 8.5 %copy-start.12 = (bf16[512,1024]{1,0:T(8,128)(2,1)}, bf16[512,1024]{1,0:T(8,128)(2,1)S(1)}, u32[]{:S(2)}) copy-start(bf16[512,1024]{1,0:T(8,128)(2,1)S(1)} %collective-permute-done.17.refs_18_) | copy-start | bytes 3145732
  141.0 5.8 %copy-start.13 = (bf16[512,1024]{1,0:T(8,128)(2,1)}, bf16[512,1024]{1,0:T(8,128)(2,1)S(1)}, u32[]{:S(2)}) copy-start(bf16[512,1024]{1,0:T(8,128)(2,1)S(1)} %collective-permute-done.18.refs_19_) | copy-start | bytes 3145732
  141.0 49.0 %copy-start.17 = (s32[3]{0:T(128)S(1)}, s32[3]{0:T(128)}, u32[]{:S(2)}) copy-start(s32[3]{0:T(128)} %live_ref.1) | copy-start | bytes 40
  141.0 23.6 %collective-permute-start.21 = (bf16[512,1024]{1,0:T(8,128)(2,1)}, bf16[512,1024]{1,0:T(8,128)(2,1)}, u32[]{:S(2)}, u32[]{:S(2)}) collective-permute-start(bf16[512,1024]{1,0:T(8,128)(2,1)} %get-tuple-element.62), channel_id=1, source_target_pairs={{0,2},{1,3},{2,0},{3,1},{4,6},{5,7},{6,4},{7,5},{8,10},{9,11},{10,... | collective-permute-start | bytes 3145736 | tf_op jit(solution)/shard_map/ppermute | solution.py:499
  141.3 36.4 %collective-permute-start.19 = (bf16[768,1024]{1,0:T(8,128)(2,1)}, bf16[768,1024]{1,0:T(8,128)(2,1)S(1)}, u32[]{:S(2)}, u32[]{:S(2)}) collective-permute-start(bf16[768,1024]{1,0:T(8,128)(2,1)} %copy-done.2), channel_id=1, source_target_pairs={{0,4},{4,8},{8,12},{1,5},{5,9},{9,13},{2,6},{6,10},{10,14},{3,7},{... | collective-permute-start | bytes 4718600 | tf_op jit(solution)/shard_map/ppermute | solution.py:526
  144.5 36.2 %collective-permute-start.20 = (bf16[768,1024]{1,0:T(8,128)(2,1)}, bf16[768,1024]{1,0:T(8,128)(2,1)S(1)}, u32[]{:S(2)}, u32[]{:S(2)}) collective-permute-start(bf16[768,1024]{1,0:T(8,128)(2,1)} %copy-done.3), channel_id=1, source_target_pairs={{4,0},{8,4},{12,8},{5,1},{9,5},{13,9},{6,2},{10,6},{14,10},{7,3},{... | collective-permute-start | bytes 4718600 | tf_op jit(solution)/shard_map/ppermute | solution.py:526
  146.9 22.8 %collective-permute-start.27 = (bf16[512,1024]{1,0:T(8,128)(2,1)}, bf16[512,1024]{1,0:T(8,128)(2,1)}, u32[]{:S(2)}, u32[]{:S(2)}) collective-permute-start(bf16[512,1024]{1,0:T(8,128)(2,1)} %collective-permute-done.16.refs_13_), channel_id=1, source_target_pairs={{0,16},{16,0},{1,17},{17,1},{2,18},{18,2},{3,19},{19,3},{4,20},{20... | collective-permute-start | bytes 3145736 | tf_op jit(solution)/shard_map/ppermute | solution.py:564
  164.7 18.8 %collective-permute-start.22 = (bf16[3,64,1664]{2,1,0:T(8,128)(2,1)}, bf16[3,64,1664]{2,1,0:T(8,128)(2,1)}, u32[]{:S(2)}, u32[]{:S(2)}) collective-permute-start(bf16[3,64,1664]{2,1,0:T(8,128)(2,1)} %get-tuple-element.80.refs_0_), channel_id=1, source_target_pairs={{0,2},{1,3},{2,0},{3,1},{4,6},{5,7},{6,4},{7,5},{8,10},{9,11},{10,... | collective-permute-start | bytes 1916936 | tf_op jit(solution)/shard_map/ppermute | solution.py:499
  164.9 18.6 %collective-permute-start.23 = (bf16[512,1024]{1,0:T(8,128)(2,1)}, bf16[512,1024]{1,0:T(8,128)(2,1)}, u32[]{:S(2)}, u32[]{:S(2)}) collective-permute-start(bf16[512,1024]{1,0:T(8,128)(2,1)} %collective-permute-done.14.refs_11_), channel_id=1, source_target_pairs={{0,1},{1,0},{2,3},{3,2},{4,5},{5,4},{6,7},{7,6},{8,9},{9,8},{10,11... | collective-permute-start | bytes 3145736 | tf_op jit(solution)/shard_map/ppermute | solution.py:499
  169.7 13.8 %collective-permute-start.24 = (bf16[512,1024]{1,0:T(8,128)(2,1)}, bf16[512,1024]{1,0:T(8,128)(2,1)}, u32[]{:S(2)}, u32[]{:S(2)}) collective-permute-start(bf16[512,1024]{1,0:T(8,128)(2,1)} %collective-permute-done.16.refs_13_), channel_id=1, source_target_pairs={{0,1},{1,0},{2,3},{3,2},{4,5},{5,4},{6,7},{7,6},{8,9},{9,8},{10,11... | collective-permute-start | bytes 3145736 | tf_op jit(solution)/shard_map/ppermute | solution.py:499
  177.7 12.9 %copy-start.4 = (bf16[768,1024]{1,0:T(8,128)(2,1)}, bf16[768,1024]{1,0:T(8,128)(2,1)S(1)}, u32[]{:S(2)}) copy-start(bf16[768,1024]{1,0:T(8,128)(2,1)S(1)} %collective-permute-done.19.refs_5_) | copy-start | bytes 4718596
  177.7 5.8 %collective-permute-start.25 = (bf16[512,1024]{1,0:T(8,128)(2,1)}, bf16[512,1024]{1,0:T(8,128)(2,1)}, u32[]{:S(2)}, u32[]{:S(2)}) collective-permute-start(bf16[512,1024]{1,0:T(8,128)(2,1)} %collective-permute-done.21.refs_15_), channel_id=1, source_target_pairs={{0,1},{1,0},{2,3},{3,2},{4,5},{5,4},{6,7},{7,6},{8,9},{9,8},{10,11... | collective-permute-start | bytes 3145736 | tf_op jit(solution)/shard_map/ppermute | solution.py:499
  180.7 10.0 %copy-start.5 = (bf16[768,1024]{1,0:T(8,128)(2,1)}, bf16[768,1024]{1,0:T(8,128)(2,1)S(1)}, u32[]{:S(2)}) copy-start(bf16[768,1024]{1,0:T(8,128)(2,1)S(1)} %collective-permute-done.20.refs_6_) | copy-start | bytes 4718596
  180.7 5.4 %collective-permute-start.26 = (bf16[512,1024]{1,0:T(8,128)(2,1)}, bf16[512,1024]{1,0:T(8,128)(2,1)}, u32[]{:S(2)}, u32[]{:S(2)}) collective-permute-start(bf16[512,1024]{1,0:T(8,128)(2,1)} %copy-done.13), channel_id=1, source_target_pairs={{0,1},{1,0},{2,3},{3,2},{4,5},{5,4},{6,7},{7,6},{8,9},{9,8},{10,11... | collective-permute-start | bytes 3145736 | tf_op jit(solution)/shard_map/ppermute | solution.py:499
  183.4 4.1 %collective-permute-start.28 = (bf16[512,1024]{1,0:T(8,128)(2,1)}, bf16[512,1024]{1,0:T(8,128)(2,1)}, u32[]{:S(2)}, u32[]{:S(2)}) collective-permute-start(bf16[512,1024]{1,0:T(8,128)(2,1)} %collective-permute-done.27.refs_21_), channel_id=1, source_target_pairs={{0,1},{1,0},{2,3},{3,2},{4,5},{5,4},{6,7},{7,6},{8,9},{9,8},{10,11... | collective-permute-start | bytes 3145736 | tf_op jit(solution)/shard_map/ppermute | solution.py:499
  187.6 37.5 %collective-permute-start.30 = (bf16[3,64,3456]{2,1,0:T(8,128)(2,1)}, bf16[3,64,3456]{2,1,0:T(8,128)(2,1)}, u32[]{:S(2)}, u32[]{:S(2)}) collective-permute-start(bf16[3,64,3456]{2,1,0:T(8,128)(2,1)} %get-tuple-element.81.refs_1_), channel_id=1, source_target_pairs={{0,2},{1,3},{2,0},{3,1},{4,6},{5,7},{6,4},{7,5},{8,10},{9,11},{10,... | collective-permute-start | bytes 3981320 | tf_op jit(solution)/shard_map/ppermute | solution.py:499
  188.8 36.3 %collective-permute-start.29 = (bf16[512,1024]{1,0:T(8,128)(2,1)}, bf16[512,1024]{1,0:T(8,128)(2,1)}, u32[]{:S(2)}, u32[]{:S(2)}) collective-permute-start(bf16[512,1024]{1,0:T(8,128)(2,1)} %collective-permute-done.21.refs_15_), channel_id=1, source_target_pairs={{0,16},{16,0},{1,17},{17,1},{2,18},{18,2},{3,19},{19,3},{4,20},{20... | collective-permute-start | bytes 3145736 | tf_op jit(solution)/shard_map/ppermute | solution.py:564
  225.1 3.3 %collective-permute-start.31 = (bf16[512,1024]{1,0:T(8,128)(2,1)}, bf16[512,1024]{1,0:T(8,128)(2,1)S(1)}, u32[]{:S(2)}, u32[]{:S(2)}) collective-permute-start(bf16[512,1024]{1,0:T(8,128)(2,1)} %collective-permute-done.29.refs_9_), channel_id=1, source_target_pairs={{0,1},{1,0},{2,3},{3,2},{4,5},{5,4},{6,7},{7,6},{8,9},{9,8},{10,11... | collective-permute-start | bytes 3145736 | tf_op jit(solution)/shard_map/ppermute | solution.py:499
  226.5 18.6 %collective-permute-start.33 = (bf16[3,64,3456]{2,1,0:T(8,128)(2,1)}, bf16[3,64,3456]{2,1,0:T(8,128)(2,1)S(1)}, u32[]{:S(2)}, u32[]{:S(2)}) collective-permute-start(bf16[3,64,3456]{2,1,0:T(8,128)(2,1)} %get-tuple-element.81.refs_1_), channel_id=1, source_target_pairs={{0,1},{1,0},{2,3},{3,2},{4,5},{5,4},{6,7},{7,6},{8,9},{9,8},{10,11... | collective-permute-start | bytes 3981320 | tf_op jit(solution)/shard_map/ppermute | solution.py:499
  228.4 1.0 copy-start.14
  229.4 11.1 %copy-start.15 = (bf16[3,64,1664]{2,1,0:T(8,128)(2,1)S(1)}, bf16[3,64,1664]{2,1,0:T(8,128)(2,1)}, u32[]{:S(2)}) copy-start(bf16[3,64,1664]{2,1,0:T(8,128)(2,1)} %get-tuple-element.80.refs_0_) | copy-start | bytes 1916932
  240.0 5.3 %collective-permute-start.35 = (bf16[3,64,3456]{2,1,0:T(8,128)(2,1)}, bf16[3,64,3456]{2,1,0:T(8,128)(2,1)S(1)}, u32[]{:S(2)}, u32[]{:S(2)}) collective-permute-start(bf16[3,64,3456]{2,1,0:T(8,128)(2,1)} %collective-permute-done.30.refs_5_), channel_id=1, source_target_pairs={{0,1},{1,0},{2,3},{3,2},{4,5},{5,4},{6,7},{7,6},{8,9},{9,8},{10,11... | collective-permute-start | bytes 3981320 | tf_op jit(solution)/shard_map/ppermute | solution.py:499
  240.4 4.6 %collective-permute-start.32 = (bf16[3,64,1664]{2,1,0:T(8,128)(2,1)S(1)}, bf16[3,64,1664]{2,1,0:T(8,128)(2,1)}, u32[]{:S(2)}, u32[]{:S(2)}) collective-permute-start(bf16[3,64,1664]{2,1,0:T(8,128)(2,1)S(1)} %copy-done.15), channel_id=1, source_target_pairs={{0,1},{1,0},{2,3},{3,2},{4,5},{5,4},{6,7},{7,6},{8,9},{9,8},{10,11... | collective-permute-start | bytes 1916936 | tf_op jit(solution)/shard_map/ppermute | solution.py:499
  240.6 4.7 %collective-permute-start.34 = (bf16[3,64,1664]{2,1,0:T(8,128)(2,1)}, bf16[3,64,1664]{2,1,0:T(8,128)(2,1)}, u32[]{:S(2)}, u32[]{:S(2)}) collective-permute-start(bf16[3,64,1664]{2,1,0:T(8,128)(2,1)} %collective-permute-done.22.refs_4_), channel_id=1, source_target_pairs={{0,1},{1,0},{2,3},{3,2},{4,5},{5,4},{6,7},{7,6},{8,9},{9,8},{10,11... | collective-permute-start | bytes 1916936 | tf_op jit(solution)/shard_map/ppermute | solution.py:499
  245.1 1.1 copy-start.8
  245.3 1.3 copy-start.9

commit v4 on v3

--- a/solution.py
+++ b/solution.py
@@ -567,8 +567,6 @@
         for piece in chunks:
             piece.update(spread({top: behind(piece[top], *after)}))
 
-    cross(far_slots)
-
     first = jnp.swapaxes(adapter_first_factors, 1, 2)
     a_near = spread({0: first})
     b_near = spread({0: adapter_second_factors})
@@ -581,17 +579,14 @@
         return index, jnp.where((owner ^ me) < top, owner ^ me, len(near))
 
     picked = pick(*places(far_slots), a_near, b_near)
+    far = swap(picked, top)
+    whole = spread({0: behind(frozen_down_weight, picked)})
     both_slots = spread({0: behind(jnp.concatenate([slots, far_slots]), picked)})
-    past = [picked, *first_hop, *flat(both_slots, *crossed)]
-    far = swap(behind(picked, *past[1:]), top)
-    whole = spread({0: behind(frozen_down_weight, *past)})
-    turn(*past)
-    past = [far, *hop(*past), *flat(*turned[0])]
-
-    ready = behind(slots, *flat(whole, both_slots), *past)
+    past = [far, *first_hop, *flat(whole, both_slots)]
     part, block_a, grad_a, grad_b = project(
-        *places(ready), a_near, b_near, far, hidden, output_gradient
-    )
+        *places(behind(slots, *past)), a_near, b_near, far, hidden, output_gradient
+    )
+    second_hop = hop(*past)
     cross(*past)
     cross(*past)
     sums = [part]
@@ -602,7 +597,9 @@
             sums.append(sums[-2] + sums[-1])
         bit *= 2
     total, other = sums[-2:]
-    past = [sums[2], *flat(*crossed[1:2])]
+    turn(*past)
+    past = [sums[2], *second_hop, *flat(*crossed, *sum(turned, []))]
+    cross(*past)
     turn(*past)
     fill(crossed[:1], *past)
     fill(turned[0], *past)
@@ -615,12 +612,12 @@
     )
     far_low = swap(behind(low_terms, *flat(*crossed)), top)
     past = flat(*crossed[3:])
+    turn(low_terms, *past)
     fill(crossed[1:], *past)
     for pieces in turned[1:3]:
         fill(pieces, *past)
     past = [far_low, *third_hop, *flat(*crossed, *sum(turned, []))]
     far_high = swap(behind(high_terms, *past), top)
-    turn(*past)
     if line:
         at = jnp.stack(at).astype(i32)
     else:

time: 256 us -> 260 us (1.016); the launches traced: 254 us -> 255 us
  waiting for transfers between devices: 117 us -> 124 us
  Pallas kernels: 75.8 us -> 71.1 us
    ppermute x4, waiting for transfers between devices: 30 us -> 15.8 us  [turn(): turned[j].append({top: lax.ppermute(piece, 'groups', ring)})]
    ppermute x6, waiting for transfers between devices: 20.5 us -> 34.7 us  [hop(): pieces_of_kept.append(lax.ppermute(behind(piece, *after), 'fsdp', pairs))]
    ppermute x26, waiting for transfers between devices: 66.7 us -> 73.9 us  [swap(): return lax.ppermute(value, axis, [(i, i ^ bit) for i in range(size)])]
    pallas_call x1, Pallas kernels: 7.43 us -> 3.75 us  [add_terms(): pl.pallas_call(functools.partial(add_kernel, n, count), grid_spec=pltpu.P...]
  transfers between devices with their start and end apart: 36 -> 36, of which waited for: 20 -> 20; matrix products, arithmetic and copies ran while one was open for 4% -> 4% of each run, Pallas kernels for 27% -> 24%
where the time goes in v4:
time: 260 us; the launch traced here: 255 us
  waiting for transfers between devices  124 us (48%)
  Pallas kernels  71.1 us (27%)
  starting transfers between devices  47 us (18%)
  local copies, waits for them, and re-layouts  6.9 us (3%)
  other arithmetic  4.85 us (2%)
    ppermute x26, waiting for transfers between devices, swap(): return lax.ppermute(value, axis, [(i, i ^ bit) for i in range(size)])  73.9 us
    pallas_call x2, Pallas kernels, base(): pl.pallas_call(functools.partial(base_kernel, 2 * top, tiles, len(chunks)...  45.1 us
    ppermute x6, waiting for transfers between devices, hop(): pieces_of_kept.append(lax.ppermute(behind(piece, *after), 'fsdp', pairs))  34.7 us
    ppermute x26, starting transfers between devices, swap(): return lax.ppermute(value, axis, [(i, i ^ bit) for i in range(size)])  25.1 us
    ppermute x6, starting transfers between devices, hop(): pieces_of_kept.append(lax.ppermute(behind(piece, *after), 'fsdp', pairs))  17.9 us
    ppermute x4, waiting for transfers between devices, turn(): turned[j].append({top: lax.ppermute(piece, 'groups', ring)})  15.8 us
    pallas_call x1, Pallas kernels, project(): pl.pallas_call(functools.partial(project_kernel, pieces), grid_spec=pltpu...  10.4 us
    pallas_call x1, Pallas kernels, block_terms(): pl.pallas_call(terms_kernel, grid_spec=pltpu.PrefetchScalarGridSpec(num_s...  6.91 us
  transfers between devices with their start and end apart: 36, of which 20 were waited for; matrix products, arithmetic and copies ran while one was open for 4% of the time, Pallas kernels for 24%

profile of v4, /device:TPU:11, one launch (start us, length us, event | category | flops | bytes accessed | tf_op | source)
XLA Modules:
  0.0 255.2 jit_solution(4063659274216585267)
XLA Ops:
  0.6 0.7 collective-permute-start.3
  1.5 0.9 select_reduce_fusion
  2.6 2.1 collective-permute-done.2
  4.8 0.5 compare_select_fusion.1
  5.3 0.6 pad_add_fusion
  5.9 3.9 %collective-permute-done.4.refs_3_ = bf16[8,64,1024]{2,1,0:T(8,128)(2,1)S(1)} collective-permute-done((bf16[8,64,1024]{2,1,0:T(8,128)(2,1)}, bf16[8,64,1024]{2,1,0:T(8,128)(2,1)S(1)}, u32[]{:S(2)}, u32[]{:S(2)}) %collective-permute-start.4) | collective-permute-done | bytes 1048608 | tf_op jit(solution)/shard_map/ppermute | solution.py:499
  10.0 0.7 copy-done.4
  10.7 4.9 %shard_map.103 = bf16[3,64,5120]{2,1,0:T(8,128)(2,1)} custom-call(s32[6]{0:T(128)} %get-tuple-element.99.index_ref, s32[3]{0:T(128)} %get-tuple-element.97.source_ref, bf16[8,64,4096]{2,1,0:T(8,128)(2,1)} %bitcast.22, bf16[8,64,4096]{2,1,0:T(8,128)(2,1)} %collective-permute-done.3.refs_1_, bf16[8,64,1024]{2,1,0:T(8,128)(2,1)} %refs_2_.3, ...), custom_call_target="tpu_custom_call" | custom-call | bytes 5898240 | tf_op jit(solution)/shard_map/pallas_call | solution.py:54
  15.9 3.2 %collective-permute-start = (bf16[768,1024]{1,0:T(8,128)(2,1)S(1)}, bf16[768,1024]{1,0:T(8,128)(2,1)S(1)}, u32[]{:S(2)}, u32[]{:S(2)}) collective-permute-start(bf16[768,1024]{1,0:T(8,128)(2,1)S(1)} %copy-done), channel_id=1, source_target_pairs={{0,4},{4,8},{8,12},{1,5},{5,9},{9,13},{2,6},{6,10},{10,14},{3,7},{... | collective-permute-start | bytes 4718600 | tf_op jit(solution)/shard_map/ppermute | solution.py:526
  19.1 2.2 collective-permute-start.1
  21.3 3.9 %constant_dynamic-slice_fusion = (bf16[512,1024]{1,0:T(8,128)(2,1)}, bf16[512,1024]{1,0:T(8,128)(2,1)}, bf16[512,1024]{1,0:T(8,128)(2,1)S(1)}, bf16[512,1024]{1,0:T(8,128)(2,1)}) fusion(bf16[4096,1024]{1,0:T(8,128)(2,1)} %refs_7_.1, s32[]{:T(128)S(6)} %select_n.79, s32[]{:T(128)S(6)} %select_n.77, s32[]{:T(128)S(6)} %select_n.76, s32[]{:T(128)S(6)} %select_n.78), kind=kLoop, calls=%fused_computation.13 | loop fusion | bytes 8388624 | tf_op jit(solution)/shard_map/dynamic_slice | solution.py:552
  25.3 0.8 collective-permute-start.7
  26.1 27.5 %collective-permute-done.refs_1_ = bf16[768,1024]{1,0:T(8,128)(2,1)S(1)} collective-permute-done((bf16[768,1024]{1,0:T(8,128)(2,1)S(1)}, bf16[768,1024]{1,0:T(8,128)(2,1)S(1)}, u32[]{:S(2)}, u32[]{:S(2)}) %collective-permute-start) | collective-permute-done | bytes 1572896 | tf_op jit(solution)/shard_map/ppermute | solution.py:526
  53.6 2.9 %collective-permute-done.1.refs_2_ = bf16[768,1024]{1,0:T(8,128)(2,1)} collective-permute-done((bf16[768,1024]{1,0:T(8,128)(2,1)S(1)}, bf16[768,1024]{1,0:T(8,128)(2,1)}, u32[]{:S(2)}, u32[]{:S(2)}) %collective-permute-start.1) | collective-permute-done | bytes 1572896 | tf_op jit(solution)/shard_map/ppermute | solution.py:526
  56.5 3.4 %collective-permute-done.5.refs_4_ = bf16[3,64,5120]{2,1,0:T(8,128)(2,1)} collective-permute-done((bf16[3,64,5120]{2,1,0:T(8,128)(2,1)}, bf16[3,64,5120]{2,1,0:T(8,128)(2,1)}, u32[]{:S(2)}, u32[]{:S(2)}) %collective-permute-start.5) | collective-permute-done | bytes 1966112 | tf_op jit(solution)/shard_map/ppermute | solution.py:499
  59.9 0.8 collective-permute-start.12
  60.7 3.2 %collective-permute-start.8 = (bf16[768,1024]{1,0:T(8,128)(2,1)S(1)}, bf16[768,1024]{1,0:T(8,128)(2,1)S(1)}, u32[]{:S(2)}, u32[]{:S(2)}) collective-permute-start(bf16[768,1024]{1,0:T(8,128)(2,1)S(1)} %collective-permute-done.refs_1_), channel_id=1, source_target_pairs={{0,4},{4,8},{8,12},{1,5},{5,9},{9,13},{2,6},{6,10},{10,14},{3,7},{... | collective-permute-start | bytes 4718600 | tf_op jit(solution)/shard_map/ppermute | solution.py:526
  63.9 2.2 collective-permute-start.9
  66.1 0.8 collective-permute-start.13
  66.9 16.6 %collective-permute-done.12.refs_9_ = bf16[512,1024]{1,0:T(8,128)(2,1)} collective-permute-done((bf16[512,1024]{1,0:T(8,128)(2,1)S(1)}, bf16[512,1024]{1,0:T(8,128)(2,1)}, u32[]{:S(2)}, u32[]{:S(2)}) %collective-permute-start.12) | collective-permute-done | bytes 1048608 | tf_op jit(solution)/shard_map/ppermute | solution.py:499
  83.4 1.0 collective-permute-start.14
  84.5 0.5 compare_select_fusion
  85.0 0.7 pad_add_fusion.2.index_ref
  85.6 10.4 %shard_map.104 = (f32[3,256,128]{2,1,0:T(8,128)}, bf16[3,64,4096]{2,1,0:T(8,128)(2,1)}, f32[8,64,4096]{2,1,0:T(8,128)}, f32[8,64,1024]{2,1,0:T(8,128)}) custom-call(s32[6]{0:T(128)} %pad_add_fusion.2.index_ref, s32[3]{0:T(128)} %get-tuple-element.95.source_ref, bf16[8,64,4096]{2,1,0:T(8,128)(2,1)} %bitcast.23, ...), custom_call_target="tpu_custom_call" | custom-call | flops 503316480 | bytes 15728640 | tf_op jit(solution)/shard_map/pallas_call | solution.py:121
  96.3 10.4 %collective-permute-done.10 = f32[3,256,128]{2,1,0:T(8,128)S(1)} collective-permute-done((f32[3,256,128]{2,1,0:T(8,128)}, f32[3,256,128]{2,1,0:T(8,128)S(1)}, u32[]{:S(2)}, u32[]{:S(2)}) %collective-permute-start.10) | collective-permute-done | bytes 393248 | tf_op jit(solution)/shard_map/ppermute | solution.py:499
  106.7 1.0 add.109.here_ref
  107.8 2.8 %collective-permute-start.15 = (bf16[512,1024]{1,0:T(8,128)(2,1)}, bf16[512,1024]{1,0:T(8,128)(2,1)S(1)}, u32[]{:S(2)}, u32[]{:S(2)}) collective-permute-start(bf16[512,1024]{1,0:T(8,128)(2,1)} %collective-permute-done.12.refs_9_), channel_id=1, source_target_pairs={{0,1},{1,0},{2,3},{3,2},{4,5},{5,4},{6,7},{7,6},{8,9},{9,8},{10,11... | collective-permute-start | bytes 3145736 | tf_op jit(solution)/shard_map/ppermute | solution.py:499
  110.6 0.7 collective-permute-start.16
  111.3 0.3 collective-permute-start.17
  111.7 1.1 collective-permute-start.18
  112.8 2.2 collective-permute-start.11
  115.0 16.5 %collective-permute-done.11.there_ref = f32[3,256,128]{2,1,0:T(8,128)S(1)} collective-permute-done((f32[3,256,128]{2,1,0:T(8,128)S(1)}, f32[3,256,128]{2,1,0:T(8,128)S(1)}, u32[]{:S(2)}, u32[]{:S(2)}) %collective-permute-start.11) | collective-permute-done | bytes 393248 | tf_op jit(solution)/shard_map/ppermute | solution.py:499
  131.5 4.2 %collective-permute-done.16.refs_13_ = bf16[512,1024]{1,0:T(8,128)(2,1)} collective-permute-done((bf16[512,1024]{1,0:T(8,128)(2,1)}, bf16[512,1024]{1,0:T(8,128)(2,1)}, u32[]{:S(2)}, u32[]{:S(2)}) %collective-permute-start.16) | collective-permute-done | bytes 1048608 | tf_op jit(solution)/shard_map/ppermute | solution.py:499
  135.7 0.8 collective-permute-done.18.refs_19_
  136.5 0.8 collective-permute-start.21
  137.2 5.0 %collective-permute-start.19 = (bf16[768,1024]{1,0:T(8,128)(2,1)S(1)}, bf16[768,1024]{1,0:T(8,128)(2,1)S(1)}, u32[]{:S(2)}, u32[]{:S(2)}) collective-permute-start(bf16[768,1024]{1,0:T(8,128)(2,1)S(1)} %collective-permute-done.8.refs_3_), channel_id=1, source_target_pairs={{0,4},{4,8},{8,12},{1,5},{5,9},{9,13},{2,6},{6,10},{10,14},{3,7},{... | collective-permute-start | bytes 4718600 | tf_op jit(solution)/shard_map/ppermute | solution.py:526
  142.3 2.1 collective-permute-start.20
  144.4 0.8 collective-permute-start.27
  145.2 6.9 %shard_map.105 = (bf16[3,64,1664]{2,1,0:T(8,128)(2,1)}, bf16[3,64,3456]{2,1,0:T(8,128)(2,1)}, bf16[3,256,64]{2,1,0:T(8,128)(2,1)}) custom-call(s32[3]{0:T(128)} %live_ref.1, f32[3,256,128]{2,1,0:T(8,128)} %copy-done.5, f32[3,256,128]{2,1,0:T(8,128)} %copy-done.12, bf16[768,4096]{1,0:T(8,128)(2,1)} %hid_ref.1, bf16[768,1024]{1,0:T(8,128)(2,1)} %refs_0_.3), custom_call_target="tpu_custom_call" | custom-call | flops 503316480 | bytes 9830400 | tf_op jit(solution)/shard_map/pallas_call | solution.py:186
  152.1 8.4 %collective-permute-done.21.refs_15_ = bf16[512,1024]{1,0:T(8,128)(2,1)} collective-permute-done((bf16[512,1024]{1,0:T(8,128)(2,1)}, bf16[512,1024]{1,0:T(8,128)(2,1)}, u32[]{:S(2)}, u32[]{:S(2)}) %collective-permute-start.21) | collective-permute-done | bytes 1048608 | tf_op jit(solution)/shard_map/ppermute | solution.py:499
  160.5 1.1 collective-permute-start.22
  161.6 0.4 collective-permute-start.29
  162.0 5.9 %collective-permute-done.27.refs_21_ = bf16[512,1024]{1,0:T(8,128)(2,1)} collective-permute-done((bf16[512,1024]{1,0:T(8,128)(2,1)}, bf16[512,1024]{1,0:T(8,128)(2,1)}, u32[]{:S(2)}, u32[]{:S(2)}) %collective-permute-start.27) | collective-permute-done | bytes 1048608 | tf_op jit(solution)/shard_map/ppermute | solution.py:564
  167.9 4.5 %collective-permute-start.23 = (bf16[512,1024]{1,0:T(8,128)(2,1)}, bf16[512,1024]{1,0:T(8,128)(2,1)}, u32[]{:S(2)}, u32[]{:S(2)}) collective-permute-start(bf16[512,1024]{1,0:T(8,128)(2,1)} %collective-permute-done.13.refs_11_), channel_id=1, source_target_pairs={{0,1},{1,0},{2,3},{3,2},{4,5},{5,4},{6,7},{7,6},{8,9},{9,8},{10,11... | collective-permute-start | bytes 3145736 | tf_op jit(solution)/shard_map/ppermute | solution.py:499
  172.4 2.3 collective-permute-done.19.refs_5_
  174.7 2.2 collective-permute-start.24
  176.9 2.0 collective-permute-done.20.refs_6_
  178.9 2.5 collective-permute-start.25
  181.3 9.1 %collective-permute-done.22.refs_9_ = bf16[512,1024]{1,0:T(8,128)(2,1)} collective-permute-done((bf16[512,1024]{1,0:T(8,128)(2,1)}, bf16[512,1024]{1,0:T(8,128)(2,1)}, u32[]{:S(2)}, u32[]{:S(2)}) %collective-permute-start.22) | collective-permute-done | bytes 1048608 | tf_op jit(solution)/shard_map/ppermute | solution.py:564
  190.4 2.5 collective-permute-start.28
  192.8 2.6 %collective-permute-done.28.refs_22_ = bf16[512,1024]{1,0:T(8,128)(2,1)} collective-permute-done((bf16[512,1024]{1,0:T(8,128)(2,1)}, bf16[512,1024]{1,0:T(8,128)(2,1)}, u32[]{:S(2)}, u32[]{:S(2)}) %collective-permute-start.28) | collective-permute-done | bytes 1048608 | tf_op jit(solution)/shard_map/ppermute | solution.py:499
  195.5 0.7 collective-permute-start.30
  196.2 0.6 concatenate.25.scalars_ref
  196.8 34.5 %shard_map.106 = (bf16[768,4096]{1,0:T(8,128)(2,1)}, f32[8,128]{1,0:T(8,128)}) custom-call(s32[21]{0:T(128)} %concatenate.25.scalars_ref, bf16[768,1024]{1,0:T(8,128)(2,1)} %refs_0_.3, bf16[768,1024]{1,0:T(8,128)(2,1)} %copy-done.1, bf16[768,1024]{1,0:T(8,128)(2,1)} %collective-permute-done.1.refs_2_, bf16[768,1024]{1,0:T(8,128)(2,1)} %copy-done.2, ...), custom_call_target="tpu_custom_call" | custom-call | flops 1 | bytes 1 | tf_op jit(solution)/shard_map/pallas_call | solution.py:356
  231.3 0.5 collective-permute-start.31
  231.8 0.6 concatenate.21.scalars_ref
  232.5 2.0 collective-permute-done.31.refs_10_
  234.5 10.6 %shard_map.107 = (bf16[768,4096]{1,0:T(8,128)(2,1)}, f32[8,128]{1,0:T(8,128)}) custom-call(s32[15]{0:T(128)} %concatenate.21.scalars_ref, bf16[768,1024]{1,0:T(8,128)(2,1)} %refs_0_.3, bf16[768,1024]{1,0:T(8,128)(2,1)} %copy-done.1, bf16[768,1024]{1,0:T(8,128)(2,1)} %collective-permute-done.1.refs_2_, ...), custom_call_target="tpu_custom_call", output_to_operand_aliasing={{0}: (15, {})} | custom-call | flops 1 | bytes 1 | tf_op jit(solution)/shard_map/pallas_call | solution.py:356
  245.1 0.4 collective-permute-start.35
  245.7 0.4 collective-permute-start.34
  246.2 0.7 add_subtract_fusion.slots_ref
  246.9 3.3 %collective-permute-done.32.refs_2_ = bf16[3,64,1664]{2,1,0:T(8,128)(2,1)} collective-permute-done((bf16[3,64,1664]{2,1,0:T(8,128)(2,1)S(1)}, bf16[3,64,1664]{2,1,0:T(8,128)(2,1)}, u32[]{:S(2)}, u32[]{:S(2)}) %collective-permute-start.32) | collective-permute-done | bytes 639008 | tf_op jit(solution)/shard_map/ppermute | solution.py:499
  250.4 0.9 copy-done.7
  251.3 3.8 %shard_map.108 = (f32[8,64,4096]{2,1,0:T(8,128)}, f32[8,64,1024]{2,1,0:T(8,128)}) custom-call(s32[12]{0:T(128)} %add_subtract_fusion.slots_ref, bf16[3,64,1664]{2,1,0:T(8,128)(2,1)} %get-tuple-element.78.refs_0_, bf16[3,64,3456]{2,1,0:T(8,128)(2,1)} %get-tuple-element.79.refs_1_, ...), custom_call_target="tpu_custom_call", output_to_operand_aliasing={{0}: (10, {}), {1}: (11, {})} | custom-call | flops 1 | bytes 1 | tf_op jit(solution)/shard_map/pallas_call | solution.py:451
  (54 shorter events, 1.8 us)
Async XLA Ops:
  0.6 9.4 %collective-permute-start.3 = (bf16[8,64,4096]{2,1,0:T(8,128)(2,1)}, bf16[8,64,4096]{2,1,0:T(8,128)(2,1)}, u32[]{:S(2)}, u32[]{:S(2)}) collective-permute-start(bf16[8,64,4096]{2,1,0:T(8,128)(2,1)} %bitcast.21), channel_id=1, source_target_pairs={{0,1},{1,0},{2,3},{3,2},{4,5},{5,4},{6,7},{7,6},{8,9},{9,8},{10,11... | collective-permute-start | bytes 12582920 | tf_op jit(solution)/shard_map/ppermute | solution.py:499
  1.4 8.4 %collective-permute-start.4 = (bf16[8,64,1024]{2,1,0:T(8,128)(2,1)}, bf16[8,64,1024]{2,1,0:T(8,128)(2,1)S(1)}, u32[]{:S(2)}, u32[]{:S(2)}) collective-permute-start(bf16[8,64,1024]{2,1,0:T(8,128)(2,1)} %refs_2_.3), channel_id=1, source_target_pairs={{0,1},{1,0},{2,3},{3,2},{4,5},{5,4},{6,7},{7,6},{8,9},{9,8},{10,11... | collective-permute-start | bytes 3145736 | tf_op jit(solution)/shard_map/ppermute | solution.py:499
  2.3 2.4 collective-permute-start.2
  9.7 1.0 copy-start.4
  10.7 5.2 %copy-start = (bf16[768,1024]{1,0:T(8,128)(2,1)S(1)}, bf16[768,1024]{1,0:T(8,128)(2,1)}, u32[]{:S(2)}) copy-start(bf16[768,1024]{1,0:T(8,128)(2,1)} %refs_0_.3) | copy-start | bytes 4718596
  15.6 44.3 %collective-permute-start.6 = (bf16[4096,1024]{1,0:T(8,128)(2,1)}, bf16[4096,1024]{1,0:T(8,128)(2,1)}, u32[]{:S(2)}, u32[]{:S(2)}) collective-permute-start(bf16[4096,1024]{1,0:T(8,128)(2,1)} %refs_7_.1), channel_id=1, source_target_pairs={{0,1},{1,0},{2,3},{3,2},{4,5},{5,4},{6,7},{7,6},{8,9},{9,8},{10,11... | collective-permute-start | bytes 25165832 | tf_op jit(solution)/shard_map/ppermute | solution.py:499
  15.7 44.3 %collective-permute-start.5 = (bf16[3,64,5120]{2,1,0:T(8,128)(2,1)}, bf16[3,64,5120]{2,1,0:T(8,128)(2,1)}, u32[]{:S(2)}, u32[]{:S(2)}) collective-permute-start(bf16[3,64,5120]{2,1,0:T(8,128)(2,1)} %shard_map.103), channel_id=1, source_target_pairs={{0,2},{1,3},{2,0},{3,1},{4,6},{5,7},{6,4},{7,5},{8,10},{9,11},{10,... | collective-permute-start | bytes 5898248 | tf_op jit(solution)/shard_map/ppermute | solution.py:499
  15.9 37.7 %collective-permute-start = (bf16[768,1024]{1,0:T(8,128)(2,1)S(1)}, bf16[768,1024]{1,0:T(8,128)(2,1)S(1)}, u32[]{:S(2)}, u32[]{:S(2)}) collective-permute-start(bf16[768,1024]{1,0:T(8,128)(2,1)S(1)} %copy-done), channel_id=1, source_target_pairs={{0,4},{4,8},{8,12},{1,5},{5,9},{9,13},{2,6},{6,10},{10,14},{3,7},{... | collective-permute-start | bytes 4718600 | tf_op jit(solution)/shard_map/ppermute | solution.py:526
  19.1 37.4 %collective-permute-start.1 = (bf16[768,1024]{1,0:T(8,128)(2,1)S(1)}, bf16[768,1024]{1,0:T(8,128)(2,1)}, u32[]{:S(2)}, u32[]{:S(2)}) collective-permute-start(bf16[768,1024]{1,0:T(8,128)(2,1)S(1)} %copy-done), channel_id=1, source_target_pairs={{4,0},{8,4},{12,8},{5,1},{9,5},{13,9},{6,2},{10,6},{14,10},{7,3},{... | collective-permute-start | bytes 4718600 | tf_op jit(solution)/shard_map/ppermute | solution.py:526
  25.3 31.3 %collective-permute-start.7 = (s32[6]{0:T(128)S(1)}, s32[6]{0:T(128)S(1)}, u32[]{:S(2)}, u32[]{:S(2)}) collective-permute-start(s32[6]{0:T(128)S(1)} %get-tuple-element.46), channel_id=1, source_target_pairs={{0,1},{1,0},{2,3},{3,2},{4,5},{5,4},{6,7},{7,6},{8,9},{9,8},{10,11... | collective-permute-start | bytes 80 | tf_op jit(solution)/shard_map/ppermute | solution.py:499
  53.6 42.5 %copy-start.1 = (bf16[768,1024]{1,0:T(8,128)(2,1)}, bf16[768,1024]{1,0:T(8,128)(2,1)S(1)}, u32[]{:S(2)}) copy-start(bf16[768,1024]{1,0:T(8,128)(2,1)S(1)} %collective-permute-done.refs_1_) | copy-start | bytes 4718596
  59.9 23.5 %collective-permute-start.12 = (bf16[512,1024]{1,0:T(8,128)(2,1)S(1)}, bf16[512,1024]{1,0:T(8,128)(2,1)}, u32[]{:S(2)}, u32[]{:S(2)}) collective-permute-start(bf16[512,1024]{1,0:T(8,128)(2,1)S(1)} %get-tuple-element.51), channel_id=1, source_target_pairs={{0,2},{1,3},{2,0},{3,1},{4,6},{5,7},{6,4},{7,5},{8,10},{9,11},{10,... | collective-permute-start | bytes 3145736 | tf_op jit(solution)/shard_map/ppermute | solution.py:499
  60.7 47.1 %collective-permute-start.8 = (bf16[768,1024]{1,0:T(8,128)(2,1)S(1)}, bf16[768,1024]{1,0:T(8,128)(2,1)S(1)}, u32[]{:S(2)}, u32[]{:S(2)}) collective-permute-start(bf16[768,1024]{1,0:T(8,128)(2,1)S(1)} %collective-permute-done.refs_1_), channel_id=1, source_target_pairs={{0,4},{4,8},{8,12},{1,5},{5,9},{9,13},{2,6},{6,10},{10,14},{3,7},{... | collective-permute-start | bytes 4718600 | tf_op jit(solution)/shard_map/ppermute | solution.py:526
  63.9 43.9 %collective-permute-start.9 = (bf16[768,1024]{1,0:T(8,128)(2,1)}, bf16[768,1024]{1,0:T(8,128)(2,1)}, u32[]{:S(2)}, u32[]{:S(2)}) collective-permute-start(bf16[768,1024]{1,0:T(8,128)(2,1)} %collective-permute-done.1.refs_2_), channel_id=1, source_target_pairs={{4,0},{8,4},{12,8},{5,1},{9,5},{13,9},{6,2},{10,6},{14,10},{7,3},{... | collective-permute-start | bytes 4718600 | tf_op jit(solution)/shard_map/ppermute | solution.py:526
  66.1 41.7 %collective-permute-start.13 = (bf16[512,1024]{1,0:T(8,128)(2,1)}, bf16[512,1024]{1,0:T(8,128)(2,1)}, u32[]{:S(2)}, u32[]{:S(2)}) collective-permute-start(bf16[512,1024]{1,0:T(8,128)(2,1)} %get-tuple-element.52), channel_id=1, source_target_pairs={{0,2},{1,3},{2,0},{3,1},{4,6},{5,7},{6,4},{7,5},{8,10},{9,11},{10,... | collective-permute-start | bytes 3145736 | tf_op jit(solution)/shard_map/ppermute | solution.py:499
  83.4 24.4 %collective-permute-start.14 = (bf16[512,1024]{1,0:T(8,128)(2,1)}, bf16[512,1024]{1,0:T(8,128)(2,1)}, u32[]{:S(2)}, u32[]{:S(2)}) collective-permute-start(bf16[512,1024]{1,0:T(8,128)(2,1)} %collective-permute-done.12.refs_9_), channel_id=1, source_target_pairs={{0,16},{16,0},{1,17},{17,1},{2,18},{18,2},{3,19},{19,3},{4,20},{20... | collective-permute-start | bytes 3145736 | tf_op jit(solution)/shard_map/ppermute | solution.py:564
  96.1 10.6 %collective-permute-start.10 = (f32[3,256,128]{2,1,0:T(8,128)}, f32[3,256,128]{2,1,0:T(8,128)S(1)}, u32[]{:S(2)}, u32[]{:S(2)}) collective-permute-start(f32[3,256,128]{2,1,0:T(8,128)} %get-tuple-element.50), channel_id=1, source_target_pairs={{0,4},{4,0},{8,12},{12,8},{1,5},{5,1},{9,13},{13,9},{2,6},{6,2},{1... | collective-permute-start | bytes 1179656 | tf_op jit(solution)/shard_map/ppermute | solution.py:499
  107.8 37.4 %copy-start.5 = (f32[3,256,128]{2,1,0:T(8,128)}, f32[3,256,128]{2,1,0:T(8,128)S(1)}, u32[]{:S(2)}) copy-start(f32[3,256,128]{2,1,0:T(8,128)S(1)} %add.109.here_ref) | copy-start | bytes 1179652
  107.8 44.3 %copy-start.2 = (bf16[768,1024]{1,0:T(8,128)(2,1)}, bf16[768,1024]{1,0:T(8,128)(2,1)S(1)}, u32[]{:S(2)}) copy-start(bf16[768,1024]{1,0:T(8,128)(2,1)S(1)} %collective-permute-done.8.refs_3_) | copy-start | bytes 4718596
  107.8 23.6 %collective-permute-start.15 = (bf16[512,1024]{1,0:T(8,128)(2,1)}, bf16[512,1024]{1,0:T(8,128)(2,1)S(1)}, u32[]{:S(2)}, u32[]{:S(2)}) collective-permute-start(bf16[512,1024]{1,0:T(8,128)(2,1)} %collective-permute-done.12.refs_9_), channel_id=1, source_target_pairs={{0,1},{1,0},{2,3},{3,2},{4,5},{5,4},{6,7},{7,6},{8,9},{9,8},{10,11... | collective-permute-start | bytes 3145736 | tf_op jit(solution)/shard_map/ppermute | solution.py:499
  110.6 25.1 %collective-permute-start.16 = (bf16[512,1024]{1,0:T(8,128)(2,1)}, bf16[512,1024]{1,0:T(8,128)(2,1)}, u32[]{:S(2)}, u32[]{:S(2)}) collective-permute-start(bf16[512,1024]{1,0:T(8,128)(2,1)} %get-tuple-element.55), channel_id=1, source_target_pairs={{0,2},{1,3},{2,0},{3,1},{4,6},{5,7},{6,4},{7,5},{8,10},{9,11},{10,... | collective-permute-start | bytes 3145736 | tf_op jit(solution)/shard_map/ppermute | solution.py:499
  111.3 24.3 %collective-permute-start.17 = (bf16[512,1024]{1,0:T(8,128)(2,1)}, bf16[512,1024]{1,0:T(8,128)(2,1)S(1)}, u32[]{:S(2)}, u32[]{:S(2)}) collective-permute-start(bf16[512,1024]{1,0:T(8,128)(2,1)} %collective-permute-done.14.refs_17_), channel_id=1, source_target_pairs={{0,1},{1,0},{2,3},{3,2},{4,5},{5,4},{6,7},{7,6},{8,9},{9,8},{10,11... | collective-permute-start | bytes 3145736 | tf_op jit(solution)/shard_map/ppermute | solution.py:499
  111.7 24.8 %collective-permute-start.18 = (bf16[512,1024]{1,0:T(8,128)(2,1)}, bf16[512,1024]{1,0:T(8,128)(2,1)S(1)}, u32[]{:S(2)}, u32[]{:S(2)}) collective-permute-start(bf16[512,1024]{1,0:T(8,128)(2,1)} %collective-permute-done.13.refs_11_), channel_id=1, source_target_pairs={{0,16},{16,0},{1,17},{17,1},{2,18},{18,2},{3,19},{19,3},{4,20},{20... | collective-permute-start | bytes 3145736 | tf_op jit(solution)/shard_map/ppermute | solution.py:564
  112.8 18.7 %collective-permute-start.11 = (f32[3,256,128]{2,1,0:T(8,128)S(1)}, f32[3,256,128]{2,1,0:T(8,128)S(1)}, u32[]{:S(2)}, u32[]{:S(2)}) collective-permute-start(f32[3,256,128]{2,1,0:T(8,128)S(1)} %add.109.here_ref), channel_id=1, source_target_pairs={{0,8},{4,12},{8,0},{12,4},{1,9},{5,13},{9,1},{13,5},{2,10},{6,14},... | collective-permute-start | bytes 1179656 | tf_op jit(solution)/shard_map/ppermute | solution.py:499
  131.4 13.7 %copy-start.12 = (f32[3,256,128]{2,1,0:T(8,128)}, f32[3,256,128]{2,1,0:T(8,128)S(1)}, u32[]{:S(2)}) copy-start(f32[3,256,128]{2,1,0:T(8,128)S(1)} %collective-permute-done.11.there_ref) | copy-start | bytes 1179652
  131.5 5.0 %copy-start.8 = (bf16[512,1024]{1,0:T(8,128)(2,1)}, bf16[512,1024]{1,0:T(8,128)(2,1)S(1)}, u32[]{:S(2)}) copy-start(bf16[512,1024]{1,0:T(8,128)(2,1)S(1)} %collective-permute-done.15.refs_10_) | copy-start | bytes 3145732
  135.7 1.6 copy-start.9
  136.5 5.8 %copy-start.10 = (bf16[512,1024]{1,0:T(8,128)(2,1)}, bf16[512,1024]{1,0:T(8,128)(2,1)S(1)}, u32[]{:S(2)}) copy-start(bf16[512,1024]{1,0:T(8,128)(2,1)S(1)} %collective-permute-done.18.refs_19_) | copy-start | bytes 3145732
  136.5 59.7 %copy-start.13 = (s32[3]{0:T(128)S(1)}, s32[3]{0:T(128)}, u32[]{:S(2)}) copy-start(s32[3]{0:T(128)} %live_ref.1) | copy-start | bytes 40
  136.5 24.0 %collective-permute-start.21 = (bf16[512,1024]{1,0:T(8,128)(2,1)}, bf16[512,1024]{1,0:T(8,128)(2,1)}, u32[]{:S(2)}, u32[]{:S(2)}) collective-permute-start(bf16[512,1024]{1,0:T(8,128)(2,1)} %get-tuple-element.60), channel_id=1, source_target_pairs={{0,2},{1,3},{2,0},{3,1},{4,6},{5,7},{6,4},{7,5},{8,10},{9,11},{10,... | collective-permute-start | bytes 3145736 | tf_op jit(solution)/shard_map/ppermute | solution.py:499
  137.2 37.4 %collective-permute-start.19 = (bf16[768,1024]{1,0:T(8,128)(2,1)S(1)}, bf16[768,1024]{1,0:T(8,128)(2,1)S(1)}, u32[]{:S(2)}, u32[]{:S(2)}) collective-permute-start(bf16[768,1024]{1,0:T(8,128)(2,1)S(1)} %collective-permute-done.8.refs_3_), channel_id=1, source_target_pairs={{0,4},{4,8},{8,12},{1,5},{5,9},{9,13},{2,6},{6,10},{10,14},{3,7},{... | collective-permute-start | bytes 4718600 | tf_op jit(solution)/shard_map/ppermute | solution.py:526
  142.3 36.6 %collective-permute-start.20 = (bf16[768,1024]{1,0:T(8,128)(2,1)}, bf16[768,1024]{1,0:T(8,128)(2,1)}, u32[]{:S(2)}, u32[]{:S(2)}) collective-permute-start(bf16[768,1024]{1,0:T(8,128)(2,1)} %collective-permute-done.9.refs_4_), channel_id=1, source_target_pairs={{4,0},{8,4},{12,8},{5,1},{9,5},{13,9},{6,2},{10,6},{14,10},{7,3},{... | collective-permute-start | bytes 4718600 | tf_op jit(solution)/shard_map/ppermute | solution.py:526
  144.4 23.5 %collective-permute-start.27 = (bf16[512,1024]{1,0:T(8,128)(2,1)}, bf16[512,1024]{1,0:T(8,128)(2,1)}, u32[]{:S(2)}, u32[]{:S(2)}) collective-permute-start(bf16[512,1024]{1,0:T(8,128)(2,1)} %collective-permute-done.16.refs_13_), channel_id=1, source_target_pairs={{0,16},{16,0},{1,17},{17,1},{2,18},{18,2},{3,19},{19,3},{4,20},{20... | collective-permute-start | bytes 3145736 | tf_op jit(solution)/shard_map/ppermute | solution.py:564
  160.5 29.9 %collective-permute-start.22 = (bf16[512,1024]{1,0:T(8,128)(2,1)}, bf16[512,1024]{1,0:T(8,128)(2,1)}, u32[]{:S(2)}, u32[]{:S(2)}) collective-permute-start(bf16[512,1024]{1,0:T(8,128)(2,1)} %collective-permute-done.21.refs_15_), channel_id=1, source_target_pairs={{0,16},{16,0},{1,17},{17,1},{2,18},{18,2},{3,19},{19,3},{4,20},{20... | collective-permute-start | bytes 3145736 | tf_op jit(solution)/shard_map/ppermute | solution.py:564
  161.6 19.7 %collective-permute-start.29 = (bf16[3,64,1664]{2,1,0:T(8,128)(2,1)}, bf16[3,64,1664]{2,1,0:T(8,128)(2,1)}, u32[]{:S(2)}, u32[]{:S(2)}) collective-permute-start(bf16[3,64,1664]{2,1,0:T(8,128)(2,1)} %get-tuple-element.78.refs_0_), channel_id=1, source_target_pairs={{0,2},{1,3},{2,0},{3,1},{4,6},{5,7},{6,4},{7,5},{8,10},{9,11},{10,... | collective-permute-start | bytes 1916936 | tf_op jit(solution)/shard_map/ppermute | solution.py:499
  167.9 24.9 %collective-permute-start.23 = (bf16[512,1024]{1,0:T(8,128)(2,1)}, bf16[512,1024]{1,0:T(8,128)(2,1)}, u32[]{:S(2)}, u32[]{:S(2)}) collective-permute-start(bf16[512,1024]{1,0:T(8,128)(2,1)} %collective-permute-done.13.refs_11_), channel_id=1, source_target_pairs={{0,1},{1,0},{2,3},{3,2},{4,5},{5,4},{6,7},{7,6},{8,9},{9,8},{10,11... | collective-permute-start | bytes 3145736 | tf_op jit(solution)/shard_map/ppermute | solution.py:499
  174.7 22.1 %copy-start.3 = (bf16[768,1024]{1,0:T(8,128)(2,1)}, bf16[768,1024]{1,0:T(8,128)(2,1)S(1)}, u32[]{:S(2)}) copy-start(bf16[768,1024]{1,0:T(8,128)(2,1)S(1)} %collective-permute-done.19.refs_5_) | copy-start | bytes 4718596
  174.7 18.1 %collective-permute-start.24 = (bf16[512,1024]{1,0:T(8,128)(2,1)}, bf16[512,1024]{1,0:T(8,128)(2,1)}, u32[]{:S(2)}, u32[]{:S(2)}) collective-permute-start(bf16[512,1024]{1,0:T(8,128)(2,1)} %collective-permute-done.16.refs_13_), channel_id=1, source_target_pairs={{0,1},{1,0},{2,3},{3,2},{4,5},{5,4},{6,7},{7,6},{8,9},{9,8},{10,11... | collective-permute-start | bytes 3145736 | tf_op jit(solution)/shard_map/ppermute | solution.py:499
  178.9 14.0 %collective-permute-start.25 = (bf16[512,1024]{1,0:T(8,128)(2,1)}, bf16[512,1024]{1,0:T(8,128)(2,1)}, u32[]{:S(2)}, u32[]{:S(2)}) collective-permute-start(bf16[512,1024]{1,0:T(8,128)(2,1)} %collective-permute-done.21.refs_15_), channel_id=1, source_target_pairs={{0,1},{1,0},{2,3},{3,2},{4,5},{5,4},{6,7},{7,6},{8,9},{9,8},{10,11... | collective-permute-start | bytes 3145736 | tf_op jit(solution)/shard_map/ppermute | solution.py:499
  181.3 11.5 %collective-permute-start.26 = (bf16[512,1024]{1,0:T(8,128)(2,1)}, bf16[512,1024]{1,0:T(8,128)(2,1)}, u32[]{:S(2)}, u32[]{:S(2)}) collective-permute-start(bf16[512,1024]{1,0:T(8,128)(2,1)} %copy-done.10), channel_id=1, source_target_pairs={{0,1},{1,0},{2,3},{3,2},{4,5},{5,4},{6,7},{7,6},{8,9},{9,8},{10,11... | collective-permute-start | bytes 3145736 | tf_op jit(solution)/shard_map/ppermute | solution.py:499
  190.4 5.1 %collective-permute-start.28 = (bf16[512,1024]{1,0:T(8,128)(2,1)}, bf16[512,1024]{1,0:T(8,128)(2,1)}, u32[]{:S(2)}, u32[]{:S(2)}) collective-permute-start(bf16[512,1024]{1,0:T(8,128)(2,1)} %collective-permute-done.27.refs_21_), channel_id=1, source_target_pairs={{0,1},{1,0},{2,3},{3,2},{4,5},{5,4},{6,7},{7,6},{8,9},{9,8},{10,11... | collective-permute-start | bytes 3145736 | tf_op jit(solution)/shard_map/ppermute | solution.py:499
  195.5 35.9 %collective-permute-start.30 = (bf16[3,64,3456]{2,1,0:T(8,128)(2,1)}, bf16[3,64,3456]{2,1,0:T(8,128)(2,1)}, u32[]{:S(2)}, u32[]{:S(2)}) collective-permute-start(bf16[3,64,3456]{2,1,0:T(8,128)(2,1)} %get-tuple-element.79.refs_1_), channel_id=1, source_target_pairs={{0,2},{1,3},{2,0},{3,1},{4,6},{5,7},{6,4},{7,5},{8,10},{9,11},{10,... | collective-permute-start | bytes 3981320 | tf_op jit(solution)/shard_map/ppermute | solution.py:499
  196.8 35.7 %copy-start.6 = (bf16[3,64,3456]{2,1,0:T(8,128)(2,1)S(1)}, bf16[3,64,3456]{2,1,0:T(8,128)(2,1)}, u32[]{:S(2)}) copy-start(bf16[3,64,3456]{2,1,0:T(8,128)(2,1)} %get-tuple-element.79.refs_1_) | copy-start | bytes 3981316
  231.3 3.2 %collective-permute-start.31 = (bf16[512,1024]{1,0:T(8,128)(2,1)}, bf16[512,1024]{1,0:T(8,128)(2,1)}, u32[]{:S(2)}, u32[]{:S(2)}) collective-permute-start(bf16[512,1024]{1,0:T(8,128)(2,1)} %collective-permute-done.22.refs_9_), channel_id=1, source_target_pairs={{0,1},{1,0},{2,3},{3,2},{4,5},{5,4},{6,7},{7,6},{8,9},{9,8},{10,11... | collective-permute-start | bytes 3145736 | tf_op jit(solution)/shard_map/ppermute | solution.py:499
  232.4 17.8 %collective-permute-start.33 = (bf16[3,64,3456]{2,1,0:T(8,128)(2,1)S(1)}, bf16[3,64,3456]{2,1,0:T(8,128)(2,1)S(1)}, u32[]{:S(2)}, u32[]{:S(2)}) collective-permute-start(bf16[3,64,3456]{2,1,0:T(8,128)(2,1)S(1)} %copy-done.6), channel_id=1, source_target_pairs={{0,1},{1,0},{2,3},{3,2},{4,5},{5,4},{6,7},{7,6},{8,9},{9,8},{10,11... | collective-permute-start | bytes 3981320 | tf_op jit(solution)/shard_map/ppermute | solution.py:499
  234.5 11.1 %copy-start.11 = (bf16[3,64,1664]{2,1,0:T(8,128)(2,1)S(1)}, bf16[3,64,1664]{2,1,0:T(8,128)(2,1)}, u32[]{:S(2)}) copy-start(bf16[3,64,1664]{2,1,0:T(8,128)(2,1)} %get-tuple-element.78.refs_0_) | copy-start | bytes 1916932
  245.1 5.3 %collective-permute-start.35 = (bf16[3,64,3456]{2,1,0:T(8,128)(2,1)}, bf16[3,64,3456]{2,1,0:T(8,128)(2,1)}, u32[]{:S(2)}, u32[]{:S(2)}) collective-permute-start(bf16[3,64,3456]{2,1,0:T(8,128)(2,1)} %collective-permute-done.30.refs_5_), channel_id=1, source_target_pairs={{0,1},{1,0},{2,3},{3,2},{4,5},{5,4},{6,7},{7,6},{8,9},{9,8},{10,11... | collective-permute-start | bytes 3981320 | tf_op jit(solution)/shard_map/ppermute | solution.py:499
  245.5 4.6 %collective-permute-start.32 = (bf16[3,64,1664]{2,1,0:T(8,128)(2,1)S(1)}, bf16[3,64,1664]{2,1,0:T(8,128)(2,1)}, u32[]{:S(2)}, u32[]{:S(2)}) collective-permute-start(bf16[3,64,1664]{2,1,0:T(8,128)(2,1)S(1)} %copy-done.11), channel_id=1, source_target_pairs={{0,1},{1,0},{2,3},{3,2},{4,5},{5,4},{6,7},{7,6},{8,9},{9,8},{10,11... | collective-permute-start | bytes 1916936 | tf_op jit(solution)/shard_map/ppermute | solution.py:499
  245.7 4.7 %collective-permute-start.34 = (bf16[3,64,1664]{2,1,0:T(8,128)(2,1)}, bf16[3,64,1664]{2,1,0:T(8,128)(2,1)}, u32[]{:S(2)}, u32[]{:S(2)}) collective-permute-start(bf16[3,64,1664]{2,1,0:T(8,128)(2,1)} %collective-permute-done.29.refs_4_), channel_id=1, source_target_pairs={{0,1},{1,0},{2,3},{3,2},{4,5},{5,4},{6,7},{7,6},{8,9},{9,8},{10,11... | collective-permute-start | bytes 1916936 | tf_op jit(solution)/shard_map/ppermute | solution.py:499
  250.2 1.1 copy-start.7

commit v5 on v4

--- a/solution.py
+++ b/solution.py
@@ -209,9 +209,8 @@
     )(live, here, there, hidden, grad)
 
 
-def base_kernel(n_dp, tiles, n_chunks, n_kept, count, scalars_ref, *refs):
+def base_kernel(n_dp, tiles, n_chunks, count, scalars_ref, kept_ref, *refs):
     near = n_dp // 2
-    kept_refs, refs = refs[:n_kept], refs[n_kept:]
     near_refs = refs[:near]
     far_refs = refs[near : near + n_chunks * near]
     coef_ref, block_ref = refs[near + n_chunks * near : near + n_chunks * near + 2]
@@ -253,12 +252,8 @@
             block_ref.at[:, :, span(j)], factor.at[slot], factor_sem.at[slot]
         )
 
-    at = [scalars_ref[steps + n_dp + count + k] for k in range(n_kept)]
-
-    def columns(k):
-        wide = kept_refs[k].shape[1]
-        place = pl.ds(pl.multiple_of(at[k] * wide, wide), wide)
-        return pltpu.make_async_copy(kept_refs[k], kept.at[:, place], kept_sem.at[k])
+    def columns(r):
+        return pltpu.make_async_copy(kept_ref.at[:, lanes(r)], kept.at[:, lanes(r)], kept_sem.at[r])
 
     def store(j, slot):
         return pltpu.make_async_copy(result.at[slot], out_ref.at[:, span(j)], out_sem.at[slot])
@@ -280,23 +275,16 @@
                 bf16
             )
 
-    for k in range(n_kept):
-        pl.when(at[k] >= 0)(lambda k=k: columns(k).start())
     for r in range(n_dp):
+        columns(r).start()
         for copy in loads(0, 0, r):
             copy.start()
     factors(0, 0).start()
     if steps > 1:
         load(1, 1)
-    matching = kept_refs[0].shape[1] == deep
-    if not matching:
-        for k in range(n_kept):
-            pl.when(at[k] >= 0)(lambda k=k: columns(k).wait())
     total = None
     for r in range(n_dp):
-        if matching:
-            for k in range(n_kept):
-                pl.when(at[k] == scalars_ref[steps + r])(lambda k=k: columns(k).wait())
+        columns(r).wait()
         for copy in loads(0, 0, r):
             copy.wait()
         part = lax.dot_general(
@@ -335,12 +323,11 @@
 
 
 def base(places, scalars, kept, near, chunks, tiles, tile, coef, block_a, held, token):
-    rows = kept[0].shape[0]
+    rows, depth = kept.shape
     count, rank, ff = block_a.shape
     top = len(near)
-    depth = 2 * top * near[0].shape[1]
     anywhere = pl.BlockSpec(memory_space=pl.ANY)
-    operands = [*kept, *[near[r] for r in range(top)]]
+    operands = [kept, *[near[r] for r in range(top)]]
     for piece in chunks:
         operands += [piece[r] for r in range(top, 2 * top)]
     in_specs = [anywhere] * len(operands)
@@ -354,7 +341,7 @@
     most = max(len(segments) for segments in tiles)
     span = tile * len(tiles)
     return pl.pallas_call(
-        functools.partial(base_kernel, 2 * top, tiles, len(chunks), len(kept), count),
+        functools.partial(base_kernel, 2 * top, tiles, len(chunks), count),
         grid_spec=pltpu.PrefetchScalarGridSpec(
             num_scalar_prefetch=1,
             grid=(1,),
@@ -365,7 +352,7 @@
                 pltpu.VMEM((2, tile, depth), bf16),
                 pltpu.VMEM((2, count, rank, tile), bf16),
                 pltpu.VMEM((2, rows, tile), bf16),
-                pltpu.SemaphoreType.DMA((len(kept),)),
+                pltpu.SemaphoreType.DMA((2 * top,)),
                 pltpu.SemaphoreType.DMA((2, 2 * top, most)),
                 pltpu.SemaphoreType.DMA((2,)),
                 pltpu.SemaphoreType.DMA((2,)),
@@ -511,29 +498,12 @@
     slots = jnp.sum(jnp.where(match, jnp.arange(n_slots, dtype=i32)[None, :], 0), axis=1)
     far_slots = swap(slots, top)
 
-    place = lax.axis_index("fsdp")
-    line = n_fsdp <= 4
-    pieces_of_kept, at = [output_gradient], [place]
-
-    def hop(*after):
-        k = len(pieces_of_kept) // 2
-        if not line or k + 1 >= n_fsdp:
-            return []
-        right = [(i, i + 1) for i in range(n_fsdp - 1)]
-        left = [(i + 1, i) for i in range(n_fsdp - 1)]
-        ends = pieces_of_kept[-2:] if k else pieces_of_kept * 2
-        for piece, pairs in zip(ends, (right, left)):
-            pieces_of_kept.append(lax.ppermute(behind(piece, *after), "fsdp", pairs))
-        at.append(place - k - 1)
-        at.append(jnp.where(place + k + 1 < n_fsdp, place + k + 1, -1))
-        return pieces_of_kept[-2:]
-
-    first_hop = hop()
+    kept = lax.all_gather(output_gradient, "fsdp", axis=1, tiled=True)
 
     share = ff // n_groups
     if share % 2048 == 0:
         unit, tile = share // 8, share // 4
-        sizes = [2 * unit] * 4
+        sizes = [2 * unit, 2 * unit, 3 * unit, unit]
     else:
         tile = share
         sizes = [share]
@@ -545,14 +515,18 @@
     def flat(*pieces):
         return [v for piece in pieces for v in piece.values()]
 
+    def piece_of(j, shift, *after):
+        start, size = parts[j]
+        owner = lax.rem(group + n_groups - shift, n_groups)
+        piece = lax.dynamic_slice_in_dim(frozen_down_weight, owner * share + start, size, axis=0)
+        return {top: swap(behind(piece, *after), top)}
+
     def cross(*after):
         j = len(crossed)
         if j < len(parts):
-            start, size = parts[j]
-            piece = lax.dynamic_slice_in_dim(
-                frozen_down_weight, group * share + start, size, axis=0
-            )
-            crossed.append({top: swap(behind(piece, *after), top)})
+            crossed.append(piece_of(j, 0, *after))
+            if j and j + 1 == len(parts):
+                turned.append([piece_of(j, shift, *after) for shift in range(1, n_groups)])
 
     def turn(*after):
         j = len(turned)
@@ -582,13 +556,12 @@
     far = swap(picked, top)
     whole = spread({0: behind(frozen_down_weight, picked)})
     both_slots = spread({0: behind(jnp.concatenate([slots, far_slots]), picked)})
-    past = [far, *first_hop, *flat(whole, both_slots)]
+    past = [far, *flat(whole, both_slots)]
     part, block_a, grad_a, grad_b = project(
         *places(behind(slots, *past)), a_near, b_near, far, hidden, output_gradient
     )
-    second_hop = hop(*past)
-    cross(*past)
-    cross(*past)
+    cross(far)
+    cross(far)
     sums = [part]
     bit = 1
     while bit < n_fsdp:
@@ -597,38 +570,34 @@
             sums.append(sums[-2] + sums[-1])
         bit *= 2
     total, other = sums[-2:]
-    turn(*past)
-    past = [sums[2], *second_hop, *flat(*crossed, *sum(turned, []))]
+    past = [part, *flat(*crossed[:1])]
     cross(*past)
     turn(*past)
     fill(crossed[:1], *past)
+    past = [part, *flat(*crossed[:2], *turned[0])]
+    turn(*past)
+    fill(crossed[1:2], *past)
     fill(turned[0], *past)
-    past = [other, *flat(*crossed, *sum(turned, []))]
-    third_hop = hop(*past)
+    past = [sums[2], *flat(*crossed[:3], *sum(turned, []))]
+    turn(*past)
     cross(*past)
-    turn(*past)
+    fill(crossed[2:3], *past)
+    for pieces in turned[1:2]:
+        fill(pieces, *past)
     low_terms, high_terms, coef = block_terms(
         island_live_rows, total, other, hidden, output_gradient
     )
-    far_low = swap(behind(low_terms, *flat(*crossed)), top)
-    past = flat(*crossed[3:])
-    turn(low_terms, *past)
-    fill(crossed[1:], *past)
-    for pieces in turned[1:3]:
-        fill(pieces, *past)
-    past = [far_low, *third_hop, *flat(*crossed, *sum(turned, []))]
-    far_high = swap(behind(high_terms, *past), top)
-    if line:
-        at = jnp.stack(at).astype(i32)
-    else:
-        pieces_of_kept = [lax.all_gather(output_gradient, "fsdp", axis=1, tiled=True)]
-        at = jnp.zeros((1,), i32)
+    far_high = swap(behind(high_terms, *flat(*crossed[3:], *sum(turned[3:], []))), top)
+    far_low = swap(low_terms, top)
+    fill(crossed[3:], other)
+    for pieces in turned[3:]:
+        fill(pieces, other)
 
     relative = [both_slots[r][:count] for r in near] + [both_slots[r][count:] for r in near]
     relative = jnp.concatenate(relative) - me * local
 
     scalars = jnp.concatenate(
-        [jnp.stack([me ^ r for r in range(n_dp)]).astype(i32), island_live_rows, at]
+        [jnp.stack([me ^ r for r in range(n_dp)]).astype(i32), island_live_rows]
     )
     grad_hidden = token = None
 
@@ -647,24 +616,24 @@
                     tiles[-1].append((chunks.index((shift, j)), low - first, high - low))
         pieces = [turned[j][shift - 1] if shift else crossed[j] for shift, j in chunks]
         grad_hidden, token = base(
-            places, scalars, pieces_of_kept, whole, pieces, tiles, tile, coef, block_a,
+            places, scalars, kept, whole, pieces, tiles, tile, coef, block_a,
             grad_hidden, token,
         )
 
     others = range(1, n_groups)
     if share > tile:
-        multiply(*[(0, t) for t in range(4)], *[(g, t) for g in others for t in range(3)])
+        multiply(*[(0, t) for t in range(4)], *[(g, 0) for g in others])
         past = [token, far_high]
-        for pieces in turned[3:]:
+        for pieces in turned[2:3]:
             fill(pieces, *past)
-        multiply(*[(g, 3) for g in others])
+        multiply(*[(g, t) for g in others for t in range(1, 4)])
     else:
         multiply(*[(g, 0) for g in range(n_groups)])
 
     near_low = spread({0: behind(low_terms, *past)})
     near_high = spread({0: behind(high_terms, *past)})
+    all_high = spread({top: behind(far_high, *past)})
     all_low = spread({top: behind(far_low, token)})
-    all_high = spread({top: behind(far_high, token)})
     terms = [p for r in near for p in (near_low[r], near_high[r])]
     terms += [p for r in near for p in (all_low[r + top], all_high[r + top])]
     grad_a, grad_b = add_terms(relative, terms, grad_a, grad_b, token)

time: 260 us -> 253 us (0.973); the launches traced: 255 us -> 252 us
  starting transfers between devices: 47 us -> 24.8 us
  between operations: 1 us -> 14.2 us
  local copies, waits for them, and re-layouts: 6.9 us -> 12.7 us
  Pallas kernels: 71.1 us -> 74.4 us
  waiting for transfers between devices: 124 us -> 121 us
    ppermute x26 -> x27, waiting for transfers between devices: 73.9 us -> 115 us  [swap(): return lax.ppermute(value, axis, [(i, i ^ bit) for i in range(size)])]
    ppermute x6 -> x0, waiting for transfers between devices: 34.7 us -> none  [hop(): pieces_of_kept.append(lax.ppermute(behind(piece, *after), 'fsdp', pairs))]
    ppermute x6 -> x0, starting transfers between devices: 17.9 us -> none  [hop(): pieces_of_kept.append(lax.ppermute(behind(piece, *after), 'fsdp', pairs))]
    ppermute x4 -> x3, waiting for transfers between devices: 15.8 us -> 6.27 us  [turn(): turned[j].append({top: lax.ppermute(piece, 'groups', ring)})]
    pallas_call x1, Pallas kernels: 3.75 us -> 8.18 us  [add_terms(): pl.pallas_call(functools.partial(add_kernel, n, count), grid_spec=pltpu.P...]
    ppermute x26 -> x27, starting transfers between devices: 25.1 us -> 20.7 us  [swap(): return lax.ppermute(value, axis, [(i, i ^ bit) for i in range(size)])]
    unnamed x28 -> x24, local copies, waits for them, and re-layouts: 1.63 us -> 4.7 us
    dynamic_slice x1 -> x3, local copies, waits for them, and re-layouts: 3.94 us -> 6.47 us  [piece_of(): lax.dynamic_slice_in_dim(frozen_down_weight, owner * share + start, size,...]
  transfers between devices with their start and end apart: 36 -> 31, of which waited for: 20 -> 14; matrix products, arithmetic and copies ran while one was open for 4% -> 5% of each run, Pallas kernels for 24% -> 24%
where the time goes in v5:
time: 253 us; the launch traced here: 252 us
  waiting for transfers between devices  121 us (48%)
  Pallas kernels  74.4 us (29%)
  starting transfers between devices  24.8 us (10%)
  between operations  14.2 us (6%)
  local copies, waits for them, and re-layouts  12.7 us (5%)
  other arithmetic  4.86 us (2%)
    ppermute x27, waiting for transfers between devices, swap(): return lax.ppermute(value, axis, [(i, i ^ bit) for i in range(size)])  115 us
    pallas_call x2, Pallas kernels, base(): pl.pallas_call(functools.partial(base_kernel, 2 * top, tiles, len(chunks)...  43.3 us
    ppermute x27, starting transfers between devices, swap(): return lax.ppermute(value, axis, [(i, i ^ bit) for i in range(size)])  20.7 us
    pallas_call x1, Pallas kernels, project(): pl.pallas_call(functools.partial(project_kernel, pieces), grid_spec=pltpu...  11.2 us
    pallas_call x1, Pallas kernels, add_terms(): pl.pallas_call(functools.partial(add_kernel, n, count), grid_spec=pltpu.P...  8.18 us
    pallas_call x1, Pallas kernels, block_terms(): pl.pallas_call(terms_kernel, grid_spec=pltpu.PrefetchScalarGridSpec(num_s...  6.91 us
    dynamic_slice x3, local copies, waits for them, and re-layouts, piece_of(): lax.dynamic_slice_in_dim(frozen_down_weight, owner * share + start, size,...  6.47 us
    ppermute x3, waiting for transfers between devices, turn(): turned[j].append({top: lax.ppermute(piece, 'groups', ring)})  6.27 us
  transfers between devices with their start and end apart: 31, of which 14 were waited for; matrix products, arithmetic and copies ran while one was open for 5% of the time, Pallas kernels for 24%

profile of v5, /device:TPU:11, one launch (start us, length us, event | category | flops | bytes accessed | tf_op | source)
XLA Modules:
  0.0 252.4 jit_solution(12651106204368813549)
XLA Ops:
  7.2 0.7 collective-permute-start.1
  8.0 0.1 collective-permute-start.2
  8.0 0.9 select_reduce_fusion
  8.9 0.3 collective-permute-start
  9.2 2.1 collective-permute-done
  11.3 0.5 compare_select_fusion.1
  11.9 0.6 pad_add_fusion
  12.4 3.9 %collective-permute-done.2.refs_3_ = bf16[8,64,1024]{2,1,0:T(8,128)(2,1)S(1)} collective-permute-done((bf16[8,64,1024]{2,1,0:T(8,128)(2,1)}, bf16[8,64,1024]{2,1,0:T(8,128)(2,1)S(1)}, u32[]{:S(2)}, u32[]{:S(2)}) %collective-permute-start.2) | collective-permute-done | bytes 1048608 | tf_op jit(solution)/shard_map/ppermute | solution.py:486
  16.3 0.3 collective-permute-done.1.refs_1_
  16.6 0.7 copy-done
  17.3 4.8 %shard_map.103 = bf16[3,64,5120]{2,1,0:T(8,128)(2,1)} custom-call(s32[6]{0:T(128)} %get-tuple-element.83.index_ref, s32[3]{0:T(128)} %get-tuple-element.81.source_ref, bf16[8,64,4096]{2,1,0:T(8,128)(2,1)} %bitcast.15, bf16[8,64,4096]{2,1,0:T(8,128)(2,1)} %collective-permute-done.1.refs_1_, bf16[8,64,1024]{2,1,0:T(8,128)(2,1)} %refs_2_.3, ...), custom_call_target="tpu_custom_call" | custom-call | bytes 5898240 | tf_op jit(solution)/shard_map/pallas_call | solution.py:54
  22.1 0.1 collective-permute-start.3
  22.2 0.3 collective-permute-start.4
  22.6 2.7 %constant_dynamic-slice_fusion.3 = (bf16[512,1024]{1,0:T(8,128)(2,1)S(1)}, bf16[512,1024]{1,0:T(8,128)(2,1)}) fusion(bf16[4096,1024]{1,0:T(8,128)(2,1)} %refs_0_.1, s32[]{:T(128)S(6)} %select_n.67, s32[]{:T(128)S(6)} %select_n.63), kind=kLoop, calls=%fused_computation.10 | loop fusion | bytes 4194312 | tf_op jit(solution)/shard_map/dynamic_slice | solution.py:521
  25.3 41.4 %collective-permute-done.4.refs_4_ = bf16[3,64,5120]{2,1,0:T(8,128)(2,1)S(1)} collective-permute-done((bf16[3,64,5120]{2,1,0:T(8,128)(2,1)}, bf16[3,64,5120]{2,1,0:T(8,128)(2,1)S(1)}, u32[]{:S(2)}, u32[]{:S(2)}) %collective-permute-start.4) | collective-permute-done | bytes 1966112 | tf_op jit(solution)/shard_map/ppermute | solution.py:486
  66.7 0.3 collective-permute-start.7
  67.0 1.3 collective-permute-start.6
  68.3 1.2 collective-permute-start.5
  69.5 0.6 compare_select_fusion
  70.1 0.6 pad_add_fusion.2.index_ref
  70.7 11.2 %shard_map.104 = (f32[3,256,128]{2,1,0:T(8,128)}, bf16[3,64,4096]{2,1,0:T(8,128)(2,1)}, f32[8,64,4096]{2,1,0:T(8,128)}, f32[8,64,1024]{2,1,0:T(8,128)}) custom-call(s32[6]{0:T(128)} %pad_add_fusion.2.index_ref, s32[3]{0:T(128)} %get-tuple-element.79.source_ref, bf16[8,64,4096]{2,1,0:T(8,128)(2,1)} %bitcast.16, ...), custom_call_target="tpu_custom_call" | custom-call | flops 503316480 | bytes 15728640 | tf_op jit(solution)/shard_map/pallas_call | solution.py:121
  82.0 8.4 %collective-permute-done.7.refs_2_ = bf16[512,1024]{1,0:T(8,128)(2,1)} collective-permute-done((bf16[512,1024]{1,0:T(8,128)(2,1)S(1)}, bf16[512,1024]{1,0:T(8,128)(2,1)}, u32[]{:S(2)}, u32[]{:S(2)}) %collective-permute-start.7) | collective-permute-done | bytes 1048608 | tf_op jit(solution)/shard_map/ppermute | solution.py:486
  90.3 3.6 %collective-permute-start.8 = (bf16[512,1024]{1,0:T(8,128)(2,1)}, bf16[512,1024]{1,0:T(8,128)(2,1)}, u32[]{:S(2)}, u32[]{:S(2)}) collective-permute-start(bf16[512,1024]{1,0:T(8,128)(2,1)} %collective-permute-done.7.refs_2_), channel_id=1, source_target_pairs={{0,1},{1,0},{2,3},{3,2},{4,5},{5,4},{6,7},{7,6},{8,9},{9,8},{10,11... | collective-permute-start | bytes 3145736 | tf_op jit(solution)/shard_map/ppermute | solution.py:486
  94.0 1.2 collective-permute-start.9
  95.1 1.5 constant_dynamic-slice_fusion.2
  96.7 0.4 collective-permute-start.13
  97.0 15.7 %collective-permute-done.5.refs_4_ = bf16[512,1024]{1,0:T(8,128)(2,1)} collective-permute-done((bf16[512,1024]{1,0:T(8,128)(2,1)}, bf16[512,1024]{1,0:T(8,128)(2,1)}, u32[]{:S(2)}, u32[]{:S(2)}) %collective-permute-start.5) | collective-permute-done | bytes 1048608 | tf_op jit(solution)/shard_map/ppermute | solution.py:486
  112.8 6.3 %collective-permute-done.9.refs_10_ = bf16[512,1024]{1,0:T(8,128)(2,1)} collective-permute-done((bf16[512,1024]{1,0:T(8,128)(2,1)}, bf16[512,1024]{1,0:T(8,128)(2,1)}, u32[]{:S(2)}, u32[]{:S(2)}) %collective-permute-start.9) | collective-permute-done | bytes 1048608 | tf_op jit(solution)/shard_map/ppermute | solution.py:538
  119.1 1.2 collective-permute-start.10
  120.3 1.1 collective-permute-start.12
  121.3 0.2 collective-permute-start.11
  121.5 2.2 constant_dynamic-slice_fusion
  123.7 18.4 %collective-permute-done.11 = f32[3,256,128]{2,1,0:T(8,128)} collective-permute-done((f32[3,256,128]{2,1,0:T(8,128)S(1)}, f32[3,256,128]{2,1,0:T(8,128)}, u32[]{:S(2)}, u32[]{:S(2)}) %collective-permute-start.11) | collective-permute-done | bytes 393248 | tf_op jit(solution)/shard_map/ppermute | solution.py:486
  142.1 1.0 add.97.here_ref
  143.2 3.2 %collective-permute-done.13.refs_6_ = bf16[768,1024]{1,0:T(8,128)(2,1)S(1)} collective-permute-done((bf16[768,1024]{1,0:T(8,128)(2,1)S(1)}, bf16[768,1024]{1,0:T(8,128)(2,1)S(1)}, u32[]{:S(2)}, u32[]{:S(2)}) %collective-permute-start.13) | collective-permute-done | bytes 1572896 | tf_op jit(solution)/shard_map/ppermute | solution.py:486
  146.4 0.5 collective-permute-start.18
  146.9 1.0 collective-permute-start.21
  147.9 2.3 collective-permute-start.19
  150.3 2.9 %collective-permute-start.17 = (bf16[768,1024]{1,0:T(8,128)(2,1)S(1)}, bf16[768,1024]{1,0:T(8,128)(2,1)S(1)}, u32[]{:S(2)}, u32[]{:S(2)}) collective-permute-start(bf16[768,1024]{1,0:T(8,128)(2,1)S(1)} %collective-permute-done.13.refs_6_), channel_id=1, source_target_pairs={{0,1},{1,0},{2,3},{3,2},{4,5},{5,4},{6,7},{7,6},{8,9},{9,8},{10,11... | collective-permute-start | bytes 4718600 | tf_op jit(solution)/shard_map/ppermute | solution.py:486
  153.1 1.7 collective-permute-start.16
  154.8 12.6 %collective-permute-done.19.there_ref = f32[3,256,128]{2,1,0:T(8,128)S(1)} collective-permute-done((f32[3,256,128]{2,1,0:T(8,128)S(1)}, f32[3,256,128]{2,1,0:T(8,128)S(1)}, u32[]{:S(2)}, u32[]{:S(2)}) %collective-permute-start.19) | collective-permute-done | bytes 393248 | tf_op jit(solution)/shard_map/ppermute | solution.py:486
  167.4 0.7 copy-done.9
  168.2 6.9 %shard_map.105 = (bf16[3,64,1664]{2,1,0:T(8,128)(2,1)}, bf16[3,64,3456]{2,1,0:T(8,128)(2,1)}, bf16[3,256,64]{2,1,0:T(8,128)(2,1)}) custom-call(s32[3]{0:T(128)} %live_ref.1, f32[3,256,128]{2,1,0:T(8,128)} %copy-done.4, f32[3,256,128]{2,1,0:T(8,128)} %copy-done.9, bf16[768,4096]{1,0:T(8,128)(2,1)} %hid_ref.1, bf16[768,1024]{1,0:T(8,128)(2,1)} %grad_ref.1), custom_call_target="tpu_custom_call" | custom-call | flops 503316480 | bytes 9830400 | tf_op jit(solution)/shard_map/pallas_call | solution.py:186
  175.1 0.5 collective-permute-start.22
  175.6 0.8 collective-permute-start.20
  176.3 0.7 concatenate.25.scalars_ref
  177.0 1.2 collective-permute-done.20.refs_9_
  178.2 1.2 copy-done.3
  179.4 25.4 %shard_map.106 = (bf16[768,4096]{1,0:T(8,128)(2,1)}, f32[8,128]{1,0:T(8,128)}) custom-call(s32[12]{0:T(128)} %concatenate.25.scalars_ref, bf16[768,4096]{1,0:T(8,128)(2,1)} %all-gather.2.cloned.1.call-done.kept_ref, bf16[4096,1024]{1,0:T(8,128)(2,1)} %refs_0_.1, bf16[4096,1024]{1,0:T(8,128)(2,1)} %collective-permute-done.3.refs_1_, ...), custom_call_target="tpu_custom_call" | custom-call | flops 1 | bytes 1 | tf_op jit(solution)/shard_map/pallas_call | solution.py:343
  204.8 0.8 collective-permute-done.22.refs_5_
  205.7 1.3 collective-permute-start.23
  207.0 0.5 collective-permute-start.29
  207.5 0.4 collective-permute-start.27
  207.9 0.3 collective-permute-start.24
  208.2 0.7 concatenate.21.scalars_ref
  208.9 6.0 %collective-permute-done.24.refs_7_ = bf16[256,1024]{1,0:T(8,128)(2,1)} collective-permute-done((bf16[256,1024]{1,0:T(8,128)(2,1)}, bf16[256,1024]{1,0:T(8,128)(2,1)}, u32[]{:S(2)}, u32[]{:S(2)}) %collective-permute-start.24) | collective-permute-done | bytes 524320 | tf_op jit(solution)/shard_map/ppermute | solution.py:486
  214.9 0.4 collective-permute-start.25
  215.3 1.2 copy-done.5
  216.5 17.9 %shard_map.107 = (bf16[768,4096]{1,0:T(8,128)(2,1)}, f32[8,128]{1,0:T(8,128)}) custom-call(s32[10]{0:T(128)} %concatenate.21.scalars_ref, bf16[768,4096]{1,0:T(8,128)(2,1)} %all-gather.2.cloned.1.call-done.kept_ref, bf16[4096,1024]{1,0:T(8,128)(2,1)} %refs_0_.1, bf16[4096,1024]{1,0:T(8,128)(2,1)} %collective-permute-done.3.refs_1_, ...), custom_call_target="tpu_custom_call", output_to_operand_aliasing={{0}: (13, {})} | custom-call | flops 1 | bytes 1 | tf_op jit(solution)/shard_map/pallas_call | solution.py:343
  234.4 0.2 collective-permute-start.28
  234.7 0.7 add_subtract_fusion.slots_ref
  235.4 1.1 collective-permute-done.28.refs_6_
  236.5 0.8 copy-done.8
  237.4 8.2 %shard_map.108 = (f32[8,64,4096]{2,1,0:T(8,128)}, f32[8,64,1024]{2,1,0:T(8,128)}) custom-call(s32[12]{0:T(128)} %add_subtract_fusion.slots_ref, bf16[3,64,1664]{2,1,0:T(8,128)(2,1)} %get-tuple-element.62.refs_0_, bf16[3,64,3456]{2,1,0:T(8,128)(2,1)} %get-tuple-element.63.refs_1_, ...), custom_call_target="tpu_custom_call", output_to_operand_aliasing={{0}: (10, {}), {1}: (11, {})} | custom-call | flops 1 | bytes 1 | tf_op jit(solution)/shard_map/pallas_call | solution.py:438
  (43 shorter events, 0.3 us)
Async XLA Ops:
  7.2 169.9 %all-gather.2.cloned.1.call-start = ((), (), s32[]{:S(2)}) async-start(), calls=%async_computation | async-start | bytes 7864320 | tf_op jit(solution)/shard_map/all_gather | solution.py:501
  7.2 9.4 %collective-permute-start.1 = (bf16[8,64,4096]{2,1,0:T(8,128)(2,1)}, bf16[8,64,4096]{2,1,0:T(8,128)(2,1)}, u32[]{:S(2)}, u32[]{:S(2)}) collective-permute-start(bf16[8,64,4096]{2,1,0:T(8,128)(2,1)} %bitcast.14), channel_id=1, source_target_pairs={{0,1},{1,0},{2,3},{3,2},{4,5},{5,4},{6,7},{7,6},{8,9},{9,8},{10,11... | collective-permute-start | bytes 12582920 | tf_op jit(solution)/shard_map/ppermute | solution.py:486
  8.0 8.4 %collective-permute-start.2 = (bf16[8,64,1024]{2,1,0:T(8,128)(2,1)}, bf16[8,64,1024]{2,1,0:T(8,128)(2,1)S(1)}, u32[]{:S(2)}, u32[]{:S(2)}) collective-permute-start(bf16[8,64,1024]{2,1,0:T(8,128)(2,1)} %refs_2_.3), channel_id=1, source_target_pairs={{0,1},{1,0},{2,3},{3,2},{4,5},{5,4},{6,7},{7,6},{8,9},{9,8},{10,11... | collective-permute-start | bytes 3145736 | tf_op jit(solution)/shard_map/ppermute | solution.py:486
  8.9 2.4 collective-permute-start
  16.3 1.0 copy-start
  22.1 47.4 %collective-permute-start.3 = (bf16[4096,1024]{1,0:T(8,128)(2,1)}, bf16[4096,1024]{1,0:T(8,128)(2,1)}, u32[]{:S(2)}, u32[]{:S(2)}) collective-permute-start(bf16[4096,1024]{1,0:T(8,128)(2,1)} %refs_0_.1), channel_id=1, source_target_pairs={{0,1},{1,0},{2,3},{3,2},{4,5},{5,4},{6,7},{7,6},{8,9},{9,8},{10,11... | collective-permute-start | bytes 25165832 | tf_op jit(solution)/shard_map/ppermute | solution.py:486
  22.2 44.4 %collective-permute-start.4 = (bf16[3,64,5120]{2,1,0:T(8,128)(2,1)}, bf16[3,64,5120]{2,1,0:T(8,128)(2,1)S(1)}, u32[]{:S(2)}, u32[]{:S(2)}) collective-permute-start(bf16[3,64,5120]{2,1,0:T(8,128)(2,1)} %shard_map.103), channel_id=1, source_target_pairs={{0,2},{1,3},{2,0},{3,1},{4,6},{5,7},{6,4},{7,5},{8,10},{9,11},{10,... | collective-permute-start | bytes 5898248 | tf_op jit(solution)/shard_map/ppermute | solution.py:486
  66.7 4.0 %copy-start.1 = (bf16[3,64,5120]{2,1,0:T(8,128)(2,1)}, bf16[3,64,5120]{2,1,0:T(8,128)(2,1)S(1)}, u32[]{:S(2)}) copy-start(bf16[3,64,5120]{2,1,0:T(8,128)(2,1)S(1)} %collective-permute-done.4.refs_4_) | copy-start | bytes 5898244
  66.7 23.7 %collective-permute-start.7 = (bf16[512,1024]{1,0:T(8,128)(2,1)S(1)}, bf16[512,1024]{1,0:T(8,128)(2,1)}, u32[]{:S(2)}, u32[]{:S(2)}) collective-permute-start(bf16[512,1024]{1,0:T(8,128)(2,1)S(1)} %get-tuple-element.42), channel_id=1, source_target_pairs={{0,2},{1,3},{2,0},{3,1},{4,6},{5,7},{6,4},{7,5},{8,10},{9,11},{10,... | collective-permute-start | bytes 3145736 | tf_op jit(solution)/shard_map/ppermute | solution.py:486
  67.0 2.5 collective-permute-start.6
  68.3 44.5 %collective-permute-start.5 = (bf16[512,1024]{1,0:T(8,128)(2,1)}, bf16[512,1024]{1,0:T(8,128)(2,1)}, u32[]{:S(2)}, u32[]{:S(2)}) collective-permute-start(bf16[512,1024]{1,0:T(8,128)(2,1)} %get-tuple-element.38), channel_id=1, source_target_pairs={{0,2},{1,3},{2,0},{3,1},{4,6},{5,7},{6,4},{7,5},{8,10},{9,11},{10,... | collective-permute-start | bytes 3145736 | tf_op jit(solution)/shard_map/ppermute | solution.py:486
  82.0 39.4 %copy-start.10 = (f32[3,256,128]{2,1,0:T(8,128)S(1)}, f32[3,256,128]{2,1,0:T(8,128)}, u32[]{:S(2)}) copy-start(f32[3,256,128]{2,1,0:T(8,128)} %get-tuple-element.41) | copy-start | bytes 1179652
  90.3 22.5 %collective-permute-start.8 = (bf16[512,1024]{1,0:T(8,128)(2,1)}, bf16[512,1024]{1,0:T(8,128)(2,1)}, u32[]{:S(2)}, u32[]{:S(2)}) collective-permute-start(bf16[512,1024]{1,0:T(8,128)(2,1)} %collective-permute-done.7.refs_2_), channel_id=1, source_target_pairs={{0,1},{1,0},{2,3},{3,2},{4,5},{5,4},{6,7},{7,6},{8,9},{9,8},{10,11... | collective-permute-start | bytes 3145736 | tf_op jit(solution)/shard_map/ppermute | solution.py:486
  94.0 25.1 %collective-permute-start.9 = (bf16[512,1024]{1,0:T(8,128)(2,1)}, bf16[512,1024]{1,0:T(8,128)(2,1)}, u32[]{:S(2)}, u32[]{:S(2)}) collective-permute-start(bf16[512,1024]{1,0:T(8,128)(2,1)} %collective-permute-done.7.refs_2_), channel_id=1, source_target_pairs={{0,16},{16,0},{1,17},{17,1},{2,18},{18,2},{3,19},{19,3},{4,20},{20... | collective-permute-start | bytes 3145736 | tf_op jit(solution)/shard_map/ppermute | solution.py:538
  96.7 49.7 %collective-permute-start.13 = (bf16[768,1024]{1,0:T(8,128)(2,1)S(1)}, bf16[768,1024]{1,0:T(8,128)(2,1)S(1)}, u32[]{:S(2)}, u32[]{:S(2)}) collective-permute-start(bf16[768,1024]{1,0:T(8,128)(2,1)S(1)} %constant_dynamic-slice_fusion.2), channel_id=1, source_target_pairs={{0,2},{1,3},{2,0},{3,1},{4,6},{5,7},{6,4},{7,5},{8,10},{9,11},{10,... | collective-permute-start | bytes 4718600 | tf_op jit(solution)/shard_map/ppermute | solution.py:486
  119.1 27.3 %collective-permute-start.10 = (bf16[512,1024]{1,0:T(8,128)(2,1)}, bf16[512,1024]{1,0:T(8,128)(2,1)}, u32[]{:S(2)}, u32[]{:S(2)}) collective-permute-start(bf16[512,1024]{1,0:T(8,128)(2,1)} %collective-permute-done.5.refs_4_), channel_id=1, source_target_pairs={{0,16},{16,0},{1,17},{17,1},{2,18},{18,2},{3,19},{19,3},{4,20},{20... | collective-permute-start | bytes 3145736 | tf_op jit(solution)/shard_map/ppermute | solution.py:538
  120.3 26.1 %collective-permute-start.12 = (bf16[512,1024]{1,0:T(8,128)(2,1)}, bf16[512,1024]{1,0:T(8,128)(2,1)}, u32[]{:S(2)}, u32[]{:S(2)}) collective-permute-start(bf16[512,1024]{1,0:T(8,128)(2,1)} %collective-permute-done.5.refs_4_), channel_id=1, source_target_pairs={{0,1},{1,0},{2,3},{3,2},{4,5},{5,4},{6,7},{7,6},{8,9},{9,8},{10,11... | collective-permute-start | bytes 3145736 | tf_op jit(solution)/shard_map/ppermute | solution.py:486
  121.3 25.1 %collective-permute-start.14 = (bf16[512,1024]{1,0:T(8,128)(2,1)}, bf16[512,1024]{1,0:T(8,128)(2,1)}, u32[]{:S(2)}, u32[]{:S(2)}) collective-permute-start(bf16[512,1024]{1,0:T(8,128)(2,1)} %collective-permute-done.9.refs_10_), channel_id=1, source_target_pairs={{0,1},{1,0},{2,3},{3,2},{4,5},{5,4},{6,7},{7,6},{8,9},{9,8},{10,11... | collective-permute-start | bytes 3145736 | tf_op jit(solution)/shard_map/ppermute | solution.py:486
  121.3 20.8 %collective-permute-start.11 = (f32[3,256,128]{2,1,0:T(8,128)S(1)}, f32[3,256,128]{2,1,0:T(8,128)}, u32[]{:S(2)}, u32[]{:S(2)}) collective-permute-start(f32[3,256,128]{2,1,0:T(8,128)S(1)} %copy-done.10), channel_id=1, source_target_pairs={{0,4},{4,0},{8,12},{12,8},{1,5},{5,1},{9,13},{13,9},{2,6},{6,2},{1... | collective-permute-start | bytes 1179656 | tf_op jit(solution)/shard_map/ppermute | solution.py:486
  143.2 24.2 %copy-start.4 = (f32[3,256,128]{2,1,0:T(8,128)}, f32[3,256,128]{2,1,0:T(8,128)S(1)}, u32[]{:S(2)}) copy-start(f32[3,256,128]{2,1,0:T(8,128)S(1)} %add.97.here_ref) | copy-start | bytes 1179652
  146.4 28.7 %copy-start.2 = (bf16[768,1024]{1,0:T(8,128)(2,1)}, bf16[768,1024]{1,0:T(8,128)(2,1)S(1)}, u32[]{:S(2)}) copy-start(bf16[768,1024]{1,0:T(8,128)(2,1)S(1)} %collective-permute-done.13.refs_6_) | copy-start | bytes 4718596
  146.4 28.7 %collective-permute-start.18 = (bf16[256,1024]{1,0:T(8,128)(2,1)}, bf16[256,1024]{1,0:T(8,128)(2,1)}, u32[]{:S(2)}, u32[]{:S(2)}) collective-permute-start(bf16[256,1024]{1,0:T(8,128)(2,1)} %get-tuple-element.49), channel_id=1, source_target_pairs={{0,2},{1,3},{2,0},{3,1},{4,6},{5,7},{6,4},{7,5},{8,10},{9,11},{10,... | collective-permute-start | bytes 1572872 | tf_op jit(solution)/shard_map/ppermute | solution.py:486
  146.9 29.4 %copy-start.11 = (s32[3]{0:T(128)S(1)}, s32[3]{0:T(128)}, u32[]{:S(2)}) copy-start(s32[3]{0:T(128)} %live_ref.1) | copy-start | bytes 40
  146.9 28.2 %collective-permute-start.21 = (bf16[256,1024]{1,0:T(8,128)(2,1)}, bf16[256,1024]{1,0:T(8,128)(2,1)}, u32[]{:S(2)}, u32[]{:S(2)}) collective-permute-start(bf16[256,1024]{1,0:T(8,128)(2,1)} %get-tuple-element.55), channel_id=1, source_target_pairs={{0,2},{1,3},{2,0},{3,1},{4,6},{5,7},{6,4},{7,5},{8,10},{9,11},{10,... | collective-permute-start | bytes 1572872 | tf_op jit(solution)/shard_map/ppermute | solution.py:486
  147.9 19.5 %collective-permute-start.19 = (f32[3,256,128]{2,1,0:T(8,128)S(1)}, f32[3,256,128]{2,1,0:T(8,128)S(1)}, u32[]{:S(2)}, u32[]{:S(2)}) collective-permute-start(f32[3,256,128]{2,1,0:T(8,128)S(1)} %add.97.here_ref), channel_id=1, source_target_pairs={{0,8},{4,12},{8,0},{12,4},{1,9},{5,13},{9,1},{13,5},{2,10},{6,14},... | collective-permute-start | bytes 1179656 | tf_op jit(solution)/shard_map/ppermute | solution.py:486
  150.3 28.0 %collective-permute-start.17 = (bf16[768,1024]{1,0:T(8,128)(2,1)S(1)}, bf16[768,1024]{1,0:T(8,128)(2,1)S(1)}, u32[]{:S(2)}, u32[]{:S(2)}) collective-permute-start(bf16[768,1024]{1,0:T(8,128)(2,1)S(1)} %collective-permute-done.13.refs_6_), channel_id=1, source_target_pairs={{0,1},{1,0},{2,3},{3,2},{4,5},{5,4},{6,7},{7,6},{8,9},{9,8},{10,11... | collective-permute-start | bytes 4718600 | tf_op jit(solution)/shard_map/ppermute | solution.py:486
  153.1 51.7 %collective-permute-start.16 = (bf16[768,1024]{1,0:T(8,128)(2,1)S(1)}, bf16[768,1024]{1,0:T(8,128)(2,1)}, u32[]{:S(2)}, u32[]{:S(2)}) collective-permute-start(bf16[768,1024]{1,0:T(8,128)(2,1)S(1)} %collective-permute-done.13.refs_6_), channel_id=1, source_target_pairs={{0,16},{16,0},{1,17},{17,1},{2,18},{18,2},{3,19},{19,3},{4,20},{20... | collective-permute-start | bytes 4718600 | tf_op jit(solution)/shard_map/ppermute | solution.py:538
  167.4 0.7 copy-start.9
  175.1 30.6 %collective-permute-start.22 = (bf16[3,64,3456]{2,1,0:T(8,128)(2,1)}, bf16[3,64,3456]{2,1,0:T(8,128)(2,1)}, u32[]{:S(2)}, u32[]{:S(2)}) collective-permute-start(bf16[3,64,3456]{2,1,0:T(8,128)(2,1)} %get-tuple-element.63.refs_1_), channel_id=1, source_target_pairs={{0,2},{1,3},{2,0},{3,1},{4,6},{5,7},{6,4},{7,5},{8,10},{9,11},{10,... | collective-permute-start | bytes 3981320 | tf_op jit(solution)/shard_map/ppermute | solution.py:486
  175.6 2.6 %collective-permute-start.20 = (bf16[256,1024]{1,0:T(8,128)(2,1)}, bf16[256,1024]{1,0:T(8,128)(2,1)}, u32[]{:S(2)}, u32[]{:S(2)}) collective-permute-start(bf16[256,1024]{1,0:T(8,128)(2,1)} %collective-permute-done.18.refs_8_), channel_id=1, source_target_pairs={{0,1},{1,0},{2,3},{3,2},{4,5},{5,4},{6,7},{7,6},{8,9},{9,8},{10,11... | collective-permute-start | bytes 1572872 | tf_op jit(solution)/shard_map/ppermute | solution.py:486
  177.0 30.9 %collective-permute-start.15 = (bf16[512,1024]{1,0:T(8,128)(2,1)}, bf16[512,1024]{1,0:T(8,128)(2,1)}, u32[]{:S(2)}, u32[]{:S(2)}) collective-permute-start(bf16[512,1024]{1,0:T(8,128)(2,1)} %collective-permute-done.10.refs_2_), channel_id=1, source_target_pairs={{0,1},{1,0},{2,3},{3,2},{4,5},{5,4},{6,7},{7,6},{8,9},{9,8},{10,11... | collective-permute-start | bytes 3145736 | tf_op jit(solution)/shard_map/ppermute | solution.py:486
  178.2 1.2 copy-start.3
  205.7 9.6 %collective-permute-start.23 = (bf16[768,1024]{1,0:T(8,128)(2,1)}, bf16[768,1024]{1,0:T(8,128)(2,1)S(1)}, u32[]{:S(2)}, u32[]{:S(2)}) collective-permute-start(bf16[768,1024]{1,0:T(8,128)(2,1)} %collective-permute-done.16.refs_4_), channel_id=1, source_target_pairs={{0,1},{1,0},{2,3},{3,2},{4,5},{5,4},{6,7},{7,6},{8,9},{9,8},{10,11... | collective-permute-start | bytes 4718600 | tf_op jit(solution)/shard_map/ppermute | solution.py:486
  207.0 28.4 %collective-permute-start.26 = (bf16[3,64,3456]{2,1,0:T(8,128)(2,1)}, bf16[3,64,3456]{2,1,0:T(8,128)(2,1)S(1)}, u32[]{:S(2)}, u32[]{:S(2)}) collective-permute-start(bf16[3,64,3456]{2,1,0:T(8,128)(2,1)} %get-tuple-element.63.refs_1_), channel_id=1, source_target_pairs={{0,1},{1,0},{2,3},{3,2},{4,5},{5,4},{6,7},{7,6},{8,9},{9,8},{10,11... | collective-permute-start | bytes 3981320 | tf_op jit(solution)/shard_map/ppermute | solution.py:486
  207.0 28.4 %collective-permute-start.29 = (bf16[3,64,3456]{2,1,0:T(8,128)(2,1)}, bf16[3,64,3456]{2,1,0:T(8,128)(2,1)}, u32[]{:S(2)}, u32[]{:S(2)}) collective-permute-start(bf16[3,64,3456]{2,1,0:T(8,128)(2,1)} %collective-permute-done.22.refs_5_), channel_id=1, source_target_pairs={{0,1},{1,0},{2,3},{3,2},{4,5},{5,4},{6,7},{7,6},{8,9},{9,8},{10,11... | collective-permute-start | bytes 3981320 | tf_op jit(solution)/shard_map/ppermute | solution.py:486
  207.5 26.9 %collective-permute-start.27 = (bf16[3,64,1664]{2,1,0:T(8,128)(2,1)}, bf16[3,64,1664]{2,1,0:T(8,128)(2,1)S(1)}, u32[]{:S(2)}, u32[]{:S(2)}) collective-permute-start(bf16[3,64,1664]{2,1,0:T(8,128)(2,1)} %get-tuple-element.62.refs_0_), channel_id=1, source_target_pairs={{0,2},{1,3},{2,0},{3,1},{4,6},{5,7},{6,4},{7,5},{8,10},{9,11},{10,... | collective-permute-start | bytes 1916936 | tf_op jit(solution)/shard_map/ppermute | solution.py:486
  207.9 7.0 %collective-permute-start.24 = (bf16[256,1024]{1,0:T(8,128)(2,1)}, bf16[256,1024]{1,0:T(8,128)(2,1)}, u32[]{:S(2)}, u32[]{:S(2)}) collective-permute-start(bf16[256,1024]{1,0:T(8,128)(2,1)} %collective-permute-done.21.refs_6_), channel_id=1, source_target_pairs={{0,1},{1,0},{2,3},{3,2},{4,5},{5,4},{6,7},{7,6},{8,9},{9,8},{10,11... | collective-permute-start | bytes 1572872 | tf_op jit(solution)/shard_map/ppermute | solution.py:486
  214.9 20.5 %collective-permute-start.25 = (bf16[3,64,1664]{2,1,0:T(8,128)(2,1)}, bf16[3,64,1664]{2,1,0:T(8,128)(2,1)}, u32[]{:S(2)}, u32[]{:S(2)}) collective-permute-start(bf16[3,64,1664]{2,1,0:T(8,128)(2,1)} %get-tuple-element.62.refs_0_), channel_id=1, source_target_pairs={{0,1},{1,0},{2,3},{3,2},{4,5},{5,4},{6,7},{7,6},{8,9},{9,8},{10,11... | collective-permute-start | bytes 1916936 | tf_op jit(solution)/shard_map/ppermute | solution.py:486
  215.3 1.2 copy-start.5
  234.4 2.2 copy-start.7
  234.4 2.1 collective-permute-start.28
  235.4 1.1 copy-start.6
  236.5 0.8 copy-start.8
Sparse Core Ops, SparseCore 0:
  22.4 121.5 all-gather.1

commit v6 on v3

--- a/solution.py
+++ b/solution.py
@@ -209,8 +209,9 @@
     )(live, here, there, hidden, grad)
 
 
-def base_kernel(n_dp, tiles, n_chunks, n_kept, count, scalars_ref, *refs):
+def base_kernel(n_dp, tiles, n_chunks, kept_rows, count, scalars_ref, *refs):
     near = n_dp // 2
+    n_kept = len(kept_rows)
     kept_refs, refs = refs[:n_kept], refs[n_kept:]
     near_refs = refs[:near]
     far_refs = refs[near : near + n_chunks * near]
@@ -258,7 +259,8 @@
     def columns(k):
         wide = kept_refs[k].shape[1]
         place = pl.ds(pl.multiple_of(at[k] * wide, wide), wide)
-        return pltpu.make_async_copy(kept_refs[k], kept.at[:, place], kept_sem.at[k])
+        rows = pl.ds(kept_rows[k], kept_refs[k].shape[0])
+        return pltpu.make_async_copy(kept_refs[k], kept.at[rows, place], kept_sem.at[k])
 
     def store(j, slot):
         return pltpu.make_async_copy(result.at[slot], out_ref.at[:, span(j)], out_sem.at[slot])
@@ -335,12 +337,12 @@
 
 
 def base(places, scalars, kept, near, chunks, tiles, tile, coef, block_a, held, token):
-    rows = kept[0].shape[0]
+    rows = kept[0][0].shape[0]
     count, rank, ff = block_a.shape
     top = len(near)
     depth = 2 * top * near[0].shape[1]
     anywhere = pl.BlockSpec(memory_space=pl.ANY)
-    operands = [*kept, *[near[r] for r in range(top)]]
+    operands = [piece for piece, _ in kept] + [near[r] for r in range(top)]
     for piece in chunks:
         operands += [piece[r] for r in range(top, 2 * top)]
     in_specs = [anywhere] * len(operands)
@@ -354,7 +356,9 @@
     most = max(len(segments) for segments in tiles)
     span = tile * len(tiles)
     return pl.pallas_call(
-        functools.partial(base_kernel, 2 * top, tiles, len(chunks), len(kept), count),
+        functools.partial(
+            base_kernel, 2 * top, tiles, len(chunks), [low for _, low in kept], count
+        ),
         grid_spec=pltpu.PrefetchScalarGridSpec(
             num_scalar_prefetch=1,
             grid=(1,),
@@ -513,21 +517,30 @@
 
     place = lax.axis_index("fsdp")
     line = n_fsdp <= 4
-    pieces_of_kept, at = [output_gradient], [place]
-
-    def hop(*after):
-        k = len(pieces_of_kept) // 2
-        if not line or k + 1 >= n_fsdp:
+    height = rows // count
+    pieces_of_kept, at = [(output_gradient, 0)], [None]
+
+    def hop(*after, low=0, high=None):
+        step = len(at) // 2
+        if not line or step + 1 >= n_fsdp:
             return []
+        if low == 0:
+            ends[:] = next_ends or [output_gradient] * 2
+            next_ends.clear()
         right = [(i, i + 1) for i in range(n_fsdp - 1)]
         left = [(i + 1, i) for i in range(n_fsdp - 1)]
-        ends = pieces_of_kept[-2:] if k else pieces_of_kept * 2
-        for piece, pairs in zip(ends, (right, left)):
-            pieces_of_kept.append(lax.ppermute(behind(piece, *after), "fsdp", pairs))
-        at.append(place - k - 1)
-        at.append(jnp.where(place + k + 1 < n_fsdp, place + k + 1, -1))
-        return pieces_of_kept[-2:]
-
+        sent = []
+        for piece, pairs, place_of in zip(ends, (right, left), (place - step - 1, place + step + 1)):
+            piece = behind(piece[low:high], *after)
+            sent.append(lax.ppermute(piece, "fsdp", pairs))
+            pieces_of_kept.append((sent[-1], low))
+            where.append(jnp.where(place_of < n_fsdp, place_of, -1))
+        if high is None:
+            at.extend([None, None])
+            next_ends.extend(sent)
+        return sent
+
+    ends, next_ends, where = [], [], [place]
     first_hop = hop()
 
     share = ff // n_groups
@@ -594,6 +607,7 @@
     )
     cross(*past)
     cross(*past)
+    third = hop(*past, high=height)
     sums = [part]
     bit = 1
     while bit < n_fsdp:
@@ -602,29 +616,26 @@
             sums.append(sums[-2] + sums[-1])
         bit *= 2
     total, other = sums[-2:]
-    past = [sums[2], *flat(*crossed[1:2])]
+    past = [sums[2], *third, *flat(*crossed[1:2])]
     turn(*past)
     fill(crossed[:1], *past)
     fill(turned[0], *past)
     past = [other, *flat(*crossed, *sum(turned, []))]
-    third_hop = hop(*past)
+    third = hop(*past, low=height)
     cross(*past)
     turn(*past)
     low_terms, high_terms, coef = block_terms(
         island_live_rows, total, other, hidden, output_gradient
     )
-    far_low = swap(behind(low_terms, *flat(*crossed)), top)
-    past = flat(*crossed[3:])
+    past = [coef, *third, *flat(*crossed[3:], *sum(turned[2:], []))]
+    far_high = swap(behind(high_terms, *past), top)
+    far_low = swap(behind(low_terms, *past), top)
+    turn(*past)
     fill(crossed[1:], *past)
-    for pieces in turned[1:3]:
-        fill(pieces, *past)
-    past = [far_low, *third_hop, *flat(*crossed, *sum(turned, []))]
-    far_high = swap(behind(high_terms, *past), top)
-    turn(*past)
     if line:
-        at = jnp.stack(at).astype(i32)
+        at = jnp.stack(where).astype(i32)
     else:
-        pieces_of_kept = [lax.all_gather(output_gradient, "fsdp", axis=1, tiled=True)]
+        pieces_of_kept = [(lax.all_gather(output_gradient, "fsdp", axis=1, tiled=True), 0)]
         at = jnp.zeros((1,), i32)
 
     relative = [both_slots[r][:count] for r in near] + [both_slots[r][count:] for r in near]
@@ -656,18 +667,18 @@
 
     others = range(1, n_groups)
     if share > tile:
-        multiply(*[(0, t) for t in range(4)], *[(g, t) for g in others for t in range(3)])
+        multiply(*[(0, t) for t in range(4)], *[(g, 0) for g in others])
         past = [token, far_high]
-        for pieces in turned[3:]:
+        for pieces in turned[1:]:
             fill(pieces, *past)
-        multiply(*[(g, 3) for g in others])
+        multiply(*[(g, t) for g in others for t in range(1, 4)])
     else:
         multiply(*[(g, 0) for g in range(n_groups)])
 
     near_low = spread({0: behind(low_terms, *past)})
     near_high = spread({0: behind(high_terms, *past)})
+    all_high = spread({top: behind(far_high, *past)})
     all_low = spread({top: behind(far_low, token)})
-    all_high = spread({top: behind(far_high, token)})
     terms = [p for r in near for p in (near_low[r], near_high[r])]
     terms += [p for r in near for p in (all_low[r + top], all_high[r + top])]
     grad_a, grad_b = add_terms(relative, terms, grad_a, grad_b, token)

time: 256 us -> 250 us (0.977)
  waiting for transfers between devices: 117 us -> 109 us
    ppermute x26, waiting for transfers between devices: 66.7 us -> 53 us  [swap(): return lax.ppermute(value, axis, [(i, i ^ bit) for i in range(size)])]
    ppermute x6 -> x8, waiting for transfers between devices: 20.5 us -> 28.6 us  [hop(): sent.append(lax.ppermute(piece, 'fsdp', pairs))]
    ppermute x6 -> x8, starting transfers between devices: 16.3 us -> 22.6 us  [hop(): sent.append(lax.ppermute(piece, 'fsdp', pairs))]
    ppermute x26, starting transfers between devices: 24.6 us -> 18.8 us  [swap(): return lax.ppermute(value, axis, [(i, i ^ bit) for i in range(size)])]
    slice x0 -> x4, local copies, waits for them, and re-layouts: none -> 3.76 us  [hop(): piece = behind(piece[low:high], *after)]
  transfers between devices with their start and end apart: 36 -> 38, of which waited for: 20 -> 22; matrix products, arithmetic and copies ran while one was open for 4% -> 6% of each run, Pallas kernels for 27% -> 28%
where the time goes in v6:
time: 250 us; the launch traced here: 247 us
  waiting for transfers between devices  109 us (44%)
  Pallas kernels  75.5 us (30%)
  starting transfers between devices  44.7 us (18%)
  local copies, waits for them, and re-layouts  11.6 us (5%)
  other arithmetic  4.97 us (2%)
    ppermute x26, waiting for transfers between devices, swap(): return lax.ppermute(value, axis, [(i, i ^ bit) for i in range(size)])  53 us
    pallas_call x2, Pallas kernels, base(): pl.pallas_call(functools.partial(base_kernel, 2 * top, tiles, len(chunks)...  45.2 us
    ppermute x8, waiting for transfers between devices, hop(): sent.append(lax.ppermute(piece, 'fsdp', pairs))  28.6 us
    ppermute x4, waiting for transfers between devices, turn(): turned[j].append({top: lax.ppermute(piece, 'groups', ring)})  27.8 us
    ppermute x8, starting transfers between devices, hop(): sent.append(lax.ppermute(piece, 'fsdp', pairs))  22.6 us
    ppermute x26, starting transfers between devices, swap(): return lax.ppermute(value, axis, [(i, i ^ bit) for i in range(size)])  18.8 us
    pallas_call x1, Pallas kernels, project(): pl.pallas_call(functools.partial(project_kernel, pieces), grid_spec=pltpu...  11.7 us
    pallas_call x1, Pallas kernels, block_terms(): pl.pallas_call(terms_kernel, grid_spec=pltpu.PrefetchScalarGridSpec(num_s...  6.93 us
  transfers between devices with their start and end apart: 38, of which 22 were waited for; matrix products, arithmetic and copies ran while one was open for 6% of the time, Pallas kernels for 28%

profile of v6, /device:TPU:11, one launch (start us, length us, event | category | flops | bytes accessed | tf_op | source)
XLA Modules:
  0.0 247.2 jit_solution(13592708891788774206)
XLA Ops:
  0.6 0.7 collective-permute-start.3
  1.4 3.2 %collective-permute-start = (bf16[768,1024]{1,0:T(8,128)(2,1)}, bf16[768,1024]{1,0:T(8,128)(2,1)}, u32[]{:S(2)}, u32[]{:S(2)}) collective-permute-start(bf16[768,1024]{1,0:T(8,128)(2,1)} %refs_0_.3), channel_id=1, source_target_pairs={{0,4},{4,8},{8,12},{1,5},{5,9},{9,13},{2,6},{6,10},{10,14},{3,7},{... | collective-permute-start | bytes 4718600 | tf_op jit(solution)/shard_map/ppermute | solution.py:535
  4.6 3.3 %collective-permute-start.1 = (bf16[768,1024]{1,0:T(8,128)(2,1)}, bf16[768,1024]{1,0:T(8,128)(2,1)S(1)}, u32[]{:S(2)}, u32[]{:S(2)}) collective-permute-start(bf16[768,1024]{1,0:T(8,128)(2,1)} %refs_0_.3), channel_id=1, source_target_pairs={{4,0},{8,4},{12,8},{5,1},{9,5},{13,9},{6,2},{10,6},{14,10},{7,3},{... | collective-permute-start | bytes 4718600 | tf_op jit(solution)/shard_map/ppermute | solution.py:535
  7.8 0.9 select_reduce_fusion
  9.0 0.9 collective-permute-start.4
  9.9 4.3 %constant_dynamic-slice_fusion = (bf16[512,1024]{1,0:T(8,128)(2,1)}, bf16[512,1024]{1,0:T(8,128)(2,1)}, bf16[512,1024]{1,0:T(8,128)(2,1)}, bf16[512,1024]{1,0:T(8,128)(2,1)}) fusion(bf16[4096,1024]{1,0:T(8,128)(2,1)} %refs_9_.1, s32[]{:T(128)S(6)} %select_n.94, s32[]{:T(128)S(6)} %select_n.91, s32[]{:T(128)S(6)} %select_n.87, s32[]{:T(128)S(6)} %select_n.92), kind=kLoop, calls=%fused_computation.13 | loop fusion | bytes 8388624 | tf_op jit(solution)/shard_map/dynamic_slice | solution.py:565
  14.2 1.2 collective-permute-start.6
  15.4 0.5 compare_select_fusion.1
  15.9 0.6 pad_add_fusion.index_ref
  16.6 1.0 copy-done.3
  17.5 4.8 %shard_map.103 = bf16[3,64,5120]{2,1,0:T(8,128)(2,1)} custom-call(s32[6]{0:T(128)} %pad_add_fusion.index_ref, s32[3]{0:T(128)} %get-tuple-element.101.source_ref, bf16[8,64,4096]{2,1,0:T(8,128)(2,1)} %bitcast.22, bf16[8,64,4096]{2,1,0:T(8,128)(2,1)} %collective-permute-done.3.refs_1_, bf16[8,64,1024]{2,1,0:T(8,128)(2,1)} %refs_2_.3, ...), custom_call_target="tpu_custom_call" | custom-call | bytes 5898240 | tf_op jit(solution)/shard_map/pallas_call | solution.py:54
  22.6 16.7 %collective-permute-done.6.refs_11_ = bf16[512,1024]{1,0:T(8,128)(2,1)} collective-permute-done((bf16[512,1024]{1,0:T(8,128)(2,1)}, bf16[512,1024]{1,0:T(8,128)(2,1)}, u32[]{:S(2)}, u32[]{:S(2)}) %collective-permute-start.6) | collective-permute-done | bytes 1048608 | tf_op jit(solution)/shard_map/ppermute | solution.py:503
  39.6 2.8 %collective-permute-done.1.refs_2_ = bf16[768,1024]{1,0:T(8,128)(2,1)S(1)} collective-permute-done((bf16[768,1024]{1,0:T(8,128)(2,1)}, bf16[768,1024]{1,0:T(8,128)(2,1)S(1)}, u32[]{:S(2)}, u32[]{:S(2)}) %collective-permute-start.1) | collective-permute-done | bytes 1572896 | tf_op jit(solution)/shard_map/ppermute | solution.py:535
  42.4 1.1 collective-permute-start.13
  43.8 3.2 %collective-permute-start.7 = (bf16[768,1024]{1,0:T(8,128)(2,1)}, bf16[768,1024]{1,0:T(8,128)(2,1)S(1)}, u32[]{:S(2)}, u32[]{:S(2)}) collective-permute-start(bf16[768,1024]{1,0:T(8,128)(2,1)} %collective-permute-done.refs_1_), channel_id=1, source_target_pairs={{0,4},{4,8},{8,12},{1,5},{5,9},{9,13},{2,6},{6,10},{10,14},{3,7},{... | collective-permute-start | bytes 4718600 | tf_op jit(solution)/shard_map/ppermute | solution.py:535
  47.0 2.2 collective-permute-start.8
  49.1 1.3 collective-permute-start.10
  50.4 21.8 %collective-permute-done.10.refs_19_ = bf16[512,1024]{1,0:T(8,128)(2,1)S(1)} collective-permute-done((bf16[512,1024]{1,0:T(8,128)(2,1)}, bf16[512,1024]{1,0:T(8,128)(2,1)S(1)}, u32[]{:S(2)}, u32[]{:S(2)}) %collective-permute-start.10) | collective-permute-done | bytes 1048608 | tf_op jit(solution)/shard_map/ppermute | solution.py:577
  72.2 8.2 %collective-permute-done.7.refs_3_ = bf16[768,1024]{1,0:T(8,128)(2,1)S(1)} collective-permute-done((bf16[768,1024]{1,0:T(8,128)(2,1)}, bf16[768,1024]{1,0:T(8,128)(2,1)S(1)}, u32[]{:S(2)}, u32[]{:S(2)}) %collective-permute-start.7) | collective-permute-done | bytes 1572896 | tf_op jit(solution)/shard_map/ppermute | solution.py:535
  80.4 2.9 %collective-permute-done.8.refs_4_ = bf16[768,1024]{1,0:T(8,128)(2,1)S(1)} collective-permute-done((bf16[768,1024]{1,0:T(8,128)(2,1)}, bf16[768,1024]{1,0:T(8,128)(2,1)S(1)}, u32[]{:S(2)}, u32[]{:S(2)}) %collective-permute-start.8) | collective-permute-done | bytes 1572896 | tf_op jit(solution)/shard_map/ppermute | solution.py:535
  83.4 3.6 %collective-permute-done.9.refs_4_ = bf16[3,64,5120]{2,1,0:T(8,128)(2,1)} collective-permute-done((bf16[3,64,5120]{2,1,0:T(8,128)(2,1)}, bf16[3,64,5120]{2,1,0:T(8,128)(2,1)}, u32[]{:S(2)}, u32[]{:S(2)}) %collective-permute-start.9) | collective-permute-done | bytes 1966112 | tf_op jit(solution)/shard_map/ppermute | solution.py:503
  87.3 0.9 slice.32
  88.1 0.8 slice.33
  88.9 3.2 %collective-permute-start.11 = (bf16[256,1024]{1,0:T(8,128)(2,1)}, bf16[256,1024]{1,0:T(8,128)(2,1)S(1)}, u32[]{:S(2)}, u32[]{:S(2)}) collective-permute-start(bf16[256,1024]{1,0:T(8,128)(2,1)} %slice.32), channel_id=1, source_target_pairs={{0,4},{4,8},{8,12},{1,5},{5,9},{9,13},{2,6},{6,10},{10,14},{3,7},{... | collective-permute-start | bytes 1572872 | tf_op jit(solution)/shard_map/ppermute | solution.py:535
  92.1 2.1 collective-permute-start.12
  94.3 0.6 compare_select_fusion
  94.8 0.7 pad_add_fusion.2.index_ref
  95.5 11.7 %shard_map.104 = (f32[3,256,128]{2,1,0:T(8,128)}, bf16[3,64,4096]{2,1,0:T(8,128)(2,1)}, f32[8,64,4096]{2,1,0:T(8,128)}, f32[8,64,1024]{2,1,0:T(8,128)}) custom-call(s32[6]{0:T(128)} %pad_add_fusion.2.index_ref, s32[3]{0:T(128)} %get-tuple-element.99.source_ref, bf16[8,64,4096]{2,1,0:T(8,128)(2,1)} %bitcast.23, ...), custom_call_target="tpu_custom_call" | custom-call | flops 503316480 | bytes 15728640 | tf_op jit(solution)/shard_map/pallas_call | solution.py:121
  107.3 1.3 collective-permute-start.18
  108.5 6.7 %collective-permute-done.14 = f32[3,256,128]{2,1,0:T(8,128)S(1)} collective-permute-done((f32[3,256,128]{2,1,0:T(8,128)}, f32[3,256,128]{2,1,0:T(8,128)S(1)}, u32[]{:S(2)}, u32[]{:S(2)}) %collective-permute-start.14) | collective-permute-done | bytes 393248 | tf_op jit(solution)/shard_map/ppermute | solution.py:503
  115.3 1.0 add.109.here_ref
  116.4 3.8 %collective-permute-start.17 = (bf16[512,1024]{1,0:T(8,128)(2,1)}, bf16[512,1024]{1,0:T(8,128)(2,1)S(1)}, u32[]{:S(2)}, u32[]{:S(2)}) collective-permute-start(bf16[512,1024]{1,0:T(8,128)(2,1)} %collective-permute-done.6.refs_11_), channel_id=1, source_target_pairs={{0,1},{1,0},{2,3},{3,2},{4,5},{5,4},{6,7},{7,6},{8,9},{9,8},{10,11... | collective-permute-start | bytes 3145736 | tf_op jit(solution)/shard_map/ppermute | solution.py:503
  120.2 0.8 collective-permute-start.20
  121.0 1.8 collective-permute-start.15
  122.8 1.0 slice.34
  123.8 1.0 slice.35
  124.9 8.0 %collective-permute-done.18.refs_15_ = bf16[512,1024]{1,0:T(8,128)(2,1)} collective-permute-done((bf16[512,1024]{1,0:T(8,128)(2,1)}, bf16[512,1024]{1,0:T(8,128)(2,1)}, u32[]{:S(2)}, u32[]{:S(2)}) %collective-permute-start.18) | collective-permute-done | bytes 1048608 | tf_op jit(solution)/shard_map/ppermute | solution.py:503
  132.9 6.7 %collective-permute-done.15.there_ref = f32[3,256,128]{2,1,0:T(8,128)S(1)} collective-permute-done((f32[3,256,128]{2,1,0:T(8,128)S(1)}, f32[3,256,128]{2,1,0:T(8,128)S(1)}, u32[]{:S(2)}, u32[]{:S(2)}) %collective-permute-start.15) | collective-permute-done | bytes 393248 | tf_op jit(solution)/shard_map/ppermute | solution.py:503
  139.7 5.1 %collective-permute-done.20.refs_11_ = bf16[512,1024]{1,0:T(8,128)(2,1)S(1)} collective-permute-done((bf16[512,1024]{1,0:T(8,128)(2,1)}, bf16[512,1024]{1,0:T(8,128)(2,1)S(1)}, u32[]{:S(2)}, u32[]{:S(2)}) %collective-permute-start.20) | collective-permute-done | bytes 1048608 | tf_op jit(solution)/shard_map/ppermute | solution.py:577
  144.8 1.0 copy-done.10
  145.8 3.2 %collective-permute-start.21 = (bf16[512,1024]{1,0:T(8,128)(2,1)}, bf16[512,1024]{1,0:T(8,128)(2,1)S(1)}, u32[]{:S(2)}, u32[]{:S(2)}) collective-permute-start(bf16[512,1024]{1,0:T(8,128)(2,1)} %slice.34), channel_id=1, source_target_pairs={{0,4},{4,8},{8,12},{1,5},{5,9},{9,13},{2,6},{6,10},{10,14},{3,7},{... | collective-permute-start | bytes 3145736 | tf_op jit(solution)/shard_map/ppermute | solution.py:535
  148.9 2.3 collective-permute-start.22
  151.3 1.3 collective-permute-start.23
  152.6 0.4 collective-permute-start.24
  153.0 6.9 %shard_map.105 = (bf16[3,64,1664]{2,1,0:T(8,128)(2,1)}, bf16[3,64,3456]{2,1,0:T(8,128)(2,1)}, bf16[3,256,64]{2,1,0:T(8,128)(2,1)}) custom-call(s32[3]{0:T(128)} %live_ref.1, f32[3,256,128]{2,1,0:T(8,128)} %copy-done.7, f32[3,256,128]{2,1,0:T(8,128)} %copy-done.16, bf16[768,4096]{1,0:T(8,128)(2,1)} %hid_ref.1, bf16[768,1024]{1,0:T(8,128)(2,1)} %refs_0_.3), custom_call_target="tpu_custom_call" | custom-call | flops 503316480 | bytes 9830400 | tf_op jit(solution)/shard_map/pallas_call | solution.py:186
  159.9 11.4 %collective-permute-done.21.refs_7_ = bf16[512,1024]{1,0:T(8,128)(2,1)S(1)} collective-permute-done((bf16[512,1024]{1,0:T(8,128)(2,1)}, bf16[512,1024]{1,0:T(8,128)(2,1)S(1)}, u32[]{:S(2)}, u32[]{:S(2)}) %collective-permute-start.21) | collective-permute-done | bytes 1048608 | tf_op jit(solution)/shard_map/ppermute | solution.py:535
  171.4 2.9 %collective-permute-done.22.refs_8_ = bf16[512,1024]{1,0:T(8,128)(2,1)S(1)} collective-permute-done((bf16[512,1024]{1,0:T(8,128)(2,1)}, bf16[512,1024]{1,0:T(8,128)(2,1)S(1)}, u32[]{:S(2)}, u32[]{:S(2)}) %collective-permute-start.22) | collective-permute-done | bytes 1048608 | tf_op jit(solution)/shard_map/ppermute | solution.py:535
  174.5 0.9 collective-permute-done.24.refs_13_
  175.7 3.2 %collective-permute-start.25 = (bf16[512,1024]{1,0:T(8,128)(2,1)}, bf16[512,1024]{1,0:T(8,128)(2,1)}, u32[]{:S(2)}, u32[]{:S(2)}) collective-permute-start(bf16[512,1024]{1,0:T(8,128)(2,1)} %collective-permute-done.16.refs_13_), channel_id=1, source_target_pairs={{0,1},{1,0},{2,3},{3,2},{4,5},{5,4},{6,7},{7,6},{8,9},{9,8},{10,11... | collective-permute-start | bytes 3145736 | tf_op jit(solution)/shard_map/ppermute | solution.py:503
  178.9 0.5 collective-permute-start.27
  179.4 0.8 collective-permute-start.31
  180.2 0.6 concatenate.25.scalars_ref
  180.9 0.7 collective-permute-done.25.refs_14_
  181.6 1.5 collective-permute-done.26.refs_16_
  183.1 1.5 collective-permute-done.27.refs_18_
  184.6 26.3 %shard_map.106 = (bf16[768,4096]{1,0:T(8,128)(2,1)}, f32[8,128]{1,0:T(8,128)}) custom-call(s32[21]{0:T(128)} %concatenate.25.scalars_ref, bf16[768,1024]{1,0:T(8,128)(2,1)} %refs_0_.3, bf16[768,1024]{1,0:T(8,128)(2,1)} %collective-permute-done.refs_1_, bf16[768,1024]{1,0:T(8,128)(2,1)} %copy-done.2, bf16[768,1024]{1,0:T(8,128)(2,1)} %copy-done, ...), custom_call_target="tpu_custom_call" | custom-call | flops 1 | bytes 1 | tf_op jit(solution)/shard_map/pallas_call | solution.py:358
  212.2 1.8 collective-permute-done.29.refs_12_
  214.0 0.7 concatenate.21.scalars_ref
  214.7 2.3 collective-permute-done.30.refs_14_
  217.2 1.7 collective-permute-done.32.refs_16_
  218.9 18.9 %shard_map.107 = (bf16[768,4096]{1,0:T(8,128)(2,1)}, f32[8,128]{1,0:T(8,128)}) custom-call(s32[19]{0:T(128)} %concatenate.21.scalars_ref, bf16[768,1024]{1,0:T(8,128)(2,1)} %refs_0_.3, bf16[768,1024]{1,0:T(8,128)(2,1)} %collective-permute-done.refs_1_, bf16[768,1024]{1,0:T(8,128)(2,1)} %copy-done.2, ...), custom_call_target="tpu_custom_call", output_to_operand_aliasing={{0}: (21, {})} | custom-call | flops 1 | bytes 1 | tf_op jit(solution)/shard_map/pallas_call | solution.py:358
  238.0 0.7 add_subtract_fusion.slots_ref
  238.7 1.4 collective-permute-done.36.refs_6_
  240.1 6.9 %shard_map.108 = (f32[8,64,4096]{2,1,0:T(8,128)}, f32[8,64,1024]{2,1,0:T(8,128)}) custom-call(s32[12]{0:T(128)} %add_subtract_fusion.slots_ref, bf16[3,64,1664]{2,1,0:T(8,128)(2,1)} %get-tuple-element.83.refs_0_, bf16[3,64,3456]{2,1,0:T(8,128)(2,1)} %get-tuple-element.82.refs_1_, ...), custom_call_target="tpu_custom_call", output_to_operand_aliasing={{0}: (10, {}), {1}: (11, {})} | custom-call | flops 1 | bytes 1 | tf_op jit(solution)/shard_map/pallas_call | solution.py:455
  (71 shorter events, 3.9 us)
Async XLA Ops:
  0.6 15.9 %collective-permute-start.3 = (bf16[8,64,4096]{2,1,0:T(8,128)(2,1)}, bf16[8,64,4096]{2,1,0:T(8,128)(2,1)}, u32[]{:S(2)}, u32[]{:S(2)}) collective-permute-start(bf16[8,64,4096]{2,1,0:T(8,128)(2,1)} %bitcast.21), channel_id=1, source_target_pairs={{0,1},{1,0},{2,3},{3,2},{4,5},{5,4},{6,7},{7,6},{8,9},{9,8},{10,11... | collective-permute-start | bytes 12582920 | tf_op jit(solution)/shard_map/ppermute | solution.py:503
  1.4 38.2 %collective-permute-start = (bf16[768,1024]{1,0:T(8,128)(2,1)}, bf16[768,1024]{1,0:T(8,128)(2,1)}, u32[]{:S(2)}, u32[]{:S(2)}) collective-permute-start(bf16[768,1024]{1,0:T(8,128)(2,1)} %refs_0_.3), channel_id=1, source_target_pairs={{0,4},{4,8},{8,12},{1,5},{5,9},{9,13},{2,6},{6,10},{10,14},{3,7},{... | collective-permute-start | bytes 4718600 | tf_op jit(solution)/shard_map/ppermute | solution.py:535
  4.6 37.8 %collective-permute-start.1 = (bf16[768,1024]{1,0:T(8,128)(2,1)}, bf16[768,1024]{1,0:T(8,128)(2,1)S(1)}, u32[]{:S(2)}, u32[]{:S(2)}) collective-permute-start(bf16[768,1024]{1,0:T(8,128)(2,1)} %refs_0_.3), channel_id=1, source_target_pairs={{4,0},{8,4},{12,8},{5,1},{9,5},{13,9},{6,2},{10,6},{14,10},{7,3},{... | collective-permute-start | bytes 4718600 | tf_op jit(solution)/shard_map/ppermute | solution.py:535
  8.7 5.5 %collective-permute-start.2 = (s32[3]{0:T(128)S(1)}, s32[3]{0:T(128)S(1)}, u32[]{:S(2)}, u32[]{:S(2)}) collective-permute-start(s32[3]{0:T(128)S(1)} %select_reduce_fusion), channel_id=1, source_target_pairs={{0,2},{1,3},{2,0},{3,1},{4,6},{5,7},{6,4},{7,5},{8,10},{9,11},{10,... | collective-permute-start | bytes 44 | tf_op jit(solution)/shard_map/ppermute | solution.py:503
  9.0 7.6 %collective-permute-start.4 = (bf16[8,64,1024]{2,1,0:T(8,128)(2,1)}, bf16[8,64,1024]{2,1,0:T(8,128)(2,1)S(1)}, u32[]{:S(2)}, u32[]{:S(2)}) collective-permute-start(bf16[8,64,1024]{2,1,0:T(8,128)(2,1)} %refs_2_.3), channel_id=1, source_target_pairs={{0,1},{1,0},{2,3},{3,2},{4,5},{5,4},{6,7},{7,6},{8,9},{9,8},{10,11... | collective-permute-start | bytes 3145736 | tf_op jit(solution)/shard_map/ppermute | solution.py:503
  14.2 25.1 %collective-permute-start.6 = (bf16[512,1024]{1,0:T(8,128)(2,1)}, bf16[512,1024]{1,0:T(8,128)(2,1)}, u32[]{:S(2)}, u32[]{:S(2)}) collective-permute-start(bf16[512,1024]{1,0:T(8,128)(2,1)} %get-tuple-element.48), channel_id=1, source_target_pairs={{0,2},{1,3},{2,0},{3,1},{4,6},{5,7},{6,4},{7,5},{8,10},{9,11},{10,... | collective-permute-start | bytes 3145736 | tf_op jit(solution)/shard_map/ppermute | solution.py:503
  16.6 1.0 copy-start.3
  22.3 20.1 %collective-permute-start.5 = (s32[6]{0:T(128)S(1)}, s32[6]{0:T(128)S(1)}, u32[]{:S(2)}, u32[]{:S(2)}) collective-permute-start(s32[6]{0:T(128)S(1)} %pad_add_fusion.1), channel_id=1, source_target_pairs={{0,1},{1,0},{2,3},{3,2},{4,5},{5,4},{6,7},{7,6},{8,9},{9,8},{10,11... | collective-permute-start | bytes 80 | tf_op jit(solution)/shard_map/ppermute | solution.py:503
  42.4 1.1 copy-start.2
  42.4 51.9 %collective-permute-start.13 = (bf16[4096,1024]{1,0:T(8,128)(2,1)}, bf16[4096,1024]{1,0:T(8,128)(2,1)}, u32[]{:S(2)}, u32[]{:S(2)}) collective-permute-start(bf16[4096,1024]{1,0:T(8,128)(2,1)} %refs_9_.1), channel_id=1, source_target_pairs={{0,1},{1,0},{2,3},{3,2},{4,5},{5,4},{6,7},{7,6},{8,9},{9,8},{10,11... | collective-permute-start | bytes 25165832 | tf_op jit(solution)/shard_map/ppermute | solution.py:503
  43.5 43.5 %collective-permute-start.9 = (bf16[3,64,5120]{2,1,0:T(8,128)(2,1)}, bf16[3,64,5120]{2,1,0:T(8,128)(2,1)}, u32[]{:S(2)}, u32[]{:S(2)}) collective-permute-start(bf16[3,64,5120]{2,1,0:T(8,128)(2,1)} %shard_map.103), channel_id=1, source_target_pairs={{0,2},{1,3},{2,0},{3,1},{4,6},{5,7},{6,4},{7,5},{8,10},{9,11},{10,... | collective-permute-start | bytes 5898248 | tf_op jit(solution)/shard_map/ppermute | solution.py:503
  43.8 36.7 %collective-permute-start.7 = (bf16[768,1024]{1,0:T(8,128)(2,1)}, bf16[768,1024]{1,0:T(8,128)(2,1)S(1)}, u32[]{:S(2)}, u32[]{:S(2)}) collective-permute-start(bf16[768,1024]{1,0:T(8,128)(2,1)} %collective-permute-done.refs_1_), channel_id=1, source_target_pairs={{0,4},{4,8},{8,12},{1,5},{5,9},{9,13},{2,6},{6,10},{10,14},{3,7},{... | collective-permute-start | bytes 4718600 | tf_op jit(solution)/shard_map/ppermute | solution.py:535
  47.0 36.4 %collective-permute-start.8 = (bf16[768,1024]{1,0:T(8,128)(2,1)}, bf16[768,1024]{1,0:T(8,128)(2,1)S(1)}, u32[]{:S(2)}, u32[]{:S(2)}) collective-permute-start(bf16[768,1024]{1,0:T(8,128)(2,1)} %copy-done.2), channel_id=1, source_target_pairs={{4,0},{8,4},{12,8},{5,1},{9,5},{13,9},{6,2},{10,6},{14,10},{7,3},{... | collective-permute-start | bytes 4718600 | tf_op jit(solution)/shard_map/ppermute | solution.py:535
  49.1 23.1 %collective-permute-start.10 = (bf16[512,1024]{1,0:T(8,128)(2,1)}, bf16[512,1024]{1,0:T(8,128)(2,1)S(1)}, u32[]{:S(2)}, u32[]{:S(2)}) collective-permute-start(bf16[512,1024]{1,0:T(8,128)(2,1)} %collective-permute-done.6.refs_11_), channel_id=1, source_target_pairs={{0,16},{16,0},{1,17},{17,1},{2,18},{18,2},{3,19},{19,3},{4,20},{20... | collective-permute-start | bytes 3145736 | tf_op jit(solution)/shard_map/ppermute | solution.py:577
  72.2 11.2 %copy-start.12 = (bf16[512,1024]{1,0:T(8,128)(2,1)}, bf16[512,1024]{1,0:T(8,128)(2,1)S(1)}, u32[]{:S(2)}) copy-start(bf16[512,1024]{1,0:T(8,128)(2,1)S(1)} %collective-permute-done.10.refs_19_) | copy-start | bytes 3145732
  80.4 42.4 %copy-start = (bf16[768,1024]{1,0:T(8,128)(2,1)}, bf16[768,1024]{1,0:T(8,128)(2,1)S(1)}, u32[]{:S(2)}) copy-start(bf16[768,1024]{1,0:T(8,128)(2,1)S(1)} %collective-permute-done.7.refs_3_) | copy-start | bytes 4718596
  83.4 40.5 %copy-start.1 = (bf16[768,1024]{1,0:T(8,128)(2,1)}, bf16[768,1024]{1,0:T(8,128)(2,1)S(1)}, u32[]{:S(2)}) copy-start(bf16[768,1024]{1,0:T(8,128)(2,1)S(1)} %collective-permute-done.8.refs_4_) | copy-start | bytes 4718596
  87.0 29.4 %collective-permute-start.16 = (bf16[512,1024]{1,0:T(8,128)(2,1)}, bf16[512,1024]{1,0:T(8,128)(2,1)}, u32[]{:S(2)}, u32[]{:S(2)}) collective-permute-start(bf16[512,1024]{1,0:T(8,128)(2,1)} %get-tuple-element.58), channel_id=1, source_target_pairs={{0,2},{1,3},{2,0},{3,1},{4,6},{5,7},{6,4},{7,5},{8,10},{9,11},{10,... | collective-permute-start | bytes 3145736 | tf_op jit(solution)/shard_map/ppermute | solution.py:503
  88.9 27.4 %collective-permute-start.11 = (bf16[256,1024]{1,0:T(8,128)(2,1)}, bf16[256,1024]{1,0:T(8,128)(2,1)S(1)}, u32[]{:S(2)}, u32[]{:S(2)}) collective-permute-start(bf16[256,1024]{1,0:T(8,128)(2,1)} %slice.32), channel_id=1, source_target_pairs={{0,4},{4,8},{8,12},{1,5},{5,9},{9,13},{2,6},{6,10},{10,14},{3,7},{... | collective-permute-start | bytes 1572872 | tf_op jit(solution)/shard_map/ppermute | solution.py:535
  92.1 24.2 %collective-permute-start.12 = (bf16[256,1024]{1,0:T(8,128)(2,1)}, bf16[256,1024]{1,0:T(8,128)(2,1)}, u32[]{:S(2)}, u32[]{:S(2)}) collective-permute-start(bf16[256,1024]{1,0:T(8,128)(2,1)} %slice.33), channel_id=1, source_target_pairs={{4,0},{8,4},{12,8},{5,1},{9,5},{13,9},{6,2},{10,6},{14,10},{7,3},{... | collective-permute-start | bytes 1572872 | tf_op jit(solution)/shard_map/ppermute | solution.py:535
  107.2 8.1 %collective-permute-start.14 = (f32[3,256,128]{2,1,0:T(8,128)}, f32[3,256,128]{2,1,0:T(8,128)S(1)}, u32[]{:S(2)}, u32[]{:S(2)}) collective-permute-start(f32[3,256,128]{2,1,0:T(8,128)} %get-tuple-element.57), channel_id=1, source_target_pairs={{0,4},{4,0},{8,12},{12,8},{1,5},{5,1},{9,13},{13,9},{2,6},{6,2},{1... | collective-permute-start | bytes 1179656 | tf_op jit(solution)/shard_map/ppermute | solution.py:503
  107.3 25.6 %collective-permute-start.18 = (bf16[512,1024]{1,0:T(8,128)(2,1)}, bf16[512,1024]{1,0:T(8,128)(2,1)}, u32[]{:S(2)}, u32[]{:S(2)}) collective-permute-start(bf16[512,1024]{1,0:T(8,128)(2,1)} %get-tuple-element.60), channel_id=1, source_target_pairs={{0,2},{1,3},{2,0},{3,1},{4,6},{5,7},{6,4},{7,5},{8,10},{9,11},{10,... | collective-permute-start | bytes 3145736 | tf_op jit(solution)/shard_map/ppermute | solution.py:503
  116.3 8.5 %copy-start.7 = (f32[3,256,128]{2,1,0:T(8,128)}, f32[3,256,128]{2,1,0:T(8,128)S(1)}, u32[]{:S(2)}) copy-start(f32[3,256,128]{2,1,0:T(8,128)S(1)} %add.109.here_ref) | copy-start | bytes 1179652
  116.4 8.5 %copy-start.6 = (bf16[256,1024]{1,0:T(8,128)(2,1)}, bf16[256,1024]{1,0:T(8,128)(2,1)S(1)}, u32[]{:S(2)}) copy-start(bf16[256,1024]{1,0:T(8,128)(2,1)S(1)} %collective-permute-done.11.refs_5_) | copy-start | bytes 1572868
  116.4 23.3 %collective-permute-start.17 = (bf16[512,1024]{1,0:T(8,128)(2,1)}, bf16[512,1024]{1,0:T(8,128)(2,1)S(1)}, u32[]{:S(2)}, u32[]{:S(2)}) collective-permute-start(bf16[512,1024]{1,0:T(8,128)(2,1)} %collective-permute-done.6.refs_11_), channel_id=1, source_target_pairs={{0,1},{1,0},{2,3},{3,2},{4,5},{5,4},{6,7},{7,6},{8,9},{9,8},{10,11... | collective-permute-start | bytes 3145736 | tf_op jit(solution)/shard_map/ppermute | solution.py:503
  120.2 19.5 %collective-permute-start.19 = (bf16[512,1024]{1,0:T(8,128)(2,1)}, bf16[512,1024]{1,0:T(8,128)(2,1)S(1)}, u32[]{:S(2)}, u32[]{:S(2)}) collective-permute-start(bf16[512,1024]{1,0:T(8,128)(2,1)} %copy-done.12), channel_id=1, source_target_pairs={{0,1},{1,0},{2,3},{3,2},{4,5},{5,4},{6,7},{7,6},{8,9},{9,8},{10,11... | collective-permute-start | bytes 3145736 | tf_op jit(solution)/shard_map/ppermute | solution.py:503
  120.2 24.5 %collective-permute-start.20 = (bf16[512,1024]{1,0:T(8,128)(2,1)}, bf16[512,1024]{1,0:T(8,128)(2,1)S(1)}, u32[]{:S(2)}, u32[]{:S(2)}) collective-permute-start(bf16[512,1024]{1,0:T(8,128)(2,1)} %collective-permute-done.16.refs_13_), channel_id=1, source_target_pairs={{0,16},{16,0},{1,17},{17,1},{2,18},{18,2},{3,19},{19,3},{4,20},{20... | collective-permute-start | bytes 3145736 | tf_op jit(solution)/shard_map/ppermute | solution.py:577
  121.0 18.6 %collective-permute-start.15 = (f32[3,256,128]{2,1,0:T(8,128)S(1)}, f32[3,256,128]{2,1,0:T(8,128)S(1)}, u32[]{:S(2)}, u32[]{:S(2)}) collective-permute-start(f32[3,256,128]{2,1,0:T(8,128)S(1)} %add.109.here_ref), channel_id=1, source_target_pairs={{0,8},{4,12},{8,0},{12,4},{1,9},{5,13},{9,1},{13,5},{2,10},{6,14},... | collective-permute-start | bytes 1179656 | tf_op jit(solution)/shard_map/ppermute | solution.py:503
  139.6 13.4 %copy-start.16 = (f32[3,256,128]{2,1,0:T(8,128)}, f32[3,256,128]{2,1,0:T(8,128)S(1)}, u32[]{:S(2)}) copy-start(f32[3,256,128]{2,1,0:T(8,128)S(1)} %collective-permute-done.15.there_ref) | copy-start | bytes 1179652
  139.6 11.7 %copy-start.13 = (bf16[512,1024]{1,0:T(8,128)(2,1)}, bf16[512,1024]{1,0:T(8,128)(2,1)S(1)}, u32[]{:S(2)}) copy-start(bf16[512,1024]{1,0:T(8,128)(2,1)S(1)} %collective-permute-done.17.refs_12_) | copy-start | bytes 3145732
  139.7 13.0 %copy-start.14 = (bf16[512,1024]{1,0:T(8,128)(2,1)}, bf16[512,1024]{1,0:T(8,128)(2,1)S(1)}, u32[]{:S(2)}) copy-start(bf16[512,1024]{1,0:T(8,128)(2,1)S(1)} %collective-permute-done.19.refs_20_) | copy-start | bytes 3145732
  144.8 1.0 copy-start.10
  145.8 25.6 %collective-permute-start.21 = (bf16[512,1024]{1,0:T(8,128)(2,1)}, bf16[512,1024]{1,0:T(8,128)(2,1)S(1)}, u32[]{:S(2)}, u32[]{:S(2)}) collective-permute-start(bf16[512,1024]{1,0:T(8,128)(2,1)} %slice.34), channel_id=1, source_target_pairs={{0,4},{4,8},{8,12},{1,5},{5,9},{9,13},{2,6},{6,10},{10,14},{3,7},{... | collective-permute-start | bytes 3145736 | tf_op jit(solution)/shard_map/ppermute | solution.py:535
  148.9 25.3 %collective-permute-start.22 = (bf16[512,1024]{1,0:T(8,128)(2,1)}, bf16[512,1024]{1,0:T(8,128)(2,1)S(1)}, u32[]{:S(2)}, u32[]{:S(2)}) collective-permute-start(bf16[512,1024]{1,0:T(8,128)(2,1)} %slice.35), channel_id=1, source_target_pairs={{4,0},{8,4},{12,8},{5,1},{9,5},{13,9},{6,2},{10,6},{14,10},{7,3},{... | collective-permute-start | bytes 3145736 | tf_op jit(solution)/shard_map/ppermute | solution.py:535
  151.3 28.9 %copy-start.17 = (s32[3]{0:T(128)S(1)}, s32[3]{0:T(128)}, u32[]{:S(2)}) copy-start(s32[3]{0:T(128)} %live_ref.1) | copy-start | bytes 40
  151.3 23.2 %collective-permute-start.23 = (bf16[512,1024]{1,0:T(8,128)(2,1)}, bf16[512,1024]{1,0:T(8,128)(2,1)}, u32[]{:S(2)}, u32[]{:S(2)}) collective-permute-start(bf16[512,1024]{1,0:T(8,128)(2,1)} %get-tuple-element.66), channel_id=1, source_target_pairs={{0,2},{1,3},{2,0},{3,1},{4,6},{5,7},{6,4},{7,5},{8,10},{9,11},{10,... | collective-permute-start | bytes 3145736 | tf_op jit(solution)/shard_map/ppermute | solution.py:503
  152.6 22.9 %collective-permute-start.24 = (bf16[512,1024]{1,0:T(8,128)(2,1)}, bf16[512,1024]{1,0:T(8,128)(2,1)S(1)}, u32[]{:S(2)}, u32[]{:S(2)}) collective-permute-start(bf16[512,1024]{1,0:T(8,128)(2,1)} %collective-permute-done.18.refs_15_), channel_id=1, source_target_pairs={{0,16},{16,0},{1,17},{17,1},{2,18},{18,2},{3,19},{19,3},{4,20},{20... | collective-permute-start | bytes 3145736 | tf_op jit(solution)/shard_map/ppermute | solution.py:577
  171.4 13.2 %copy-start.4 = (bf16[512,1024]{1,0:T(8,128)(2,1)}, bf16[512,1024]{1,0:T(8,128)(2,1)S(1)}, u32[]{:S(2)}) copy-start(bf16[512,1024]{1,0:T(8,128)(2,1)S(1)} %collective-permute-done.21.refs_7_) | copy-start | bytes 3145732
  174.3 10.3 %copy-start.5 = (bf16[512,1024]{1,0:T(8,128)(2,1)}, bf16[512,1024]{1,0:T(8,128)(2,1)S(1)}, u32[]{:S(2)}) copy-start(bf16[512,1024]{1,0:T(8,128)(2,1)S(1)} %collective-permute-done.22.refs_8_) | copy-start | bytes 3145732
  175.5 9.1 %copy-start.11 = (bf16[512,1024]{1,0:T(8,128)(2,1)}, bf16[512,1024]{1,0:T(8,128)(2,1)S(1)}, u32[]{:S(2)}) copy-start(bf16[512,1024]{1,0:T(8,128)(2,1)S(1)} %collective-permute-done.24.refs_13_) | copy-start | bytes 3145732
  175.5 35.5 %collective-permute-start.28 = (bf16[3,64,3456]{2,1,0:T(8,128)(2,1)}, bf16[3,64,3456]{2,1,0:T(8,128)(2,1)}, u32[]{:S(2)}, u32[]{:S(2)}) collective-permute-start(bf16[3,64,3456]{2,1,0:T(8,128)(2,1)} %get-tuple-element.82.refs_1_), channel_id=1, source_target_pairs={{0,2},{1,3},{2,0},{3,1},{4,6},{5,7},{6,4},{7,5},{8,10},{9,11},{10,... | collective-permute-start | bytes 3981320 | tf_op jit(solution)/shard_map/ppermute | solution.py:503
  175.7 5.8 %collective-permute-start.25 = (bf16[512,1024]{1,0:T(8,128)(2,1)}, bf16[512,1024]{1,0:T(8,128)(2,1)}, u32[]{:S(2)}, u32[]{:S(2)}) collective-permute-start(bf16[512,1024]{1,0:T(8,128)(2,1)} %collective-permute-done.16.refs_13_), channel_id=1, source_target_pairs={{0,1},{1,0},{2,3},{3,2},{4,5},{5,4},{6,7},{7,6},{8,9},{9,8},{10,11... | collective-permute-start | bytes 3145736 | tf_op jit(solution)/shard_map/ppermute | solution.py:503
  178.9 4.1 %collective-permute-start.26 = (bf16[512,1024]{1,0:T(8,128)(2,1)}, bf16[512,1024]{1,0:T(8,128)(2,1)}, u32[]{:S(2)}, u32[]{:S(2)}) collective-permute-start(bf16[512,1024]{1,0:T(8,128)(2,1)} %collective-permute-done.18.refs_15_), channel_id=1, source_target_pairs={{0,1},{1,0},{2,3},{3,2},{4,5},{5,4},{6,7},{7,6},{8,9},{9,8},{10,11... | collective-permute-start | bytes 3145736 | tf_op jit(solution)/shard_map/ppermute | solution.py:503
  178.9 5.6 %collective-permute-start.27 = (bf16[512,1024]{1,0:T(8,128)(2,1)}, bf16[512,1024]{1,0:T(8,128)(2,1)}, u32[]{:S(2)}, u32[]{:S(2)}) collective-permute-start(bf16[512,1024]{1,0:T(8,128)(2,1)} %collective-permute-done.23.refs_17_), channel_id=1, source_target_pairs={{0,1},{1,0},{2,3},{3,2},{4,5},{5,4},{6,7},{7,6},{8,9},{9,8},{10,11... | collective-permute-start | bytes 3145736 | tf_op jit(solution)/shard_map/ppermute | solution.py:503
  179.4 32.1 %collective-permute-start.31 = (bf16[512,1024]{1,0:T(8,128)(2,1)}, bf16[512,1024]{1,0:T(8,128)(2,1)}, u32[]{:S(2)}, u32[]{:S(2)}) collective-permute-start(bf16[512,1024]{1,0:T(8,128)(2,1)} %collective-permute-done.23.refs_17_), channel_id=1, source_target_pairs={{0,16},{16,0},{1,17},{17,1},{2,18},{18,2},{3,19},{19,3},{4,20},{20... | collective-permute-start | bytes 3145736 | tf_op jit(solution)/shard_map/ppermute | solution.py:577
  184.6 27.1 %copy-start.8 = (bf16[3,64,3456]{2,1,0:T(8,128)(2,1)S(1)}, bf16[3,64,3456]{2,1,0:T(8,128)(2,1)}, u32[]{:S(2)}) copy-start(bf16[3,64,3456]{2,1,0:T(8,128)(2,1)} %get-tuple-element.82.refs_1_) | copy-start | bytes 3981316
  210.9 3.1 %collective-permute-start.29 = (bf16[512,1024]{1,0:T(8,128)(2,1)}, bf16[512,1024]{1,0:T(8,128)(2,1)}, u32[]{:S(2)}, u32[]{:S(2)}) collective-permute-start(bf16[512,1024]{1,0:T(8,128)(2,1)} %copy-done.10), channel_id=1, source_target_pairs={{0,1},{1,0},{2,3},{3,2},{4,5},{5,4},{6,7},{7,6},{8,9},{9,8},{10,11... | collective-permute-start | bytes 3145736 | tf_op jit(solution)/shard_map/ppermute | solution.py:503
  211.2 5.8 %collective-permute-start.30 = (bf16[512,1024]{1,0:T(8,128)(2,1)}, bf16[512,1024]{1,0:T(8,128)(2,1)}, u32[]{:S(2)}, u32[]{:S(2)}) collective-permute-start(bf16[512,1024]{1,0:T(8,128)(2,1)} %copy-done.11), channel_id=1, source_target_pairs={{0,1},{1,0},{2,3},{3,2},{4,5},{5,4},{6,7},{7,6},{8,9},{9,8},{10,11... | collective-permute-start | bytes 3145736 | tf_op jit(solution)/shard_map/ppermute | solution.py:503
  211.5 7.4 %collective-permute-start.32 = (bf16[512,1024]{1,0:T(8,128)(2,1)}, bf16[512,1024]{1,0:T(8,128)(2,1)}, u32[]{:S(2)}, u32[]{:S(2)}) collective-permute-start(bf16[512,1024]{1,0:T(8,128)(2,1)} %collective-permute-done.31.refs_15_), channel_id=1, source_target_pairs={{0,1},{1,0},{2,3},{3,2},{4,5},{5,4},{6,7},{7,6},{8,9},{9,8},{10,11... | collective-permute-start | bytes 3145736 | tf_op jit(solution)/shard_map/ppermute | solution.py:503
  211.7 27.0 %collective-permute-start.34 = (bf16[3,64,3456]{2,1,0:T(8,128)(2,1)S(1)}, bf16[3,64,3456]{2,1,0:T(8,128)(2,1)S(1)}, u32[]{:S(2)}, u32[]{:S(2)}) collective-permute-start(bf16[3,64,3456]{2,1,0:T(8,128)(2,1)S(1)} %copy-done.8), channel_id=1, source_target_pairs={{0,1},{1,0},{2,3},{3,2},{4,5},{5,4},{6,7},{7,6},{8,9},{9,8},{10,11... | collective-permute-start | bytes 3981320 | tf_op jit(solution)/shard_map/ppermute | solution.py:503
  212.0 26.7 %collective-permute-start.37 = (bf16[3,64,3456]{2,1,0:T(8,128)(2,1)}, bf16[3,64,3456]{2,1,0:T(8,128)(2,1)}, u32[]{:S(2)}, u32[]{:S(2)}) collective-permute-start(bf16[3,64,3456]{2,1,0:T(8,128)(2,1)} %collective-permute-done.28.refs_5_), channel_id=1, source_target_pairs={{0,1},{1,0},{2,3},{3,2},{4,5},{5,4},{6,7},{7,6},{8,9},{9,8},{10,11... | collective-permute-start | bytes 3981320 | tf_op jit(solution)/shard_map/ppermute | solution.py:503
  214.0 23.8 %collective-permute-start.35 = (bf16[3,64,1664]{2,1,0:T(8,128)(2,1)}, bf16[3,64,1664]{2,1,0:T(8,128)(2,1)S(1)}, u32[]{:S(2)}, u32[]{:S(2)}) collective-permute-start(bf16[3,64,1664]{2,1,0:T(8,128)(2,1)} %get-tuple-element.83.refs_0_), channel_id=1, source_target_pairs={{0,2},{1,3},{2,0},{3,1},{4,6},{5,7},{6,4},{7,5},{8,10},{9,11},{10,... | collective-permute-start | bytes 1916936 | tf_op jit(solution)/shard_map/ppermute | solution.py:503
  217.0 21.7 %collective-permute-start.33 = (bf16[3,64,1664]{2,1,0:T(8,128)(2,1)}, bf16[3,64,1664]{2,1,0:T(8,128)(2,1)}, u32[]{:S(2)}, u32[]{:S(2)}) collective-permute-start(bf16[3,64,1664]{2,1,0:T(8,128)(2,1)} %get-tuple-element.83.refs_0_), channel_id=1, source_target_pairs={{0,1},{1,0},{2,3},{3,2},{4,5},{5,4},{6,7},{7,6},{8,9},{9,8},{10,11... | collective-permute-start | bytes 1916936 | tf_op jit(solution)/shard_map/ppermute | solution.py:503
  237.8 2.3 copy-start.15
  237.8 2.3 collective-permute-start.36
  238.7 1.4 copy-start.9

commit v7 on v6

--- a/solution.py
+++ b/solution.py
@@ -209,142 +209,264 @@
     )(live, here, there, hidden, grad)
 
 
-def base_kernel(n_dp, tiles, n_chunks, kept_rows, count, scalars_ref, *refs):
-    near = n_dp // 2
-    n_kept = len(kept_rows)
-    kept_refs, refs = refs[:n_kept], refs[n_kept:]
-    near_refs = refs[:near]
-    far_refs = refs[near : near + n_chunks * near]
-    coef_ref, block_ref = refs[near + n_chunks * near : near + n_chunks * near + 2]
-    out_ref, token_ref, kept, weight, factor, result = refs[-10:-4]
-    kept_sem, in_sem, factor_sem, out_sem = refs[-4:]
-    _, tile, depth = weight.shape
-    deep = depth // n_dp
-    height = coef_ref.shape[1]
-    steps = len(tiles)
-    token_ref[...] = jnp.zeros_like(token_ref)
-
-    def lanes(r):
-        return pl.ds(pl.multiple_of(scalars_ref[steps + r] * deep, deep), deep)
-
-    def span(j):
-        return pl.ds(pl.multiple_of(scalars_ref[j] * tile, tile), tile)
-
-    def loads(j, slot, r):
-        if r < near:
+class Tiles:
+    def __init__(self, n_dp, tiles, n_chunks, kept_rows, scalars_ref, refs):
+        self.near, self.n_dp, self.tiles, self.kept_rows = n_dp // 2, n_dp, tiles, kept_rows
+        n_kept = len(kept_rows)
+        self.scalars_ref, self.kept_refs, refs = scalars_ref, refs[:n_kept], refs[n_kept:]
+        self.near_refs, refs = refs[: self.near], refs[self.near :]
+        self.far_refs, self.rest = refs[: n_chunks * self.near], refs[n_chunks * self.near :]
+        self.deep = self.near_refs[0].shape[1]
+        self.at = [scalars_ref[len(tiles) + 2 * n_dp + k] for k in range(n_kept)]
+
+    def lanes(self, r):
+        start = self.scalars_ref[len(self.tiles) + r] * self.deep
+        return pl.ds(pl.multiple_of(start, self.deep), self.deep)
+
+    def early(self, r):
+        return self.scalars_ref[len(self.tiles) + self.n_dp + r] == 1
+
+    def span(self, j, tile):
+        return pl.ds(pl.multiple_of(self.scalars_ref[j] * tile, tile), tile)
+
+    def loads(self, j, r, weight, slot, sem):
+        if r < self.near:
+            rows = self.near_refs[r].at[self.span(j, weight.shape[1]), :]
             return [
-                pltpu.make_async_copy(
-                    near_refs[r].at[span(j), :], weight.at[slot, :, lanes(r)], in_sem.at[slot, r, 0]
-                )
+                pltpu.make_async_copy(rows, weight.at[slot, :, self.lanes(r)], sem.at[slot, r, 0])
             ]
         copies, low = [], 0
-        for k, (chunk, start, size) in enumerate(tiles[j]):
+        for k, (chunk, start, size) in enumerate(self.tiles[j]):
             copies.append(
                 pltpu.make_async_copy(
-                    far_refs[chunk * near + r - near].at[pl.ds(start, size)],
-                    weight.at[slot, pl.ds(low, size), lanes(r)],
-                    in_sem.at[slot, r, k],
+                    self.far_refs[chunk * self.near + r - self.near].at[pl.ds(start, size)],
+                    weight.at[slot, pl.ds(low, size), self.lanes(r)],
+                    sem.at[slot, r, k],
                 )
             )
             low += size
         return copies
 
-    def factors(j, slot):
+    def columns(self, k, kept, sem):
+        wide = self.kept_refs[k].shape[1]
+        place = pl.ds(pl.multiple_of(self.at[k] * wide, wide), wide)
+        rows = pl.ds(self.kept_rows[k], self.kept_refs[k].shape[0])
+        return pltpu.make_async_copy(self.kept_refs[k], kept.at[rows, place], sem.at[k])
+
+    def each_column(self, kept, sem, act):
+        for k in range(len(self.kept_refs)):
+            pl.when(self.at[k] >= 0)(lambda k=k: act(self.columns(k, kept, sem)))
+
+    def part(self, r, kept, weight, slot):
+        return lax.dot_general(
+            kept[:, self.lanes(r)],
+            weight[slot, :, self.lanes(r)],
+            (((1,), (1,)), ((), ())),
+            preferred_element_type=f32,
+        )
+
+
+def start(copies):
+    for copy in copies:
+        copy.start()
+
+
+def wait(copies):
+    for copy in copies:
+        copy.wait()
+
+
+def early_kernel(n_dp, tiles, n_chunks, kept_rows, scalars_ref, *refs):
+    me = Tiles(n_dp, tiles, n_chunks, kept_rows, scalars_ref, refs)
+    sums_refs, (kept, weight, total, kept_sem, in_sem, out_sem) = me.rest[:-6], me.rest[-6:]
+    steps = len(tiles)
+
+    def load(j, act):
+        for r in range(n_dp):
+            pl.when(me.early(r))(lambda r=r: act(me.loads(j, r, weight, j % 2, in_sem)))
+
+    def store(j):
+        return pltpu.make_async_copy(total.at[j % 2], sums_refs[j], out_sem.at[j % 2])
+
+    me.each_column(kept, kept_sem, lambda copy: copy.start())
+    load(0, start)
+    me.each_column(kept, kept_sem, lambda copy: copy.wait())
+
+    @pl.loop(0, steps)
+    def _(step):
+        slot = lax.rem(step, 2)
+        for j in range(steps):
+
+            @pl.when(step == j)
+            def _():
+                if j + 1 < steps:
+                    load(j + 1, start)
+                load(j, wait)
+                if j >= 2:
+                    store(j - 2).wait()
+
+        total[slot] = jnp.zeros(total.shape[1:], f32)
+        for r in range(n_dp):
+
+            @pl.when(me.early(r))
+            def _():
+                total[slot] += me.part(r, kept, weight, slot)
+
+        for j in range(steps):
+            pl.when(step == j)(lambda j=j: store(j).start())
+
+    for j in range(max(steps - 2, 0), steps):
+        store(j).wait()
+
+
+def base_kernel(n_dp, tiles, n_chunks, kept_rows, n_held, count, scalars_ref, *refs):
+    me = Tiles(n_dp, tiles, n_chunks, kept_rows, scalars_ref, refs)
+    held_refs, (coef_ref, block_ref) = me.rest[:n_held], me.rest[n_held : n_held + 2]
+    out_ref, token_ref, kept, weight, factor, result, total = me.rest[-12:-5]
+    kept_sem, in_sem, factor_sem, out_sem, held_sem = me.rest[-5:]
+    _, tile, _ = weight.shape
+    height = coef_ref.shape[1]
+    steps = len(tiles)
+    live = steps + 2 * n_dp + len(kept_rows)
+    token_ref[...] = jnp.zeros_like(token_ref)
+
+    def load(j, act):
+        slot = j % 2
+        for r in range(n_dp):
+            if j < n_held:
+                pl.when(jnp.logical_not(me.early(r)))(
+                    lambda r=r: act(me.loads(j, r, weight, slot, in_sem))
+                )
+            else:
+                act(me.loads(j, r, weight, slot, in_sem))
+        if j < n_held:
+            act([pltpu.make_async_copy(held_refs[j], total.at[slot], held_sem.at[slot])])
+        act(
+            [
+                pltpu.make_async_copy(
+                    block_ref.at[:, :, me.span(j, tile)], factor.at[slot], factor_sem.at[slot]
+                )
+            ]
+        )
+
+    def store(j):
         return pltpu.make_async_copy(
-            block_ref.at[:, :, span(j)], factor.at[slot], factor_sem.at[slot]
+            result.at[j % 2], out_ref.at[:, me.span(j, tile)], out_sem.at[j % 2]
         )
 
-    at = [scalars_ref[steps + n_dp + count + k] for k in range(n_kept)]
-
-    def columns(k):
-        wide = kept_refs[k].shape[1]
-        place = pl.ds(pl.multiple_of(at[k] * wide, wide), wide)
-        rows = pl.ds(kept_rows[k], kept_refs[k].shape[0])
-        return pltpu.make_async_copy(kept_refs[k], kept.at[rows, place], kept_sem.at[k])
-
-    def store(j, slot):
-        return pltpu.make_async_copy(result.at[slot], out_ref.at[:, span(j)], out_sem.at[slot])
-
-    def load(j, slot):
-        for r in range(n_dp):
-            for copy in loads(j, slot, r):
-                copy.start()
-        factors(j, slot).start()
-
-    over_last = (((1,), (1,)), ((), ()))
-
-    def finish(slot, total):
+    def finish(slot, sums):
         for b in range(count):
             extra = jnp.dot(coef_ref[b], factor[slot, b], preferred_element_type=f32)
-            here = total[b * height : (b + 1) * height] + extra
-            valid = lax.broadcasted_iota(i32, here.shape, 0) < scalars_ref[steps + n_dp + b]
+            here = sums[b * height : (b + 1) * height] + extra
+            valid = lax.broadcasted_iota(i32, here.shape, 0) < scalars_ref[live + b]
             result[slot, b * height : (b + 1) * height, :] = jnp.where(valid, here, 0.0).astype(
                 bf16
             )
 
-    for k in range(n_kept):
-        pl.when(at[k] >= 0)(lambda k=k: columns(k).start())
-    for r in range(n_dp):
-        for copy in loads(0, 0, r):
-            copy.start()
-    factors(0, 0).start()
+    load(0, start)
+    me.each_column(kept, kept_sem, lambda copy: copy.start())
     if steps > 1:
-        load(1, 1)
-    matching = kept_refs[0].shape[1] == deep
-    if not matching:
-        for k in range(n_kept):
-            pl.when(at[k] >= 0)(lambda k=k: columns(k).wait())
-    total = None
-    for r in range(n_dp):
-        if matching:
-            for k in range(n_kept):
-                pl.when(at[k] == scalars_ref[steps + r])(lambda k=k: columns(k).wait())
-        for copy in loads(0, 0, r):
-            copy.wait()
-        part = lax.dot_general(
-            kept[:, lanes(r)], weight[0, :, lanes(r)], over_last, preferred_element_type=f32
-        )
-        total = part if total is None else total + part
-    factors(0, 0).wait()
-    finish(0, total)
-    store(0, 0).start()
-
-    @pl.loop(1, steps)
+        load(1, start)
+    me.each_column(kept, kept_sem, lambda copy: copy.wait())
+
+    @pl.loop(0, steps)
     def _(step):
         slot = lax.rem(step, 2)
-        for j in range(1, steps):
+        for j in range(steps):
 
             @pl.when(step == j)
             def _():
-                if j + 1 < steps:
-                    load(j + 1, (j + 1) % 2)
+                if 1 < j + 1 < steps:
+                    load(j + 1, start)
+                load(j, wait)
+                if j >= 2:
+                    store(j - 2).wait()
+
+        if n_held:
+
+            @pl.when(step < n_held)
+            def _():
                 for r in range(n_dp):
-                    for copy in loads(j, j % 2, r):
-                        copy.wait()
-                factors(j, j % 2).wait()
-                if j >= 2:
-                    store(j - 2, j % 2).wait()
-
-        finish(
-            slot,
-            lax.dot_general(kept[...], weight[slot], over_last, preferred_element_type=f32),
-        )
-        for j in range(1, steps):
-            pl.when(step == j)(lambda j=j: store(j, j % 2).start())
+
+                    @pl.when(jnp.logical_not(me.early(r)))
+                    def _():
+                        total[slot] += me.part(r, kept, weight, slot)
+
+                finish(slot, total[slot])
+
+        if n_held < steps:
+
+            @pl.when(step >= n_held)
+            def _():
+                finish(
+                    slot,
+                    lax.dot_general(
+                        kept[...],
+                        weight[slot],
+                        (((1,), (1,)), ((), ())),
+                        preferred_element_type=f32,
+                    ),
+                )
+
+        for j in range(steps):
+            pl.when(step == j)(lambda j=j: store(j).start())
 
     for j in range(max(steps - 2, 0), steps):
-        store(j, j % 2).wait()
-
-
-def base(places, scalars, kept, near, chunks, tiles, tile, coef, block_a, held, token):
-    rows = kept[0][0].shape[0]
-    count, rank, ff = block_a.shape
+        store(j).wait()
+
+
+def tile_scratch(rows, tile, depth, n_kept, n_dp, tiles):
+    most = max(len(segments) for segments in tiles)
+    return [
+        pltpu.VMEM((rows, depth), bf16),
+        pltpu.VMEM((2, tile, depth), bf16),
+    ], [
+        pltpu.SemaphoreType.DMA((n_kept,)),
+        pltpu.SemaphoreType.DMA((2, n_dp, most)),
+    ]
+
+
+def tile_operands(kept, near, chunks):
     top = len(near)
-    depth = 2 * top * near[0].shape[1]
-    anywhere = pl.BlockSpec(memory_space=pl.ANY)
     operands = [piece for piece, _ in kept] + [near[r] for r in range(top)]
     for piece in chunks:
         operands += [piece[r] for r in range(top, 2 * top)]
+    return operands
+
+
+def early_sums(places, scalars, kept, near, chunks, tiles, tile):
+    rows = kept[0][0].shape[0]
+    n_dp = 2 * len(near)
+    depth = n_dp * near[0].shape[1]
+    anywhere = pl.BlockSpec(memory_space=pl.ANY)
+    operands = tile_operands(kept, near, chunks)
+    buffers, semaphores = tile_scratch(rows, tile, depth, len(kept), n_dp, tiles)
+    return pl.pallas_call(
+        functools.partial(early_kernel, n_dp, tiles, len(chunks), [low for _, low in kept]),
+        grid_spec=pltpu.PrefetchScalarGridSpec(
+            num_scalar_prefetch=1,
+            grid=(1,),
+            in_specs=[anywhere] * len(operands),
+            out_specs=[anywhere] * len(tiles),
+            scratch_shapes=[
+                *buffers,
+                pltpu.VMEM((2, rows, tile), f32),
+                *semaphores,
+                pltpu.SemaphoreType.DMA((2,)),
+            ],
+        ),
+        out_shape=[jax.ShapeDtypeStruct((rows, tile), f32)] * len(tiles),
+        **params((1, 1)),
+    )(jnp.concatenate([jnp.stack(places).astype(i32), scalars]), *operands)
+
+
+def base(places, scalars, kept, near, chunks, tiles, tile, early, coef, block_a, held, token):
+    rows = kept[0][0].shape[0]
+    count, rank, ff = block_a.shape
+    n_dp = 2 * len(near)
+    depth = n_dp * near[0].shape[1]
+    anywhere = pl.BlockSpec(memory_space=pl.ANY)
+    operands = tile_operands(kept, near, chunks) + early
     in_specs = [anywhere] * len(operands)
     in_specs += [pl.BlockSpec(coef.shape, lambda i, s: (0, 0, 0)), anywhere]
     operands += [coef, block_a]
@@ -353,11 +475,10 @@
         in_specs += [anywhere, anywhere]
         operands += [token, held]
         aliases = {len(operands): 0}
-    most = max(len(segments) for segments in tiles)
-    span = tile * len(tiles)
+    buffers, semaphores = tile_scratch(rows, tile, depth, len(kept), n_dp, tiles)
     return pl.pallas_call(
         functools.partial(
-            base_kernel, 2 * top, tiles, len(chunks), [low for _, low in kept], count
+            base_kernel, n_dp, tiles, len(chunks), [low for _, low in kept], len(early), count
         ),
         grid_spec=pltpu.PrefetchScalarGridSpec(
             num_scalar_prefetch=1,
@@ -365,12 +486,12 @@
             in_specs=in_specs,
             out_specs=[anywhere, pl.BlockSpec((8, 128), lambda i, s: (0, 0))],
             scratch_shapes=[
-                pltpu.VMEM((rows, depth), bf16),
-                pltpu.VMEM((2, tile, depth), bf16),
+                *buffers,
                 pltpu.VMEM((2, count, rank, tile), bf16),
                 pltpu.VMEM((2, rows, tile), bf16),
-                pltpu.SemaphoreType.DMA((len(kept),)),
-                pltpu.SemaphoreType.DMA((2, 2 * top, most)),
+                pltpu.VMEM((2, rows, tile), f32),
+                *semaphores,
+                pltpu.SemaphoreType.DMA((2,)),
                 pltpu.SemaphoreType.DMA((2,)),
                 pltpu.SemaphoreType.DMA((2,)),
             ],
@@ -417,14 +538,6 @@
         for slot in wanted[1:]:
             any_here = any_here | (slot == j)
         hit.append(any_here)
-
-    def start(copies):
-        for copy in copies:
-            copy.start()
-
-    def wait(copies):
-        for copy in copies:
-            copy.wait()
 
     for j in range(local):
         pl.when(hit[j])(lambda j=j: start(whole(j, True)))
@@ -545,8 +658,8 @@
 
     share = ff // n_groups
     if share % 2048 == 0:
-        unit, tile = share // 8, share // 4
-        sizes = [2 * unit] * 4
+        unit, tile = share // 16, share // 4
+        sizes = [4 * unit, 5 * unit, 5 * unit, 2 * unit]
     else:
         tile = share
         sizes = [share]
@@ -558,14 +671,22 @@
     def flat(*pieces):
         return [v for piece in pieces for v in piece.values()]
 
+    def piece_of(j, shift, *after):
+        first_row, size = parts[j]
+        owner = lax.rem(group + n_groups - shift, n_groups)
+        piece = lax.dynamic_slice_in_dim(
+            frozen_down_weight, owner * share + first_row, size, axis=0
+        )
+        return {top: swap(behind(piece, *after), top)}
+
     def cross(*after):
         j = len(crossed)
         if j < len(parts):
-            start, size = parts[j]
-            piece = lax.dynamic_slice_in_dim(
-                frozen_down_weight, group * share + start, size, axis=0
-            )
-            crossed.append({top: swap(behind(piece, *after), top)})
+            crossed.append(piece_of(j, 0, *after))
+            if j and j + 1 == len(parts):
+                direct.extend(piece_of(j, shift, *after) for shift in range(1, n_groups))
+
+    direct = []
 
     def turn(*after):
         j = len(turned)
@@ -606,7 +727,7 @@
         *places(ready), a_near, b_near, far, hidden, output_gradient
     )
     cross(*past)
-    cross(*past)
+    cross(part, *past)
     third = hop(*past, high=height)
     sums = [part]
     bit = 1
@@ -618,40 +739,22 @@
     total, other = sums[-2:]
     past = [sums[2], *third, *flat(*crossed[1:2])]
     turn(*past)
-    fill(crossed[:1], *past)
+    fill(crossed[:2], *past)
     fill(turned[0], *past)
-    past = [other, *flat(*crossed, *sum(turned, []))]
-    third = hop(*past, low=height)
-    cross(*past)
-    turn(*past)
-    low_terms, high_terms, coef = block_terms(
-        island_live_rows, total, other, hidden, output_gradient
-    )
-    past = [coef, *third, *flat(*crossed[3:], *sum(turned[2:], []))]
-    far_high = swap(behind(high_terms, *past), top)
-    far_low = swap(behind(low_terms, *past), top)
-    turn(*past)
-    fill(crossed[1:], *past)
+
+    order = [me ^ r for r in range(n_dp)]
+    steps_away = [jnp.abs(place - q) for q in order]
     if line:
-        at = jnp.stack(where).astype(i32)
+        early = jnp.stack([(steps < n_fsdp - 1).astype(i32) for steps in steps_away])
     else:
-        pieces_of_kept = [(lax.all_gather(output_gradient, "fsdp", axis=1, tiled=True), 0)]
-        at = jnp.zeros((1,), i32)
-
-    relative = [both_slots[r][:count] for r in near] + [both_slots[r][count:] for r in near]
-    relative = jnp.concatenate(relative) - me * local
-
-    scalars = jnp.concatenate(
-        [jnp.stack([me ^ r for r in range(n_dp)]).astype(i32), island_live_rows, at]
-    )
-    grad_hidden = token = None
-
-    def multiply(*where):
-        nonlocal grad_hidden, token
-        chunks, tiles, places = [], [], []
-        for shift, t in where:
-            start = lax.rem(group + n_groups - shift, n_groups) * share
-            places.append(start // tile + t)
+        early = jnp.zeros((n_dp,), i32)
+    order = jnp.stack(order).astype(i32)
+
+    def collect(named):
+        chunks, tiles, places_of = [], [], []
+        for shift, t in named:
+            first_row = lax.rem(group + n_groups - shift, n_groups) * share
+            places_of.append(first_row // tile + t)
             tiles.append([])
             for j, (first, size) in enumerate(parts):
                 low, high = max(first, t * tile), min(first + size, (t + 1) * tile)
@@ -659,19 +762,66 @@
                     if (shift, j) not in chunks:
                         chunks.append((shift, j))
                     tiles[-1].append((chunks.index((shift, j)), low - first, high - low))
-        pieces = [turned[j][shift - 1] if shift else crossed[j] for shift, j in chunks]
+        return places_of, [turned[j][shift - 1] if shift else crossed[j] for shift, j in chunks], tiles
+
+    sums_of = {}
+
+    def begin(*named):
+        n = 2 * (n_fsdp - 2) + 1
+        at = jnp.stack(where[:n]).astype(i32)
+        places_of, chunks, tiles = collect(named)
+        got = early_sums(
+            places_of, jnp.concatenate([order, early, at]), pieces_of_kept[:n], whole, chunks, tiles, tile
+        )
+        sums_of.update(zip(named, got))
+        return got
+
+    others = range(1, n_groups)
+    ahead = line and share > tile
+    begun = begin((0, 0), (0, 1), *[(g, 0) for g in others]) if ahead else []
+    past = [other, *begun, *flat(*crossed, *sum(turned, []))]
+    third = hop(*past, low=height)
+    cross(*past)
+    turn(*past)
+    if direct:
+        turned.append(direct)
+    live = behind(island_live_rows, *past)
+    low_terms, high_terms, coef = block_terms(live, total, other, hidden, output_gradient)
+    far_low = swap(behind(low_terms, *flat(*crossed[3:], *direct)), top)
+    fill(crossed[3:])
+    fill(direct)
+    past = [coef, *third, *flat(*crossed, *sum(turned, []))]
+    far_high = swap(behind(high_terms, *past), top)
+    fill(crossed[2:3], *past)
+    for pieces in turned[1:2]:
+        fill(pieces, *past)
+    if line:
+        at = jnp.stack(where).astype(i32)
+    else:
+        pieces_of_kept = [(lax.all_gather(output_gradient, "fsdp", axis=1, tiled=True), 0)]
+        at = jnp.zeros((1,), i32)
+
+    relative = [both_slots[r][:count] for r in near] + [both_slots[r][count:] for r in near]
+    relative = jnp.concatenate(relative) - me * local
+
+    scalars = jnp.concatenate([order, early, at, island_live_rows])
+    grad_hidden = token = None
+
+    def multiply(*named):
+        nonlocal grad_hidden, token
+        named = sorted(named, key=lambda name: name not in sums_of)
+        places_of, chunks, tiles = collect(named)
         grad_hidden, token = base(
-            places, scalars, pieces_of_kept, whole, pieces, tiles, tile, coef, block_a,
-            grad_hidden, token,
+            places_of, scalars, pieces_of_kept, whole, chunks, tiles, tile,
+            [sums_of[name] for name in named if name in sums_of], coef, block_a, grad_hidden, token,
         )
 
-    others = range(1, n_groups)
     if share > tile:
-        multiply(*[(0, t) for t in range(4)], *[(g, 0) for g in others])
+        multiply(*[(0, t) for t in range(4)], *[(g, t) for g in others for t in range(2)])
         past = [token, far_high]
-        for pieces in turned[1:]:
+        for pieces in turned[2:3]:
             fill(pieces, *past)
-        multiply(*[(g, t) for g in others for t in range(1, 4)])
+        multiply(*[(g, t) for g in others for t in range(2, 4)])
     else:
         multiply(*[(g, 0) for g in range(n_groups)])
 

time: 250 us -> 260 us (1.040)
  waiting for transfers between devices: 109 us -> 95.1 us
  Pallas kernels: 75.5 us -> 85.1 us
  starting transfers between devices: 44.7 us -> 53.6 us
  local copies, waits for them, and re-layouts: 11.6 us -> 19.1 us
    ppermute x8, waiting for transfers between devices: 28.6 us -> 17.2 us  [hop(): sent.append(lax.ppermute(piece, 'fsdp', pairs))]
    pallas_call x2 -> x3, Pallas kernels: 45.2 us -> 55.8 us  [the longest x2 37.2 us: base(): pl.pallas_call(functools.partial(base_kernel, n_dp, tiles, len(chunks), [...]
    ppermute x26 -> x27, starting transfers between devices: 18.8 us -> 28.9 us  [swap(): return lax.ppermute(value, axis, [(i, i ^ bit) for i in range(size)])]
    ppermute x4 -> x3, waiting for transfers between devices: 27.8 us -> 19.1 us  [turn(): turned[j].append({top: lax.ppermute(piece, 'groups', ring)})]
    ppermute x26 -> x27, waiting for transfers between devices: 53 us -> 58.8 us  [swap(): return lax.ppermute(value, axis, [(i, i ^ bit) for i in range(size)])]
    unnamed x36 -> x38, local copies, waits for them, and re-layouts: 2.04 us -> 6.18 us
    dynamic_slice x1 -> x3, local copies, waits for them, and re-layouts: 4.31 us -> 7.02 us  [piece_of(): lax.dynamic_slice_in_dim(frozen_down_weight, owner * share + first_row, s...]
  transfers between devices with their start and end apart: 38 -> 38, of which waited for: 22 -> 19; matrix products, arithmetic and copies ran while one was open for 6% -> 7% of each run, Pallas kernels for 28% -> 30%
where the time goes in v7:
time: 260 us; the launch traced here: 259 us
  waiting for transfers between devices  95.1 us (37%)
  Pallas kernels  85.1 us (33%)
  starting transfers between devices  53.6 us (21%)
  local copies, waits for them, and re-layouts  19.1 us (7%)
  other arithmetic  4.87 us (2%)
    ppermute x27, waiting for transfers between devices, swap(): return lax.ppermute(value, axis, [(i, i ^ bit) for i in range(size)])  58.8 us
    pallas_call x2, Pallas kernels, base(): pl.pallas_call(functools.partial(base_kernel, n_dp, tiles, len(chunks), [...  37.2 us
    ppermute x27, starting transfers between devices, swap(): return lax.ppermute(value, axis, [(i, i ^ bit) for i in range(size)])  28.9 us
    ppermute x8, starting transfers between devices, hop(): sent.append(lax.ppermute(piece, 'fsdp', pairs))  22.6 us
    ppermute x3, waiting for transfers between devices, turn(): turned[j].append({top: lax.ppermute(piece, 'groups', ring)})  19.1 us
    pallas_call x1, Pallas kernels, early_sums(): pl.pallas_call(functools.partial(early_kernel, n_dp, tiles, len(chunks),...  18.6 us
    ppermute x8, waiting for transfers between devices, hop(): sent.append(lax.ppermute(piece, 'fsdp', pairs))  17.2 us
    pallas_call x1, Pallas kernels, project(): pl.pallas_call(functools.partial(project_kernel, pieces), grid_spec=pltpu...  10.4 us
  transfers between devices with their start and end apart: 38, of which 19 were waited for; matrix products, arithmetic and copies ran while one was open for 7% of the time, Pallas kernels for 30%

profile of v7, /device:TPU:11, one launch (start us, length us, event | category | flops | bytes accessed | tf_op | source)
XLA Modules:
  0.0 258.8 jit_solution(11192401983316754515)
XLA Ops:
  0.6 0.7 collective-permute-start.3
  1.4 3.2 %collective-permute-start = (bf16[768,1024]{1,0:T(8,128)(2,1)}, bf16[768,1024]{1,0:T(8,128)(2,1)}, u32[]{:S(2)}, u32[]{:S(2)}) collective-permute-start(bf16[768,1024]{1,0:T(8,128)(2,1)} %refs_0_.5), channel_id=1, source_target_pairs={{0,4},{4,8},{8,12},{1,5},{5,9},{9,13},{2,6},{6,10},{10,14},{3,7},{... | collective-permute-start | bytes 4718600 | tf_op jit(solution)/shard_map/ppermute | solution.py:648
  4.6 3.2 %collective-permute-start.1 = (bf16[768,1024]{1,0:T(8,128)(2,1)}, bf16[768,1024]{1,0:T(8,128)(2,1)S(1)}, u32[]{:S(2)}, u32[]{:S(2)}) collective-permute-start(bf16[768,1024]{1,0:T(8,128)(2,1)} %refs_0_.5), channel_id=1, source_target_pairs={{4,0},{8,4},{12,8},{5,1},{9,5},{13,9},{6,2},{10,6},{14,10},{7,3},{... | collective-permute-start | bytes 4718600 | tf_op jit(solution)/shard_map/ppermute | solution.py:648
  7.8 0.9 select_reduce_fusion
  9.0 0.9 collective-permute-start.4
  9.8 2.3 constant_dynamic-slice_fusion.4
  12.1 1.2 collective-permute-start.6
  14.5 1.1 copy-done.10
  15.6 4.8 %shard_map.103 = bf16[3,64,5120]{2,1,0:T(8,128)(2,1)} custom-call(s32[6]{0:T(128)} %pad_add_fusion.index_ref, s32[3]{0:T(128)} %get-tuple-element.105.source_ref, bf16[8,64,4096]{2,1,0:T(8,128)(2,1)} %bitcast.26, bf16[8,64,4096]{2,1,0:T(8,128)(2,1)} %collective-permute-done.3.refs_1_, bf16[8,64,1024]{2,1,0:T(8,128)(2,1)} %refs_2_.3, ...), custom_call_target="tpu_custom_call" | custom-call | bytes 5898240 | tf_op jit(solution)/shard_map/pallas_call | solution.py:54
  20.6 15.7 %collective-permute-done.6.refs_7_.refs_11_ = bf16[512,1024]{1,0:T(8,128)(2,1)} collective-permute-done((bf16[512,1024]{1,0:T(8,128)(2,1)}, bf16[512,1024]{1,0:T(8,128)(2,1)}, u32[]{:S(2)}, u32[]{:S(2)}) %collective-permute-start.6) | collective-permute-done | bytes 1048608 | tf_op jit(solution)/shard_map/ppermute | solution.py:616
  36.4 3.2 %collective-permute-done.refs_1_ = bf16[768,1024]{1,0:T(8,128)(2,1)} collective-permute-done((bf16[768,1024]{1,0:T(8,128)(2,1)}, bf16[768,1024]{1,0:T(8,128)(2,1)}, u32[]{:S(2)}, u32[]{:S(2)}) %collective-permute-start) | collective-permute-done | bytes 1572896 | tf_op jit(solution)/shard_map/ppermute | solution.py:648
  39.6 2.8 %collective-permute-done.1.refs_2_ = bf16[768,1024]{1,0:T(8,128)(2,1)S(1)} collective-permute-done((bf16[768,1024]{1,0:T(8,128)(2,1)}, bf16[768,1024]{1,0:T(8,128)(2,1)S(1)}, u32[]{:S(2)}, u32[]{:S(2)}) %collective-permute-start.1) | collective-permute-done | bytes 1572896 | tf_op jit(solution)/shard_map/ppermute | solution.py:648
  42.4 1.1 collective-permute-start.13
  43.8 3.2 %collective-permute-start.7 = (bf16[768,1024]{1,0:T(8,128)(2,1)}, bf16[768,1024]{1,0:T(8,128)(2,1)S(1)}, u32[]{:S(2)}, u32[]{:S(2)}) collective-permute-start(bf16[768,1024]{1,0:T(8,128)(2,1)} %collective-permute-done.refs_1_), channel_id=1, source_target_pairs={{0,4},{4,8},{8,12},{1,5},{5,9},{9,13},{2,6},{6,10},{10,14},{3,7},{... | collective-permute-start | bytes 4718600 | tf_op jit(solution)/shard_map/ppermute | solution.py:648
  47.0 2.2 collective-permute-start.8
  49.2 1.3 collective-permute-start.10
  50.5 3.4 %constant_dynamic-slice_fusion.2 = (bf16[640,1024]{1,0:T(8,128)(2,1)}, bf16[640,1024]{1,0:T(8,128)(2,1)}) fusion(bf16[4096,1024]{1,0:T(8,128)(2,1)} %refs_9_.1, s32[]{:T(128)S(6)} %select_n.99, s32[]{:T(128)S(6)} %select_n.98), kind=kLoop, calls=%fused_computation.9 | loop fusion | bytes 5242888 | tf_op jit(solution)/shard_map/dynamic_slice | solution.py:677
  53.9 18.3 %collective-permute-done.10.refs_11_.refs_15_ = bf16[512,1024]{1,0:T(8,128)(2,1)} collective-permute-done((bf16[512,1024]{1,0:T(8,128)(2,1)}, bf16[512,1024]{1,0:T(8,128)(2,1)}, u32[]{:S(2)}, u32[]{:S(2)}) %collective-permute-start.10) | collective-permute-done | bytes 1048608 | tf_op jit(solution)/shard_map/ppermute | solution.py:698
  72.2 8.2 %collective-permute-done.7.refs_3_ = bf16[768,1024]{1,0:T(8,128)(2,1)S(1)} collective-permute-done((bf16[768,1024]{1,0:T(8,128)(2,1)}, bf16[768,1024]{1,0:T(8,128)(2,1)S(1)}, u32[]{:S(2)}, u32[]{:S(2)}) %collective-permute-start.7) | collective-permute-done | bytes 1572896 | tf_op jit(solution)/shard_map/ppermute | solution.py:648
  80.5 2.9 %collective-permute-done.8.refs_4_ = bf16[768,1024]{1,0:T(8,128)(2,1)S(1)} collective-permute-done((bf16[768,1024]{1,0:T(8,128)(2,1)}, bf16[768,1024]{1,0:T(8,128)(2,1)S(1)}, u32[]{:S(2)}, u32[]{:S(2)}) %collective-permute-start.8) | collective-permute-done | bytes 1572896 | tf_op jit(solution)/shard_map/ppermute | solution.py:648
  83.4 3.6 %collective-permute-done.9.refs_4_ = bf16[3,64,5120]{2,1,0:T(8,128)(2,1)} collective-permute-done((bf16[3,64,5120]{2,1,0:T(8,128)(2,1)}, bf16[3,64,5120]{2,1,0:T(8,128)(2,1)}, u32[]{:S(2)}, u32[]{:S(2)}) %collective-permute-start.9) | collective-permute-done | bytes 1966112 | tf_op jit(solution)/shard_map/ppermute | solution.py:616
  87.3 0.8 slice.32
  88.1 0.9 slice.33
  89.0 3.2 %collective-permute-start.11 = (bf16[256,1024]{1,0:T(8,128)(2,1)}, bf16[256,1024]{1,0:T(8,128)(2,1)S(1)}, u32[]{:S(2)}, u32[]{:S(2)}) collective-permute-start(bf16[256,1024]{1,0:T(8,128)(2,1)} %slice.32), channel_id=1, source_target_pairs={{0,4},{4,8},{8,12},{1,5},{5,9},{9,13},{2,6},{6,10},{10,14},{3,7},{... | collective-permute-start | bytes 1572872 | tf_op jit(solution)/shard_map/ppermute | solution.py:648
  92.2 2.1 collective-permute-start.12
  95.5 10.4 %shard_map.104 = (f32[3,256,128]{2,1,0:T(8,128)}, bf16[3,64,4096]{2,1,0:T(8,128)(2,1)}, f32[8,64,4096]{2,1,0:T(8,128)}, f32[8,64,1024]{2,1,0:T(8,128)}) custom-call(s32[6]{0:T(128)} %pad_add_fusion.2.index_ref, s32[3]{0:T(128)} %get-tuple-element.103.source_ref, bf16[8,64,4096]{2,1,0:T(8,128)(2,1)} %bitcast.27, ...), custom_call_target="tpu_custom_call" | custom-call | flops 503316480 | bytes 15728640 | tf_op jit(solution)/shard_map/pallas_call | solution.py:121
  106.0 7.2 %collective-permute-done.14 = f32[3,256,128]{2,1,0:T(8,128)S(1)} collective-permute-done((f32[3,256,128]{2,1,0:T(8,128)}, f32[3,256,128]{2,1,0:T(8,128)S(1)}, u32[]{:S(2)}, u32[]{:S(2)}) %collective-permute-start.14) | collective-permute-done | bytes 393248 | tf_op jit(solution)/shard_map/ppermute | solution.py:616
  113.2 1.0 add.126.here_ref
  114.3 1.2 collective-permute-done.16.refs_9_.refs_13_
  115.6 3.7 %collective-permute-start.17 = (bf16[512,1024]{1,0:T(8,128)(2,1)}, bf16[512,1024]{1,0:T(8,128)(2,1)}, u32[]{:S(2)}, u32[]{:S(2)}) collective-permute-start(bf16[512,1024]{1,0:T(8,128)(2,1)} %collective-permute-done.6.refs_7_.refs_11_), channel_id=1, source_target_pairs={{0,1},{1,0},{2,3},{3,2},{4,5},{5,4},{6,7},{7,6},{8,9},{9,8},{10,11... | collective-permute-start | bytes 3145736 | tf_op jit(solution)/shard_map/ppermute | solution.py:616
  119.4 2.1 collective-permute-start.20
  121.8 1.2 collective-permute-start.19
  123.1 1.5 collective-permute-start.15
  125.7 1.1 copy-done.6
  126.7 18.6 %shard_map.105 = (f32[768,512]{1,0:T(8,128)}, f32[768,512]{1,0:T(8,128)}, f32[768,512]{1,0:T(8,128)}) custom-call(s32[16]{0:T(128)} %concatenate.30.scalars_ref, bf16[768,1024]{1,0:T(8,128)(2,1)} %refs_0_.5, bf16[768,1024]{1,0:T(8,128)(2,1)} %collective-permute-done.refs_1_, bf16[768,1024]{1,0:T(8,128)(2,1)} %copy-done.4, bf16[768,1024]{1,0:T(8,128)(2,1)} %copy-done, ...), custom_call_target="tpu_custom_call" | custom-call | flops 1 | bytes 1 | tf_op jit(solution)/shard_map/pallas_call | solution.py:444
  145.4 4.9 %collective-permute-done.20.refs_17_ = bf16[640,1024]{1,0:T(8,128)(2,1)} collective-permute-done((bf16[640,1024]{1,0:T(8,128)(2,1)}, bf16[640,1024]{1,0:T(8,128)(2,1)}, u32[]{:S(2)}, u32[]{:S(2)}) %collective-permute-start.20) | collective-permute-done | bytes 1310752 | tf_op jit(solution)/shard_map/ppermute | solution.py:616
  150.3 0.8 collective-permute-done.21.refs_21_.refs_11_
  151.5 1.3 constant_dynamic-slice_fusion
  152.9 1.0 slice.34
  153.9 0.7 copy-done.3
  154.6 1.1 slice.35
  155.7 3.2 %collective-permute-start.22 = (bf16[512,1024]{1,0:T(8,128)(2,1)}, bf16[512,1024]{1,0:T(8,128)(2,1)S(1)}, u32[]{:S(2)}, u32[]{:S(2)}) collective-permute-start(bf16[512,1024]{1,0:T(8,128)(2,1)} %slice.34), channel_id=1, source_target_pairs={{0,4},{4,8},{8,12},{1,5},{5,9},{9,13},{2,6},{6,10},{10,14},{3,7},{... | collective-permute-start | bytes 3145736 | tf_op jit(solution)/shard_map/ppermute | solution.py:648
  158.9 2.3 collective-permute-start.23
  161.2 0.7 collective-permute-start.24
  161.9 0.9 collective-permute-start.27
  162.8 9.5 %collective-permute-done.24.refs_19_ = bf16[256,1024]{1,0:T(8,128)(2,1)} collective-permute-done((bf16[256,1024]{1,0:T(8,128)(2,1)S(1)}, bf16[256,1024]{1,0:T(8,128)(2,1)}, u32[]{:S(2)}, u32[]{:S(2)}) %collective-permute-start.24) | collective-permute-done | bytes 524320 | tf_op jit(solution)/shard_map/ppermute | solution.py:616
  172.3 6.5 %collective-permute-start.25 = (bf16[256,1024]{1,0:T(8,128)(2,1)}, bf16[256,1024]{1,0:T(8,128)(2,1)}, u32[]{:S(2)}, u32[]{:S(2)}) collective-permute-start(bf16[256,1024]{1,0:T(8,128)(2,1)} %collective-permute-done.24.refs_19_), channel_id=1, source_target_pairs={{0,1},{1,0},{2,3},{3,2},{4,5},{5,4},{6,7},{7,6},{8,9},{9,8},{10,11... | collective-permute-start | bytes 1572872 | tf_op jit(solution)/shard_map/ppermute | solution.py:616
  178.8 4.6 %collective-permute-done.27.refs_15_ = bf16[256,1024]{1,0:T(8,128)(2,1)S(1)} collective-permute-done((bf16[256,1024]{1,0:T(8,128)(2,1)S(1)}, bf16[256,1024]{1,0:T(8,128)(2,1)S(1)}, u32[]{:S(2)}, u32[]{:S(2)}) %collective-permute-start.27) | collective-permute-done | bytes 524320 | tf_op jit(solution)/shard_map/ppermute | solution.py:616
  183.4 3.4 %collective-permute-start.28 = (bf16[256,1024]{1,0:T(8,128)(2,1)S(1)}, bf16[256,1024]{1,0:T(8,128)(2,1)}, u32[]{:S(2)}, u32[]{:S(2)}) collective-permute-start(bf16[256,1024]{1,0:T(8,128)(2,1)S(1)} %collective-permute-done.27.refs_15_), channel_id=1, source_target_pairs={{0,1},{1,0},{2,3},{3,2},{4,5},{5,4},{6,7},{7,6},{8,9},{9,8},{10,11... | collective-permute-start | bytes 1572872 | tf_op jit(solution)/shard_map/ppermute | solution.py:616
  186.9 6.9 %shard_map.106 = (bf16[3,64,1664]{2,1,0:T(8,128)(2,1)}, bf16[3,64,3456]{2,1,0:T(8,128)(2,1)}, bf16[3,256,64]{2,1,0:T(8,128)(2,1)}) custom-call(s32[3]{0:T(128)} %live_ref, f32[3,256,128]{2,1,0:T(8,128)} %copy-done.12, f32[3,256,128]{2,1,0:T(8,128)} %collective-permute-done.15.there_ref, bf16[768,4096]{1,0:T(8,128)(2,1)} %hid_ref.1, bf16[768,1024]{1,0:T(8,128)(2,1)} %refs_0_.5), custom_call_target="tpu_custom_call" | custom-call | flops 503316480 | bytes 9830400 | tf_op jit(solution)/shard_map/pallas_call | solution.py:186
  193.9 0.9 copy-done.8
  196.3 0.6 concatenate.31.scalars_ref
  196.9 1.9 collective-permute-done.29.refs_22_.refs_12_
  198.8 2.2 collective-permute-done.30.refs_18_
  201.0 21.7 %shard_map.107 = (bf16[768,4096]{1,0:T(8,128)(2,1)}, f32[8,128]{1,0:T(8,128)}) custom-call(s32[26]{0:T(128)} %concatenate.31.scalars_ref, bf16[768,1024]{1,0:T(8,128)(2,1)} %refs_0_.5, bf16[768,1024]{1,0:T(8,128)(2,1)} %collective-permute-done.refs_1_, bf16[768,1024]{1,0:T(8,128)(2,1)} %copy-done.4, bf16[768,1024]{1,0:T(8,128)(2,1)} %copy-done, ...), custom_call_target="tpu_custom_call" | custom-call | flops 1 | bytes 1 | tf_op jit(solution)/shard_map/pallas_call | solution.py:479
  222.8 3.5 %collective-permute-done.31.refs_5_ = bf16[3,64,3456]{2,1,0:T(8,128)(2,1)} collective-permute-done((bf16[3,64,3456]{2,1,0:T(8,128)(2,1)}, bf16[3,64,3456]{2,1,0:T(8,128)(2,1)}, u32[]{:S(2)}, u32[]{:S(2)}) %collective-permute-start.31) | collective-permute-done | bytes 1327136 | tf_op jit(solution)/shard_map/ppermute | solution.py:616
  226.3 0.8 collective-permute-start.32
  228.2 0.7 concatenate.26.scalars_ref
  229.1 2.6 %collective-permute-done.32.refs_14_ = bf16[640,1024]{1,0:T(8,128)(2,1)S(1)} collective-permute-done((bf16[640,1024]{1,0:T(8,128)(2,1)}, bf16[640,1024]{1,0:T(8,128)(2,1)S(1)}, u32[]{:S(2)}, u32[]{:S(2)}) %collective-permute-start.32) | collective-permute-done | bytes 1310752 | tf_op jit(solution)/shard_map/ppermute | solution.py:616
  231.7 1.1 copy-done.14
  232.8 15.5 %shard_map.108 = (bf16[768,4096]{1,0:T(8,128)(2,1)}, f32[8,128]{1,0:T(8,128)}) custom-call(s32[22]{0:T(128)} %concatenate.26.scalars_ref, bf16[768,1024]{1,0:T(8,128)(2,1)} %refs_0_.5, bf16[768,1024]{1,0:T(8,128)(2,1)} %collective-permute-done.refs_1_, bf16[768,1024]{1,0:T(8,128)(2,1)} %copy-done.4, ...), custom_call_target="tpu_custom_call", output_to_operand_aliasing={{0}: (21, {})} | custom-call | flops 1 | bytes 1 | tf_op jit(solution)/shard_map/pallas_call | solution.py:479
  249.5 1.1 collective-permute-done.36.refs_6_
  250.7 0.8 copy-done.16
  251.5 7.1 %shard_map.109 = (f32[8,64,4096]{2,1,0:T(8,128)}, f32[8,64,1024]{2,1,0:T(8,128)}) custom-call(s32[12]{0:T(128)} %add_subtract_fusion.slots_ref, bf16[3,64,1664]{2,1,0:T(8,128)(2,1)} %get-tuple-element.87.refs_0_, bf16[3,64,3456]{2,1,0:T(8,128)(2,1)} %get-tuple-element.86.refs_1_, ...), custom_call_target="tpu_custom_call", output_to_operand_aliasing={{0}: (10, {}), {1}: (11, {})} | custom-call | flops 1 | bytes 1 | tf_op jit(solution)/shard_map/pallas_call | solution.py:568
  (77 shorter events, 9.8 us)
Async XLA Ops:
  0.6 13.9 %collective-permute-start.3 = (bf16[8,64,4096]{2,1,0:T(8,128)(2,1)}, bf16[8,64,4096]{2,1,0:T(8,128)(2,1)}, u32[]{:S(2)}, u32[]{:S(2)}) collective-permute-start(bf16[8,64,4096]{2,1,0:T(8,128)(2,1)} %bitcast.25), channel_id=1, source_target_pairs={{0,1},{1,0},{2,3},{3,2},{4,5},{5,4},{6,7},{7,6},{8,9},{9,8},{10,11... | collective-permute-start | bytes 12582920 | tf_op jit(solution)/shard_map/ppermute | solution.py:616
  1.4 38.2 %collective-permute-start = (bf16[768,1024]{1,0:T(8,128)(2,1)}, bf16[768,1024]{1,0:T(8,128)(2,1)}, u32[]{:S(2)}, u32[]{:S(2)}) collective-permute-start(bf16[768,1024]{1,0:T(8,128)(2,1)} %refs_0_.5), channel_id=1, source_target_pairs={{0,4},{4,8},{8,12},{1,5},{5,9},{9,13},{2,6},{6,10},{10,14},{3,7},{... | collective-permute-start | bytes 4718600 | tf_op jit(solution)/shard_map/ppermute | solution.py:648
  4.6 37.8 %collective-permute-start.1 = (bf16[768,1024]{1,0:T(8,128)(2,1)}, bf16[768,1024]{1,0:T(8,128)(2,1)S(1)}, u32[]{:S(2)}, u32[]{:S(2)}) collective-permute-start(bf16[768,1024]{1,0:T(8,128)(2,1)} %refs_0_.5), channel_id=1, source_target_pairs={{4,0},{8,4},{12,8},{5,1},{9,5},{13,9},{6,2},{10,6},{14,10},{7,3},{... | collective-permute-start | bytes 4718600 | tf_op jit(solution)/shard_map/ppermute | solution.py:648
  8.7 3.4 %collective-permute-start.2 = (s32[3]{0:T(128)S(1)}, s32[3]{0:T(128)S(1)}, u32[]{:S(2)}, u32[]{:S(2)}) collective-permute-start(s32[3]{0:T(128)S(1)} %select_reduce_fusion), channel_id=1, source_target_pairs={{0,2},{1,3},{2,0},{3,1},{4,6},{5,7},{6,4},{7,5},{8,10},{9,11},{10,... | collective-permute-start | bytes 44 | tf_op jit(solution)/shard_map/ppermute | solution.py:616
  9.0 5.5 %collective-permute-start.4 = (bf16[8,64,1024]{2,1,0:T(8,128)(2,1)}, bf16[8,64,1024]{2,1,0:T(8,128)(2,1)S(1)}, u32[]{:S(2)}, u32[]{:S(2)}) collective-permute-start(bf16[8,64,1024]{2,1,0:T(8,128)(2,1)} %refs_2_.3), channel_id=1, source_target_pairs={{0,1},{1,0},{2,3},{3,2},{4,5},{5,4},{6,7},{7,6},{8,9},{9,8},{10,11... | collective-permute-start | bytes 3145736 | tf_op jit(solution)/shard_map/ppermute | solution.py:616
  12.1 24.3 %collective-permute-start.6 = (bf16[512,1024]{1,0:T(8,128)(2,1)}, bf16[512,1024]{1,0:T(8,128)(2,1)}, u32[]{:S(2)}, u32[]{:S(2)}) collective-permute-start(bf16[512,1024]{1,0:T(8,128)(2,1)} %constant_dynamic-slice_fusion.4), channel_id=1, source_target_pairs={{0,2},{1,3},{2,0},{3,1},{4,6},{5,7},{6,4},{7,5},{8,10},{9,11},{10,... | collective-permute-start | bytes 3145736 | tf_op jit(solution)/shard_map/ppermute | solution.py:616
  14.5 1.1 copy-start.10
  20.4 22.0 %collective-permute-start.5 = (s32[6]{0:T(128)S(1)}, s32[6]{0:T(128)S(1)}, u32[]{:S(2)}, u32[]{:S(2)}) collective-permute-start(s32[6]{0:T(128)S(1)} %pad_add_fusion.1), channel_id=1, source_target_pairs={{0,1},{1,0},{2,3},{3,2},{4,5},{5,4},{6,7},{7,6},{8,9},{9,8},{10,11... | collective-permute-start | bytes 80 | tf_op jit(solution)/shard_map/ppermute | solution.py:616
  42.4 1.2 copy-start.4
  42.4 52.0 %collective-permute-start.13 = (bf16[4096,1024]{1,0:T(8,128)(2,1)}, bf16[4096,1024]{1,0:T(8,128)(2,1)}, u32[]{:S(2)}, u32[]{:S(2)}) collective-permute-start(bf16[4096,1024]{1,0:T(8,128)(2,1)} %refs_9_.1), channel_id=1, source_target_pairs={{0,1},{1,0},{2,3},{3,2},{4,5},{5,4},{6,7},{7,6},{8,9},{9,8},{10,11... | collective-permute-start | bytes 25165832 | tf_op jit(solution)/shard_map/ppermute | solution.py:616
  43.5 43.5 %collective-permute-start.9 = (bf16[3,64,5120]{2,1,0:T(8,128)(2,1)}, bf16[3,64,5120]{2,1,0:T(8,128)(2,1)}, u32[]{:S(2)}, u32[]{:S(2)}) collective-permute-start(bf16[3,64,5120]{2,1,0:T(8,128)(2,1)} %shard_map.103), channel_id=1, source_target_pairs={{0,2},{1,3},{2,0},{3,1},{4,6},{5,7},{6,4},{7,5},{8,10},{9,11},{10,... | collective-permute-start | bytes 5898248 | tf_op jit(solution)/shard_map/ppermute | solution.py:616
  43.8 36.7 %collective-permute-start.7 = (bf16[768,1024]{1,0:T(8,128)(2,1)}, bf16[768,1024]{1,0:T(8,128)(2,1)S(1)}, u32[]{:S(2)}, u32[]{:S(2)}) collective-permute-start(bf16[768,1024]{1,0:T(8,128)(2,1)} %collective-permute-done.refs_1_), channel_id=1, source_target_pairs={{0,4},{4,8},{8,12},{1,5},{5,9},{9,13},{2,6},{6,10},{10,14},{3,7},{... | collective-permute-start | bytes 4718600 | tf_op jit(solution)/shard_map/ppermute | solution.py:648
  47.0 36.4 %collective-permute-start.8 = (bf16[768,1024]{1,0:T(8,128)(2,1)}, bf16[768,1024]{1,0:T(8,128)(2,1)S(1)}, u32[]{:S(2)}, u32[]{:S(2)}) collective-permute-start(bf16[768,1024]{1,0:T(8,128)(2,1)} %copy-done.4), channel_id=1, source_target_pairs={{4,0},{8,4},{12,8},{5,1},{9,5},{13,9},{6,2},{10,6},{14,10},{7,3},{... | collective-permute-start | bytes 4718600 | tf_op jit(solution)/shard_map/ppermute | solution.py:648
  49.2 23.1 %collective-permute-start.10 = (bf16[512,1024]{1,0:T(8,128)(2,1)}, bf16[512,1024]{1,0:T(8,128)(2,1)}, u32[]{:S(2)}, u32[]{:S(2)}) collective-permute-start(bf16[512,1024]{1,0:T(8,128)(2,1)} %collective-permute-done.6.refs_7_.refs_11_), channel_id=1, source_target_pairs={{0,16},{16,0},{1,17},{17,1},{2,18},{18,2},{3,19},{19,3},{4,20},{20... | collective-permute-start | bytes 3145736 | tf_op jit(solution)/shard_map/ppermute | solution.py:698
  80.5 25.5 %copy-start = (bf16[768,1024]{1,0:T(8,128)(2,1)}, bf16[768,1024]{1,0:T(8,128)(2,1)S(1)}, u32[]{:S(2)}) copy-start(bf16[768,1024]{1,0:T(8,128)(2,1)S(1)} %collective-permute-done.7.refs_3_) | copy-start | bytes 4718596
  83.4 22.5 %copy-start.2 = (bf16[768,1024]{1,0:T(8,128)(2,1)}, bf16[768,1024]{1,0:T(8,128)(2,1)S(1)}, u32[]{:S(2)}) copy-start(bf16[768,1024]{1,0:T(8,128)(2,1)S(1)} %collective-permute-done.8.refs_4_) | copy-start | bytes 4718596
  87.0 28.5 %collective-permute-start.16 = (bf16[640,1024]{1,0:T(8,128)(2,1)}, bf16[640,1024]{1,0:T(8,128)(2,1)}, u32[]{:S(2)}, u32[]{:S(2)}) collective-permute-start(bf16[640,1024]{1,0:T(8,128)(2,1)} %get-tuple-element.60), channel_id=1, source_target_pairs={{0,2},{1,3},{2,0},{3,1},{4,6},{5,7},{6,4},{7,5},{8,10},{9,11},{10,... | collective-permute-start | bytes 3932168 | tf_op jit(solution)/shard_map/ppermute | solution.py:616
  89.0 25.3 %collective-permute-start.11 = (bf16[256,1024]{1,0:T(8,128)(2,1)}, bf16[256,1024]{1,0:T(8,128)(2,1)S(1)}, u32[]{:S(2)}, u32[]{:S(2)}) collective-permute-start(bf16[256,1024]{1,0:T(8,128)(2,1)} %slice.32), channel_id=1, source_target_pairs={{0,4},{4,8},{8,12},{1,5},{5,9},{9,13},{2,6},{6,10},{10,14},{3,7},{... | collective-permute-start | bytes 1572872 | tf_op jit(solution)/shard_map/ppermute | solution.py:648
  92.2 22.1 %collective-permute-start.12 = (bf16[256,1024]{1,0:T(8,128)(2,1)}, bf16[256,1024]{1,0:T(8,128)(2,1)}, u32[]{:S(2)}, u32[]{:S(2)}) collective-permute-start(bf16[256,1024]{1,0:T(8,128)(2,1)} %slice.33), channel_id=1, source_target_pairs={{4,0},{8,4},{12,8},{5,1},{9,5},{13,9},{6,2},{10,6},{14,10},{7,3},{... | collective-permute-start | bytes 1572872 | tf_op jit(solution)/shard_map/ppermute | solution.py:648
  105.9 7.3 %collective-permute-start.14 = (f32[3,256,128]{2,1,0:T(8,128)}, f32[3,256,128]{2,1,0:T(8,128)S(1)}, u32[]{:S(2)}, u32[]{:S(2)}) collective-permute-start(f32[3,256,128]{2,1,0:T(8,128)} %get-tuple-element.59), channel_id=1, source_target_pairs={{0,4},{4,0},{8,12},{12,8},{1,5},{5,1},{9,13},{13,9},{2,6},{6,2},{1... | collective-permute-start | bytes 1179656 | tf_op jit(solution)/shard_map/ppermute | solution.py:616
  114.3 31.1 %copy-start.12 = (f32[3,256,128]{2,1,0:T(8,128)}, f32[3,256,128]{2,1,0:T(8,128)S(1)}, u32[]{:S(2)}) copy-start(f32[3,256,128]{2,1,0:T(8,128)S(1)} %add.126.here_ref) | copy-start | bytes 1179652
  114.3 5.1 %copy-start.11 = (bf16[256,1024]{1,0:T(8,128)(2,1)}, bf16[256,1024]{1,0:T(8,128)(2,1)S(1)}, u32[]{:S(2)}) copy-start(bf16[256,1024]{1,0:T(8,128)(2,1)S(1)} %collective-permute-done.11.refs_5_) | copy-start | bytes 1572868
  115.6 7.5 %collective-permute-start.17 = (bf16[512,1024]{1,0:T(8,128)(2,1)}, bf16[512,1024]{1,0:T(8,128)(2,1)}, u32[]{:S(2)}, u32[]{:S(2)}) collective-permute-start(bf16[512,1024]{1,0:T(8,128)(2,1)} %collective-permute-done.6.refs_7_.refs_11_), channel_id=1, source_target_pairs={{0,1},{1,0},{2,3},{3,2},{4,5},{5,4},{6,7},{7,6},{8,9},{9,8},{10,11... | collective-permute-start | bytes 3145736 | tf_op jit(solution)/shard_map/ppermute | solution.py:616
  119.3 6.4 %collective-permute-start.18 = (bf16[640,1024]{1,0:T(8,128)(2,1)}, bf16[640,1024]{1,0:T(8,128)(2,1)S(1)}, u32[]{:S(2)}, u32[]{:S(2)}) collective-permute-start(bf16[640,1024]{1,0:T(8,128)(2,1)} %collective-permute-done.16.refs_9_.refs_13_), channel_id=1, source_target_pairs={{0,1},{1,0},{2,3},{3,2},{4,5},{5,4},{6,7},{7,6},{8,9},{9,8},{10,11... | collective-permute-start | bytes 3932168 | tf_op jit(solution)/shard_map/ppermute | solution.py:616
  119.4 30.9 %collective-permute-start.20 = (bf16[640,1024]{1,0:T(8,128)(2,1)}, bf16[640,1024]{1,0:T(8,128)(2,1)}, u32[]{:S(2)}, u32[]{:S(2)}) collective-permute-start(bf16[640,1024]{1,0:T(8,128)(2,1)} %get-tuple-element.67), channel_id=1, source_target_pairs={{0,2},{1,3},{2,0},{3,1},{4,6},{5,7},{6,4},{7,5},{8,10},{9,11},{10,... | collective-permute-start | bytes 3932168 | tf_op jit(solution)/shard_map/ppermute | solution.py:616
  121.5 29.7 %collective-permute-start.21 = (bf16[640,1024]{1,0:T(8,128)(2,1)}, bf16[640,1024]{1,0:T(8,128)(2,1)S(1)}, u32[]{:S(2)}, u32[]{:S(2)}) collective-permute-start(bf16[640,1024]{1,0:T(8,128)(2,1)} %collective-permute-done.16.refs_9_.refs_13_), channel_id=1, source_target_pairs={{0,16},{16,0},{1,17},{17,1},{2,18},{18,2},{3,19},{19,3},{4,20},{20... | collective-permute-start | bytes 3932168 | tf_op jit(solution)/shard_map/ppermute | solution.py:698
  121.8 3.8 %collective-permute-start.19 = (bf16[512,1024]{1,0:T(8,128)(2,1)}, bf16[512,1024]{1,0:T(8,128)(2,1)}, u32[]{:S(2)}, u32[]{:S(2)}) collective-permute-start(bf16[512,1024]{1,0:T(8,128)(2,1)} %collective-permute-done.10.refs_11_.refs_15_), channel_id=1, source_target_pairs={{0,1},{1,0},{2,3},{3,2},{4,5},{5,4},{6,7},{7,6},{8,9},{9,8},{10,11... | collective-permute-start | bytes 3145736 | tf_op jit(solution)/shard_map/ppermute | solution.py:616
  123.1 22.3 %collective-permute-start.15 = (f32[3,256,128]{2,1,0:T(8,128)S(1)}, f32[3,256,128]{2,1,0:T(8,128)}, u32[]{:S(2)}, u32[]{:S(2)}) collective-permute-start(f32[3,256,128]{2,1,0:T(8,128)S(1)} %add.126.here_ref), channel_id=1, source_target_pairs={{0,8},{4,12},{8,0},{12,4},{1,9},{5,13},{9,1},{13,5},{2,10},{6,14},... | collective-permute-start | bytes 1179656 | tf_op jit(solution)/shard_map/ppermute | solution.py:616
  125.7 1.1 copy-start.6
  145.4 7.5 %copy-start.1 = (bf16[768,1024]{1,0:T(8,128)(2,1)S(1)}, bf16[768,1024]{1,0:T(8,128)(2,1)}, u32[]{:S(2)}) copy-start(bf16[768,1024]{1,0:T(8,128)(2,1)} %copy-done) | copy-start | bytes 4718596
  151.1 44.7 %copy-start.5 = (bf16[640,1024]{1,0:T(8,128)(2,1)}, bf16[640,1024]{1,0:T(8,128)(2,1)S(1)}, u32[]{:S(2)}) copy-start(bf16[640,1024]{1,0:T(8,128)(2,1)S(1)} %collective-permute-done.21.refs_21_.refs_11_) | copy-start | bytes 3932164
  151.1 42.7 %collective-permute-start.26 = (bf16[640,1024]{1,0:T(8,128)(2,1)}, bf16[640,1024]{1,0:T(8,128)(2,1)}, u32[]{:S(2)}, u32[]{:S(2)}) collective-permute-start(bf16[640,1024]{1,0:T(8,128)(2,1)} %collective-permute-done.20.refs_17_), channel_id=1, source_target_pairs={{0,16},{16,0},{1,17},{17,1},{2,18},{18,2},{3,19},{19,3},{4,20},{20... | collective-permute-start | bytes 3932168 | tf_op jit(solution)/shard_map/ppermute | solution.py:698
  152.8 1.8 copy-start.3
  155.7 38.1 %collective-permute-start.22 = (bf16[512,1024]{1,0:T(8,128)(2,1)}, bf16[512,1024]{1,0:T(8,128)(2,1)S(1)}, u32[]{:S(2)}, u32[]{:S(2)}) collective-permute-start(bf16[512,1024]{1,0:T(8,128)(2,1)} %slice.34), channel_id=1, source_target_pairs={{0,4},{4,8},{8,12},{1,5},{5,9},{9,13},{2,6},{6,10},{10,14},{3,7},{... | collective-permute-start | bytes 3145736 | tf_op jit(solution)/shard_map/ppermute | solution.py:648
  158.9 34.9 %collective-permute-start.23 = (bf16[512,1024]{1,0:T(8,128)(2,1)}, bf16[512,1024]{1,0:T(8,128)(2,1)S(1)}, u32[]{:S(2)}, u32[]{:S(2)}) collective-permute-start(bf16[512,1024]{1,0:T(8,128)(2,1)} %slice.35), channel_id=1, source_target_pairs={{4,0},{8,4},{12,8},{5,1},{9,5},{13,9},{6,2},{10,6},{14,10},{7,3},{... | collective-permute-start | bytes 3145736 | tf_op jit(solution)/shard_map/ppermute | solution.py:648
  161.2 11.1 %collective-permute-start.24 = (bf16[256,1024]{1,0:T(8,128)(2,1)S(1)}, bf16[256,1024]{1,0:T(8,128)(2,1)}, u32[]{:S(2)}, u32[]{:S(2)}) collective-permute-start(bf16[256,1024]{1,0:T(8,128)(2,1)S(1)} %get-tuple-element.72), channel_id=1, source_target_pairs={{0,2},{1,3},{2,0},{3,1},{4,6},{5,7},{6,4},{7,5},{8,10},{9,11},{10,... | collective-permute-start | bytes 1572872 | tf_op jit(solution)/shard_map/ppermute | solution.py:616
  161.9 34.4 %copy-start.18 = (s32[3]{0:T(128)S(1)}, s32[3]{0:T(128)}, u32[]{:S(2)}) copy-start(s32[3]{0:T(128)} %live_ref) | copy-start | bytes 40
  161.9 21.5 %collective-permute-start.27 = (bf16[256,1024]{1,0:T(8,128)(2,1)S(1)}, bf16[256,1024]{1,0:T(8,128)(2,1)S(1)}, u32[]{:S(2)}, u32[]{:S(2)}) collective-permute-start(bf16[256,1024]{1,0:T(8,128)(2,1)S(1)} %get-tuple-element.74), channel_id=1, source_target_pairs={{0,2},{1,3},{2,0},{3,1},{4,6},{5,7},{6,4},{7,5},{8,10},{9,11},{10,... | collective-permute-start | bytes 1572872 | tf_op jit(solution)/shard_map/ppermute | solution.py:616
  172.3 21.5 %collective-permute-start.25 = (bf16[256,1024]{1,0:T(8,128)(2,1)}, bf16[256,1024]{1,0:T(8,128)(2,1)}, u32[]{:S(2)}, u32[]{:S(2)}) collective-permute-start(bf16[256,1024]{1,0:T(8,128)(2,1)} %collective-permute-done.24.refs_19_), channel_id=1, source_target_pairs={{0,1},{1,0},{2,3},{3,2},{4,5},{5,4},{6,7},{7,6},{8,9},{9,8},{10,11... | collective-permute-start | bytes 1572872 | tf_op jit(solution)/shard_map/ppermute | solution.py:616
  183.4 10.4 %copy-start.17 = (bf16[256,1024]{1,0:T(8,128)(2,1)}, bf16[256,1024]{1,0:T(8,128)(2,1)S(1)}, u32[]{:S(2)}) copy-start(bf16[256,1024]{1,0:T(8,128)(2,1)S(1)} %collective-permute-done.27.refs_15_) | copy-start | bytes 1572868
  183.4 10.4 %collective-permute-start.28 = (bf16[256,1024]{1,0:T(8,128)(2,1)S(1)}, bf16[256,1024]{1,0:T(8,128)(2,1)}, u32[]{:S(2)}, u32[]{:S(2)}) collective-permute-start(bf16[256,1024]{1,0:T(8,128)(2,1)S(1)} %collective-permute-done.27.refs_15_), channel_id=1, source_target_pairs={{0,1},{1,0},{2,3},{3,2},{4,5},{5,4},{6,7},{7,6},{8,9},{9,8},{10,11... | collective-permute-start | bytes 1572872 | tf_op jit(solution)/shard_map/ppermute | solution.py:616
  193.8 1.0 copy-start.8
  193.8 1.4 copy-start.9
  195.2 31.1 %collective-permute-start.31 = (bf16[3,64,3456]{2,1,0:T(8,128)(2,1)}, bf16[3,64,3456]{2,1,0:T(8,128)(2,1)}, u32[]{:S(2)}, u32[]{:S(2)}) collective-permute-start(bf16[3,64,3456]{2,1,0:T(8,128)(2,1)} %get-tuple-element.86.refs_1_), channel_id=1, source_target_pairs={{0,2},{1,3},{2,0},{3,1},{4,6},{5,7},{6,4},{7,5},{8,10},{9,11},{10,... | collective-permute-start | bytes 3981320 | tf_op jit(solution)/shard_map/ppermute | solution.py:616
  195.8 3.0 %collective-permute-start.29 = (bf16[640,1024]{1,0:T(8,128)(2,1)S(1)}, bf16[640,1024]{1,0:T(8,128)(2,1)S(1)}, u32[]{:S(2)}, u32[]{:S(2)}) collective-permute-start(bf16[640,1024]{1,0:T(8,128)(2,1)S(1)} %collective-permute-done.21.refs_21_.refs_11_), channel_id=1, source_target_pairs={{0,1},{1,0},{2,3},{3,2},{4,5},{5,4},{6,7},{7,6},{8,9},{9,8},{10,11... | collective-permute-start | bytes 3932168 | tf_op jit(solution)/shard_map/ppermute | solution.py:616
  196.1 5.0 %collective-permute-start.30 = (bf16[640,1024]{1,0:T(8,128)(2,1)}, bf16[640,1024]{1,0:T(8,128)(2,1)}, u32[]{:S(2)}, u32[]{:S(2)}) collective-permute-start(bf16[640,1024]{1,0:T(8,128)(2,1)} %collective-permute-done.20.refs_17_), channel_id=1, source_target_pairs={{0,1},{1,0},{2,3},{3,2},{4,5},{5,4},{6,7},{7,6},{8,9},{9,8},{10,11... | collective-permute-start | bytes 3932168 | tf_op jit(solution)/shard_map/ppermute | solution.py:616
  198.8 2.2 copy-start.7
  201.0 26.0 %copy-start.13 = (bf16[3,64,3456]{2,1,0:T(8,128)(2,1)S(1)}, bf16[3,64,3456]{2,1,0:T(8,128)(2,1)}, u32[]{:S(2)}) copy-start(bf16[3,64,3456]{2,1,0:T(8,128)(2,1)} %get-tuple-element.86.refs_1_) | copy-start | bytes 3981316
  201.0 26.5 %copy-start.15 = (bf16[3,64,1664]{2,1,0:T(8,128)(2,1)S(1)}, bf16[3,64,1664]{2,1,0:T(8,128)(2,1)}, u32[]{:S(2)}) copy-start(bf16[3,64,1664]{2,1,0:T(8,128)(2,1)} %get-tuple-element.87.refs_0_) | copy-start | bytes 1916932
  226.3 5.5 %collective-permute-start.32 = (bf16[640,1024]{1,0:T(8,128)(2,1)}, bf16[640,1024]{1,0:T(8,128)(2,1)S(1)}, u32[]{:S(2)}, u32[]{:S(2)}) collective-permute-start(bf16[640,1024]{1,0:T(8,128)(2,1)} %collective-permute-done.26.refs_13_), channel_id=1, source_target_pairs={{0,1},{1,0},{2,3},{3,2},{4,5},{5,4},{6,7},{7,6},{8,9},{9,8},{10,11... | collective-permute-start | bytes 3932168 | tf_op jit(solution)/shard_map/ppermute | solution.py:616
  227.0 22.5 %collective-permute-start.34 = (bf16[3,64,3456]{2,1,0:T(8,128)(2,1)S(1)}, bf16[3,64,3456]{2,1,0:T(8,128)(2,1)}, u32[]{:S(2)}, u32[]{:S(2)}) collective-permute-start(bf16[3,64,3456]{2,1,0:T(8,128)(2,1)S(1)} %copy-done.13), channel_id=1, source_target_pairs={{0,1},{1,0},{2,3},{3,2},{4,5},{5,4},{6,7},{7,6},{8,9},{9,8},{10,11... | collective-permute-start | bytes 3981320 | tf_op jit(solution)/shard_map/ppermute | solution.py:616
  227.0 22.5 %collective-permute-start.37 = (bf16[3,64,3456]{2,1,0:T(8,128)(2,1)}, bf16[3,64,3456]{2,1,0:T(8,128)(2,1)}, u32[]{:S(2)}, u32[]{:S(2)}) collective-permute-start(bf16[3,64,3456]{2,1,0:T(8,128)(2,1)} %collective-permute-done.31.refs_5_), channel_id=1, source_target_pairs={{0,1},{1,0},{2,3},{3,2},{4,5},{5,4},{6,7},{7,6},{8,9},{9,8},{10,11... | collective-permute-start | bytes 3981320 | tf_op jit(solution)/shard_map/ppermute | solution.py:616
  227.6 20.8 %collective-permute-start.35 = (bf16[3,64,1664]{2,1,0:T(8,128)(2,1)S(1)}, bf16[3,64,1664]{2,1,0:T(8,128)(2,1)}, u32[]{:S(2)}, u32[]{:S(2)}) collective-permute-start(bf16[3,64,1664]{2,1,0:T(8,128)(2,1)S(1)} %copy-done.15), channel_id=1, source_target_pairs={{0,2},{1,3},{2,0},{3,1},{4,6},{5,7},{6,4},{7,5},{8,10},{9,11},{10,... | collective-permute-start | bytes 1916936 | tf_op jit(solution)/shard_map/ppermute | solution.py:616
  228.8 20.7 %collective-permute-start.33 = (bf16[3,64,1664]{2,1,0:T(8,128)(2,1)S(1)}, bf16[3,64,1664]{2,1,0:T(8,128)(2,1)}, u32[]{:S(2)}, u32[]{:S(2)}) collective-permute-start(bf16[3,64,1664]{2,1,0:T(8,128)(2,1)S(1)} %copy-done.15), channel_id=1, source_target_pairs={{0,1},{1,0},{2,3},{3,2},{4,5},{5,4},{6,7},{7,6},{8,9},{9,8},{10,11... | collective-permute-start | bytes 1916936 | tf_op jit(solution)/shard_map/ppermute | solution.py:616
  231.7 1.1 copy-start.14
  248.3 2.4 collective-permute-start.36
  250.7 0.8 copy-start.16

commit v8 on v7

--- a/solution.py
+++ b/solution.py
@@ -180,7 +180,7 @@
     rank = both // 2
     rows, ff = hidden.shape
     d = grad.shape[1]
-    cut = (ff + d) // 384 * 128
+    cut = (ff + d) // 256 * 128
     own = lambda i, live: (i, 0)
     own3 = lambda i, live: (i, 0, 0)
     return pl.pallas_call(
@@ -658,8 +658,8 @@
 
     share = ff // n_groups
     if share % 2048 == 0:
-        unit, tile = share // 16, share // 4
-        sizes = [4 * unit, 5 * unit, 5 * unit, 2 * unit]
+        unit, tile = share // 8, share // 4
+        sizes = [2 * unit] * 4
     else:
         tile = share
         sizes = [share]
@@ -671,22 +671,14 @@
     def flat(*pieces):
         return [v for piece in pieces for v in piece.values()]
 
-    def piece_of(j, shift, *after):
-        first_row, size = parts[j]
-        owner = lax.rem(group + n_groups - shift, n_groups)
-        piece = lax.dynamic_slice_in_dim(
-            frozen_down_weight, owner * share + first_row, size, axis=0
-        )
-        return {top: swap(behind(piece, *after), top)}
-
     def cross(*after):
         j = len(crossed)
         if j < len(parts):
-            crossed.append(piece_of(j, 0, *after))
-            if j and j + 1 == len(parts):
-                direct.extend(piece_of(j, shift, *after) for shift in range(1, n_groups))
-
-    direct = []
+            first_row, size = parts[j]
+            piece = lax.dynamic_slice_in_dim(
+                frozen_down_weight, group * share + first_row, size, axis=0
+            )
+            crossed.append({top: swap(behind(piece, *after), top)})
 
     def turn(*after):
         j = len(turned)
@@ -726,9 +718,9 @@
     part, block_a, grad_a, grad_b = project(
         *places(ready), a_near, b_near, far, hidden, output_gradient
     )
+    third_hop = hop(*past)
     cross(*past)
-    cross(part, *past)
-    third = hop(*past, high=height)
+    cross(*past)
     sums = [part]
     bit = 1
     while bit < n_fsdp:
@@ -737,17 +729,15 @@
             sums.append(sums[-2] + sums[-1])
         bit *= 2
     total, other = sums[-2:]
-    past = [sums[2], *third, *flat(*crossed[1:2])]
+    turn(part)
+    past = [sums[2], *flat(*crossed[:3], *sum(turned[:2], [])), *third_hop]
+    cross(*past)
     turn(*past)
     fill(crossed[:2], *past)
     fill(turned[0], *past)
 
     order = [me ^ r for r in range(n_dp)]
-    steps_away = [jnp.abs(place - q) for q in order]
-    if line:
-        early = jnp.stack([(steps < n_fsdp - 1).astype(i32) for steps in steps_away])
-    else:
-        early = jnp.zeros((n_dp,), i32)
+    early = jnp.full((n_dp,), int(line), i32)
     order = jnp.stack(order).astype(i32)
 
     def collect(named):
@@ -767,11 +757,10 @@
     sums_of = {}
 
     def begin(*named):
-        n = 2 * (n_fsdp - 2) + 1
-        at = jnp.stack(where[:n]).astype(i32)
+        at = jnp.stack(where).astype(i32)
         places_of, chunks, tiles = collect(named)
         got = early_sums(
-            places_of, jnp.concatenate([order, early, at]), pieces_of_kept[:n], whole, chunks, tiles, tile
+            places_of, jnp.concatenate([order, early, at]), pieces_of_kept, whole, chunks, tiles, tile
         )
         sums_of.update(zip(named, got))
         return got
@@ -780,18 +769,12 @@
     ahead = line and share > tile
     begun = begin((0, 0), (0, 1), *[(g, 0) for g in others]) if ahead else []
     past = [other, *begun, *flat(*crossed, *sum(turned, []))]
-    third = hop(*past, low=height)
-    cross(*past)
+    low_terms, high_terms, coef = block_terms(
+        island_live_rows, total, other, hidden, output_gradient
+    )
+    far_high = swap(high_terms, top)
+    far_low = swap(low_terms, top)
     turn(*past)
-    if direct:
-        turned.append(direct)
-    live = behind(island_live_rows, *past)
-    low_terms, high_terms, coef = block_terms(live, total, other, hidden, output_gradient)
-    far_low = swap(behind(low_terms, *flat(*crossed[3:], *direct)), top)
-    fill(crossed[3:])
-    fill(direct)
-    past = [coef, *third, *flat(*crossed, *sum(turned, []))]
-    far_high = swap(behind(high_terms, *past), top)
     fill(crossed[2:3], *past)
     for pieces in turned[1:2]:
         fill(pieces, *past)
@@ -817,11 +800,13 @@
         )
 
     if share > tile:
-        multiply(*[(0, t) for t in range(4)], *[(g, t) for g in others for t in range(2)])
+        multiply(*[(0, t) for t in range(3)], *[(g, t) for g in others for t in range(2)])
+        past = [token]
+        fill(crossed[3:], *past)
+        for pieces in turned[2:]:
+            fill(pieces, *past)
         past = [token, far_high]
-        for pieces in turned[2:3]:
-            fill(pieces, *past)
-        multiply(*[(g, t) for g in others for t in range(2, 4)])
+        multiply((0, 3), *[(g, t) for g in others for t in range(2, 4)])
     else:
         multiply(*[(g, 0) for g in range(n_groups)])
 

time: 260 us -> 256 us (0.985)
  waiting for transfers between devices: 95.1 us -> 109 us
  starting transfers between devices: 53.6 us -> 40.2 us
  local copies, waits for them, and re-layouts: 19.1 us -> 12.7 us
    ppermute x27 -> x26, waiting for transfers between devices: 58.8 us -> 71.8 us  [swap(): return lax.ppermute(value, axis, [(i, i ^ bit) for i in range(size)])]
    ppermute x27 -> x26, starting transfers between devices: 28.9 us -> 20 us  [swap(): return lax.ppermute(value, axis, [(i, i ^ bit) for i in range(size)])]
    ppermute x8 -> x6, starting transfers between devices: 22.6 us -> 15.9 us  [hop(): sent.append(lax.ppermute(piece, 'fsdp', pairs))]
    slice x4 -> x0, local copies, waits for them, and re-layouts: 3.84 us -> none  [hop(): piece = behind(piece[low:high], *after)]
    ppermute x3 -> x4, waiting for transfers between devices: 19.1 us -> 22.8 us  [turn(): turned[j].append({top: lax.ppermute(piece, 'groups', ring)})]
    ppermute x8 -> x6, waiting for transfers between devices: 17.2 us -> 14.2 us  [hop(): sent.append(lax.ppermute(piece, 'fsdp', pairs))]
    dynamic_slice x3 -> x1, local copies, waits for them, and re-layouts: 7.02 us -> 4.33 us  [cross(): lax.dynamic_slice_in_dim(frozen_down_weight, group * share + first_row, s...]
    unnamed x38 -> x34, local copies, waits for them, and re-layouts: 6.18 us -> 6.26 us
  transfers between devices with their start and end apart: 38 -> 36, of which waited for: 19 -> 11; matrix products, arithmetic and copies ran while one was open for 7% -> 4% of each run, Pallas kernels for 30% -> 31%
where the time goes in v8:
time: 256 us; the launch traced here: 255 us
  waiting for transfers between devices  109 us (43%)
  Pallas kernels  87 us (34%)
  starting transfers between devices  40.2 us (16%)
  local copies, waits for them, and re-layouts  12.7 us (5%)
  other arithmetic  4.94 us (2%)
    ppermute x26, waiting for transfers between devices, swap(): return lax.ppermute(value, axis, [(i, i ^ bit) for i in range(size)])  71.8 us
    pallas_call x2, Pallas kernels, base(): pl.pallas_call(functools.partial(base_kernel, n_dp, tiles, len(chunks), [...  36.8 us
    ppermute x4, waiting for transfers between devices, turn(): turned[j].append({top: lax.ppermute(piece, 'groups', ring)})  22.8 us
    ppermute x26, starting transfers between devices, swap(): return lax.ppermute(value, axis, [(i, i ^ bit) for i in range(size)])  20 us
    pallas_call x1, Pallas kernels, early_sums(): pl.pallas_call(functools.partial(early_kernel, n_dp, tiles, len(chunks),...  18.6 us
    ppermute x6, starting transfers between devices, hop(): sent.append(lax.ppermute(piece, 'fsdp', pairs))  15.9 us
    ppermute x6, waiting for transfers between devices, hop(): sent.append(lax.ppermute(piece, 'fsdp', pairs))  14.2 us
    pallas_call x1, Pallas kernels, project(): pl.pallas_call(functools.partial(project_kernel, pieces), grid_spec=pltpu...  11.9 us
  transfers between devices with their start and end apart: 36, of which 11 were waited for; matrix products, arithmetic and copies ran while one was open for 4% of the time, Pallas kernels for 31%

profile of v8, /device:TPU:11, one launch (start us, length us, event | category | flops | bytes accessed | tf_op | source)
XLA Modules:
  0.0 254.8 jit_solution(3499490291487739705)
XLA Ops:
  0.6 0.7 collective-permute-start.3
  1.4 3.2 %collective-permute-start = (bf16[768,1024]{1,0:T(8,128)(2,1)}, bf16[768,1024]{1,0:T(8,128)(2,1)S(1)}, u32[]{:S(2)}, u32[]{:S(2)}) collective-permute-start(bf16[768,1024]{1,0:T(8,128)(2,1)} %refs_0_.5), channel_id=1, source_target_pairs={{0,4},{4,8},{8,12},{1,5},{5,9},{9,13},{2,6},{6,10},{10,14},{3,7},{... | collective-permute-start | bytes 4718600 | tf_op jit(solution)/shard_map/ppermute | solution.py:648
  4.6 2.2 collective-permute-start.1
  6.8 0.9 select_reduce_fusion
  7.6 0.3 collective-permute-start.2
  7.9 0.9 collective-permute-start.4
  8.8 4.3 %constant_dynamic-slice_fusion = (bf16[512,1024]{1,0:T(8,128)(2,1)}, bf16[512,1024]{1,0:T(8,128)(2,1)}, bf16[512,1024]{1,0:T(8,128)(2,1)}, bf16[512,1024]{1,0:T(8,128)(2,1)}) fusion(bf16[4096,1024]{1,0:T(8,128)(2,1)} %refs_7_.2, s32[]{:T(128)S(6)} %select_n.95, s32[]{:T(128)S(6)} %select_n.90, s32[]{:T(128)S(6)} %select_n.89, s32[]{:T(128)S(6)} %select_n.94), kind=kLoop, calls=%fused_computation.13 | loop fusion | bytes 8388624 | tf_op jit(solution)/shard_map/dynamic_slice | solution.py:678
  13.1 1.2 collective-permute-start.6
  14.3 0.5 compare_select_fusion.1
  14.9 0.6 pad_add_fusion.index_ref
  15.6 4.8 %shard_map.103 = bf16[3,64,5120]{2,1,0:T(8,128)(2,1)} custom-call(s32[6]{0:T(128)} %pad_add_fusion.index_ref, s32[3]{0:T(128)} %get-tuple-element.101.source_ref, bf16[8,64,4096]{2,1,0:T(8,128)(2,1)} %bitcast.22, bf16[8,64,4096]{2,1,0:T(8,128)(2,1)} %collective-permute-done.3.refs_1_, bf16[8,64,1024]{2,1,0:T(8,128)(2,1)} %refs_2_.3, ...), custom_call_target="tpu_custom_call" | custom-call | bytes 5898240 | tf_op jit(solution)/shard_map/pallas_call | solution.py:54
  20.6 17.6 %collective-permute-done.6.refs_9_ = bf16[512,1024]{1,0:T(8,128)(2,1)} collective-permute-done((bf16[512,1024]{1,0:T(8,128)(2,1)}, bf16[512,1024]{1,0:T(8,128)(2,1)}, u32[]{:S(2)}, u32[]{:S(2)}) %collective-permute-start.6) | collective-permute-done | bytes 1048608 | tf_op jit(solution)/shard_map/ppermute | solution.py:616
  38.2 1.2 collective-permute-done.refs_1_
  39.5 2.9 %collective-permute-done.1.refs_2_ = bf16[768,1024]{1,0:T(8,128)(2,1)S(1)} collective-permute-done((bf16[768,1024]{1,0:T(8,128)(2,1)}, bf16[768,1024]{1,0:T(8,128)(2,1)S(1)}, u32[]{:S(2)}, u32[]{:S(2)}) %collective-permute-start.1) | collective-permute-done | bytes 1572896 | tf_op jit(solution)/shard_map/ppermute | solution.py:648
  42.4 1.1 collective-permute-start.13
  43.8 2.2 collective-permute-start.8
  45.9 3.1 %collective-permute-start.7 = (bf16[768,1024]{1,0:T(8,128)(2,1)S(1)}, bf16[768,1024]{1,0:T(8,128)(2,1)}, u32[]{:S(2)}, u32[]{:S(2)}) collective-permute-start(bf16[768,1024]{1,0:T(8,128)(2,1)S(1)} %collective-permute-done.refs_1_), channel_id=1, source_target_pairs={{0,4},{4,8},{8,12},{1,5},{5,9},{9,13},{2,6},{6,10},{10,14},{3,7},{... | collective-permute-start | bytes 4718600 | tf_op jit(solution)/shard_map/ppermute | solution.py:648
  49.0 1.3 collective-permute-start.10
  50.3 22.8 %collective-permute-done.10.refs_13_ = bf16[512,1024]{1,0:T(8,128)(2,1)S(1)} collective-permute-done((bf16[512,1024]{1,0:T(8,128)(2,1)}, bf16[512,1024]{1,0:T(8,128)(2,1)S(1)}, u32[]{:S(2)}, u32[]{:S(2)}) %collective-permute-start.10) | collective-permute-done | bytes 1048608 | tf_op jit(solution)/shard_map/ppermute | solution.py:690
  73.2 8.2 %collective-permute-done.8.refs_4_ = bf16[768,1024]{1,0:T(8,128)(2,1)} collective-permute-done((bf16[768,1024]{1,0:T(8,128)(2,1)S(1)}, bf16[768,1024]{1,0:T(8,128)(2,1)}, u32[]{:S(2)}, u32[]{:S(2)}) %collective-permute-start.8) | collective-permute-done | bytes 1572896 | tf_op jit(solution)/shard_map/ppermute | solution.py:648
  81.4 1.9 collective-permute-done.7.refs_3_
  83.2 4.8 %collective-permute-done.9.refs_4_ = bf16[3,64,5120]{2,1,0:T(8,128)(2,1)S(1)} collective-permute-done((bf16[3,64,5120]{2,1,0:T(8,128)(2,1)}, bf16[3,64,5120]{2,1,0:T(8,128)(2,1)S(1)}, u32[]{:S(2)}, u32[]{:S(2)}) %collective-permute-start.9) | collective-permute-done | bytes 1966112 | tf_op jit(solution)/shard_map/ppermute | solution.py:616
  88.1 1.3 copy-done.6
  89.6 2.2 collective-permute-start.12
  91.8 3.1 %collective-permute-start.11 = (bf16[768,1024]{1,0:T(8,128)(2,1)}, bf16[768,1024]{1,0:T(8,128)(2,1)}, u32[]{:S(2)}, u32[]{:S(2)}) collective-permute-start(bf16[768,1024]{1,0:T(8,128)(2,1)} %collective-permute-done.7.refs_3_), channel_id=1, source_target_pairs={{0,4},{4,8},{8,12},{1,5},{5,9},{9,13},{2,6},{6,10},{10,14},{3,7},{... | collective-permute-start | bytes 4718600 | tf_op jit(solution)/shard_map/ppermute | solution.py:648
  94.9 1.3 collective-permute-start.16
  96.2 0.6 compare_select_fusion
  96.8 0.6 pad_add_fusion.2.index_ref
  97.3 11.9 %shard_map.104 = (f32[3,256,128]{2,1,0:T(8,128)}, bf16[3,64,4096]{2,1,0:T(8,128)(2,1)}, f32[8,64,4096]{2,1,0:T(8,128)}, f32[8,64,1024]{2,1,0:T(8,128)}) custom-call(s32[6]{0:T(128)} %pad_add_fusion.2.index_ref, s32[3]{0:T(128)} %get-tuple-element.99.source_ref, bf16[8,64,4096]{2,1,0:T(8,128)(2,1)} %bitcast.23, ...), custom_call_target="tpu_custom_call" | custom-call | flops 503316480 | bytes 15728640 | tf_op jit(solution)/shard_map/pallas_call | solution.py:121
  109.2 4.3 %collective-permute-done.15.refs_11_ = bf16[512,1024]{1,0:T(8,128)(2,1)} collective-permute-done((bf16[512,1024]{1,0:T(8,128)(2,1)}, bf16[512,1024]{1,0:T(8,128)(2,1)}, u32[]{:S(2)}, u32[]{:S(2)}) %collective-permute-start.15) | collective-permute-done | bytes 1048608 | tf_op jit(solution)/shard_map/ppermute | solution.py:616
  113.5 1.2 collective-permute-start.17
  115.0 21.9 %collective-permute-done.14 = f32[3,256,128]{2,1,0:T(8,128)S(1)} collective-permute-done((f32[3,256,128]{2,1,0:T(8,128)}, f32[3,256,128]{2,1,0:T(8,128)S(1)}, u32[]{:S(2)}, u32[]{:S(2)}) %collective-permute-start.14) | collective-permute-done | bytes 393248 | tf_op jit(solution)/shard_map/ppermute | solution.py:616
  136.9 1.0 add.114.here_ref
  138.0 2.3 collective-permute-start.21
  140.3 1.3 collective-permute-start.23
  141.6 0.3 collective-permute-start.20
  142.1 1.2 collective-permute-start.18
  143.3 3.4 %collective-permute-start.22 = (f32[3,256,128]{2,1,0:T(8,128)S(1)}, f32[3,256,128]{2,1,0:T(8,128)}, u32[]{:S(2)}, u32[]{:S(2)}) collective-permute-start(f32[3,256,128]{2,1,0:T(8,128)S(1)} %add.114.here_ref), channel_id=1, source_target_pairs={{0,8},{4,12},{8,0},{12,4},{1,9},{5,13},{9,1},{13,5},{2,10},{6,14},... | collective-permute-start | bytes 1179656 | tf_op jit(solution)/shard_map/ppermute | solution.py:616
  146.7 0.7 concatenate.31.scalars_ref
  147.4 1.0 copy-done.4
  148.4 1.0 copy-done.5
  149.4 18.6 %shard_map.105 = (f32[768,512]{1,0:T(8,128)}, f32[768,512]{1,0:T(8,128)}, f32[768,512]{1,0:T(8,128)}) custom-call(s32[18]{0:T(128)} %concatenate.31.scalars_ref, bf16[768,1024]{1,0:T(8,128)(2,1)} %refs_0_.5, bf16[768,1024]{1,0:T(8,128)(2,1)} %copy-done, bf16[768,1024]{1,0:T(8,128)(2,1)} %copy-done.1, bf16[768,1024]{1,0:T(8,128)(2,1)} %collective-permute-done.7.refs_3_, ...), custom_call_target="tpu_custom_call" | custom-call | flops 1 | bytes 1 | tf_op jit(solution)/shard_map/pallas_call | solution.py:444
  168.1 1.0 collective-permute-start.25
  169.1 0.4 collective-permute-start.28
  169.6 0.6 concatenate.30.scalars_ref
  170.2 6.8 %shard_map.106 = (bf16[3,64,2560]{2,1,0:T(8,128)(2,1)}, bf16[3,64,2560]{2,1,0:T(8,128)(2,1)}, bf16[3,256,64]{2,1,0:T(8,128)(2,1)}) custom-call(s32[3]{0:T(128)} %live_ref.1, f32[3,256,128]{2,1,0:T(8,128)} %copy-done.7, f32[3,256,128]{2,1,0:T(8,128)} %collective-permute-done.22.there_ref, bf16[768,4096]{1,0:T(8,128)(2,1)} %hid_ref.1, bf16[768,1024]{1,0:T(8,128)(2,1)} %refs_0_.5), custom_call_target="tpu_custom_call" | custom-call | flops 503316480 | bytes 9830400 | tf_op jit(solution)/shard_map/pallas_call | solution.py:186
  177.0 1.0 copy-done.12
  178.0 0.3 copy-done.13
  178.3 17.9 %shard_map.107 = (bf16[768,4096]{1,0:T(8,128)(2,1)}, f32[8,128]{1,0:T(8,128)}) custom-call(s32[23]{0:T(128)} %concatenate.30.scalars_ref, bf16[768,1024]{1,0:T(8,128)(2,1)} %refs_0_.5, bf16[768,1024]{1,0:T(8,128)(2,1)} %copy-done, bf16[768,1024]{1,0:T(8,128)(2,1)} %copy-done.1, bf16[768,1024]{1,0:T(8,128)(2,1)} %collective-permute-done.7.refs_3_, ...), custom_call_target="tpu_custom_call" | custom-call | flops 1 | bytes 1 | tf_op jit(solution)/shard_map/pallas_call | solution.py:479
  196.2 0.8 collective-permute-start.29
  197.0 0.4 collective-permute-start.26
  197.4 1.2 collective-permute-start.30
  198.9 0.7 concatenate.26.scalars_ref
  199.6 21.5 %collective-permute-done.30.refs_5_ = bf16[3,64,2560]{2,1,0:T(8,128)(2,1)} collective-permute-done((bf16[3,64,2560]{2,1,0:T(8,128)(2,1)}, bf16[3,64,2560]{2,1,0:T(8,128)(2,1)}, u32[]{:S(2)}, u32[]{:S(2)}) %collective-permute-start.30) | collective-permute-done | bytes 983072 | tf_op jit(solution)/shard_map/ppermute | solution.py:616
  221.1 1.3 collective-permute-start.35
  222.5 0.4 collective-permute-start.31
  222.9 0.5 copy-done.10
  223.4 0.3 copy-done.11
  223.7 18.9 %shard_map.108 = (bf16[768,4096]{1,0:T(8,128)(2,1)}, f32[8,128]{1,0:T(8,128)}) custom-call(s32[21]{0:T(128)} %concatenate.26.scalars_ref, bf16[768,1024]{1,0:T(8,128)(2,1)} %refs_0_.5, bf16[768,1024]{1,0:T(8,128)(2,1)} %copy-done, bf16[768,1024]{1,0:T(8,128)(2,1)} %copy-done.1, ...), custom_call_target="tpu_custom_call", output_to_operand_aliasing={{0}: (19, {})} | custom-call | flops 1 | bytes 1 | tf_op jit(solution)/shard_map/pallas_call | solution.py:479
  242.6 0.4 collective-permute-start.34
  243.2 0.7 add_subtract_fusion.slots_ref
  243.8 1.6 collective-permute-done.34.refs_6_
  245.5 0.9 copy-done.14
  246.4 8.2 %shard_map.109 = (f32[8,64,4096]{2,1,0:T(8,128)}, f32[8,64,1024]{2,1,0:T(8,128)}) custom-call(s32[12]{0:T(128)} %add_subtract_fusion.slots_ref, bf16[3,64,2560]{2,1,0:T(8,128)(2,1)} %get-tuple-element.82.refs_0_, bf16[3,64,2560]{2,1,0:T(8,128)(2,1)} %get-tuple-element.83.refs_1_, ...), custom_call_target="tpu_custom_call", output_to_operand_aliasing={{0}: (10, {}), {1}: (11, {})} | custom-call | flops 1 | bytes 1 | tf_op jit(solution)/shard_map/pallas_call | solution.py:568
  (64 shorter events, 2.0 us)
Async XLA Ops:
  0.6 14.9 %collective-permute-start.3 = (bf16[8,64,4096]{2,1,0:T(8,128)(2,1)}, bf16[8,64,4096]{2,1,0:T(8,128)(2,1)}, u32[]{:S(2)}, u32[]{:S(2)}) collective-permute-start(bf16[8,64,4096]{2,1,0:T(8,128)(2,1)} %bitcast.21), channel_id=1, source_target_pairs={{0,1},{1,0},{2,3},{3,2},{4,5},{5,4},{6,7},{7,6},{8,9},{9,8},{10,11... | collective-permute-start | bytes 12582920 | tf_op jit(solution)/shard_map/ppermute | solution.py:616
  1.4 38.1 %collective-permute-start = (bf16[768,1024]{1,0:T(8,128)(2,1)}, bf16[768,1024]{1,0:T(8,128)(2,1)S(1)}, u32[]{:S(2)}, u32[]{:S(2)}) collective-permute-start(bf16[768,1024]{1,0:T(8,128)(2,1)} %refs_0_.5), channel_id=1, source_target_pairs={{0,4},{4,8},{8,12},{1,5},{5,9},{9,13},{2,6},{6,10},{10,14},{3,7},{... | collective-permute-start | bytes 4718600 | tf_op jit(solution)/shard_map/ppermute | solution.py:648
  4.6 37.8 %collective-permute-start.1 = (bf16[768,1024]{1,0:T(8,128)(2,1)}, bf16[768,1024]{1,0:T(8,128)(2,1)S(1)}, u32[]{:S(2)}, u32[]{:S(2)}) collective-permute-start(bf16[768,1024]{1,0:T(8,128)(2,1)} %refs_0_.5), channel_id=1, source_target_pairs={{4,0},{8,4},{12,8},{5,1},{9,5},{13,9},{6,2},{10,6},{14,10},{7,3},{... | collective-permute-start | bytes 4718600 | tf_op jit(solution)/shard_map/ppermute | solution.py:648
  7.6 5.5 %collective-permute-start.2 = (s32[3]{0:T(128)S(1)}, s32[3]{0:T(128)S(1)}, u32[]{:S(2)}, u32[]{:S(2)}) collective-permute-start(s32[3]{0:T(128)S(1)} %select_reduce_fusion), channel_id=1, source_target_pairs={{0,2},{1,3},{2,0},{3,1},{4,6},{5,7},{6,4},{7,5},{8,10},{9,11},{10,... | collective-permute-start | bytes 44 | tf_op jit(solution)/shard_map/ppermute | solution.py:616
  7.9 7.6 %collective-permute-start.4 = (bf16[8,64,1024]{2,1,0:T(8,128)(2,1)}, bf16[8,64,1024]{2,1,0:T(8,128)(2,1)}, u32[]{:S(2)}, u32[]{:S(2)}) collective-permute-start(bf16[8,64,1024]{2,1,0:T(8,128)(2,1)} %refs_2_.3), channel_id=1, source_target_pairs={{0,1},{1,0},{2,3},{3,2},{4,5},{5,4},{6,7},{7,6},{8,9},{9,8},{10,11... | collective-permute-start | bytes 3145736 | tf_op jit(solution)/shard_map/ppermute | solution.py:616
  13.1 25.1 %collective-permute-start.6 = (bf16[512,1024]{1,0:T(8,128)(2,1)}, bf16[512,1024]{1,0:T(8,128)(2,1)}, u32[]{:S(2)}, u32[]{:S(2)}) collective-permute-start(bf16[512,1024]{1,0:T(8,128)(2,1)} %get-tuple-element.48), channel_id=1, source_target_pairs={{0,2},{1,3},{2,0},{3,1},{4,6},{5,7},{6,4},{7,5},{8,10},{9,11},{10,... | collective-permute-start | bytes 3145736 | tf_op jit(solution)/shard_map/ppermute | solution.py:616
  20.3 22.0 %collective-permute-start.5 = (s32[6]{0:T(128)S(1)}, s32[6]{0:T(128)S(1)}, u32[]{:S(2)}, u32[]{:S(2)}) collective-permute-start(s32[6]{0:T(128)S(1)} %pad_add_fusion.1), channel_id=1, source_target_pairs={{0,1},{1,0},{2,3},{3,2},{4,5},{5,4},{6,7},{7,6},{8,9},{9,8},{10,11... | collective-permute-start | bytes 80 | tf_op jit(solution)/shard_map/ppermute | solution.py:616
  39.5 69.7 %copy-start = (bf16[768,1024]{1,0:T(8,128)(2,1)}, bf16[768,1024]{1,0:T(8,128)(2,1)S(1)}, u32[]{:S(2)}) copy-start(bf16[768,1024]{1,0:T(8,128)(2,1)S(1)} %collective-permute-done.refs_1_) | copy-start | bytes 4718596
  42.4 66.8 %copy-start.1 = (bf16[768,1024]{1,0:T(8,128)(2,1)}, bf16[768,1024]{1,0:T(8,128)(2,1)S(1)}, u32[]{:S(2)}) copy-start(bf16[768,1024]{1,0:T(8,128)(2,1)S(1)} %collective-permute-done.1.refs_2_) | copy-start | bytes 4718596
  42.4 53.8 %collective-permute-start.13 = (bf16[4096,1024]{1,0:T(8,128)(2,1)}, bf16[4096,1024]{1,0:T(8,128)(2,1)}, u32[]{:S(2)}, u32[]{:S(2)}) collective-permute-start(bf16[4096,1024]{1,0:T(8,128)(2,1)} %refs_7_.2), channel_id=1, source_target_pairs={{0,1},{1,0},{2,3},{3,2},{4,5},{5,4},{6,7},{7,6},{8,9},{9,8},{10,11... | collective-permute-start | bytes 25165832 | tf_op jit(solution)/shard_map/ppermute | solution.py:616
  43.5 44.6 %collective-permute-start.9 = (bf16[3,64,5120]{2,1,0:T(8,128)(2,1)}, bf16[3,64,5120]{2,1,0:T(8,128)(2,1)S(1)}, u32[]{:S(2)}, u32[]{:S(2)}) collective-permute-start(bf16[3,64,5120]{2,1,0:T(8,128)(2,1)} %shard_map.103), channel_id=1, source_target_pairs={{0,2},{1,3},{2,0},{3,1},{4,6},{5,7},{6,4},{7,5},{8,10},{9,11},{10,... | collective-permute-start | bytes 5898248 | tf_op jit(solution)/shard_map/ppermute | solution.py:616
  43.8 37.6 %collective-permute-start.8 = (bf16[768,1024]{1,0:T(8,128)(2,1)S(1)}, bf16[768,1024]{1,0:T(8,128)(2,1)}, u32[]{:S(2)}, u32[]{:S(2)}) collective-permute-start(bf16[768,1024]{1,0:T(8,128)(2,1)S(1)} %collective-permute-done.1.refs_2_), channel_id=1, source_target_pairs={{4,0},{8,4},{12,8},{5,1},{9,5},{13,9},{6,2},{10,6},{14,10},{7,3},{... | collective-permute-start | bytes 4718600 | tf_op jit(solution)/shard_map/ppermute | solution.py:648
  45.9 37.3 %collective-permute-start.7 = (bf16[768,1024]{1,0:T(8,128)(2,1)S(1)}, bf16[768,1024]{1,0:T(8,128)(2,1)}, u32[]{:S(2)}, u32[]{:S(2)}) collective-permute-start(bf16[768,1024]{1,0:T(8,128)(2,1)S(1)} %collective-permute-done.refs_1_), channel_id=1, source_target_pairs={{0,4},{4,8},{8,12},{1,5},{5,9},{9,13},{2,6},{6,10},{10,14},{3,7},{... | collective-permute-start | bytes 4718600 | tf_op jit(solution)/shard_map/ppermute | solution.py:648
  49.0 24.1 %collective-permute-start.10 = (bf16[512,1024]{1,0:T(8,128)(2,1)}, bf16[512,1024]{1,0:T(8,128)(2,1)S(1)}, u32[]{:S(2)}, u32[]{:S(2)}) collective-permute-start(bf16[512,1024]{1,0:T(8,128)(2,1)} %collective-permute-done.6.refs_9_), channel_id=1, source_target_pairs={{0,16},{16,0},{1,17},{17,1},{2,18},{18,2},{3,19},{19,3},{4,20},{20... | collective-permute-start | bytes 3145736 | tf_op jit(solution)/shard_map/ppermute | solution.py:690
  73.2 10.1 %copy-start.2 = (bf16[512,1024]{1,0:T(8,128)(2,1)}, bf16[512,1024]{1,0:T(8,128)(2,1)S(1)}, u32[]{:S(2)}) copy-start(bf16[512,1024]{1,0:T(8,128)(2,1)S(1)} %collective-permute-done.10.refs_13_) | copy-start | bytes 3145732
  88.1 1.3 copy-start.6
  89.4 24.1 %collective-permute-start.15 = (bf16[512,1024]{1,0:T(8,128)(2,1)}, bf16[512,1024]{1,0:T(8,128)(2,1)}, u32[]{:S(2)}, u32[]{:S(2)}) collective-permute-start(bf16[512,1024]{1,0:T(8,128)(2,1)} %get-tuple-element.58), channel_id=1, source_target_pairs={{0,2},{1,3},{2,0},{3,1},{4,6},{5,7},{6,4},{7,5},{8,10},{9,11},{10,... | collective-permute-start | bytes 3145736 | tf_op jit(solution)/shard_map/ppermute | solution.py:616
  89.6 48.4 %collective-permute-start.12 = (bf16[768,1024]{1,0:T(8,128)(2,1)}, bf16[768,1024]{1,0:T(8,128)(2,1)}, u32[]{:S(2)}, u32[]{:S(2)}) collective-permute-start(bf16[768,1024]{1,0:T(8,128)(2,1)} %collective-permute-done.8.refs_4_), channel_id=1, source_target_pairs={{4,0},{8,4},{12,8},{5,1},{9,5},{13,9},{6,2},{10,6},{14,10},{7,3},{... | collective-permute-start | bytes 4718600 | tf_op jit(solution)/shard_map/ppermute | solution.py:648
  91.8 46.2 %collective-permute-start.11 = (bf16[768,1024]{1,0:T(8,128)(2,1)}, bf16[768,1024]{1,0:T(8,128)(2,1)}, u32[]{:S(2)}, u32[]{:S(2)}) collective-permute-start(bf16[768,1024]{1,0:T(8,128)(2,1)} %collective-permute-done.7.refs_3_), channel_id=1, source_target_pairs={{0,4},{4,8},{8,12},{1,5},{5,9},{9,13},{2,6},{6,10},{10,14},{3,7},{... | collective-permute-start | bytes 4718600 | tf_op jit(solution)/shard_map/ppermute | solution.py:648
  94.9 43.1 %collective-permute-start.16 = (bf16[512,1024]{1,0:T(8,128)(2,1)}, bf16[512,1024]{1,0:T(8,128)(2,1)}, u32[]{:S(2)}, u32[]{:S(2)}) collective-permute-start(bf16[512,1024]{1,0:T(8,128)(2,1)} %get-tuple-element.59), channel_id=1, source_target_pairs={{0,2},{1,3},{2,0},{3,1},{4,6},{5,7},{6,4},{7,5},{8,10},{9,11},{10,... | collective-permute-start | bytes 3145736 | tf_op jit(solution)/shard_map/ppermute | solution.py:616
  113.5 24.5 %collective-permute-start.17 = (bf16[512,1024]{1,0:T(8,128)(2,1)}, bf16[512,1024]{1,0:T(8,128)(2,1)S(1)}, u32[]{:S(2)}, u32[]{:S(2)}) collective-permute-start(bf16[512,1024]{1,0:T(8,128)(2,1)} %collective-permute-done.15.refs_11_), channel_id=1, source_target_pairs={{0,16},{16,0},{1,17},{17,1},{2,18},{18,2},{3,19},{19,3},{4,20},{20... | collective-permute-start | bytes 3145736 | tf_op jit(solution)/shard_map/ppermute | solution.py:690
  114.7 22.2 %collective-permute-start.14 = (f32[3,256,128]{2,1,0:T(8,128)}, f32[3,256,128]{2,1,0:T(8,128)S(1)}, u32[]{:S(2)}, u32[]{:S(2)}) collective-permute-start(f32[3,256,128]{2,1,0:T(8,128)} %get-tuple-element.57), channel_id=1, source_target_pairs={{0,4},{4,0},{8,12},{12,8},{1,5},{5,1},{9,13},{13,9},{2,6},{6,2},{1... | collective-permute-start | bytes 1179656 | tf_op jit(solution)/shard_map/ppermute | solution.py:616
  137.9 30.1 %copy-start.7 = (f32[3,256,128]{2,1,0:T(8,128)}, f32[3,256,128]{2,1,0:T(8,128)S(1)}, u32[]{:S(2)}) copy-start(f32[3,256,128]{2,1,0:T(8,128)S(1)} %add.114.here_ref) | copy-start | bytes 1179652
  138.0 5.3 %copy-start.8 = (bf16[512,1024]{1,0:T(8,128)(2,1)}, bf16[512,1024]{1,0:T(8,128)(2,1)S(1)}, u32[]{:S(2)}) copy-start(bf16[512,1024]{1,0:T(8,128)(2,1)S(1)} %collective-permute-done.17.refs_17_) | copy-start | bytes 3145732
  138.0 5.3 %collective-permute-start.21 = (bf16[512,1024]{1,0:T(8,128)(2,1)}, bf16[512,1024]{1,0:T(8,128)(2,1)S(1)}, u32[]{:S(2)}, u32[]{:S(2)}) collective-permute-start(bf16[512,1024]{1,0:T(8,128)(2,1)} %copy-done.2), channel_id=1, source_target_pairs={{0,1},{1,0},{2,3},{3,2},{4,5},{5,4},{6,7},{7,6},{8,9},{9,8},{10,11... | collective-permute-start | bytes 3145736 | tf_op jit(solution)/shard_map/ppermute | solution.py:616
  140.3 27.8 %collective-permute-start.23 = (bf16[512,1024]{1,0:T(8,128)(2,1)}, bf16[512,1024]{1,0:T(8,128)(2,1)}, u32[]{:S(2)}, u32[]{:S(2)}) collective-permute-start(bf16[512,1024]{1,0:T(8,128)(2,1)} %collective-permute-done.16.refs_15_), channel_id=1, source_target_pairs={{0,16},{16,0},{1,17},{17,1},{2,18},{18,2},{3,19},{19,3},{4,20},{20... | collective-permute-start | bytes 3145736 | tf_op jit(solution)/shard_map/ppermute | solution.py:690
  141.6 5.9 %collective-permute-start.20 = (bf16[512,1024]{1,0:T(8,128)(2,1)}, bf16[512,1024]{1,0:T(8,128)(2,1)S(1)}, u32[]{:S(2)}, u32[]{:S(2)}) collective-permute-start(bf16[512,1024]{1,0:T(8,128)(2,1)} %collective-permute-done.15.refs_11_), channel_id=1, source_target_pairs={{0,1},{1,0},{2,3},{3,2},{4,5},{5,4},{6,7},{7,6},{8,9},{9,8},{10,11... | collective-permute-start | bytes 3145736 | tf_op jit(solution)/shard_map/ppermute | solution.py:616
  141.9 5.5 %collective-permute-start.19 = (bf16[512,1024]{1,0:T(8,128)(2,1)}, bf16[512,1024]{1,0:T(8,128)(2,1)S(1)}, u32[]{:S(2)}, u32[]{:S(2)}) collective-permute-start(bf16[512,1024]{1,0:T(8,128)(2,1)} %collective-permute-done.6.refs_9_), channel_id=1, source_target_pairs={{0,1},{1,0},{2,3},{3,2},{4,5},{5,4},{6,7},{7,6},{8,9},{9,8},{10,11... | collective-permute-start | bytes 3145736 | tf_op jit(solution)/shard_map/ppermute | solution.py:616
  142.1 26.0 %collective-permute-start.18 = (bf16[512,1024]{1,0:T(8,128)(2,1)}, bf16[512,1024]{1,0:T(8,128)(2,1)}, u32[]{:S(2)}, u32[]{:S(2)}) collective-permute-start(bf16[512,1024]{1,0:T(8,128)(2,1)} %get-tuple-element.61), channel_id=1, source_target_pairs={{0,2},{1,3},{2,0},{3,1},{4,6},{5,7},{6,4},{7,5},{8,10},{9,11},{10,... | collective-permute-start | bytes 3145736 | tf_op jit(solution)/shard_map/ppermute | solution.py:616
  143.3 4.1 %copy-start.3 = (bf16[512,1024]{1,0:T(8,128)(2,1)}, bf16[512,1024]{1,0:T(8,128)(2,1)S(1)}, u32[]{:S(2)}) copy-start(bf16[512,1024]{1,0:T(8,128)(2,1)S(1)} %collective-permute-done.21.refs_14_) | copy-start | bytes 3145732
  143.3 24.8 %collective-permute-start.22 = (f32[3,256,128]{2,1,0:T(8,128)S(1)}, f32[3,256,128]{2,1,0:T(8,128)}, u32[]{:S(2)}, u32[]{:S(2)}) collective-permute-start(f32[3,256,128]{2,1,0:T(8,128)S(1)} %add.114.here_ref), channel_id=1, source_target_pairs={{0,8},{4,12},{8,0},{12,4},{1,9},{5,13},{9,1},{13,5},{2,10},{6,14},... | collective-permute-start | bytes 1179656 | tf_op jit(solution)/shard_map/ppermute | solution.py:616
  147.4 22.2 %copy-start.15 = (s32[3]{0:T(128)S(1)}, s32[3]{0:T(128)}, u32[]{:S(2)}) copy-start(s32[3]{0:T(128)} %live_ref.1) | copy-start | bytes 40
  147.4 1.0 copy-start.4
  148.4 1.0 copy-start.5
  168.1 8.9 %collective-permute-start.25 = (bf16[512,1024]{1,0:T(8,128)(2,1)}, bf16[512,1024]{1,0:T(8,128)(2,1)S(1)}, u32[]{:S(2)}, u32[]{:S(2)}) collective-permute-start(bf16[512,1024]{1,0:T(8,128)(2,1)} %copy-done.8), channel_id=1, source_target_pairs={{0,1},{1,0},{2,3},{3,2},{4,5},{5,4},{6,7},{7,6},{8,9},{9,8},{10,11... | collective-permute-start | bytes 3145736 | tf_op jit(solution)/shard_map/ppermute | solution.py:616
  169.0 8.0 %collective-permute-start.24 = (bf16[512,1024]{1,0:T(8,128)(2,1)}, bf16[512,1024]{1,0:T(8,128)(2,1)S(1)}, u32[]{:S(2)}, u32[]{:S(2)}) collective-permute-start(bf16[512,1024]{1,0:T(8,128)(2,1)} %collective-permute-done.16.refs_15_), channel_id=1, source_target_pairs={{0,1},{1,0},{2,3},{3,2},{4,5},{5,4},{6,7},{7,6},{8,9},{9,8},{10,11... | collective-permute-start | bytes 3145736 | tf_op jit(solution)/shard_map/ppermute | solution.py:616
  169.1 27.0 %collective-permute-start.28 = (bf16[512,1024]{1,0:T(8,128)(2,1)}, bf16[512,1024]{1,0:T(8,128)(2,1)S(1)}, u32[]{:S(2)}, u32[]{:S(2)}) collective-permute-start(bf16[512,1024]{1,0:T(8,128)(2,1)} %collective-permute-done.18.refs_9_), channel_id=1, source_target_pairs={{0,16},{16,0},{1,17},{17,1},{2,18},{18,2},{3,19},{19,3},{4,20},{20... | collective-permute-start | bytes 3145736 | tf_op jit(solution)/shard_map/ppermute | solution.py:690
  177.0 1.0 copy-start.12
  177.0 1.3 copy-start.13
  178.3 20.6 %copy-start.16 = (s32[3]{0:T(128)S(1)}, s32[3]{0:T(128)}, u32[]{:S(2)}) copy-start(s32[3]{0:T(128)} %live_ref.1) | copy-start | bytes 40
  196.2 26.8 %copy-start.9 = (bf16[512,1024]{1,0:T(8,128)(2,1)}, bf16[512,1024]{1,0:T(8,128)(2,1)S(1)}, u32[]{:S(2)}) copy-start(bf16[512,1024]{1,0:T(8,128)(2,1)S(1)} %collective-permute-done.28.refs_13_) | copy-start | bytes 3145732
  196.2 26.2 %collective-permute-start.29 = (bf16[512,1024]{1,0:T(8,128)(2,1)S(1)}, bf16[512,1024]{1,0:T(8,128)(2,1)S(1)}, u32[]{:S(2)}, u32[]{:S(2)}) collective-permute-start(bf16[512,1024]{1,0:T(8,128)(2,1)S(1)} %collective-permute-done.28.refs_13_), channel_id=1, source_target_pairs={{0,1},{1,0},{2,3},{3,2},{4,5},{5,4},{6,7},{7,6},{8,9},{9,8},{10,11... | collective-permute-start | bytes 3145736 | tf_op jit(solution)/shard_map/ppermute | solution.py:616
  196.9 25.5 %collective-permute-start.27 = (bf16[512,1024]{1,0:T(8,128)(2,1)}, bf16[512,1024]{1,0:T(8,128)(2,1)S(1)}, u32[]{:S(2)}, u32[]{:S(2)}) collective-permute-start(bf16[512,1024]{1,0:T(8,128)(2,1)} %collective-permute-done.23.refs_11_), channel_id=1, source_target_pairs={{0,1},{1,0},{2,3},{3,2},{4,5},{5,4},{6,7},{7,6},{8,9},{9,8},{10,11... | collective-permute-start | bytes 3145736 | tf_op jit(solution)/shard_map/ppermute | solution.py:616
  197.0 25.9 %collective-permute-start.26 = (bf16[512,1024]{1,0:T(8,128)(2,1)}, bf16[512,1024]{1,0:T(8,128)(2,1)}, u32[]{:S(2)}, u32[]{:S(2)}) collective-permute-start(bf16[512,1024]{1,0:T(8,128)(2,1)} %collective-permute-done.18.refs_9_), channel_id=1, source_target_pairs={{0,1},{1,0},{2,3},{3,2},{4,5},{5,4},{6,7},{7,6},{8,9},{9,8},{10,11... | collective-permute-start | bytes 3145736 | tf_op jit(solution)/shard_map/ppermute | solution.py:616
  197.4 23.6 %collective-permute-start.30 = (bf16[3,64,2560]{2,1,0:T(8,128)(2,1)}, bf16[3,64,2560]{2,1,0:T(8,128)(2,1)}, u32[]{:S(2)}, u32[]{:S(2)}) collective-permute-start(bf16[3,64,2560]{2,1,0:T(8,128)(2,1)} %get-tuple-element.83.refs_1_), channel_id=1, source_target_pairs={{0,2},{1,3},{2,0},{3,1},{4,6},{5,7},{6,4},{7,5},{8,10},{9,11},{10,... | collective-permute-start | bytes 2949128 | tf_op jit(solution)/shard_map/ppermute | solution.py:616
  198.7 43.9 %collective-permute-start.33 = (bf16[3,64,2560]{2,1,0:T(8,128)(2,1)}, bf16[3,64,2560]{2,1,0:T(8,128)(2,1)}, u32[]{:S(2)}, u32[]{:S(2)}) collective-permute-start(bf16[3,64,2560]{2,1,0:T(8,128)(2,1)} %get-tuple-element.82.refs_0_), channel_id=1, source_target_pairs={{0,2},{1,3},{2,0},{3,1},{4,6},{5,7},{6,4},{7,5},{8,10},{9,11},{10,... | collective-permute-start | bytes 2949128 | tf_op jit(solution)/shard_map/ppermute | solution.py:616
  221.1 22.7 %collective-permute-start.35 = (bf16[3,64,2560]{2,1,0:T(8,128)(2,1)}, bf16[3,64,2560]{2,1,0:T(8,128)(2,1)}, u32[]{:S(2)}, u32[]{:S(2)}) collective-permute-start(bf16[3,64,2560]{2,1,0:T(8,128)(2,1)} %collective-permute-done.30.refs_5_), channel_id=1, source_target_pairs={{0,1},{1,0},{2,3},{3,2},{4,5},{5,4},{6,7},{7,6},{8,9},{9,8},{10,11... | collective-permute-start | bytes 2949128 | tf_op jit(solution)/shard_map/ppermute | solution.py:616
  222.4 1.0 copy-start.10
  222.4 21.4 %collective-permute-start.32 = (bf16[3,64,2560]{2,1,0:T(8,128)(2,1)}, bf16[3,64,2560]{2,1,0:T(8,128)(2,1)}, u32[]{:S(2)}, u32[]{:S(2)}) collective-permute-start(bf16[3,64,2560]{2,1,0:T(8,128)(2,1)} %get-tuple-element.83.refs_1_), channel_id=1, source_target_pairs={{0,1},{1,0},{2,3},{3,2},{4,5},{5,4},{6,7},{7,6},{8,9},{9,8},{10,11... | collective-permute-start | bytes 2949128 | tf_op jit(solution)/shard_map/ppermute | solution.py:616
  222.5 1.2 copy-start.11
  222.5 21.4 %collective-permute-start.31 = (bf16[3,64,2560]{2,1,0:T(8,128)(2,1)}, bf16[3,64,2560]{2,1,0:T(8,128)(2,1)}, u32[]{:S(2)}, u32[]{:S(2)}) collective-permute-start(bf16[3,64,2560]{2,1,0:T(8,128)(2,1)} %get-tuple-element.82.refs_0_), channel_id=1, source_target_pairs={{0,1},{1,0},{2,3},{3,2},{4,5},{5,4},{6,7},{7,6},{8,9},{9,8},{10,11... | collective-permute-start | bytes 2949128 | tf_op jit(solution)/shard_map/ppermute | solution.py:616
  242.6 2.8 %collective-permute-start.34 = (bf16[3,64,2560]{2,1,0:T(8,128)(2,1)}, bf16[3,64,2560]{2,1,0:T(8,128)(2,1)S(1)}, u32[]{:S(2)}, u32[]{:S(2)}) collective-permute-start(bf16[3,64,2560]{2,1,0:T(8,128)(2,1)} %collective-permute-done.33.refs_4_), channel_id=1, source_target_pairs={{0,1},{1,0},{2,3},{3,2},{4,5},{5,4},{6,7},{7,6},{8,9},{9,8},{10,11... | collective-permute-start | bytes 2949128 | tf_op jit(solution)/shard_map/ppermute | solution.py:616
  245.5 0.9 copy-start.14

commit v9 on v8

--- a/solution.py
+++ b/solution.py
@@ -801,11 +801,10 @@
 
     if share > tile:
         multiply(*[(0, t) for t in range(3)], *[(g, t) for g in others for t in range(2)])
-        past = [token]
+        past = [token, far_high]
         fill(crossed[3:], *past)
         for pieces in turned[2:]:
             fill(pieces, *past)
-        past = [token, far_high]
         multiply((0, 3), *[(g, t) for g in others for t in range(2, 4)])
     else:
         multiply(*[(g, 0) for g in range(n_groups)])

time: 256 us -> 240 us (0.938)
  waiting for transfers between devices: 109 us -> 92 us
    ppermute x26, waiting for transfers between devices: 71.8 us -> 55 us  [swap(): return lax.ppermute(value, axis, [(i, i ^ bit) for i in range(size)])]
    unnamed x34 -> x32, local copies, waits for them, and re-layouts: 6.26 us -> 6.2 us
  transfers between devices with their start and end apart: 36 -> 36, of which waited for: 11 -> 14; matrix products, arithmetic and copies ran while one was open for 4% -> 5% of each run, Pallas kernels for 31% -> 33%
where the time goes in v9:
time: 240 us; the launch traced here: 237 us
  waiting for transfers between devices  92 us (38%)
  Pallas kernels  85.3 us (36%)
  starting transfers between devices  40.8 us (17%)
  local copies, waits for them, and re-layouts  12.6 us (5%)
  other arithmetic  4.81 us (2%)
    ppermute x26, waiting for transfers between devices, swap(): return lax.ppermute(value, axis, [(i, i ^ bit) for i in range(size)])  55 us
    pallas_call x2, Pallas kernels, base(): pl.pallas_call(functools.partial(base_kernel, n_dp, tiles, len(chunks), [...  36.7 us
    ppermute x4, waiting for transfers between devices, turn(): turned[j].append({top: lax.ppermute(piece, 'groups', ring)})  22.8 us
    ppermute x26, starting transfers between devices, swap(): return lax.ppermute(value, axis, [(i, i ^ bit) for i in range(size)])  20.7 us
    pallas_call x1, Pallas kernels, early_sums(): pl.pallas_call(functools.partial(early_kernel, n_dp, tiles, len(chunks),...  18.6 us
    ppermute x6, starting transfers between devices, hop(): sent.append(lax.ppermute(piece, 'fsdp', pairs))  15.9 us
    ppermute x6, waiting for transfers between devices, hop(): sent.append(lax.ppermute(piece, 'fsdp', pairs))  14.2 us
    pallas_call x1, Pallas kernels, project(): pl.pallas_call(functools.partial(project_kernel, pieces), grid_spec=pltpu...  11.9 us
  transfers between devices with their start and end apart: 36, of which 14 were waited for; matrix products, arithmetic and copies ran while one was open for 5% of the time, Pallas kernels for 33%

profile of v9, /device:TPU:11, one launch (start us, length us, event | category | flops | bytes accessed | tf_op | source)
XLA Modules:
  0.0 236.7 jit_solution(15444218949178971171)
XLA Ops:
  0.6 0.7 collective-permute-start.3
  1.4 3.2 %collective-permute-start = (bf16[768,1024]{1,0:T(8,128)(2,1)}, bf16[768,1024]{1,0:T(8,128)(2,1)S(1)}, u32[]{:S(2)}, u32[]{:S(2)}) collective-permute-start(bf16[768,1024]{1,0:T(8,128)(2,1)} %refs_0_.5), channel_id=1, source_target_pairs={{0,4},{4,8},{8,12},{1,5},{5,9},{9,13},{2,6},{6,10},{10,14},{3,7},{... | collective-permute-start | bytes 4718600 | tf_op jit(solution)/shard_map/ppermute | solution.py:648
  4.6 2.2 collective-permute-start.1
  6.8 0.9 select_reduce_fusion
  7.6 0.3 collective-permute-start.2
  7.9 0.9 collective-permute-start.4
  8.8 4.3 %constant_dynamic-slice_fusion = (bf16[512,1024]{1,0:T(8,128)(2,1)}, bf16[512,1024]{1,0:T(8,128)(2,1)}, bf16[512,1024]{1,0:T(8,128)(2,1)}, bf16[512,1024]{1,0:T(8,128)(2,1)}) fusion(bf16[4096,1024]{1,0:T(8,128)(2,1)} %refs_7_.2, s32[]{:T(128)S(6)} %select_n.95, s32[]{:T(128)S(6)} %select_n.90, s32[]{:T(128)S(6)} %select_n.89, s32[]{:T(128)S(6)} %select_n.94), kind=kLoop, calls=%fused_computation.13 | loop fusion | bytes 8388624 | tf_op jit(solution)/shard_map/dynamic_slice | solution.py:678
  13.1 1.2 collective-permute-start.6
  14.4 0.5 compare_select_fusion.1
  14.9 0.6 pad_add_fusion.index_ref
  15.5 4.8 %shard_map.103 = bf16[3,64,5120]{2,1,0:T(8,128)(2,1)} custom-call(s32[6]{0:T(128)} %pad_add_fusion.index_ref, s32[3]{0:T(128)} %get-tuple-element.101.source_ref, bf16[8,64,4096]{2,1,0:T(8,128)(2,1)} %bitcast.22, bf16[8,64,4096]{2,1,0:T(8,128)(2,1)} %collective-permute-done.3.refs_1_, bf16[8,64,1024]{2,1,0:T(8,128)(2,1)} %refs_2_.3, ...), custom_call_target="tpu_custom_call" | custom-call | bytes 5898240 | tf_op jit(solution)/shard_map/pallas_call | solution.py:54
  20.6 17.7 %collective-permute-done.6.refs_9_ = bf16[512,1024]{1,0:T(8,128)(2,1)} collective-permute-done((bf16[512,1024]{1,0:T(8,128)(2,1)}, bf16[512,1024]{1,0:T(8,128)(2,1)}, u32[]{:S(2)}, u32[]{:S(2)}) %collective-permute-start.6) | collective-permute-done | bytes 1048608 | tf_op jit(solution)/shard_map/ppermute | solution.py:616
  38.2 1.2 collective-permute-done.refs_1_
  39.5 2.9 %collective-permute-done.1.refs_2_ = bf16[768,1024]{1,0:T(8,128)(2,1)S(1)} collective-permute-done((bf16[768,1024]{1,0:T(8,128)(2,1)}, bf16[768,1024]{1,0:T(8,128)(2,1)S(1)}, u32[]{:S(2)}, u32[]{:S(2)}) %collective-permute-start.1) | collective-permute-done | bytes 1572896 | tf_op jit(solution)/shard_map/ppermute | solution.py:648
  42.4 1.1 collective-permute-start.13
  43.8 2.2 collective-permute-start.8
  45.9 3.1 %collective-permute-start.7 = (bf16[768,1024]{1,0:T(8,128)(2,1)S(1)}, bf16[768,1024]{1,0:T(8,128)(2,1)}, u32[]{:S(2)}, u32[]{:S(2)}) collective-permute-start(bf16[768,1024]{1,0:T(8,128)(2,1)S(1)} %collective-permute-done.refs_1_), channel_id=1, source_target_pairs={{0,4},{4,8},{8,12},{1,5},{5,9},{9,13},{2,6},{6,10},{10,14},{3,7},{... | collective-permute-start | bytes 4718600 | tf_op jit(solution)/shard_map/ppermute | solution.py:648
  49.0 1.3 collective-permute-start.10
  50.3 22.8 %collective-permute-done.10.refs_13_ = bf16[512,1024]{1,0:T(8,128)(2,1)S(1)} collective-permute-done((bf16[512,1024]{1,0:T(8,128)(2,1)}, bf16[512,1024]{1,0:T(8,128)(2,1)S(1)}, u32[]{:S(2)}, u32[]{:S(2)}) %collective-permute-start.10) | collective-permute-done | bytes 1048608 | tf_op jit(solution)/shard_map/ppermute | solution.py:690
  73.2 8.2 %collective-permute-done.8.refs_4_ = bf16[768,1024]{1,0:T(8,128)(2,1)} collective-permute-done((bf16[768,1024]{1,0:T(8,128)(2,1)S(1)}, bf16[768,1024]{1,0:T(8,128)(2,1)}, u32[]{:S(2)}, u32[]{:S(2)}) %collective-permute-start.8) | collective-permute-done | bytes 1572896 | tf_op jit(solution)/shard_map/ppermute | solution.py:648
  81.4 1.9 collective-permute-done.7.refs_3_
  83.2 4.8 %collective-permute-done.9.refs_4_ = bf16[3,64,5120]{2,1,0:T(8,128)(2,1)S(1)} collective-permute-done((bf16[3,64,5120]{2,1,0:T(8,128)(2,1)}, bf16[3,64,5120]{2,1,0:T(8,128)(2,1)S(1)}, u32[]{:S(2)}, u32[]{:S(2)}) %collective-permute-start.9) | collective-permute-done | bytes 1966112 | tf_op jit(solution)/shard_map/ppermute | solution.py:616
  88.1 1.3 copy-done.6
  89.6 2.2 collective-permute-start.12
  91.8 3.1 %collective-permute-start.11 = (bf16[768,1024]{1,0:T(8,128)(2,1)}, bf16[768,1024]{1,0:T(8,128)(2,1)}, u32[]{:S(2)}, u32[]{:S(2)}) collective-permute-start(bf16[768,1024]{1,0:T(8,128)(2,1)} %collective-permute-done.7.refs_3_), channel_id=1, source_target_pairs={{0,4},{4,8},{8,12},{1,5},{5,9},{9,13},{2,6},{6,10},{10,14},{3,7},{... | collective-permute-start | bytes 4718600 | tf_op jit(solution)/shard_map/ppermute | solution.py:648
  94.9 1.3 collective-permute-start.16
  96.2 0.5 compare_select_fusion
  96.7 0.6 pad_add_fusion.2.index_ref
  97.3 11.9 %shard_map.104 = (f32[3,256,128]{2,1,0:T(8,128)}, bf16[3,64,4096]{2,1,0:T(8,128)(2,1)}, f32[8,64,4096]{2,1,0:T(8,128)}, f32[8,64,1024]{2,1,0:T(8,128)}) custom-call(s32[6]{0:T(128)} %pad_add_fusion.2.index_ref, s32[3]{0:T(128)} %get-tuple-element.99.source_ref, bf16[8,64,4096]{2,1,0:T(8,128)(2,1)} %bitcast.23, ...), custom_call_target="tpu_custom_call" | custom-call | flops 503316480 | bytes 15728640 | tf_op jit(solution)/shard_map/pallas_call | solution.py:121
  109.3 4.2 %collective-permute-done.15.refs_11_ = bf16[512,1024]{1,0:T(8,128)(2,1)} collective-permute-done((bf16[512,1024]{1,0:T(8,128)(2,1)}, bf16[512,1024]{1,0:T(8,128)(2,1)}, u32[]{:S(2)}, u32[]{:S(2)}) %collective-permute-start.15) | collective-permute-done | bytes 1048608 | tf_op jit(solution)/shard_map/ppermute | solution.py:616
  113.5 1.2 collective-permute-start.17
  115.0 21.9 %collective-permute-done.14 = f32[3,256,128]{2,1,0:T(8,128)S(1)} collective-permute-done((f32[3,256,128]{2,1,0:T(8,128)}, f32[3,256,128]{2,1,0:T(8,128)S(1)}, u32[]{:S(2)}, u32[]{:S(2)}) %collective-permute-start.14) | collective-permute-done | bytes 393248 | tf_op jit(solution)/shard_map/ppermute | solution.py:616
  136.9 1.0 add.114.here_ref
  138.0 2.3 collective-permute-start.21
  140.3 1.3 collective-permute-start.23
  141.6 0.3 collective-permute-start.20
  142.1 1.2 collective-permute-start.18
  143.3 3.4 %collective-permute-start.22 = (f32[3,256,128]{2,1,0:T(8,128)S(1)}, f32[3,256,128]{2,1,0:T(8,128)}, u32[]{:S(2)}, u32[]{:S(2)}) collective-permute-start(f32[3,256,128]{2,1,0:T(8,128)S(1)} %add.114.here_ref), channel_id=1, source_target_pairs={{0,8},{4,12},{8,0},{12,4},{1,9},{5,13},{9,1},{13,5},{2,10},{6,14},... | collective-permute-start | bytes 1179656 | tf_op jit(solution)/shard_map/ppermute | solution.py:616
  146.7 0.7 concatenate.31.scalars_ref
  147.4 0.9 copy-done.4
  148.4 1.0 copy-done.5
  149.4 18.6 %shard_map.105 = (f32[768,512]{1,0:T(8,128)}, f32[768,512]{1,0:T(8,128)}, f32[768,512]{1,0:T(8,128)}) custom-call(s32[18]{0:T(128)} %concatenate.31.scalars_ref, bf16[768,1024]{1,0:T(8,128)(2,1)} %refs_0_.5, bf16[768,1024]{1,0:T(8,128)(2,1)} %copy-done, bf16[768,1024]{1,0:T(8,128)(2,1)} %copy-done.1, bf16[768,1024]{1,0:T(8,128)(2,1)} %collective-permute-done.7.refs_3_, ...), custom_call_target="tpu_custom_call" | custom-call | flops 1 | bytes 1 | tf_op jit(solution)/shard_map/pallas_call | solution.py:444
  168.1 1.0 collective-permute-start.25
  169.1 0.4 collective-permute-start.29
  169.6 6.8 %shard_map.106 = (bf16[3,64,2560]{2,1,0:T(8,128)(2,1)}, bf16[3,64,2560]{2,1,0:T(8,128)(2,1)}, bf16[3,256,64]{2,1,0:T(8,128)(2,1)}) custom-call(s32[3]{0:T(128)} %live_ref.1, f32[3,256,128]{2,1,0:T(8,128)} %copy-done.7, f32[3,256,128]{2,1,0:T(8,128)} %collective-permute-done.22.there_ref, bf16[768,4096]{1,0:T(8,128)(2,1)} %hid_ref.1, bf16[768,1024]{1,0:T(8,128)(2,1)} %refs_0_.5), custom_call_target="tpu_custom_call" | custom-call | flops 503316480 | bytes 9830400 | tf_op jit(solution)/shard_map/pallas_call | solution.py:186
  176.4 1.2 collective-permute-start.26
  177.6 0.7 concatenate.30.scalars_ref
  178.3 1.0 copy-done.12
  179.6 17.7 %shard_map.107 = (bf16[768,4096]{1,0:T(8,128)(2,1)}, f32[8,128]{1,0:T(8,128)}) custom-call(s32[23]{0:T(128)} %concatenate.30.scalars_ref, bf16[768,1024]{1,0:T(8,128)(2,1)} %refs_0_.5, bf16[768,1024]{1,0:T(8,128)(2,1)} %copy-done, bf16[768,1024]{1,0:T(8,128)(2,1)} %copy-done.1, bf16[768,1024]{1,0:T(8,128)(2,1)} %collective-permute-done.7.refs_3_, ...), custom_call_target="tpu_custom_call" | custom-call | flops 1 | bytes 1 | tf_op jit(solution)/shard_map/pallas_call | solution.py:479
  197.3 2.0 collective-permute-done.26.refs_5_
  199.3 1.6 collective-permute-start.30
  200.9 0.4 collective-permute-start.27
  201.4 1.2 collective-permute-start.33
  202.6 0.6 concatenate.26.scalars_ref
  203.2 0.3 collective-permute-start.35
  203.5 0.4 collective-permute-done.30.refs_14_
  204.0 0.4 collective-permute-start.32
  204.3 1.9 collective-permute-done.28.refs_12_
  206.5 0.7 copy-done.11
  207.2 18.9 %shard_map.108 = (bf16[768,4096]{1,0:T(8,128)(2,1)}, f32[8,128]{1,0:T(8,128)}) custom-call(s32[21]{0:T(128)} %concatenate.26.scalars_ref, bf16[768,1024]{1,0:T(8,128)(2,1)} %refs_0_.5, bf16[768,1024]{1,0:T(8,128)(2,1)} %copy-done, bf16[768,1024]{1,0:T(8,128)(2,1)} %copy-done.1, ...), custom_call_target="tpu_custom_call", output_to_operand_aliasing={{0}: (19, {})} | custom-call | flops 1 | bytes 1 | tf_op jit(solution)/shard_map/pallas_call | solution.py:479
  226.5 0.6 add_subtract_fusion.slots_ref
  227.1 1.9 collective-permute-done.34.refs_6_
  229.0 1.0 copy-done.14
  230.0 6.6 %shard_map.109 = (f32[8,64,4096]{2,1,0:T(8,128)}, f32[8,64,1024]{2,1,0:T(8,128)}) custom-call(s32[12]{0:T(128)} %add_subtract_fusion.slots_ref, bf16[3,64,2560]{2,1,0:T(8,128)(2,1)} %get-tuple-element.82.refs_0_, bf16[3,64,2560]{2,1,0:T(8,128)(2,1)} %get-tuple-element.83.refs_1_, ...), custom_call_target="tpu_custom_call", output_to_operand_aliasing={{0}: (10, {}), {1}: (11, {})} | custom-call | flops 1 | bytes 1 | tf_op jit(solution)/shard_map/pallas_call | solution.py:568
  (62 shorter events, 2.4 us)
Async XLA Ops:
  0.6 14.9 %collective-permute-start.3 = (bf16[8,64,4096]{2,1,0:T(8,128)(2,1)}, bf16[8,64,4096]{2,1,0:T(8,128)(2,1)}, u32[]{:S(2)}, u32[]{:S(2)}) collective-permute-start(bf16[8,64,4096]{2,1,0:T(8,128)(2,1)} %bitcast.21), channel_id=1, source_target_pairs={{0,1},{1,0},{2,3},{3,2},{4,5},{5,4},{6,7},{7,6},{8,9},{9,8},{10,11... | collective-permute-start | bytes 12582920 | tf_op jit(solution)/shard_map/ppermute | solution.py:616
  1.4 38.1 %collective-permute-start = (bf16[768,1024]{1,0:T(8,128)(2,1)}, bf16[768,1024]{1,0:T(8,128)(2,1)S(1)}, u32[]{:S(2)}, u32[]{:S(2)}) collective-permute-start(bf16[768,1024]{1,0:T(8,128)(2,1)} %refs_0_.5), channel_id=1, source_target_pairs={{0,4},{4,8},{8,12},{1,5},{5,9},{9,13},{2,6},{6,10},{10,14},{3,7},{... | collective-permute-start | bytes 4718600 | tf_op jit(solution)/shard_map/ppermute | solution.py:648
  4.6 37.8 %collective-permute-start.1 = (bf16[768,1024]{1,0:T(8,128)(2,1)}, bf16[768,1024]{1,0:T(8,128)(2,1)S(1)}, u32[]{:S(2)}, u32[]{:S(2)}) collective-permute-start(bf16[768,1024]{1,0:T(8,128)(2,1)} %refs_0_.5), channel_id=1, source_target_pairs={{4,0},{8,4},{12,8},{5,1},{9,5},{13,9},{6,2},{10,6},{14,10},{7,3},{... | collective-permute-start | bytes 4718600 | tf_op jit(solution)/shard_map/ppermute | solution.py:648
  7.6 5.5 %collective-permute-start.2 = (s32[3]{0:T(128)S(1)}, s32[3]{0:T(128)S(1)}, u32[]{:S(2)}, u32[]{:S(2)}) collective-permute-start(s32[3]{0:T(128)S(1)} %select_reduce_fusion), channel_id=1, source_target_pairs={{0,2},{1,3},{2,0},{3,1},{4,6},{5,7},{6,4},{7,5},{8,10},{9,11},{10,... | collective-permute-start | bytes 44 | tf_op jit(solution)/shard_map/ppermute | solution.py:616
  7.9 7.6 %collective-permute-start.4 = (bf16[8,64,1024]{2,1,0:T(8,128)(2,1)}, bf16[8,64,1024]{2,1,0:T(8,128)(2,1)}, u32[]{:S(2)}, u32[]{:S(2)}) collective-permute-start(bf16[8,64,1024]{2,1,0:T(8,128)(2,1)} %refs_2_.3), channel_id=1, source_target_pairs={{0,1},{1,0},{2,3},{3,2},{4,5},{5,4},{6,7},{7,6},{8,9},{9,8},{10,11... | collective-permute-start | bytes 3145736 | tf_op jit(solution)/shard_map/ppermute | solution.py:616
  13.1 25.1 %collective-permute-start.6 = (bf16[512,1024]{1,0:T(8,128)(2,1)}, bf16[512,1024]{1,0:T(8,128)(2,1)}, u32[]{:S(2)}, u32[]{:S(2)}) collective-permute-start(bf16[512,1024]{1,0:T(8,128)(2,1)} %get-tuple-element.48), channel_id=1, source_target_pairs={{0,2},{1,3},{2,0},{3,1},{4,6},{5,7},{6,4},{7,5},{8,10},{9,11},{10,... | collective-permute-start | bytes 3145736 | tf_op jit(solution)/shard_map/ppermute | solution.py:616
  20.3 22.1 %collective-permute-start.5 = (s32[6]{0:T(128)S(1)}, s32[6]{0:T(128)S(1)}, u32[]{:S(2)}, u32[]{:S(2)}) collective-permute-start(s32[6]{0:T(128)S(1)} %pad_add_fusion.1), channel_id=1, source_target_pairs={{0,1},{1,0},{2,3},{3,2},{4,5},{5,4},{6,7},{7,6},{8,9},{9,8},{10,11... | collective-permute-start | bytes 80 | tf_op jit(solution)/shard_map/ppermute | solution.py:616
  39.5 69.8 %copy-start = (bf16[768,1024]{1,0:T(8,128)(2,1)}, bf16[768,1024]{1,0:T(8,128)(2,1)S(1)}, u32[]{:S(2)}) copy-start(bf16[768,1024]{1,0:T(8,128)(2,1)S(1)} %collective-permute-done.refs_1_) | copy-start | bytes 4718596
  42.4 66.9 %copy-start.1 = (bf16[768,1024]{1,0:T(8,128)(2,1)}, bf16[768,1024]{1,0:T(8,128)(2,1)S(1)}, u32[]{:S(2)}) copy-start(bf16[768,1024]{1,0:T(8,128)(2,1)S(1)} %collective-permute-done.1.refs_2_) | copy-start | bytes 4718596
  42.4 53.8 %collective-permute-start.13 = (bf16[4096,1024]{1,0:T(8,128)(2,1)}, bf16[4096,1024]{1,0:T(8,128)(2,1)}, u32[]{:S(2)}, u32[]{:S(2)}) collective-permute-start(bf16[4096,1024]{1,0:T(8,128)(2,1)} %refs_7_.2), channel_id=1, source_target_pairs={{0,1},{1,0},{2,3},{3,2},{4,5},{5,4},{6,7},{7,6},{8,9},{9,8},{10,11... | collective-permute-start | bytes 25165832 | tf_op jit(solution)/shard_map/ppermute | solution.py:616
  43.5 44.6 %collective-permute-start.9 = (bf16[3,64,5120]{2,1,0:T(8,128)(2,1)}, bf16[3,64,5120]{2,1,0:T(8,128)(2,1)S(1)}, u32[]{:S(2)}, u32[]{:S(2)}) collective-permute-start(bf16[3,64,5120]{2,1,0:T(8,128)(2,1)} %shard_map.103), channel_id=1, source_target_pairs={{0,2},{1,3},{2,0},{3,1},{4,6},{5,7},{6,4},{7,5},{8,10},{9,11},{10,... | collective-permute-start | bytes 5898248 | tf_op jit(solution)/shard_map/ppermute | solution.py:616
  43.8 37.6 %collective-permute-start.8 = (bf16[768,1024]{1,0:T(8,128)(2,1)S(1)}, bf16[768,1024]{1,0:T(8,128)(2,1)}, u32[]{:S(2)}, u32[]{:S(2)}) collective-permute-start(bf16[768,1024]{1,0:T(8,128)(2,1)S(1)} %collective-permute-done.1.refs_2_), channel_id=1, source_target_pairs={{4,0},{8,4},{12,8},{5,1},{9,5},{13,9},{6,2},{10,6},{14,10},{7,3},{... | collective-permute-start | bytes 4718600 | tf_op jit(solution)/shard_map/ppermute | solution.py:648
  45.9 37.3 %collective-permute-start.7 = (bf16[768,1024]{1,0:T(8,128)(2,1)S(1)}, bf16[768,1024]{1,0:T(8,128)(2,1)}, u32[]{:S(2)}, u32[]{:S(2)}) collective-permute-start(bf16[768,1024]{1,0:T(8,128)(2,1)S(1)} %collective-permute-done.refs_1_), channel_id=1, source_target_pairs={{0,4},{4,8},{8,12},{1,5},{5,9},{9,13},{2,6},{6,10},{10,14},{3,7},{... | collective-permute-start | bytes 4718600 | tf_op jit(solution)/shard_map/ppermute | solution.py:648
  49.0 24.1 %collective-permute-start.10 = (bf16[512,1024]{1,0:T(8,128)(2,1)}, bf16[512,1024]{1,0:T(8,128)(2,1)S(1)}, u32[]{:S(2)}, u32[]{:S(2)}) collective-permute-start(bf16[512,1024]{1,0:T(8,128)(2,1)} %collective-permute-done.6.refs_9_), channel_id=1, source_target_pairs={{0,16},{16,0},{1,17},{17,1},{2,18},{18,2},{3,19},{19,3},{4,20},{20... | collective-permute-start | bytes 3145736 | tf_op jit(solution)/shard_map/ppermute | solution.py:690
  73.2 10.1 %copy-start.2 = (bf16[512,1024]{1,0:T(8,128)(2,1)}, bf16[512,1024]{1,0:T(8,128)(2,1)S(1)}, u32[]{:S(2)}) copy-start(bf16[512,1024]{1,0:T(8,128)(2,1)S(1)} %collective-permute-done.10.refs_13_) | copy-start | bytes 3145732
  88.1 1.3 copy-start.6
  89.4 24.1 %collective-permute-start.15 = (bf16[512,1024]{1,0:T(8,128)(2,1)}, bf16[512,1024]{1,0:T(8,128)(2,1)}, u32[]{:S(2)}, u32[]{:S(2)}) collective-permute-start(bf16[512,1024]{1,0:T(8,128)(2,1)} %get-tuple-element.58), channel_id=1, source_target_pairs={{0,2},{1,3},{2,0},{3,1},{4,6},{5,7},{6,4},{7,5},{8,10},{9,11},{10,... | collective-permute-start | bytes 3145736 | tf_op jit(solution)/shard_map/ppermute | solution.py:616
  89.6 48.4 %collective-permute-start.12 = (bf16[768,1024]{1,0:T(8,128)(2,1)}, bf16[768,1024]{1,0:T(8,128)(2,1)}, u32[]{:S(2)}, u32[]{:S(2)}) collective-permute-start(bf16[768,1024]{1,0:T(8,128)(2,1)} %collective-permute-done.8.refs_4_), channel_id=1, source_target_pairs={{4,0},{8,4},{12,8},{5,1},{9,5},{13,9},{6,2},{10,6},{14,10},{7,3},{... | collective-permute-start | bytes 4718600 | tf_op jit(solution)/shard_map/ppermute | solution.py:648
  91.8 46.2 %collective-permute-start.11 = (bf16[768,1024]{1,0:T(8,128)(2,1)}, bf16[768,1024]{1,0:T(8,128)(2,1)}, u32[]{:S(2)}, u32[]{:S(2)}) collective-permute-start(bf16[768,1024]{1,0:T(8,128)(2,1)} %collective-permute-done.7.refs_3_), channel_id=1, source_target_pairs={{0,4},{4,8},{8,12},{1,5},{5,9},{9,13},{2,6},{6,10},{10,14},{3,7},{... | collective-permute-start | bytes 4718600 | tf_op jit(solution)/shard_map/ppermute | solution.py:648
  94.9 43.1 %collective-permute-start.16 = (bf16[512,1024]{1,0:T(8,128)(2,1)}, bf16[512,1024]{1,0:T(8,128)(2,1)}, u32[]{:S(2)}, u32[]{:S(2)}) collective-permute-start(bf16[512,1024]{1,0:T(8,128)(2,1)} %get-tuple-element.59), channel_id=1, source_target_pairs={{0,2},{1,3},{2,0},{3,1},{4,6},{5,7},{6,4},{7,5},{8,10},{9,11},{10,... | collective-permute-start | bytes 3145736 | tf_op jit(solution)/shard_map/ppermute | solution.py:616
  113.5 24.5 %collective-permute-start.17 = (bf16[512,1024]{1,0:T(8,128)(2,1)}, bf16[512,1024]{1,0:T(8,128)(2,1)S(1)}, u32[]{:S(2)}, u32[]{:S(2)}) collective-permute-start(bf16[512,1024]{1,0:T(8,128)(2,1)} %collective-permute-done.15.refs_11_), channel_id=1, source_target_pairs={{0,16},{16,0},{1,17},{17,1},{2,18},{18,2},{3,19},{19,3},{4,20},{20... | collective-permute-start | bytes 3145736 | tf_op jit(solution)/shard_map/ppermute | solution.py:690
  114.7 22.2 %collective-permute-start.14 = (f32[3,256,128]{2,1,0:T(8,128)}, f32[3,256,128]{2,1,0:T(8,128)S(1)}, u32[]{:S(2)}, u32[]{:S(2)}) collective-permute-start(f32[3,256,128]{2,1,0:T(8,128)} %get-tuple-element.57), channel_id=1, source_target_pairs={{0,4},{4,0},{8,12},{12,8},{1,5},{5,1},{9,13},{13,9},{2,6},{6,2},{1... | collective-permute-start | bytes 1179656 | tf_op jit(solution)/shard_map/ppermute | solution.py:616
  137.9 30.1 %copy-start.7 = (f32[3,256,128]{2,1,0:T(8,128)}, f32[3,256,128]{2,1,0:T(8,128)S(1)}, u32[]{:S(2)}) copy-start(f32[3,256,128]{2,1,0:T(8,128)S(1)} %add.114.here_ref) | copy-start | bytes 1179652
  138.0 5.3 %copy-start.8 = (bf16[512,1024]{1,0:T(8,128)(2,1)}, bf16[512,1024]{1,0:T(8,128)(2,1)S(1)}, u32[]{:S(2)}) copy-start(bf16[512,1024]{1,0:T(8,128)(2,1)S(1)} %collective-permute-done.17.refs_17_) | copy-start | bytes 3145732
  138.0 5.3 %collective-permute-start.21 = (bf16[512,1024]{1,0:T(8,128)(2,1)}, bf16[512,1024]{1,0:T(8,128)(2,1)S(1)}, u32[]{:S(2)}, u32[]{:S(2)}) collective-permute-start(bf16[512,1024]{1,0:T(8,128)(2,1)} %copy-done.2), channel_id=1, source_target_pairs={{0,1},{1,0},{2,3},{3,2},{4,5},{5,4},{6,7},{7,6},{8,9},{9,8},{10,11... | collective-permute-start | bytes 3145736 | tf_op jit(solution)/shard_map/ppermute | solution.py:616
  140.3 27.7 %collective-permute-start.23 = (bf16[512,1024]{1,0:T(8,128)(2,1)}, bf16[512,1024]{1,0:T(8,128)(2,1)}, u32[]{:S(2)}, u32[]{:S(2)}) collective-permute-start(bf16[512,1024]{1,0:T(8,128)(2,1)} %collective-permute-done.16.refs_15_), channel_id=1, source_target_pairs={{0,16},{16,0},{1,17},{17,1},{2,18},{18,2},{3,19},{19,3},{4,20},{20... | collective-permute-start | bytes 3145736 | tf_op jit(solution)/shard_map/ppermute | solution.py:690
  141.6 5.9 %collective-permute-start.20 = (bf16[512,1024]{1,0:T(8,128)(2,1)}, bf16[512,1024]{1,0:T(8,128)(2,1)S(1)}, u32[]{:S(2)}, u32[]{:S(2)}) collective-permute-start(bf16[512,1024]{1,0:T(8,128)(2,1)} %collective-permute-done.15.refs_11_), channel_id=1, source_target_pairs={{0,1},{1,0},{2,3},{3,2},{4,5},{5,4},{6,7},{7,6},{8,9},{9,8},{10,11... | collective-permute-start | bytes 3145736 | tf_op jit(solution)/shard_map/ppermute | solution.py:616
  141.9 5.5 %collective-permute-start.19 = (bf16[512,1024]{1,0:T(8,128)(2,1)}, bf16[512,1024]{1,0:T(8,128)(2,1)S(1)}, u32[]{:S(2)}, u32[]{:S(2)}) collective-permute-start(bf16[512,1024]{1,0:T(8,128)(2,1)} %collective-permute-done.6.refs_9_), channel_id=1, source_target_pairs={{0,1},{1,0},{2,3},{3,2},{4,5},{5,4},{6,7},{7,6},{8,9},{9,8},{10,11... | collective-permute-start | bytes 3145736 | tf_op jit(solution)/shard_map/ppermute | solution.py:616
  142.1 26.0 %collective-permute-start.18 = (bf16[512,1024]{1,0:T(8,128)(2,1)}, bf16[512,1024]{1,0:T(8,128)(2,1)}, u32[]{:S(2)}, u32[]{:S(2)}) collective-permute-start(bf16[512,1024]{1,0:T(8,128)(2,1)} %get-tuple-element.61), channel_id=1, source_target_pairs={{0,2},{1,3},{2,0},{3,1},{4,6},{5,7},{6,4},{7,5},{8,10},{9,11},{10,... | collective-permute-start | bytes 3145736 | tf_op jit(solution)/shard_map/ppermute | solution.py:616
  143.3 4.1 %copy-start.3 = (bf16[512,1024]{1,0:T(8,128)(2,1)}, bf16[512,1024]{1,0:T(8,128)(2,1)S(1)}, u32[]{:S(2)}) copy-start(bf16[512,1024]{1,0:T(8,128)(2,1)S(1)} %collective-permute-done.21.refs_14_) | copy-start | bytes 3145732
  143.3 24.7 %collective-permute-start.22 = (f32[3,256,128]{2,1,0:T(8,128)S(1)}, f32[3,256,128]{2,1,0:T(8,128)}, u32[]{:S(2)}, u32[]{:S(2)}) collective-permute-start(f32[3,256,128]{2,1,0:T(8,128)S(1)} %add.114.here_ref), channel_id=1, source_target_pairs={{0,8},{4,12},{8,0},{12,4},{1,9},{5,13},{9,1},{13,5},{2,10},{6,14},... | collective-permute-start | bytes 1179656 | tf_op jit(solution)/shard_map/ppermute | solution.py:616
  147.4 1.0 copy-start.4
  148.4 1.0 copy-start.5
  168.1 9.5 %copy-start.15 = (s32[3]{0:T(128)S(1)}, s32[3]{0:T(128)}, u32[]{:S(2)}) copy-start(s32[3]{0:T(128)} %live_ref.1) | copy-start | bytes 40
  168.1 10.2 %collective-permute-start.25 = (bf16[512,1024]{1,0:T(8,128)(2,1)}, bf16[512,1024]{1,0:T(8,128)(2,1)S(1)}, u32[]{:S(2)}, u32[]{:S(2)}) collective-permute-start(bf16[512,1024]{1,0:T(8,128)(2,1)} %copy-done.8), channel_id=1, source_target_pairs={{0,1},{1,0},{2,3},{3,2},{4,5},{5,4},{6,7},{7,6},{8,9},{9,8},{10,11... | collective-permute-start | bytes 3145736 | tf_op jit(solution)/shard_map/ppermute | solution.py:616
  169.0 9.3 %collective-permute-start.24 = (bf16[512,1024]{1,0:T(8,128)(2,1)}, bf16[512,1024]{1,0:T(8,128)(2,1)S(1)}, u32[]{:S(2)}, u32[]{:S(2)}) collective-permute-start(bf16[512,1024]{1,0:T(8,128)(2,1)} %collective-permute-done.16.refs_15_), channel_id=1, source_target_pairs={{0,1},{1,0},{2,3},{3,2},{4,5},{5,4},{6,7},{7,6},{8,9},{9,8},{10,11... | collective-permute-start | bytes 3145736 | tf_op jit(solution)/shard_map/ppermute | solution.py:616
  169.1 30.2 %collective-permute-start.29 = (bf16[512,1024]{1,0:T(8,128)(2,1)}, bf16[512,1024]{1,0:T(8,128)(2,1)S(1)}, u32[]{:S(2)}, u32[]{:S(2)}) collective-permute-start(bf16[512,1024]{1,0:T(8,128)(2,1)} %collective-permute-done.18.refs_9_), channel_id=1, source_target_pairs={{0,16},{16,0},{1,17},{17,1},{2,18},{18,2},{3,19},{19,3},{4,20},{20... | collective-permute-start | bytes 3145736 | tf_op jit(solution)/shard_map/ppermute | solution.py:690
  176.4 22.9 %collective-permute-start.26 = (bf16[3,64,2560]{2,1,0:T(8,128)(2,1)}, bf16[3,64,2560]{2,1,0:T(8,128)(2,1)}, u32[]{:S(2)}, u32[]{:S(2)}) collective-permute-start(bf16[3,64,2560]{2,1,0:T(8,128)(2,1)} %get-tuple-element.83.refs_1_), channel_id=1, source_target_pairs={{0,2},{1,3},{2,0},{3,1},{4,6},{5,7},{6,4},{7,5},{8,10},{9,11},{10,... | collective-permute-start | bytes 2949128 | tf_op jit(solution)/shard_map/ppermute | solution.py:616
  178.3 1.0 copy-start.12
  178.3 1.3 copy-start.13
  199.3 7.2 %copy-start.9 = (bf16[512,1024]{1,0:T(8,128)(2,1)}, bf16[512,1024]{1,0:T(8,128)(2,1)S(1)}, u32[]{:S(2)}) copy-start(bf16[512,1024]{1,0:T(8,128)(2,1)S(1)} %collective-permute-done.29.refs_13_) | copy-start | bytes 3145732
  199.3 4.7 %collective-permute-start.30 = (bf16[512,1024]{1,0:T(8,128)(2,1)S(1)}, bf16[512,1024]{1,0:T(8,128)(2,1)S(1)}, u32[]{:S(2)}, u32[]{:S(2)}) collective-permute-start(bf16[512,1024]{1,0:T(8,128)(2,1)S(1)} %collective-permute-done.29.refs_13_), channel_id=1, source_target_pairs={{0,1},{1,0},{2,3},{3,2},{4,5},{5,4},{6,7},{7,6},{8,9},{9,8},{10,11... | collective-permute-start | bytes 3145736 | tf_op jit(solution)/shard_map/ppermute | solution.py:616
  200.9 5.4 %collective-permute-start.28 = (bf16[512,1024]{1,0:T(8,128)(2,1)}, bf16[512,1024]{1,0:T(8,128)(2,1)S(1)}, u32[]{:S(2)}, u32[]{:S(2)}) collective-permute-start(bf16[512,1024]{1,0:T(8,128)(2,1)} %collective-permute-done.23.refs_11_), channel_id=1, source_target_pairs={{0,1},{1,0},{2,3},{3,2},{4,5},{5,4},{6,7},{7,6},{8,9},{9,8},{10,11... | collective-permute-start | bytes 3145736 | tf_op jit(solution)/shard_map/ppermute | solution.py:616
  200.9 5.6 %collective-permute-start.27 = (bf16[512,1024]{1,0:T(8,128)(2,1)}, bf16[512,1024]{1,0:T(8,128)(2,1)}, u32[]{:S(2)}, u32[]{:S(2)}) collective-permute-start(bf16[512,1024]{1,0:T(8,128)(2,1)} %collective-permute-done.18.refs_9_), channel_id=1, source_target_pairs={{0,1},{1,0},{2,3},{3,2},{4,5},{5,4},{6,7},{7,6},{8,9},{9,8},{10,11... | collective-permute-start | bytes 3145736 | tf_op jit(solution)/shard_map/ppermute | solution.py:616
  201.4 24.8 %collective-permute-start.33 = (bf16[3,64,2560]{2,1,0:T(8,128)(2,1)}, bf16[3,64,2560]{2,1,0:T(8,128)(2,1)}, u32[]{:S(2)}, u32[]{:S(2)}) collective-permute-start(bf16[3,64,2560]{2,1,0:T(8,128)(2,1)} %get-tuple-element.82.refs_0_), channel_id=1, source_target_pairs={{0,2},{1,3},{2,0},{3,1},{4,6},{5,7},{6,4},{7,5},{8,10},{9,11},{10,... | collective-permute-start | bytes 2949128 | tf_op jit(solution)/shard_map/ppermute | solution.py:616
  203.2 23.9 %collective-permute-start.35 = (bf16[3,64,2560]{2,1,0:T(8,128)(2,1)}, bf16[3,64,2560]{2,1,0:T(8,128)(2,1)}, u32[]{:S(2)}, u32[]{:S(2)}) collective-permute-start(bf16[3,64,2560]{2,1,0:T(8,128)(2,1)} %collective-permute-done.26.refs_5_), channel_id=1, source_target_pairs={{0,1},{1,0},{2,3},{3,2},{4,5},{5,4},{6,7},{7,6},{8,9},{9,8},{10,11... | collective-permute-start | bytes 2949128 | tf_op jit(solution)/shard_map/ppermute | solution.py:616
  204.0 2.5 %copy-start.10 = (bf16[512,1024]{1,0:T(8,128)(2,1)}, bf16[512,1024]{1,0:T(8,128)(2,1)S(1)}, u32[]{:S(2)}) copy-start(bf16[512,1024]{1,0:T(8,128)(2,1)S(1)} %collective-permute-done.30.refs_14_) | copy-start | bytes 3145732
  204.0 23.1 %collective-permute-start.32 = (bf16[3,64,2560]{2,1,0:T(8,128)(2,1)}, bf16[3,64,2560]{2,1,0:T(8,128)(2,1)}, u32[]{:S(2)}, u32[]{:S(2)}) collective-permute-start(bf16[3,64,2560]{2,1,0:T(8,128)(2,1)} %get-tuple-element.83.refs_1_), channel_id=1, source_target_pairs={{0,1},{1,0},{2,3},{3,2},{4,5},{5,4},{6,7},{7,6},{8,9},{9,8},{10,11... | collective-permute-start | bytes 2949128 | tf_op jit(solution)/shard_map/ppermute | solution.py:616
  206.2 1.0 copy-start.11
  206.2 20.8 %collective-permute-start.31 = (bf16[3,64,2560]{2,1,0:T(8,128)(2,1)}, bf16[3,64,2560]{2,1,0:T(8,128)(2,1)}, u32[]{:S(2)}, u32[]{:S(2)}) collective-permute-start(bf16[3,64,2560]{2,1,0:T(8,128)(2,1)} %get-tuple-element.82.refs_0_), channel_id=1, source_target_pairs={{0,1},{1,0},{2,3},{3,2},{4,5},{5,4},{6,7},{7,6},{8,9},{9,8},{10,11... | collective-permute-start | bytes 2949128 | tf_op jit(solution)/shard_map/ppermute | solution.py:616
  226.1 2.8 %collective-permute-start.34 = (bf16[3,64,2560]{2,1,0:T(8,128)(2,1)}, bf16[3,64,2560]{2,1,0:T(8,128)(2,1)S(1)}, u32[]{:S(2)}, u32[]{:S(2)}) collective-permute-start(bf16[3,64,2560]{2,1,0:T(8,128)(2,1)} %collective-permute-done.33.refs_4_), channel_id=1, source_target_pairs={{0,1},{1,0},{2,3},{3,2},{4,5},{5,4},{6,7},{7,6},{8,9},{9,8},{10,11... | collective-permute-start | bytes 2949128 | tf_op jit(solution)/shard_map/ppermute | solution.py:616
  229.0 1.0 copy-start.14

commit v10 on v9

--- a/solution.py
+++ b/solution.py
@@ -217,14 +217,11 @@
         self.near_refs, refs = refs[: self.near], refs[self.near :]
         self.far_refs, self.rest = refs[: n_chunks * self.near], refs[n_chunks * self.near :]
         self.deep = self.near_refs[0].shape[1]
-        self.at = [scalars_ref[len(tiles) + 2 * n_dp + k] for k in range(n_kept)]
+        self.at = [scalars_ref[len(tiles) + n_dp + k] for k in range(n_kept)]
 
     def lanes(self, r):
         start = self.scalars_ref[len(self.tiles) + r] * self.deep
         return pl.ds(pl.multiple_of(start, self.deep), self.deep)
-
-    def early(self, r):
-        return self.scalars_ref[len(self.tiles) + self.n_dp + r] == 1
 
     def span(self, j, tile):
         return pl.ds(pl.multiple_of(self.scalars_ref[j] * tile, tile), tile)
@@ -266,6 +263,12 @@
         )
 
 
+    def product(self, kept, weight, slot):
+        return lax.dot_general(
+            kept[...], weight[slot], (((1,), (1,)), ((), ())), preferred_element_type=f32
+        )
+
+
 def start(copies):
     for copy in copies:
         copy.start()
@@ -283,7 +286,7 @@
 
     def load(j, act):
         for r in range(n_dp):
-            pl.when(me.early(r))(lambda r=r: act(me.loads(j, r, weight, j % 2, in_sem)))
+            act(me.loads(j, r, weight, j % 2, in_sem))
 
     def store(j):
         return pltpu.make_async_copy(total.at[j % 2], sums_refs[j], out_sem.at[j % 2])
@@ -305,13 +308,7 @@
                 if j >= 2:
                     store(j - 2).wait()
 
-        total[slot] = jnp.zeros(total.shape[1:], f32)
-        for r in range(n_dp):
-
-            @pl.when(me.early(r))
-            def _():
-                total[slot] += me.part(r, kept, weight, slot)
-
+        total[slot] = me.product(kept, weight, slot)
         for j in range(steps):
             pl.when(step == j)(lambda j=j: store(j).start())
 
@@ -327,20 +324,20 @@
     _, tile, _ = weight.shape
     height = coef_ref.shape[1]
     steps = len(tiles)
-    live = steps + 2 * n_dp + len(kept_rows)
+    live = steps + n_dp + len(kept_rows)
     token_ref[...] = jnp.zeros_like(token_ref)
 
     def load(j, act):
         slot = j % 2
-        for r in range(n_dp):
-            if j < n_held:
-                pl.when(jnp.logical_not(me.early(r)))(
-                    lambda r=r: act(me.loads(j, r, weight, slot, in_sem))
-                )
-            else:
+        if j >= n_held:
+            for r in range(n_dp):
                 act(me.loads(j, r, weight, slot, in_sem))
         if j < n_held:
             act([pltpu.make_async_copy(held_refs[j], total.at[slot], held_sem.at[slot])])
+        factors(j, act)
+
+    def factors(j, act):
+        slot = j % 2
         act(
             [
                 pltpu.make_async_copy(
@@ -364,49 +361,46 @@
             )
 
     load(0, start)
-    me.each_column(kept, kept_sem, lambda copy: copy.start())
+    if n_held < steps:
+        me.each_column(kept, kept_sem, lambda copy: copy.start())
     if steps > 1:
         load(1, start)
-    me.each_column(kept, kept_sem, lambda copy: copy.wait())
-
-    @pl.loop(0, steps)
+    first = 0
+    if not n_held and me.kept_refs[0].shape[1] == me.deep:
+        first, sums = 1, None
+        for r in range(n_dp):
+            for k in range(len(kept_rows)):
+                pl.when(me.at[k] == scalars_ref[steps + r])(
+                    lambda k=k: me.columns(k, kept, kept_sem).wait()
+                )
+            wait(me.loads(0, r, weight, 0, in_sem))
+            part = me.part(r, kept, weight, 0)
+            sums = part if sums is None else sums + part
+        factors(0, wait)
+        finish(0, sums)
+        store(0).start()
+    elif not n_held:
+        me.each_column(kept, kept_sem, lambda copy: copy.wait())
+
+    @pl.loop(first, steps)
     def _(step):
         slot = lax.rem(step, 2)
-        for j in range(steps):
+        for j in range(first, steps):
 
             @pl.when(step == j)
             def _():
                 if 1 < j + 1 < steps:
                     load(j + 1, start)
+                if 0 < j == n_held:
+                    me.each_column(kept, kept_sem, lambda copy: copy.wait())
                 load(j, wait)
                 if j >= 2:
                     store(j - 2).wait()
 
         if n_held:
-
-            @pl.when(step < n_held)
-            def _():
-                for r in range(n_dp):
-
-                    @pl.when(jnp.logical_not(me.early(r)))
-                    def _():
-                        total[slot] += me.part(r, kept, weight, slot)
-
-                finish(slot, total[slot])
-
+            pl.when(step < n_held)(lambda: finish(slot, total[slot]))
         if n_held < steps:
-
-            @pl.when(step >= n_held)
-            def _():
-                finish(
-                    slot,
-                    lax.dot_general(
-                        kept[...],
-                        weight[slot],
-                        (((1,), (1,)), ((), ())),
-                        preferred_element_type=f32,
-                    ),
-                )
+            pl.when(step >= n_held)(lambda: finish(slot, me.product(kept, weight, slot)))
 
         for j in range(steps):
             pl.when(step == j)(lambda j=j: store(j).start())
@@ -737,7 +731,6 @@
     fill(turned[0], *past)
 
     order = [me ^ r for r in range(n_dp)]
-    early = jnp.full((n_dp,), int(line), i32)
     order = jnp.stack(order).astype(i32)
 
     def collect(named):
@@ -760,7 +753,7 @@
         at = jnp.stack(where).astype(i32)
         places_of, chunks, tiles = collect(named)
         got = early_sums(
-            places_of, jnp.concatenate([order, early, at]), pieces_of_kept, whole, chunks, tiles, tile
+            places_of, jnp.concatenate([order, at]), pieces_of_kept, whole, chunks, tiles, tile
         )
         sums_of.update(zip(named, got))
         return got
@@ -787,7 +780,7 @@
     relative = [both_slots[r][:count] for r in near] + [both_slots[r][count:] for r in near]
     relative = jnp.concatenate(relative) - me * local
 
-    scalars = jnp.concatenate([order, early, at, island_live_rows])
+    scalars = jnp.concatenate([order, at, island_live_rows])
     grad_hidden = token = None
 
     def multiply(*named):
@@ -799,23 +792,29 @@
             [sums_of[name] for name in named if name in sums_of], coef, block_a, grad_hidden, token,
         )
 
+    def add_near(grad_a, grad_b):
+        low, high = spread({0: low_terms}), spread({0: high_terms})
+        pieces = [p for r in near for p in (low[r], high[r])]
+        return add_terms(relative[:edge], pieces, grad_a, grad_b, coef)
+
+    edge = count * len(near)
     if share > tile:
         multiply(*[(0, t) for t in range(3)], *[(g, t) for g in others for t in range(2)])
         past = [token, far_high]
         fill(crossed[3:], *past)
         for pieces in turned[2:]:
             fill(pieces, *past)
+        grad_a, grad_b = add_near(grad_a, grad_b)
+        scalars = behind(scalars, grad_b)
         multiply((0, 3), *[(g, t) for g in others for t in range(2, 4)])
     else:
         multiply(*[(g, 0) for g in range(n_groups)])
-
-    near_low = spread({0: behind(low_terms, *past)})
-    near_high = spread({0: behind(high_terms, *past)})
+        grad_a, grad_b = add_near(grad_a, grad_b)
+
     all_high = spread({top: behind(far_high, *past)})
     all_low = spread({top: behind(far_low, token)})
-    terms = [p for r in near for p in (near_low[r], near_high[r])]
-    terms += [p for r in near for p in (all_low[r + top], all_high[r + top])]
-    grad_a, grad_b = add_terms(relative, terms, grad_a, grad_b, token)
+    terms = [p for r in near for p in (all_low[r + top], all_high[r + top])]
+    grad_a, grad_b = add_terms(relative[edge:], terms, grad_a, grad_b, token)
     return grad_hidden, jnp.swapaxes(grad_a, 1, 2), grad_b
 
 

time: 240 us -> 243 us (1.012)
  the two profiles are of different devices: /device:TPU:11 before, /device:TPU:3 now
where the time goes in v10:
time: 243 us; the launch traced here: 240 us
  waiting for transfers between devices  97.5 us (40%)
  Pallas kernels  86.5 us (36%)
  starting transfers between devices  37.5 us (15%)
  local copies, waits for them, and re-layouts  12.3 us (5%)
  other arithmetic  4.9 us (2%)
    ppermute x26, waiting for transfers between devices, swap(): return lax.ppermute(value, axis, [(i, i ^ bit) for i in range(size)])  56.1 us
    pallas_call x2, Pallas kernels, base(): pl.pallas_call(functools.partial(base_kernel, n_dp, tiles, len(chunks), [...  36.9 us
    ppermute x4, waiting for transfers between devices, turn(): turned[j].append({top: lax.ppermute(piece, 'groups', ring)})  24.6 us
    ppermute x26, starting transfers between devices, swap(): return lax.ppermute(value, axis, [(i, i ^ bit) for i in range(size)])  16.9 us
    ppermute x6, waiting for transfers between devices, hop(): sent.append(lax.ppermute(piece, 'fsdp', pairs))  16.8 us
    pallas_call x1, Pallas kernels, early_sums(): pl.pallas_call(functools.partial(early_kernel, n_dp, tiles, len(chunks),...  16.4 us
    ppermute x6, starting transfers between devices, hop(): sent.append(lax.ppermute(piece, 'fsdp', pairs))  15.6 us
    pallas_call x1, Pallas kernels, project(): pl.pallas_call(functools.partial(project_kernel, pieces), grid_spec=pltpu...  11.7 us
  transfers between devices with their start and end apart: 36, of which 15 were waited for; matrix products, arithmetic and copies ran while one was open for 5% of the time, Pallas kernels for 34%

profile of v10, /device:TPU:3, one launch (start us, length us, event | category | flops | bytes accessed | tf_op | source)
XLA Modules:
  0.0 240.0 jit_solution(81412833807151428)
XLA Ops:
  0.6 0.7 collective-permute-start.1
  1.4 3.3 %collective-permute-start.4 = (bf16[768,1024]{1,0:T(8,128)(2,1)}, bf16[768,1024]{1,0:T(8,128)(2,1)S(1)}, u32[]{:S(2)}, u32[]{:S(2)}) collective-permute-start(bf16[768,1024]{1,0:T(8,128)(2,1)} %refs_0_.5), channel_id=1, source_target_pairs={{0,4},{4,8},{8,12},{1,5},{5,9},{9,13},{2,6},{6,10},{10,14},{3,7},{... | collective-permute-start | bytes 4718600 | tf_op jit(solution)/shard_map/ppermute | solution.py:642
  4.7 1.3 collective-permute-start.5
  6.0 0.9 select_reduce_fusion
  6.8 0.3 collective-permute-start
  7.1 0.6 collective-permute-start.2
  7.7 4.3 %constant_dynamic-slice_fusion = (bf16[512,1024]{1,0:T(8,128)(2,1)}, bf16[512,1024]{1,0:T(8,128)(2,1)}, bf16[512,1024]{1,0:T(8,128)(2,1)}, bf16[512,1024]{1,0:T(8,128)(2,1)}) fusion(bf16[4096,1024]{1,0:T(8,128)(2,1)} %refs_7_.2, s32[]{:T(128)S(6)} %select_n.95, s32[]{:T(128)S(6)} %select_n.93, s32[]{:T(128)S(6)} %select_n.89, s32[]{:T(128)S(6)} %select_n.94), kind=kLoop, calls=%fused_computation.13 | loop fusion | bytes 8388624 | tf_op jit(solution)/shard_map/dynamic_slice | solution.py:672
  12.1 1.2 collective-permute-start.6
  13.3 0.5 compare_select_fusion.1
  13.8 0.6 pad_add_fusion.1.index_ref
  14.5 4.8 %shard_map.103 = bf16[3,64,5120]{2,1,0:T(8,128)(2,1)} custom-call(s32[6]{0:T(128)} %pad_add_fusion.1.index_ref, s32[3]{0:T(128)} %get-tuple-element.105.source_ref, bf16[8,64,4096]{2,1,0:T(8,128)(2,1)} %bitcast.23, bf16[8,64,4096]{2,1,0:T(8,128)(2,1)} %collective-permute-done.1.refs_1_, bf16[8,64,1024]{2,1,0:T(8,128)(2,1)} %refs_2_.3, ...), custom_call_target="tpu_custom_call" | custom-call | bytes 5898240 | tf_op jit(solution)/shard_map/pallas_call | solution.py:54
  19.6 17.6 %collective-permute-done.6.refs_9_ = bf16[512,1024]{1,0:T(8,128)(2,1)} collective-permute-done((bf16[512,1024]{1,0:T(8,128)(2,1)}, bf16[512,1024]{1,0:T(8,128)(2,1)}, u32[]{:S(2)}, u32[]{:S(2)}) %collective-permute-start.6) | collective-permute-done | bytes 1048608 | tf_op jit(solution)/shard_map/ppermute | solution.py:610
  37.2 1.5 collective-permute-done.4.refs_1_
  38.7 3.8 %collective-permute-done.5.refs_2_ = bf16[768,1024]{1,0:T(8,128)(2,1)S(1)} collective-permute-done((bf16[768,1024]{1,0:T(8,128)(2,1)}, bf16[768,1024]{1,0:T(8,128)(2,1)S(1)}, u32[]{:S(2)}, u32[]{:S(2)}) %collective-permute-start.5) | collective-permute-done | bytes 1572896 | tf_op jit(solution)/shard_map/ppermute | solution.py:642
  42.5 1.1 collective-permute-start.7
  43.8 4.3 %collective-permute-start.9 = (bf16[768,1024]{1,0:T(8,128)(2,1)S(1)}, bf16[768,1024]{1,0:T(8,128)(2,1)}, u32[]{:S(2)}, u32[]{:S(2)}) collective-permute-start(bf16[768,1024]{1,0:T(8,128)(2,1)S(1)} %collective-permute-done.4.refs_1_), channel_id=1, source_target_pairs={{0,4},{4,8},{8,12},{1,5},{5,9},{9,13},{2,6},{6,10},{10,14},{3,7},{... | collective-permute-start | bytes 4718600 | tf_op jit(solution)/shard_map/ppermute | solution.py:642
  48.1 1.3 collective-permute-start.10
  49.4 1.3 collective-permute-start.11
  50.7 23.2 %collective-permute-done.11.refs_13_ = bf16[512,1024]{1,0:T(8,128)(2,1)S(1)} collective-permute-done((bf16[512,1024]{1,0:T(8,128)(2,1)}, bf16[512,1024]{1,0:T(8,128)(2,1)S(1)}, u32[]{:S(2)}, u32[]{:S(2)}) %collective-permute-start.11) | collective-permute-done | bytes 1048608 | tf_op jit(solution)/shard_map/ppermute | solution.py:684
  73.9 6.5 %collective-permute-done.9.refs_3_ = bf16[768,1024]{1,0:T(8,128)(2,1)} collective-permute-done((bf16[768,1024]{1,0:T(8,128)(2,1)S(1)}, bf16[768,1024]{1,0:T(8,128)(2,1)}, u32[]{:S(2)}, u32[]{:S(2)}) %collective-permute-start.9) | collective-permute-done | bytes 1572896 | tf_op jit(solution)/shard_map/ppermute | solution.py:642
  80.4 5.1 %collective-permute-done.10.refs_4_ = bf16[768,1024]{1,0:T(8,128)(2,1)} collective-permute-done((bf16[768,1024]{1,0:T(8,128)(2,1)S(1)}, bf16[768,1024]{1,0:T(8,128)(2,1)}, u32[]{:S(2)}, u32[]{:S(2)}) %collective-permute-start.10) | collective-permute-done | bytes 1572896 | tf_op jit(solution)/shard_map/ppermute | solution.py:642
  85.4 2.8 %collective-permute-done.8.refs_4_ = bf16[3,64,5120]{2,1,0:T(8,128)(2,1)S(1)} collective-permute-done((bf16[3,64,5120]{2,1,0:T(8,128)(2,1)}, bf16[3,64,5120]{2,1,0:T(8,128)(2,1)S(1)}, u32[]{:S(2)}, u32[]{:S(2)}) %collective-permute-start.8) | collective-permute-done | bytes 1966112 | tf_op jit(solution)/shard_map/ppermute | solution.py:610
  88.2 1.3 copy-done.6
  89.7 4.2 %collective-permute-start.16 = (bf16[768,1024]{1,0:T(8,128)(2,1)}, bf16[768,1024]{1,0:T(8,128)(2,1)}, u32[]{:S(2)}, u32[]{:S(2)}) collective-permute-start(bf16[768,1024]{1,0:T(8,128)(2,1)} %collective-permute-done.9.refs_3_), channel_id=1, source_target_pairs={{0,4},{4,8},{8,12},{1,5},{5,9},{9,13},{2,6},{6,10},{10,14},{3,7},{... | collective-permute-start | bytes 4718600 | tf_op jit(solution)/shard_map/ppermute | solution.py:642
  93.9 1.3 collective-permute-start.17
  95.2 1.3 collective-permute-start.19
  96.5 0.5 compare_select_fusion
  97.0 0.6 pad_add_fusion.2.index_ref
  97.6 11.7 %shard_map.104 = (f32[3,256,128]{2,1,0:T(8,128)}, bf16[3,64,4096]{2,1,0:T(8,128)(2,1)}, f32[8,64,4096]{2,1,0:T(8,128)}, f32[8,64,1024]{2,1,0:T(8,128)}) custom-call(s32[6]{0:T(128)} %pad_add_fusion.2.index_ref, s32[3]{0:T(128)} %get-tuple-element.99.source_ref, bf16[8,64,4096]{2,1,0:T(8,128)(2,1)} %bitcast.24, ...), custom_call_target="tpu_custom_call" | custom-call | flops 503316480 | bytes 15728640 | tf_op jit(solution)/shard_map/pallas_call | solution.py:121
  109.3 4.3 %collective-permute-done.18.refs_11_ = bf16[512,1024]{1,0:T(8,128)(2,1)} collective-permute-done((bf16[512,1024]{1,0:T(8,128)(2,1)}, bf16[512,1024]{1,0:T(8,128)(2,1)}, u32[]{:S(2)}, u32[]{:S(2)}) %collective-permute-start.18) | collective-permute-done | bytes 1048608 | tf_op jit(solution)/shard_map/ppermute | solution.py:610
  113.6 1.2 collective-permute-start.20
  114.8 1.2 collective-permute-start.12
  116.0 22.9 %collective-permute-done.12 = f32[3,256,128]{2,1,0:T(8,128)S(1)} collective-permute-done((f32[3,256,128]{2,1,0:T(8,128)}, f32[3,256,128]{2,1,0:T(8,128)S(1)}, u32[]{:S(2)}, u32[]{:S(2)}) %collective-permute-start.12) | collective-permute-done | bytes 393248 | tf_op jit(solution)/shard_map/ppermute | solution.py:610
  138.9 1.0 add.112.here_ref
  140.1 2.4 %collective-permute-start.22 = (bf16[512,1024]{1,0:T(8,128)(2,1)}, bf16[512,1024]{1,0:T(8,128)(2,1)S(1)}, u32[]{:S(2)}, u32[]{:S(2)}) collective-permute-start(bf16[512,1024]{1,0:T(8,128)(2,1)} %collective-permute-done.6.refs_9_), channel_id=1, source_target_pairs={{0,1},{1,0},{2,3},{3,2},{4,5},{5,4},{6,7},{7,6},{8,9},{9,8},{10,11... | collective-permute-start | bytes 3145736 | tf_op jit(solution)/shard_map/ppermute | solution.py:610
  142.5 1.2 collective-permute-start.21
  143.7 0.3 collective-permute-start.23
  144.2 1.2 collective-permute-start.25
  145.6 0.7 concatenate.34.scalars_ref
  146.6 1.5 collective-permute-done.24.refs_14_
  148.1 1.0 copy-done.5
  149.0 16.4 %shard_map.107 = (f32[768,512]{1,0:T(8,128)}, f32[768,512]{1,0:T(8,128)}, f32[768,512]{1,0:T(8,128)}) custom-call(s32[14]{0:T(128)} %concatenate.34.scalars_ref, bf16[768,1024]{1,0:T(8,128)(2,1)} %refs_0_.5, bf16[768,1024]{1,0:T(8,128)(2,1)} %copy-done, bf16[768,1024]{1,0:T(8,128)(2,1)} %copy-done.1, bf16[768,1024]{1,0:T(8,128)(2,1)} %collective-permute-done.9.refs_3_, ...), custom_call_target="tpu_custom_call" | custom-call | flops 1 | bytes 1 | tf_op jit(solution)/shard_map/pallas_call | solution.py:438
  165.5 2.0 collective-permute-done.21.refs_9_
  167.5 1.4 collective-permute-done.25.refs_11_
  168.9 1.2 collective-permute-start.26
  170.1 1.2 collective-permute-start.31
  171.3 6.8 %shard_map.105 = (bf16[3,64,2560]{2,1,0:T(8,128)(2,1)}, bf16[3,64,2560]{2,1,0:T(8,128)(2,1)}, bf16[3,256,64]{2,1,0:T(8,128)(2,1)}) custom-call(s32[3]{0:T(128)} %live_ref.1, f32[3,256,128]{2,1,0:T(8,128)} %copy-done.7, f32[3,256,128]{2,1,0:T(8,128)} %collective-permute-done.13.there_ref, bf16[768,4096]{1,0:T(8,128)(2,1)} %hid_ref.1, bf16[768,1024]{1,0:T(8,128)(2,1)} %refs_0_.5), custom_call_target="tpu_custom_call" | custom-call | flops 503316480 | bytes 9830400 | tf_op jit(solution)/shard_map/pallas_call | solution.py:186
  178.4 1.1 collective-permute-start.14
  179.6 0.8 concatenate.33.scalars_ref
  180.5 0.9 copy-done.13
  181.4 17.2 %shard_map.108 = (bf16[768,4096]{1,0:T(8,128)(2,1)}, f32[8,128]{1,0:T(8,128)}) custom-call(s32[19]{0:T(128)} %concatenate.33.scalars_ref, bf16[768,1024]{1,0:T(8,128)(2,1)} %refs_0_.5, bf16[768,1024]{1,0:T(8,128)(2,1)} %copy-done, bf16[768,1024]{1,0:T(8,128)(2,1)} %copy-done.1, bf16[768,1024]{1,0:T(8,128)(2,1)} %collective-permute-done.9.refs_3_, ...), custom_call_target="tpu_custom_call" | custom-call | flops 1 | bytes 1 | tf_op jit(solution)/shard_map/pallas_call | solution.py:473
  198.7 2.3 collective-permute-done.28.refs_1_
  201.0 1.7 collective-permute-start.29
  202.7 0.5 collective-permute-start.32
  203.8 0.6 fusion
  204.4 6.0 %shard_map.106 = (f32[8,64,4096]{2,1,0:T(8,128)}, f32[8,64,1024]{2,1,0:T(8,128)}) custom-call(s32[6]{0:T(128)} %get-tuple-element.98.slots_ref, bf16[3,64,2560]{2,1,0:T(8,128)(2,1)} %get-tuple-element.57.refs_0_, bf16[3,64,2560]{2,1,0:T(8,128)(2,1)} %get-tuple-element.58.refs_1_, ...), custom_call_target="tpu_custom_call", output_to_operand_aliasing={{0}: (6, {}), {1}: (7, {})} | custom-call | flops 1 | bytes 1 | tf_op jit(solution)/shard_map/pallas_call | solution.py:562
  210.4 0.6 pad_add_fusion.3.scalars_ref
  211.1 0.9 copy-done.10
  212.0 0.3 copy-done.11
  212.3 19.7 %shard_map.109 = (bf16[768,4096]{1,0:T(8,128)(2,1)}, f32[8,128]{1,0:T(8,128)}) custom-call(s32[17]{0:T(128)} %pad_add_fusion.3.scalars_ref, bf16[768,1024]{1,0:T(8,128)(2,1)} %refs_0_.5, bf16[768,1024]{1,0:T(8,128)(2,1)} %copy-done, bf16[768,1024]{1,0:T(8,128)(2,1)} %copy-done.1, ...), custom_call_target="tpu_custom_call", output_to_operand_aliasing={{0}: (19, {})} | custom-call | flops 1 | bytes 1 | tf_op jit(solution)/shard_map/pallas_call | solution.py:473
  232.0 0.4 collective-permute-start.34
  232.4 2.5 %collective-permute-done.34.refs_2_ = bf16[3,64,2560]{2,1,0:T(8,128)(2,1)S(1)} collective-permute-done((bf16[3,64,2560]{2,1,0:T(8,128)(2,1)}, bf16[3,64,2560]{2,1,0:T(8,128)(2,1)S(1)}, u32[]{:S(2)}, u32[]{:S(2)}) %collective-permute-start.34) | collective-permute-done | bytes 983072 | tf_op jit(solution)/shard_map/ppermute | solution.py:610
  234.9 1.0 copy-done.14
  235.9 3.9 %shard_map.110 = (f32[8,64,4096]{2,1,0:T(8,128)}, f32[8,64,1024]{2,1,0:T(8,128)}) custom-call(s32[6]{0:T(128)} %get-tuple-element.97.slots_ref, bf16[3,64,2560]{2,1,0:T(8,128)(2,1)} %collective-permute-done.33.refs_0_, bf16[3,64,2560]{2,1,0:T(8,128)(2,1)} %collective-permute-done.28.refs_1_, ...), custom_call_target="tpu_custom_call", output_to_operand_aliasing={{0}: (6, {}), {1}: (7, {})} | custom-call | flops 1 | bytes 1 | tf_op jit(solution)/shard_map/pallas_call | solution.py:562
  (64 shorter events, 2.4 us)
Async XLA Ops:
  0.6 13.9 %collective-permute-start.1 = (bf16[8,64,4096]{2,1,0:T(8,128)(2,1)}, bf16[8,64,4096]{2,1,0:T(8,128)(2,1)}, u32[]{:S(2)}, u32[]{:S(2)}) collective-permute-start(bf16[8,64,4096]{2,1,0:T(8,128)(2,1)} %bitcast.22), channel_id=1, source_target_pairs={{0,1},{1,0},{2,3},{3,2},{4,5},{5,4},{6,7},{7,6},{8,9},{9,8},{10,11... | collective-permute-start | bytes 12582920 | tf_op jit(solution)/shard_map/ppermute | solution.py:610
  1.4 37.3 %collective-permute-start.4 = (bf16[768,1024]{1,0:T(8,128)(2,1)}, bf16[768,1024]{1,0:T(8,128)(2,1)S(1)}, u32[]{:S(2)}, u32[]{:S(2)}) collective-permute-start(bf16[768,1024]{1,0:T(8,128)(2,1)} %refs_0_.5), channel_id=1, source_target_pairs={{0,4},{4,8},{8,12},{1,5},{5,9},{9,13},{2,6},{6,10},{10,14},{3,7},{... | collective-permute-start | bytes 4718600 | tf_op jit(solution)/shard_map/ppermute | solution.py:642
  4.7 37.8 %collective-permute-start.5 = (bf16[768,1024]{1,0:T(8,128)(2,1)}, bf16[768,1024]{1,0:T(8,128)(2,1)S(1)}, u32[]{:S(2)}, u32[]{:S(2)}) collective-permute-start(bf16[768,1024]{1,0:T(8,128)(2,1)} %refs_0_.5), channel_id=1, source_target_pairs={{4,0},{8,4},{12,8},{5,1},{9,5},{13,9},{6,2},{10,6},{14,10},{7,3},{... | collective-permute-start | bytes 4718600 | tf_op jit(solution)/shard_map/ppermute | solution.py:642
  6.8 5.2 %collective-permute-start = (s32[3]{0:T(128)S(1)}, s32[3]{0:T(128)S(1)}, u32[]{:S(2)}, u32[]{:S(2)}) collective-permute-start(s32[3]{0:T(128)S(1)} %select_reduce_fusion), channel_id=1, source_target_pairs={{0,2},{1,3},{2,0},{3,1},{4,6},{5,7},{6,4},{7,5},{8,10},{9,11},{10,... | collective-permute-start | bytes 44 | tf_op jit(solution)/shard_map/ppermute | solution.py:610
  7.1 7.4 %collective-permute-start.2 = (bf16[8,64,1024]{2,1,0:T(8,128)(2,1)}, bf16[8,64,1024]{2,1,0:T(8,128)(2,1)}, u32[]{:S(2)}, u32[]{:S(2)}) collective-permute-start(bf16[8,64,1024]{2,1,0:T(8,128)(2,1)} %refs_2_.3), channel_id=1, source_target_pairs={{0,1},{1,0},{2,3},{3,2},{4,5},{5,4},{6,7},{7,6},{8,9},{9,8},{10,11... | collective-permute-start | bytes 3145736 | tf_op jit(solution)/shard_map/ppermute | solution.py:610
  12.1 25.1 %collective-permute-start.6 = (bf16[512,1024]{1,0:T(8,128)(2,1)}, bf16[512,1024]{1,0:T(8,128)(2,1)}, u32[]{:S(2)}, u32[]{:S(2)}) collective-permute-start(bf16[512,1024]{1,0:T(8,128)(2,1)} %get-tuple-element.49), channel_id=1, source_target_pairs={{0,2},{1,3},{2,0},{3,1},{4,6},{5,7},{6,4},{7,5},{8,10},{9,11},{10,... | collective-permute-start | bytes 3145736 | tf_op jit(solution)/shard_map/ppermute | solution.py:610
  19.3 23.2 %collective-permute-start.3 = (s32[6]{0:T(128)S(1)}, s32[6]{0:T(128)S(1)}, u32[]{:S(2)}, u32[]{:S(2)}) collective-permute-start(s32[6]{0:T(128)S(1)} %pad_add_fusion), channel_id=1, source_target_pairs={{0,1},{1,0},{2,3},{3,2},{4,5},{5,4},{6,7},{7,6},{8,9},{9,8},{10,11... | collective-permute-start | bytes 80 | tf_op jit(solution)/shard_map/ppermute | solution.py:610
  38.7 70.6 %copy-start = (bf16[768,1024]{1,0:T(8,128)(2,1)}, bf16[768,1024]{1,0:T(8,128)(2,1)S(1)}, u32[]{:S(2)}) copy-start(bf16[768,1024]{1,0:T(8,128)(2,1)S(1)} %collective-permute-done.4.refs_1_) | copy-start | bytes 4718596
  42.5 66.9 %copy-start.1 = (bf16[768,1024]{1,0:T(8,128)(2,1)}, bf16[768,1024]{1,0:T(8,128)(2,1)S(1)}, u32[]{:S(2)}) copy-start(bf16[768,1024]{1,0:T(8,128)(2,1)S(1)} %collective-permute-done.5.refs_2_) | copy-start | bytes 4718596
  42.5 54.1 %collective-permute-start.7 = (bf16[4096,1024]{1,0:T(8,128)(2,1)}, bf16[4096,1024]{1,0:T(8,128)(2,1)}, u32[]{:S(2)}, u32[]{:S(2)}) collective-permute-start(bf16[4096,1024]{1,0:T(8,128)(2,1)} %refs_7_.2), channel_id=1, source_target_pairs={{0,1},{1,0},{2,3},{3,2},{4,5},{5,4},{6,7},{7,6},{8,9},{9,8},{10,11... | collective-permute-start | bytes 25165832 | tf_op jit(solution)/shard_map/ppermute | solution.py:610
  43.6 44.6 %collective-permute-start.8 = (bf16[3,64,5120]{2,1,0:T(8,128)(2,1)}, bf16[3,64,5120]{2,1,0:T(8,128)(2,1)S(1)}, u32[]{:S(2)}, u32[]{:S(2)}) collective-permute-start(bf16[3,64,5120]{2,1,0:T(8,128)(2,1)} %shard_map.103), channel_id=1, source_target_pairs={{0,2},{1,3},{2,0},{3,1},{4,6},{5,7},{6,4},{7,5},{8,10},{9,11},{10,... | collective-permute-start | bytes 5898248 | tf_op jit(solution)/shard_map/ppermute | solution.py:610
  43.8 36.5 %collective-permute-start.9 = (bf16[768,1024]{1,0:T(8,128)(2,1)S(1)}, bf16[768,1024]{1,0:T(8,128)(2,1)}, u32[]{:S(2)}, u32[]{:S(2)}) collective-permute-start(bf16[768,1024]{1,0:T(8,128)(2,1)S(1)} %collective-permute-done.4.refs_1_), channel_id=1, source_target_pairs={{0,4},{4,8},{8,12},{1,5},{5,9},{9,13},{2,6},{6,10},{10,14},{3,7},{... | collective-permute-start | bytes 4718600 | tf_op jit(solution)/shard_map/ppermute | solution.py:642
  48.1 37.3 %collective-permute-start.10 = (bf16[768,1024]{1,0:T(8,128)(2,1)S(1)}, bf16[768,1024]{1,0:T(8,128)(2,1)}, u32[]{:S(2)}, u32[]{:S(2)}) collective-permute-start(bf16[768,1024]{1,0:T(8,128)(2,1)S(1)} %collective-permute-done.5.refs_2_), channel_id=1, source_target_pairs={{4,0},{8,4},{12,8},{5,1},{9,5},{13,9},{6,2},{10,6},{14,10},{7,3},{... | collective-permute-start | bytes 4718600 | tf_op jit(solution)/shard_map/ppermute | solution.py:642
  49.4 24.5 %collective-permute-start.11 = (bf16[512,1024]{1,0:T(8,128)(2,1)}, bf16[512,1024]{1,0:T(8,128)(2,1)S(1)}, u32[]{:S(2)}, u32[]{:S(2)}) collective-permute-start(bf16[512,1024]{1,0:T(8,128)(2,1)} %collective-permute-done.6.refs_9_), channel_id=1, source_target_pairs={{0,16},{16,0},{1,17},{17,1},{2,18},{18,2},{3,19},{19,3},{4,20},{20... | collective-permute-start | bytes 3145736 | tf_op jit(solution)/shard_map/ppermute | solution.py:684
  73.9 11.6 %copy-start.2 = (bf16[512,1024]{1,0:T(8,128)(2,1)}, bf16[512,1024]{1,0:T(8,128)(2,1)S(1)}, u32[]{:S(2)}) copy-start(bf16[512,1024]{1,0:T(8,128)(2,1)S(1)} %collective-permute-done.11.refs_13_) | copy-start | bytes 3145732
  88.2 1.3 copy-start.6
  89.5 24.1 %collective-permute-start.18 = (bf16[512,1024]{1,0:T(8,128)(2,1)}, bf16[512,1024]{1,0:T(8,128)(2,1)}, u32[]{:S(2)}, u32[]{:S(2)}) collective-permute-start(bf16[512,1024]{1,0:T(8,128)(2,1)} %get-tuple-element.66), channel_id=1, source_target_pairs={{0,2},{1,3},{2,0},{3,1},{4,6},{5,7},{6,4},{7,5},{8,10},{9,11},{10,... | collective-permute-start | bytes 3145736 | tf_op jit(solution)/shard_map/ppermute | solution.py:610
  89.7 50.3 %collective-permute-start.16 = (bf16[768,1024]{1,0:T(8,128)(2,1)}, bf16[768,1024]{1,0:T(8,128)(2,1)}, u32[]{:S(2)}, u32[]{:S(2)}) collective-permute-start(bf16[768,1024]{1,0:T(8,128)(2,1)} %collective-permute-done.9.refs_3_), channel_id=1, source_target_pairs={{0,4},{4,8},{8,12},{1,5},{5,9},{9,13},{2,6},{6,10},{10,14},{3,7},{... | collective-permute-start | bytes 4718600 | tf_op jit(solution)/shard_map/ppermute | solution.py:642
  93.9 46.1 %collective-permute-start.17 = (bf16[768,1024]{1,0:T(8,128)(2,1)}, bf16[768,1024]{1,0:T(8,128)(2,1)}, u32[]{:S(2)}, u32[]{:S(2)}) collective-permute-start(bf16[768,1024]{1,0:T(8,128)(2,1)} %collective-permute-done.10.refs_4_), channel_id=1, source_target_pairs={{4,0},{8,4},{12,8},{5,1},{9,5},{13,9},{6,2},{10,6},{14,10},{7,3},{... | collective-permute-start | bytes 4718600 | tf_op jit(solution)/shard_map/ppermute | solution.py:642
  95.2 44.8 %collective-permute-start.19 = (bf16[512,1024]{1,0:T(8,128)(2,1)}, bf16[512,1024]{1,0:T(8,128)(2,1)}, u32[]{:S(2)}, u32[]{:S(2)}) collective-permute-start(bf16[512,1024]{1,0:T(8,128)(2,1)} %get-tuple-element.67), channel_id=1, source_target_pairs={{0,2},{1,3},{2,0},{3,1},{4,6},{5,7},{6,4},{7,5},{8,10},{9,11},{10,... | collective-permute-start | bytes 3145736 | tf_op jit(solution)/shard_map/ppermute | solution.py:610
  113.6 26.5 %collective-permute-start.20 = (bf16[512,1024]{1,0:T(8,128)(2,1)}, bf16[512,1024]{1,0:T(8,128)(2,1)S(1)}, u32[]{:S(2)}, u32[]{:S(2)}) collective-permute-start(bf16[512,1024]{1,0:T(8,128)(2,1)} %collective-permute-done.18.refs_11_), channel_id=1, source_target_pairs={{0,16},{16,0},{1,17},{17,1},{2,18},{18,2},{3,19},{19,3},{4,20},{20... | collective-permute-start | bytes 3145736 | tf_op jit(solution)/shard_map/ppermute | solution.py:684
  114.8 24.1 %collective-permute-start.12 = (f32[3,256,128]{2,1,0:T(8,128)}, f32[3,256,128]{2,1,0:T(8,128)S(1)}, u32[]{:S(2)}, u32[]{:S(2)}) collective-permute-start(f32[3,256,128]{2,1,0:T(8,128)} %get-tuple-element.56), channel_id=1, source_target_pairs={{0,4},{4,0},{8,12},{12,8},{1,5},{5,1},{9,13},{13,9},{2,6},{6,2},{1... | collective-permute-start | bytes 1179656 | tf_op jit(solution)/shard_map/ppermute | solution.py:610
  140.0 25.5 %copy-start.7 = (f32[3,256,128]{2,1,0:T(8,128)}, f32[3,256,128]{2,1,0:T(8,128)S(1)}, u32[]{:S(2)}) copy-start(f32[3,256,128]{2,1,0:T(8,128)S(1)} %add.112.here_ref) | copy-start | bytes 1179652
  140.0 5.4 %copy-start.8 = (bf16[512,1024]{1,0:T(8,128)(2,1)}, bf16[512,1024]{1,0:T(8,128)(2,1)S(1)}, u32[]{:S(2)}) copy-start(bf16[512,1024]{1,0:T(8,128)(2,1)S(1)} %collective-permute-done.20.refs_17_) | copy-start | bytes 3145732
  140.1 5.4 %collective-permute-start.22 = (bf16[512,1024]{1,0:T(8,128)(2,1)}, bf16[512,1024]{1,0:T(8,128)(2,1)S(1)}, u32[]{:S(2)}, u32[]{:S(2)}) collective-permute-start(bf16[512,1024]{1,0:T(8,128)(2,1)} %collective-permute-done.6.refs_9_), channel_id=1, source_target_pairs={{0,1},{1,0},{2,3},{3,2},{4,5},{5,4},{6,7},{7,6},{8,9},{9,8},{10,11... | collective-permute-start | bytes 3145736 | tf_op jit(solution)/shard_map/ppermute | solution.py:610
  142.5 25.1 %collective-permute-start.21 = (bf16[512,1024]{1,0:T(8,128)(2,1)}, bf16[512,1024]{1,0:T(8,128)(2,1)}, u32[]{:S(2)}, u32[]{:S(2)}) collective-permute-start(bf16[512,1024]{1,0:T(8,128)(2,1)} %get-tuple-element.69), channel_id=1, source_target_pairs={{0,2},{1,3},{2,0},{3,1},{4,6},{5,7},{6,4},{7,5},{8,10},{9,11},{10,... | collective-permute-start | bytes 3145736 | tf_op jit(solution)/shard_map/ppermute | solution.py:610
  143.7 2.9 %collective-permute-start.23 = (bf16[512,1024]{1,0:T(8,128)(2,1)}, bf16[512,1024]{1,0:T(8,128)(2,1)S(1)}, u32[]{:S(2)}, u32[]{:S(2)}) collective-permute-start(bf16[512,1024]{1,0:T(8,128)(2,1)} %collective-permute-done.18.refs_11_), channel_id=1, source_target_pairs={{0,1},{1,0},{2,3},{3,2},{4,5},{5,4},{6,7},{7,6},{8,9},{9,8},{10,11... | collective-permute-start | bytes 3145736 | tf_op jit(solution)/shard_map/ppermute | solution.py:610
  144.0 4.0 %collective-permute-start.24 = (bf16[512,1024]{1,0:T(8,128)(2,1)}, bf16[512,1024]{1,0:T(8,128)(2,1)S(1)}, u32[]{:S(2)}, u32[]{:S(2)}) collective-permute-start(bf16[512,1024]{1,0:T(8,128)(2,1)} %copy-done.2), channel_id=1, source_target_pairs={{0,1},{1,0},{2,3},{3,2},{4,5},{5,4},{6,7},{7,6},{8,9},{9,8},{10,11... | collective-permute-start | bytes 3145736 | tf_op jit(solution)/shard_map/ppermute | solution.py:610
  144.2 24.7 %collective-permute-start.25 = (bf16[512,1024]{1,0:T(8,128)(2,1)}, bf16[512,1024]{1,0:T(8,128)(2,1)}, u32[]{:S(2)}, u32[]{:S(2)}) collective-permute-start(bf16[512,1024]{1,0:T(8,128)(2,1)} %collective-permute-done.19.refs_15_), channel_id=1, source_target_pairs={{0,16},{16,0},{1,17},{17,1},{2,18},{18,2},{3,19},{19,3},{4,20},{20... | collective-permute-start | bytes 3145736 | tf_op jit(solution)/shard_map/ppermute | solution.py:684
  145.4 2.6 %copy-start.3 = (bf16[512,1024]{1,0:T(8,128)(2,1)}, bf16[512,1024]{1,0:T(8,128)(2,1)S(1)}, u32[]{:S(2)}) copy-start(bf16[512,1024]{1,0:T(8,128)(2,1)S(1)} %collective-permute-done.22.refs_10_) | copy-start | bytes 3145732
  145.4 20.1 %collective-permute-start.13 = (f32[3,256,128]{2,1,0:T(8,128)S(1)}, f32[3,256,128]{2,1,0:T(8,128)}, u32[]{:S(2)}, u32[]{:S(2)}) collective-permute-start(f32[3,256,128]{2,1,0:T(8,128)S(1)} %add.112.here_ref), channel_id=1, source_target_pairs={{0,8},{4,12},{8,0},{12,4},{1,9},{5,13},{9,1},{13,5},{2,10},{6,14},... | collective-permute-start | bytes 1179656 | tf_op jit(solution)/shard_map/ppermute | solution.py:610
  146.6 1.5 copy-start.4
  148.1 1.0 copy-start.5
  168.9 10.7 %copy-start.15 = (s32[3]{0:T(128)S(1)}, s32[3]{0:T(128)}, u32[]{:S(2)}) copy-start(s32[3]{0:T(128)} %live_ref.1) | copy-start | bytes 40
  168.9 10.6 %collective-permute-start.26 = (bf16[512,1024]{1,0:T(8,128)(2,1)}, bf16[512,1024]{1,0:T(8,128)(2,1)S(1)}, u32[]{:S(2)}, u32[]{:S(2)}) collective-permute-start(bf16[512,1024]{1,0:T(8,128)(2,1)} %collective-permute-done.19.refs_15_), channel_id=1, source_target_pairs={{0,1},{1,0},{2,3},{3,2},{4,5},{5,4},{6,7},{7,6},{8,9},{9,8},{10,11... | collective-permute-start | bytes 3145736 | tf_op jit(solution)/shard_map/ppermute | solution.py:610
  170.1 10.3 %collective-permute-start.27 = (bf16[512,1024]{1,0:T(8,128)(2,1)}, bf16[512,1024]{1,0:T(8,128)(2,1)S(1)}, u32[]{:S(2)}, u32[]{:S(2)}) collective-permute-start(bf16[512,1024]{1,0:T(8,128)(2,1)} %copy-done.8), channel_id=1, source_target_pairs={{0,1},{1,0},{2,3},{3,2},{4,5},{5,4},{6,7},{7,6},{8,9},{9,8},{10,11... | collective-permute-start | bytes 3145736 | tf_op jit(solution)/shard_map/ppermute | solution.py:610
  170.1 32.6 %collective-permute-start.31 = (bf16[512,1024]{1,0:T(8,128)(2,1)}, bf16[512,1024]{1,0:T(8,128)(2,1)S(1)}, u32[]{:S(2)}, u32[]{:S(2)}) collective-permute-start(bf16[512,1024]{1,0:T(8,128)(2,1)} %collective-permute-done.21.refs_9_), channel_id=1, source_target_pairs={{0,16},{16,0},{1,17},{17,1},{2,18},{18,2},{3,19},{19,3},{4,20},{20... | collective-permute-start | bytes 3145736 | tf_op jit(solution)/shard_map/ppermute | solution.py:684
  178.2 22.8 %collective-permute-start.28 = (bf16[3,64,2560]{2,1,0:T(8,128)(2,1)}, bf16[3,64,2560]{2,1,0:T(8,128)(2,1)}, u32[]{:S(2)}, u32[]{:S(2)}) collective-permute-start(bf16[3,64,2560]{2,1,0:T(8,128)(2,1)} %get-tuple-element.58.refs_1_), channel_id=1, source_target_pairs={{0,2},{1,3},{2,0},{3,1},{4,6},{5,7},{6,4},{7,5},{8,10},{9,11},{10,... | collective-permute-start | bytes 2949128 | tf_op jit(solution)/shard_map/ppermute | solution.py:610
  178.4 24.8 %collective-permute-start.14 = (bf16[3,64,2560]{2,1,0:T(8,128)(2,1)}, bf16[3,64,2560]{2,1,0:T(8,128)(2,1)}, u32[]{:S(2)}, u32[]{:S(2)}) collective-permute-start(bf16[3,64,2560]{2,1,0:T(8,128)(2,1)} %get-tuple-element.57.refs_0_), channel_id=1, source_target_pairs={{0,1},{1,0},{2,3},{3,2},{4,5},{5,4},{6,7},{7,6},{8,9},{9,8},{10,11... | collective-permute-start | bytes 2949128 | tf_op jit(solution)/shard_map/ppermute | solution.py:610
  179.5 1.0 copy-start.12
  179.5 24.9 %collective-permute-start.15 = (bf16[3,64,2560]{2,1,0:T(8,128)(2,1)}, bf16[3,64,2560]{2,1,0:T(8,128)(2,1)}, u32[]{:S(2)}, u32[]{:S(2)}) collective-permute-start(bf16[3,64,2560]{2,1,0:T(8,128)(2,1)} %get-tuple-element.58.refs_1_), channel_id=1, source_target_pairs={{0,1},{1,0},{2,3},{3,2},{4,5},{5,4},{6,7},{7,6},{8,9},{9,8},{10,11... | collective-permute-start | bytes 2949128 | tf_op jit(solution)/shard_map/ppermute | solution.py:610
  180.4 1.0 copy-start.13
  201.0 10.0 %collective-permute-start.29 = (bf16[512,1024]{1,0:T(8,128)(2,1)}, bf16[512,1024]{1,0:T(8,128)(2,1)S(1)}, u32[]{:S(2)}, u32[]{:S(2)}) collective-permute-start(bf16[512,1024]{1,0:T(8,128)(2,1)} %collective-permute-done.21.refs_9_), channel_id=1, source_target_pairs={{0,1},{1,0},{2,3},{3,2},{4,5},{5,4},{6,7},{7,6},{8,9},{9,8},{10,11... | collective-permute-start | bytes 3145736 | tf_op jit(solution)/shard_map/ppermute | solution.py:610
  202.7 8.4 %collective-permute-start.30 = (bf16[512,1024]{1,0:T(8,128)(2,1)}, bf16[512,1024]{1,0:T(8,128)(2,1)S(1)}, u32[]{:S(2)}, u32[]{:S(2)}) collective-permute-start(bf16[512,1024]{1,0:T(8,128)(2,1)} %collective-permute-done.25.refs_11_), channel_id=1, source_target_pairs={{0,1},{1,0},{2,3},{3,2},{4,5},{5,4},{6,7},{7,6},{8,9},{9,8},{10,11... | collective-permute-start | bytes 3145736 | tf_op jit(solution)/shard_map/ppermute | solution.py:610
  202.7 7.7 %copy-start.9 = (bf16[512,1024]{1,0:T(8,128)(2,1)}, bf16[512,1024]{1,0:T(8,128)(2,1)S(1)}, u32[]{:S(2)}) copy-start(bf16[512,1024]{1,0:T(8,128)(2,1)S(1)} %collective-permute-done.31.refs_13_) | copy-start | bytes 3145732
  202.7 8.4 %collective-permute-start.32 = (bf16[512,1024]{1,0:T(8,128)(2,1)S(1)}, bf16[512,1024]{1,0:T(8,128)(2,1)}, u32[]{:S(2)}, u32[]{:S(2)}) collective-permute-start(bf16[512,1024]{1,0:T(8,128)(2,1)S(1)} %collective-permute-done.31.refs_13_), channel_id=1, source_target_pairs={{0,1},{1,0},{2,3},{3,2},{4,5},{5,4},{6,7},{7,6},{8,9},{9,8},{10,11... | collective-permute-start | bytes 3145736 | tf_op jit(solution)/shard_map/ppermute | solution.py:610
  203.2 28.8 %collective-permute-start.33 = (bf16[3,64,2560]{2,1,0:T(8,128)(2,1)}, bf16[3,64,2560]{2,1,0:T(8,128)(2,1)}, u32[]{:S(2)}, u32[]{:S(2)}) collective-permute-start(bf16[3,64,2560]{2,1,0:T(8,128)(2,1)} %get-tuple-element.57.refs_0_), channel_id=1, source_target_pairs={{0,2},{1,3},{2,0},{3,1},{4,6},{5,7},{6,4},{7,5},{8,10},{9,11},{10,... | collective-permute-start | bytes 2949128 | tf_op jit(solution)/shard_map/ppermute | solution.py:610
  211.0 21.4 %collective-permute-start.35 = (bf16[3,64,2560]{2,1,0:T(8,128)(2,1)}, bf16[3,64,2560]{2,1,0:T(8,128)(2,1)}, u32[]{:S(2)}, u32[]{:S(2)}) collective-permute-start(bf16[3,64,2560]{2,1,0:T(8,128)(2,1)} %collective-permute-done.28.refs_1_), channel_id=1, source_target_pairs={{0,1},{1,0},{2,3},{3,2},{4,5},{5,4},{6,7},{7,6},{8,9},{9,8},{10,11... | collective-permute-start | bytes 2949128 | tf_op jit(solution)/shard_map/ppermute | solution.py:610
  211.0 1.0 copy-start.10
  211.1 1.3 copy-start.11
  232.0 2.8 %collective-permute-start.34 = (bf16[3,64,2560]{2,1,0:T(8,128)(2,1)}, bf16[3,64,2560]{2,1,0:T(8,128)(2,1)S(1)}, u32[]{:S(2)}, u32[]{:S(2)}) collective-permute-start(bf16[3,64,2560]{2,1,0:T(8,128)(2,1)} %collective-permute-done.33.refs_0_), channel_id=1, source_target_pairs={{0,1},{1,0},{2,3},{3,2},{4,5},{5,4},{6,7},{7,6},{8,9},{9,8},{10,11... | collective-permute-start | bytes 2949128 | tf_op jit(solution)/shard_map/ppermute | solution.py:610
  234.9 1.0 copy-start.14

commit v11 on v10

--- a/solution.py
+++ b/solution.py
@@ -760,7 +760,7 @@
 
     others = range(1, n_groups)
     ahead = line and share > tile
-    begun = begin((0, 0), (0, 1), *[(g, 0) for g in others]) if ahead else []
+    begun = begin((0, 0), (0, 1)) if ahead else []
     past = [other, *begun, *flat(*crossed, *sum(turned, []))]
     low_terms, high_terms, coef = block_terms(
         island_live_rows, total, other, hidden, output_gradient
@@ -792,29 +792,23 @@
             [sums_of[name] for name in named if name in sums_of], coef, block_a, grad_hidden, token,
         )
 
-    def add_near(grad_a, grad_b):
-        low, high = spread({0: low_terms}), spread({0: high_terms})
-        pieces = [p for r in near for p in (low[r], high[r])]
-        return add_terms(relative[:edge], pieces, grad_a, grad_b, coef)
-
-    edge = count * len(near)
     if share > tile:
         multiply(*[(0, t) for t in range(3)], *[(g, t) for g in others for t in range(2)])
         past = [token, far_high]
         fill(crossed[3:], *past)
         for pieces in turned[2:]:
             fill(pieces, *past)
-        grad_a, grad_b = add_near(grad_a, grad_b)
-        scalars = behind(scalars, grad_b)
         multiply((0, 3), *[(g, t) for g in others for t in range(2, 4)])
     else:
         multiply(*[(g, 0) for g in range(n_groups)])
-        grad_a, grad_b = add_near(grad_a, grad_b)
-
+
+    near_low = spread({0: behind(low_terms, *past)})
+    near_high = spread({0: behind(high_terms, *past)})
     all_high = spread({top: behind(far_high, *past)})
     all_low = spread({top: behind(far_low, token)})
-    terms = [p for r in near for p in (all_low[r + top], all_high[r + top])]
-    grad_a, grad_b = add_terms(relative[edge:], terms, grad_a, grad_b, token)
+    terms = [p for r in near for p in (near_low[r], near_high[r])]
+    terms += [p for r in near for p in (all_low[r + top], all_high[r + top])]
+    grad_a, grad_b = add_terms(relative, terms, grad_a, grad_b, token)
     return grad_hidden, jnp.swapaxes(grad_a, 1, 2), grad_b
 
 

time: 243 us -> 236 us (0.971)
  the two profiles are of different devices: /device:TPU:3 before, /device:TPU:11 now
where the time goes in v11:
time: 236 us; the launch traced here: 232 us
  waiting for transfers between devices  96 us (41%)
  Pallas kernels  80.5 us (34%)
  starting transfers between devices  40.1 us (17%)
  local copies, waits for them, and re-layouts  9.38 us (4%)
  other arithmetic  4.95 us (2%)
    ppermute x26, waiting for transfers between devices, swap(): return lax.ppermute(value, axis, [(i, i ^ bit) for i in range(size)])  56.6 us
    pallas_call x2, Pallas kernels, base(): pl.pallas_call(functools.partial(base_kernel, n_dp, tiles, len(chunks), [...  39.9 us
    ppermute x4, waiting for transfers between devices, turn(): turned[j].append({top: lax.ppermute(piece, 'groups', ring)})  25.1 us
    ppermute x26, starting transfers between devices, swap(): return lax.ppermute(value, axis, [(i, i ^ bit) for i in range(size)])  20.1 us
    ppermute x6, starting transfers between devices, hop(): sent.append(lax.ppermute(piece, 'fsdp', pairs))  15.9 us
    ppermute x6, waiting for transfers between devices, hop(): sent.append(lax.ppermute(piece, 'fsdp', pairs))  14.3 us
    pallas_call x1, Pallas kernels, early_sums(): pl.pallas_call(functools.partial(early_kernel, n_dp, tiles, len(chunks),...  12.9 us
    pallas_call x1, Pallas kernels, project(): pl.pallas_call(functools.partial(project_kernel, pieces), grid_spec=pltpu...  11.7 us
  transfers between devices with their start and end apart: 36, of which 16 were waited for; matrix products, arithmetic and copies ran while one was open for 5% of the time, Pallas kernels for 33%

profile of v11, /device:TPU:11, one launch (start us, length us, event | category | flops | bytes accessed | tf_op | source)
XLA Modules:
  0.0 231.9 jit_solution(12576820922575134397)
XLA Ops:
  0.6 0.7 collective-permute-start.3
  1.4 3.2 %collective-permute-start = (bf16[768,1024]{1,0:T(8,128)(2,1)}, bf16[768,1024]{1,0:T(8,128)(2,1)S(1)}, u32[]{:S(2)}, u32[]{:S(2)}) collective-permute-start(bf16[768,1024]{1,0:T(8,128)(2,1)} %refs_0_.5), channel_id=1, source_target_pairs={{0,4},{4,8},{8,12},{1,5},{5,9},{9,13},{2,6},{6,10},{10,14},{3,7},{... | collective-permute-start | bytes 4718600 | tf_op jit(solution)/shard_map/ppermute | solution.py:642
  4.6 2.2 collective-permute-start.1
  6.8 0.9 select_reduce_fusion
  7.6 0.3 collective-permute-start.2
  7.9 0.9 collective-permute-start.4
  8.8 4.2 %constant_dynamic-slice_fusion = (bf16[512,1024]{1,0:T(8,128)(2,1)}, bf16[512,1024]{1,0:T(8,128)(2,1)}, bf16[512,1024]{1,0:T(8,128)(2,1)}, bf16[512,1024]{1,0:T(8,128)(2,1)}) fusion(bf16[4096,1024]{1,0:T(8,128)(2,1)} %refs_7_.2, s32[]{:T(128)S(6)} %select_n.94, s32[]{:T(128)S(6)} %select_n.89, s32[]{:T(128)S(6)} %select_n.88, s32[]{:T(128)S(6)} %select_n.93), kind=kLoop, calls=%fused_computation.13 | loop fusion | bytes 8388624 | tf_op jit(solution)/shard_map/dynamic_slice | solution.py:672
  13.0 1.2 collective-permute-start.6
  14.3 0.6 compare_select_fusion.1
  14.8 0.7 pad_add_fusion.index_ref
  15.6 4.8 %shard_map.103 = bf16[3,64,5120]{2,1,0:T(8,128)(2,1)} custom-call(s32[6]{0:T(128)} %pad_add_fusion.index_ref, s32[3]{0:T(128)} %get-tuple-element.99.source_ref, bf16[8,64,4096]{2,1,0:T(8,128)(2,1)} %bitcast.22, bf16[8,64,4096]{2,1,0:T(8,128)(2,1)} %collective-permute-done.3.refs_1_, bf16[8,64,1024]{2,1,0:T(8,128)(2,1)} %refs_2_.3, ...), custom_call_target="tpu_custom_call" | custom-call | bytes 5898240 | tf_op jit(solution)/shard_map/pallas_call | solution.py:54
  20.4 17.8 %collective-permute-done.6.refs_9_ = bf16[512,1024]{1,0:T(8,128)(2,1)} collective-permute-done((bf16[512,1024]{1,0:T(8,128)(2,1)}, bf16[512,1024]{1,0:T(8,128)(2,1)}, u32[]{:S(2)}, u32[]{:S(2)}) %collective-permute-start.6) | collective-permute-done | bytes 1048608 | tf_op jit(solution)/shard_map/ppermute | solution.py:610
  38.1 1.3 collective-permute-done.refs_1_
  39.5 2.9 %collective-permute-done.1.refs_2_ = bf16[768,1024]{1,0:T(8,128)(2,1)S(1)} collective-permute-done((bf16[768,1024]{1,0:T(8,128)(2,1)}, bf16[768,1024]{1,0:T(8,128)(2,1)S(1)}, u32[]{:S(2)}, u32[]{:S(2)}) %collective-permute-start.1) | collective-permute-done | bytes 1572896 | tf_op jit(solution)/shard_map/ppermute | solution.py:642
  42.4 1.1 collective-permute-start.13
  43.5 0.3 collective-permute-start.9
  43.8 2.2 collective-permute-start.8
  45.9 3.1 %collective-permute-start.7 = (bf16[768,1024]{1,0:T(8,128)(2,1)S(1)}, bf16[768,1024]{1,0:T(8,128)(2,1)}, u32[]{:S(2)}, u32[]{:S(2)}) collective-permute-start(bf16[768,1024]{1,0:T(8,128)(2,1)S(1)} %collective-permute-done.refs_1_), channel_id=1, source_target_pairs={{0,4},{4,8},{8,12},{1,5},{5,9},{9,13},{2,6},{6,10},{10,14},{3,7},{... | collective-permute-start | bytes 4718600 | tf_op jit(solution)/shard_map/ppermute | solution.py:642
  49.0 1.3 collective-permute-start.10
  50.3 22.8 %collective-permute-done.10.refs_15_ = bf16[512,1024]{1,0:T(8,128)(2,1)} collective-permute-done((bf16[512,1024]{1,0:T(8,128)(2,1)}, bf16[512,1024]{1,0:T(8,128)(2,1)}, u32[]{:S(2)}, u32[]{:S(2)}) %collective-permute-start.10) | collective-permute-done | bytes 1048608 | tf_op jit(solution)/shard_map/ppermute | solution.py:684
  73.2 8.2 %collective-permute-done.8.refs_4_ = bf16[768,1024]{1,0:T(8,128)(2,1)} collective-permute-done((bf16[768,1024]{1,0:T(8,128)(2,1)S(1)}, bf16[768,1024]{1,0:T(8,128)(2,1)}, u32[]{:S(2)}, u32[]{:S(2)}) %collective-permute-start.8) | collective-permute-done | bytes 1572896 | tf_op jit(solution)/shard_map/ppermute | solution.py:642
  81.4 1.9 collective-permute-done.7.refs_3_
  83.2 5.0 %collective-permute-done.9.refs_4_ = bf16[3,64,5120]{2,1,0:T(8,128)(2,1)} collective-permute-done((bf16[3,64,5120]{2,1,0:T(8,128)(2,1)}, bf16[3,64,5120]{2,1,0:T(8,128)(2,1)}, u32[]{:S(2)}, u32[]{:S(2)}) %collective-permute-start.9) | collective-permute-done | bytes 1966112 | tf_op jit(solution)/shard_map/ppermute | solution.py:610
  88.2 0.3 collective-permute-start.15
  88.4 2.2 collective-permute-start.12
  90.6 3.1 %collective-permute-start.11 = (bf16[768,1024]{1,0:T(8,128)(2,1)}, bf16[768,1024]{1,0:T(8,128)(2,1)}, u32[]{:S(2)}, u32[]{:S(2)}) collective-permute-start(bf16[768,1024]{1,0:T(8,128)(2,1)} %collective-permute-done.7.refs_3_), channel_id=1, source_target_pairs={{0,4},{4,8},{8,12},{1,5},{5,9},{9,13},{2,6},{6,10},{10,14},{3,7},{... | collective-permute-start | bytes 4718600 | tf_op jit(solution)/shard_map/ppermute | solution.py:642
  93.7 1.3 collective-permute-start.16
  95.0 0.5 compare_select_fusion
  95.6 0.6 pad_add_fusion.2.index_ref
  96.1 11.7 %shard_map.104 = (f32[3,256,128]{2,1,0:T(8,128)}, bf16[3,64,4096]{2,1,0:T(8,128)(2,1)}, f32[8,64,4096]{2,1,0:T(8,128)}, f32[8,64,1024]{2,1,0:T(8,128)}) custom-call(s32[6]{0:T(128)} %pad_add_fusion.2.index_ref, s32[3]{0:T(128)} %get-tuple-element.97.source_ref, bf16[8,64,4096]{2,1,0:T(8,128)(2,1)} %bitcast.23, ...), custom_call_target="tpu_custom_call" | custom-call | flops 503316480 | bytes 15728640 | tf_op jit(solution)/shard_map/pallas_call | solution.py:121
  107.8 4.5 %collective-permute-done.15.refs_11_ = bf16[512,1024]{1,0:T(8,128)(2,1)} collective-permute-done((bf16[512,1024]{1,0:T(8,128)(2,1)}, bf16[512,1024]{1,0:T(8,128)(2,1)}, u32[]{:S(2)}, u32[]{:S(2)}) %collective-permute-start.15) | collective-permute-done | bytes 1048608 | tf_op jit(solution)/shard_map/ppermute | solution.py:610
  112.3 1.2 collective-permute-start.17
  113.6 0.3 collective-permute-start.14
  113.8 21.9 %collective-permute-done.14 = f32[3,256,128]{2,1,0:T(8,128)S(1)} collective-permute-done((f32[3,256,128]{2,1,0:T(8,128)}, f32[3,256,128]{2,1,0:T(8,128)S(1)}, u32[]{:S(2)}, u32[]{:S(2)}) %collective-permute-start.14) | collective-permute-done | bytes 393248 | tf_op jit(solution)/shard_map/ppermute | solution.py:610
  135.7 1.0 add.113.here_ref
  136.8 2.3 collective-permute-start.20
  139.1 1.3 collective-permute-start.23
  140.4 0.3 collective-permute-start.22
  140.9 1.2 collective-permute-start.18
  142.1 3.4 %collective-permute-start.21 = (f32[3,256,128]{2,1,0:T(8,128)S(1)}, f32[3,256,128]{2,1,0:T(8,128)}, u32[]{:S(2)}, u32[]{:S(2)}) collective-permute-start(f32[3,256,128]{2,1,0:T(8,128)S(1)} %add.113.here_ref), channel_id=1, source_target_pairs={{0,8},{4,12},{8,0},{12,4},{1,9},{5,13},{9,1},{13,5},{2,10},{6,14},... | collective-permute-start | bytes 1179656 | tf_op jit(solution)/shard_map/ppermute | solution.py:610
  145.6 0.7 concatenate.31.scalars_ref
  146.3 1.0 copy-done.3
  147.2 12.9 %shard_map.105 = (f32[768,512]{1,0:T(8,128)}, f32[768,512]{1,0:T(8,128)}) custom-call(s32[13]{0:T(128)} %concatenate.31.scalars_ref, bf16[768,1024]{1,0:T(8,128)(2,1)} %refs_0_.5, bf16[768,1024]{1,0:T(8,128)(2,1)} %copy-done, bf16[768,1024]{1,0:T(8,128)(2,1)} %copy-done.1, bf16[768,1024]{1,0:T(8,128)(2,1)} %collective-permute-done.7.refs_3_, ...), custom_call_target="tpu_custom_call" | custom-call | flops 1 | bytes 1 | tf_op jit(solution)/shard_map/pallas_call | solution.py:438
  160.1 1.8 collective-permute-done.21.there_ref
  161.9 2.3 collective-permute-done.23.refs_11_
  164.2 1.4 collective-permute-done.18.refs_9_
  165.6 1.2 collective-permute-start.25
  167.0 6.8 %shard_map.106 = (bf16[3,64,2560]{2,1,0:T(8,128)(2,1)}, bf16[3,64,2560]{2,1,0:T(8,128)(2,1)}, bf16[3,256,64]{2,1,0:T(8,128)(2,1)}) custom-call(s32[3]{0:T(128)} %live_ref.1, f32[3,256,128]{2,1,0:T(8,128)} %copy-done.4, f32[3,256,128]{2,1,0:T(8,128)} %collective-permute-done.21.there_ref, bf16[768,4096]{1,0:T(8,128)(2,1)} %hid_ref.1, bf16[768,1024]{1,0:T(8,128)(2,1)} %refs_0_.5), custom_call_target="tpu_custom_call" | custom-call | flops 503316480 | bytes 9830400 | tf_op jit(solution)/shard_map/pallas_call | solution.py:186
  173.9 1.2 collective-permute-start.26
  175.1 0.7 concatenate.30.scalars_ref
  175.8 1.0 copy-done.8
  176.8 20.5 %shard_map.107 = (bf16[768,4096]{1,0:T(8,128)(2,1)}, f32[8,128]{1,0:T(8,128)}) custom-call(s32[19]{0:T(128)} %concatenate.30.scalars_ref, bf16[768,1024]{1,0:T(8,128)(2,1)} %refs_0_.5, bf16[768,1024]{1,0:T(8,128)(2,1)} %copy-done, bf16[768,1024]{1,0:T(8,128)(2,1)} %copy-done.1, bf16[768,1024]{1,0:T(8,128)(2,1)} %collective-permute-done.7.refs_3_, ...), custom_call_target="tpu_custom_call" | custom-call | flops 1 | bytes 1 | tf_op jit(solution)/shard_map/pallas_call | solution.py:473
  197.3 1.1 collective-permute-start.30
  198.5 0.4 collective-permute-start.27
  198.9 1.2 collective-permute-start.33
  200.1 0.7 concatenate.26.scalars_ref
  200.8 0.3 collective-permute-start.35
  201.3 0.4 collective-permute-start.32
  201.7 2.0 collective-permute-done.28.refs_12_
  204.0 19.5 %shard_map.108 = (bf16[768,4096]{1,0:T(8,128)(2,1)}, f32[8,128]{1,0:T(8,128)}) custom-call(s32[17]{0:T(128)} %concatenate.26.scalars_ref, bf16[768,1024]{1,0:T(8,128)(2,1)} %refs_0_.5, bf16[768,1024]{1,0:T(8,128)(2,1)} %copy-done, bf16[768,1024]{1,0:T(8,128)(2,1)} %copy-done.1, ...), custom_call_target="tpu_custom_call", output_to_operand_aliasing={{0}: (19, {})} | custom-call | flops 1 | bytes 1 | tf_op jit(solution)/shard_map/pallas_call | solution.py:473
  223.9 0.6 add_subtract_fusion.slots_ref
  224.5 1.8 collective-permute-done.34.refs_6_
  226.3 1.0 copy-done.11
  227.3 4.4 %shard_map.109 = (f32[8,64,4096]{2,1,0:T(8,128)}, f32[8,64,1024]{2,1,0:T(8,128)}) custom-call(s32[12]{0:T(128)} %add_subtract_fusion.slots_ref, bf16[3,64,2560]{2,1,0:T(8,128)(2,1)} %get-tuple-element.80.refs_0_, bf16[3,64,2560]{2,1,0:T(8,128)(2,1)} %get-tuple-element.81.refs_1_, ...), custom_call_target="tpu_custom_call", output_to_operand_aliasing={{0}: (10, {}), {1}: (11, {})} | custom-call | flops 1 | bytes 1 | tf_op jit(solution)/shard_map/pallas_call | solution.py:562
  (55 shorter events, 1.5 us)
Async XLA Ops:
  0.6 15.0 %collective-permute-start.3 = (bf16[8,64,4096]{2,1,0:T(8,128)(2,1)}, bf16[8,64,4096]{2,1,0:T(8,128)(2,1)}, u32[]{:S(2)}, u32[]{:S(2)}) collective-permute-start(bf16[8,64,4096]{2,1,0:T(8,128)(2,1)} %bitcast.21), channel_id=1, source_target_pairs={{0,1},{1,0},{2,3},{3,2},{4,5},{5,4},{6,7},{7,6},{8,9},{9,8},{10,11... | collective-permute-start | bytes 12582920 | tf_op jit(solution)/shard_map/ppermute | solution.py:610
  1.4 38.1 %collective-permute-start = (bf16[768,1024]{1,0:T(8,128)(2,1)}, bf16[768,1024]{1,0:T(8,128)(2,1)S(1)}, u32[]{:S(2)}, u32[]{:S(2)}) collective-permute-start(bf16[768,1024]{1,0:T(8,128)(2,1)} %refs_0_.5), channel_id=1, source_target_pairs={{0,4},{4,8},{8,12},{1,5},{5,9},{9,13},{2,6},{6,10},{10,14},{3,7},{... | collective-permute-start | bytes 4718600 | tf_op jit(solution)/shard_map/ppermute | solution.py:642
  4.6 37.8 %collective-permute-start.1 = (bf16[768,1024]{1,0:T(8,128)(2,1)}, bf16[768,1024]{1,0:T(8,128)(2,1)S(1)}, u32[]{:S(2)}, u32[]{:S(2)}) collective-permute-start(bf16[768,1024]{1,0:T(8,128)(2,1)} %refs_0_.5), channel_id=1, source_target_pairs={{4,0},{8,4},{12,8},{5,1},{9,5},{13,9},{6,2},{10,6},{14,10},{7,3},{... | collective-permute-start | bytes 4718600 | tf_op jit(solution)/shard_map/ppermute | solution.py:642
  7.6 5.4 %collective-permute-start.2 = (s32[3]{0:T(128)S(1)}, s32[3]{0:T(128)S(1)}, u32[]{:S(2)}, u32[]{:S(2)}) collective-permute-start(s32[3]{0:T(128)S(1)} %select_reduce_fusion), channel_id=1, source_target_pairs={{0,2},{1,3},{2,0},{3,1},{4,6},{5,7},{6,4},{7,5},{8,10},{9,11},{10,... | collective-permute-start | bytes 44 | tf_op jit(solution)/shard_map/ppermute | solution.py:610
  7.9 7.7 %collective-permute-start.4 = (bf16[8,64,1024]{2,1,0:T(8,128)(2,1)}, bf16[8,64,1024]{2,1,0:T(8,128)(2,1)}, u32[]{:S(2)}, u32[]{:S(2)}) collective-permute-start(bf16[8,64,1024]{2,1,0:T(8,128)(2,1)} %refs_2_.3), channel_id=1, source_target_pairs={{0,1},{1,0},{2,3},{3,2},{4,5},{5,4},{6,7},{7,6},{8,9},{9,8},{10,11... | collective-permute-start | bytes 3145736 | tf_op jit(solution)/shard_map/ppermute | solution.py:610
  13.0 25.1 %collective-permute-start.6 = (bf16[512,1024]{1,0:T(8,128)(2,1)}, bf16[512,1024]{1,0:T(8,128)(2,1)}, u32[]{:S(2)}, u32[]{:S(2)}) collective-permute-start(bf16[512,1024]{1,0:T(8,128)(2,1)} %get-tuple-element.47), channel_id=1, source_target_pairs={{0,2},{1,3},{2,0},{3,1},{4,6},{5,7},{6,4},{7,5},{8,10},{9,11},{10,... | collective-permute-start | bytes 3145736 | tf_op jit(solution)/shard_map/ppermute | solution.py:610
  20.3 22.0 %collective-permute-start.5 = (s32[6]{0:T(128)S(1)}, s32[6]{0:T(128)S(1)}, u32[]{:S(2)}, u32[]{:S(2)}) collective-permute-start(s32[6]{0:T(128)S(1)} %pad_add_fusion.1), channel_id=1, source_target_pairs={{0,1},{1,0},{2,3},{3,2},{4,5},{5,4},{6,7},{7,6},{8,9},{9,8},{10,11... | collective-permute-start | bytes 80 | tf_op jit(solution)/shard_map/ppermute | solution.py:610
  39.5 68.4 %copy-start = (bf16[768,1024]{1,0:T(8,128)(2,1)}, bf16[768,1024]{1,0:T(8,128)(2,1)S(1)}, u32[]{:S(2)}) copy-start(bf16[768,1024]{1,0:T(8,128)(2,1)S(1)} %collective-permute-done.refs_1_) | copy-start | bytes 4718596
  42.4 65.5 %copy-start.1 = (bf16[768,1024]{1,0:T(8,128)(2,1)}, bf16[768,1024]{1,0:T(8,128)(2,1)S(1)}, u32[]{:S(2)}) copy-start(bf16[768,1024]{1,0:T(8,128)(2,1)S(1)} %collective-permute-done.1.refs_2_) | copy-start | bytes 4718596
  42.4 52.7 %collective-permute-start.13 = (bf16[4096,1024]{1,0:T(8,128)(2,1)}, bf16[4096,1024]{1,0:T(8,128)(2,1)}, u32[]{:S(2)}, u32[]{:S(2)}) collective-permute-start(bf16[4096,1024]{1,0:T(8,128)(2,1)} %refs_7_.2), channel_id=1, source_target_pairs={{0,1},{1,0},{2,3},{3,2},{4,5},{5,4},{6,7},{7,6},{8,9},{9,8},{10,11... | collective-permute-start | bytes 25165832 | tf_op jit(solution)/shard_map/ppermute | solution.py:610
  43.5 44.7 %collective-permute-start.9 = (bf16[3,64,5120]{2,1,0:T(8,128)(2,1)}, bf16[3,64,5120]{2,1,0:T(8,128)(2,1)}, u32[]{:S(2)}, u32[]{:S(2)}) collective-permute-start(bf16[3,64,5120]{2,1,0:T(8,128)(2,1)} %shard_map.103), channel_id=1, source_target_pairs={{0,2},{1,3},{2,0},{3,1},{4,6},{5,7},{6,4},{7,5},{8,10},{9,11},{10,... | collective-permute-start | bytes 5898248 | tf_op jit(solution)/shard_map/ppermute | solution.py:610
  43.8 37.6 %collective-permute-start.8 = (bf16[768,1024]{1,0:T(8,128)(2,1)S(1)}, bf16[768,1024]{1,0:T(8,128)(2,1)}, u32[]{:S(2)}, u32[]{:S(2)}) collective-permute-start(bf16[768,1024]{1,0:T(8,128)(2,1)S(1)} %collective-permute-done.1.refs_2_), channel_id=1, source_target_pairs={{4,0},{8,4},{12,8},{5,1},{9,5},{13,9},{6,2},{10,6},{14,10},{7,3},{... | collective-permute-start | bytes 4718600 | tf_op jit(solution)/shard_map/ppermute | solution.py:642
  45.9 37.3 %collective-permute-start.7 = (bf16[768,1024]{1,0:T(8,128)(2,1)S(1)}, bf16[768,1024]{1,0:T(8,128)(2,1)}, u32[]{:S(2)}, u32[]{:S(2)}) collective-permute-start(bf16[768,1024]{1,0:T(8,128)(2,1)S(1)} %collective-permute-done.refs_1_), channel_id=1, source_target_pairs={{0,4},{4,8},{8,12},{1,5},{5,9},{9,13},{2,6},{6,10},{10,14},{3,7},{... | collective-permute-start | bytes 4718600 | tf_op jit(solution)/shard_map/ppermute | solution.py:642
  49.0 24.1 %collective-permute-start.10 = (bf16[512,1024]{1,0:T(8,128)(2,1)}, bf16[512,1024]{1,0:T(8,128)(2,1)}, u32[]{:S(2)}, u32[]{:S(2)}) collective-permute-start(bf16[512,1024]{1,0:T(8,128)(2,1)} %collective-permute-done.6.refs_9_), channel_id=1, source_target_pairs={{0,16},{16,0},{1,17},{17,1},{2,18},{18,2},{3,19},{19,3},{4,20},{20... | collective-permute-start | bytes 3145736 | tf_op jit(solution)/shard_map/ppermute | solution.py:684
  88.2 24.1 %collective-permute-start.15 = (bf16[512,1024]{1,0:T(8,128)(2,1)}, bf16[512,1024]{1,0:T(8,128)(2,1)}, u32[]{:S(2)}, u32[]{:S(2)}) collective-permute-start(bf16[512,1024]{1,0:T(8,128)(2,1)} %get-tuple-element.57), channel_id=1, source_target_pairs={{0,2},{1,3},{2,0},{3,1},{4,6},{5,7},{6,4},{7,5},{8,10},{9,11},{10,... | collective-permute-start | bytes 3145736 | tf_op jit(solution)/shard_map/ppermute | solution.py:610
  88.4 48.3 %collective-permute-start.12 = (bf16[768,1024]{1,0:T(8,128)(2,1)}, bf16[768,1024]{1,0:T(8,128)(2,1)}, u32[]{:S(2)}, u32[]{:S(2)}) collective-permute-start(bf16[768,1024]{1,0:T(8,128)(2,1)} %collective-permute-done.8.refs_4_), channel_id=1, source_target_pairs={{4,0},{8,4},{12,8},{5,1},{9,5},{13,9},{6,2},{10,6},{14,10},{7,3},{... | collective-permute-start | bytes 4718600 | tf_op jit(solution)/shard_map/ppermute | solution.py:642
  90.6 46.2 %collective-permute-start.11 = (bf16[768,1024]{1,0:T(8,128)(2,1)}, bf16[768,1024]{1,0:T(8,128)(2,1)}, u32[]{:S(2)}, u32[]{:S(2)}) collective-permute-start(bf16[768,1024]{1,0:T(8,128)(2,1)} %collective-permute-done.7.refs_3_), channel_id=1, source_target_pairs={{0,4},{4,8},{8,12},{1,5},{5,9},{9,13},{2,6},{6,10},{10,14},{3,7},{... | collective-permute-start | bytes 4718600 | tf_op jit(solution)/shard_map/ppermute | solution.py:642
  93.7 43.0 %collective-permute-start.16 = (bf16[512,1024]{1,0:T(8,128)(2,1)}, bf16[512,1024]{1,0:T(8,128)(2,1)}, u32[]{:S(2)}, u32[]{:S(2)}) collective-permute-start(bf16[512,1024]{1,0:T(8,128)(2,1)} %get-tuple-element.58), channel_id=1, source_target_pairs={{0,2},{1,3},{2,0},{3,1},{4,6},{5,7},{6,4},{7,5},{8,10},{9,11},{10,... | collective-permute-start | bytes 3145736 | tf_op jit(solution)/shard_map/ppermute | solution.py:610
  112.3 24.5 %collective-permute-start.17 = (bf16[512,1024]{1,0:T(8,128)(2,1)}, bf16[512,1024]{1,0:T(8,128)(2,1)S(1)}, u32[]{:S(2)}, u32[]{:S(2)}) collective-permute-start(bf16[512,1024]{1,0:T(8,128)(2,1)} %collective-permute-done.15.refs_11_), channel_id=1, source_target_pairs={{0,16},{16,0},{1,17},{17,1},{2,18},{18,2},{3,19},{19,3},{4,20},{20... | collective-permute-start | bytes 3145736 | tf_op jit(solution)/shard_map/ppermute | solution.py:684
  113.6 22.2 %collective-permute-start.14 = (f32[3,256,128]{2,1,0:T(8,128)}, f32[3,256,128]{2,1,0:T(8,128)S(1)}, u32[]{:S(2)}, u32[]{:S(2)}) collective-permute-start(f32[3,256,128]{2,1,0:T(8,128)} %get-tuple-element.56), channel_id=1, source_target_pairs={{0,4},{4,0},{8,12},{12,8},{1,5},{5,1},{9,13},{13,9},{2,6},{6,2},{1... | collective-permute-start | bytes 1179656 | tf_op jit(solution)/shard_map/ppermute | solution.py:610
  136.8 23.3 %copy-start.4 = (f32[3,256,128]{2,1,0:T(8,128)}, f32[3,256,128]{2,1,0:T(8,128)S(1)}, u32[]{:S(2)}) copy-start(f32[3,256,128]{2,1,0:T(8,128)S(1)} %add.113.here_ref) | copy-start | bytes 1179652
  136.8 5.3 %copy-start.6 = (bf16[512,1024]{1,0:T(8,128)(2,1)}, bf16[512,1024]{1,0:T(8,128)(2,1)S(1)}, u32[]{:S(2)}) copy-start(bf16[512,1024]{1,0:T(8,128)(2,1)S(1)} %collective-permute-done.17.refs_17_) | copy-start | bytes 3145732
  136.8 5.3 %collective-permute-start.20 = (bf16[512,1024]{1,0:T(8,128)(2,1)}, bf16[512,1024]{1,0:T(8,128)(2,1)S(1)}, u32[]{:S(2)}, u32[]{:S(2)}) collective-permute-start(bf16[512,1024]{1,0:T(8,128)(2,1)} %collective-permute-done.15.refs_11_), channel_id=1, source_target_pairs={{0,1},{1,0},{2,3},{3,2},{4,5},{5,4},{6,7},{7,6},{8,9},{9,8},{10,11... | collective-permute-start | bytes 3145736 | tf_op jit(solution)/shard_map/ppermute | solution.py:610
  139.1 25.1 %collective-permute-start.23 = (bf16[512,1024]{1,0:T(8,128)(2,1)}, bf16[512,1024]{1,0:T(8,128)(2,1)S(1)}, u32[]{:S(2)}, u32[]{:S(2)}) collective-permute-start(bf16[512,1024]{1,0:T(8,128)(2,1)} %collective-permute-done.16.refs_13_), channel_id=1, source_target_pairs={{0,16},{16,0},{1,17},{17,1},{2,18},{18,2},{3,19},{19,3},{4,20},{20... | collective-permute-start | bytes 3145736 | tf_op jit(solution)/shard_map/ppermute | solution.py:684
  140.4 23.8 %collective-permute-start.22 = (bf16[512,1024]{1,0:T(8,128)(2,1)}, bf16[512,1024]{1,0:T(8,128)(2,1)}, u32[]{:S(2)}, u32[]{:S(2)}) collective-permute-start(bf16[512,1024]{1,0:T(8,128)(2,1)} %collective-permute-done.10.refs_15_), channel_id=1, source_target_pairs={{0,1},{1,0},{2,3},{3,2},{4,5},{5,4},{6,7},{7,6},{8,9},{9,8},{10,11... | collective-permute-start | bytes 3145736 | tf_op jit(solution)/shard_map/ppermute | solution.py:610
  140.7 5.5 %collective-permute-start.19 = (bf16[512,1024]{1,0:T(8,128)(2,1)}, bf16[512,1024]{1,0:T(8,128)(2,1)S(1)}, u32[]{:S(2)}, u32[]{:S(2)}) collective-permute-start(bf16[512,1024]{1,0:T(8,128)(2,1)} %collective-permute-done.6.refs_9_), channel_id=1, source_target_pairs={{0,1},{1,0},{2,3},{3,2},{4,5},{5,4},{6,7},{7,6},{8,9},{9,8},{10,11... | collective-permute-start | bytes 3145736 | tf_op jit(solution)/shard_map/ppermute | solution.py:610
  140.9 24.7 %collective-permute-start.18 = (bf16[512,1024]{1,0:T(8,128)(2,1)}, bf16[512,1024]{1,0:T(8,128)(2,1)}, u32[]{:S(2)}, u32[]{:S(2)}) collective-permute-start(bf16[512,1024]{1,0:T(8,128)(2,1)} %get-tuple-element.60), channel_id=1, source_target_pairs={{0,2},{1,3},{2,0},{3,1},{4,6},{5,7},{6,4},{7,5},{8,10},{9,11},{10,... | collective-permute-start | bytes 3145736 | tf_op jit(solution)/shard_map/ppermute | solution.py:610
  142.1 4.1 %copy-start.2 = (bf16[512,1024]{1,0:T(8,128)(2,1)}, bf16[512,1024]{1,0:T(8,128)(2,1)S(1)}, u32[]{:S(2)}) copy-start(bf16[512,1024]{1,0:T(8,128)(2,1)S(1)} %collective-permute-done.20.refs_12_) | copy-start | bytes 3145732
  142.1 19.8 %collective-permute-start.21 = (f32[3,256,128]{2,1,0:T(8,128)S(1)}, f32[3,256,128]{2,1,0:T(8,128)}, u32[]{:S(2)}, u32[]{:S(2)}) collective-permute-start(f32[3,256,128]{2,1,0:T(8,128)S(1)} %add.113.here_ref), channel_id=1, source_target_pairs={{0,8},{4,12},{8,0},{12,4},{1,9},{5,13},{9,1},{13,5},{2,10},{6,14},... | collective-permute-start | bytes 1179656 | tf_op jit(solution)/shard_map/ppermute | solution.py:610
  146.3 1.0 copy-start.3
  164.2 34.2 %copy-start.5 = (bf16[512,1024]{1,0:T(8,128)(2,1)}, bf16[512,1024]{1,0:T(8,128)(2,1)S(1)}, u32[]{:S(2)}) copy-start(bf16[512,1024]{1,0:T(8,128)(2,1)S(1)} %collective-permute-done.23.refs_11_) | copy-start | bytes 3145732
  165.6 9.5 %copy-start.12 = (s32[3]{0:T(128)S(1)}, s32[3]{0:T(128)}, u32[]{:S(2)}) copy-start(s32[3]{0:T(128)} %live_ref.1) | copy-start | bytes 40
  165.6 10.2 %collective-permute-start.25 = (bf16[512,1024]{1,0:T(8,128)(2,1)}, bf16[512,1024]{1,0:T(8,128)(2,1)S(1)}, u32[]{:S(2)}, u32[]{:S(2)}) collective-permute-start(bf16[512,1024]{1,0:T(8,128)(2,1)} %copy-done.6), channel_id=1, source_target_pairs={{0,1},{1,0},{2,3},{3,2},{4,5},{5,4},{6,7},{7,6},{8,9},{9,8},{10,11... | collective-permute-start | bytes 3145736 | tf_op jit(solution)/shard_map/ppermute | solution.py:610
  166.8 9.0 %collective-permute-start.24 = (bf16[512,1024]{1,0:T(8,128)(2,1)}, bf16[512,1024]{1,0:T(8,128)(2,1)}, u32[]{:S(2)}, u32[]{:S(2)}) collective-permute-start(bf16[512,1024]{1,0:T(8,128)(2,1)} %collective-permute-done.16.refs_13_), channel_id=1, source_target_pairs={{0,1},{1,0},{2,3},{3,2},{4,5},{5,4},{6,7},{7,6},{8,9},{9,8},{10,11... | collective-permute-start | bytes 3145736 | tf_op jit(solution)/shard_map/ppermute | solution.py:610
  166.8 30.4 %collective-permute-start.29 = (bf16[512,1024]{1,0:T(8,128)(2,1)}, bf16[512,1024]{1,0:T(8,128)(2,1)S(1)}, u32[]{:S(2)}, u32[]{:S(2)}) collective-permute-start(bf16[512,1024]{1,0:T(8,128)(2,1)} %collective-permute-done.18.refs_9_), channel_id=1, source_target_pairs={{0,16},{16,0},{1,17},{17,1},{2,18},{18,2},{3,19},{19,3},{4,20},{20... | collective-permute-start | bytes 3145736 | tf_op jit(solution)/shard_map/ppermute | solution.py:684
  173.9 23.3 %collective-permute-start.26 = (bf16[3,64,2560]{2,1,0:T(8,128)(2,1)}, bf16[3,64,2560]{2,1,0:T(8,128)(2,1)}, u32[]{:S(2)}, u32[]{:S(2)}) collective-permute-start(bf16[3,64,2560]{2,1,0:T(8,128)(2,1)} %get-tuple-element.81.refs_1_), channel_id=1, source_target_pairs={{0,2},{1,3},{2,0},{3,1},{4,6},{5,7},{6,4},{7,5},{8,10},{9,11},{10,... | collective-permute-start | bytes 2949128 | tf_op jit(solution)/shard_map/ppermute | solution.py:610
  175.8 1.0 copy-start.8
  197.2 6.8 %copy-start.7 = (bf16[512,1024]{1,0:T(8,128)(2,1)}, bf16[512,1024]{1,0:T(8,128)(2,1)S(1)}, u32[]{:S(2)}) copy-start(bf16[512,1024]{1,0:T(8,128)(2,1)S(1)} %collective-permute-done.29.refs_13_) | copy-start | bytes 3145732
  197.3 4.0 %collective-permute-start.30 = (bf16[512,1024]{1,0:T(8,128)(2,1)S(1)}, bf16[512,1024]{1,0:T(8,128)(2,1)S(1)}, u32[]{:S(2)}, u32[]{:S(2)}) collective-permute-start(bf16[512,1024]{1,0:T(8,128)(2,1)S(1)} %collective-permute-done.29.refs_13_), channel_id=1, source_target_pairs={{0,1},{1,0},{2,3},{3,2},{4,5},{5,4},{6,7},{7,6},{8,9},{9,8},{10,11... | collective-permute-start | bytes 3145736 | tf_op jit(solution)/shard_map/ppermute | solution.py:610
  198.4 5.3 %collective-permute-start.28 = (bf16[512,1024]{1,0:T(8,128)(2,1)S(1)}, bf16[512,1024]{1,0:T(8,128)(2,1)}, u32[]{:S(2)}, u32[]{:S(2)}) collective-permute-start(bf16[512,1024]{1,0:T(8,128)(2,1)S(1)} %collective-permute-done.23.refs_11_), channel_id=1, source_target_pairs={{0,1},{1,0},{2,3},{3,2},{4,5},{5,4},{6,7},{7,6},{8,9},{9,8},{10,11... | collective-permute-start | bytes 3145736 | tf_op jit(solution)/shard_map/ppermute | solution.py:610
  198.5 5.5 %collective-permute-start.27 = (bf16[512,1024]{1,0:T(8,128)(2,1)}, bf16[512,1024]{1,0:T(8,128)(2,1)}, u32[]{:S(2)}, u32[]{:S(2)}) collective-permute-start(bf16[512,1024]{1,0:T(8,128)(2,1)} %collective-permute-done.18.refs_9_), channel_id=1, source_target_pairs={{0,1},{1,0},{2,3},{3,2},{4,5},{5,4},{6,7},{7,6},{8,9},{9,8},{10,11... | collective-permute-start | bytes 3145736 | tf_op jit(solution)/shard_map/ppermute | solution.py:610
  198.9 24.6 %collective-permute-start.33 = (bf16[3,64,2560]{2,1,0:T(8,128)(2,1)}, bf16[3,64,2560]{2,1,0:T(8,128)(2,1)}, u32[]{:S(2)}, u32[]{:S(2)}) collective-permute-start(bf16[3,64,2560]{2,1,0:T(8,128)(2,1)} %get-tuple-element.80.refs_0_), channel_id=1, source_target_pairs={{0,2},{1,3},{2,0},{3,1},{4,6},{5,7},{6,4},{7,5},{8,10},{9,11},{10,... | collective-permute-start | bytes 2949128 | tf_op jit(solution)/shard_map/ppermute | solution.py:610
  200.8 23.7 %collective-permute-start.35 = (bf16[3,64,2560]{2,1,0:T(8,128)(2,1)}, bf16[3,64,2560]{2,1,0:T(8,128)(2,1)}, u32[]{:S(2)}, u32[]{:S(2)}) collective-permute-start(bf16[3,64,2560]{2,1,0:T(8,128)(2,1)} %collective-permute-done.26.refs_5_), channel_id=1, source_target_pairs={{0,1},{1,0},{2,3},{3,2},{4,5},{5,4},{6,7},{7,6},{8,9},{9,8},{10,11... | collective-permute-start | bytes 2949128 | tf_op jit(solution)/shard_map/ppermute | solution.py:610
  201.3 2.7 %copy-start.9 = (bf16[512,1024]{1,0:T(8,128)(2,1)}, bf16[512,1024]{1,0:T(8,128)(2,1)S(1)}, u32[]{:S(2)}) copy-start(bf16[512,1024]{1,0:T(8,128)(2,1)S(1)} %collective-permute-done.30.refs_14_) | copy-start | bytes 3145732
  201.3 23.2 %collective-permute-start.32 = (bf16[3,64,2560]{2,1,0:T(8,128)(2,1)}, bf16[3,64,2560]{2,1,0:T(8,128)(2,1)}, u32[]{:S(2)}, u32[]{:S(2)}) collective-permute-start(bf16[3,64,2560]{2,1,0:T(8,128)(2,1)} %get-tuple-element.81.refs_1_), channel_id=1, source_target_pairs={{0,1},{1,0},{2,3},{3,2},{4,5},{5,4},{6,7},{7,6},{8,9},{9,8},{10,11... | collective-permute-start | bytes 2949128 | tf_op jit(solution)/shard_map/ppermute | solution.py:610
  203.7 20.8 %collective-permute-start.31 = (bf16[3,64,2560]{2,1,0:T(8,128)(2,1)}, bf16[3,64,2560]{2,1,0:T(8,128)(2,1)S(1)}, u32[]{:S(2)}, u32[]{:S(2)}) collective-permute-start(bf16[3,64,2560]{2,1,0:T(8,128)(2,1)} %get-tuple-element.80.refs_0_), channel_id=1, source_target_pairs={{0,1},{1,0},{2,3},{3,2},{4,5},{5,4},{6,7},{7,6},{8,9},{9,8},{10,11... | collective-permute-start | bytes 2949128 | tf_op jit(solution)/shard_map/ppermute | solution.py:610
  223.5 2.8 %collective-permute-start.34 = (bf16[3,64,2560]{2,1,0:T(8,128)(2,1)}, bf16[3,64,2560]{2,1,0:T(8,128)(2,1)S(1)}, u32[]{:S(2)}, u32[]{:S(2)}) collective-permute-start(bf16[3,64,2560]{2,1,0:T(8,128)(2,1)} %collective-permute-done.33.refs_4_), channel_id=1, source_target_pairs={{0,1},{1,0},{2,3},{3,2},{4,5},{5,4},{6,7},{7,6},{8,9},{9,8},{10,11... | collective-permute-start | bytes 2949128 | tf_op jit(solution)/shard_map/ppermute | solution.py:610
  224.5 1.8 copy-start.10
  226.3 1.0 copy-start.11

commit v12 on v11

--- a/solution.py
+++ b/solution.py
@@ -517,11 +517,10 @@
             for part in range(2)
         ]
 
-    def whole(slot, inward):
-        pairs = [(a_ref.at[slot], a.at[slot]), (b_ref.at[slot], b.at[slot])]
+    def whole(slot):
         return [
-            pltpu.make_async_copy(*(pair if inward else pair[::-1]), sem.at[slot])
-            for pair, sem in zip(pairs, (a_sem, b_sem))
+            pltpu.make_async_copy(a.at[slot], a_ref.at[slot], a_sem.at[slot]),
+            pltpu.make_async_copy(b.at[slot], b_ref.at[slot], b_sem.at[slot]),
         ]
 
     wanted = [slots_ref[k] for k in range(pieces * count)]
@@ -533,12 +532,14 @@
             any_here = any_here | (slot == j)
         hit.append(any_here)
 
-    for j in range(local):
-        pl.when(hit[j])(lambda j=j: start(whole(j, True)))
+    def clear(j):
+        a[j] = jnp.zeros(a.shape[1:], f32)
+        b[j] = jnp.zeros(b.shape[1:], f32)
+
     for k in range(pieces * count):
         pl.when(owned[k])(lambda k=k: start(load(k)))
     for j in range(local):
-        pl.when(hit[j])(lambda j=j: wait(whole(j, True)))
+        pl.when(hit[j])(lambda j=j: clear(j))
 
     def add(k):
         wait(load(k))
@@ -548,9 +549,9 @@
     for k in range(pieces * count):
         pl.when(owned[k])(lambda k=k: add(k))
     for j in range(local):
-        pl.when(hit[j])(lambda j=j: start(whole(j, False)))
+        pl.when(hit[j])(lambda j=j: start(whole(j)))
     for j in range(local):
-        pl.when(hit[j])(lambda j=j: wait(whole(j, False)))
+        pl.when(hit[j])(lambda j=j: wait(whole(j)))
 
 
 def add_terms(slots, pieces, grad_a, grad_b, token):
@@ -761,15 +762,14 @@
     others = range(1, n_groups)
     ahead = line and share > tile
     begun = begin((0, 0), (0, 1)) if ahead else []
-    past = [other, *begun, *flat(*crossed, *sum(turned, []))]
-    low_terms, high_terms, coef = block_terms(
-        island_live_rows, total, other, hidden, output_gradient
-    )
+    live = behind(island_live_rows, *begun)
+    low_terms, high_terms, coef = block_terms(live, total, other, hidden, output_gradient)
+    past = [coef, *flat(*crossed, *sum(turned, []))]
     far_high = swap(high_terms, top)
     far_low = swap(low_terms, top)
     turn(*past)
-    fill(crossed[2:3], *past)
-    for pieces in turned[1:2]:
+    fill(crossed[2:], *past)
+    for pieces in turned[1:3]:
         fill(pieces, *past)
     if line:
         at = jnp.stack(where).astype(i32)
@@ -795,8 +795,7 @@
     if share > tile:
         multiply(*[(0, t) for t in range(3)], *[(g, t) for g in others for t in range(2)])
         past = [token, far_high]
-        fill(crossed[3:], *past)
-        for pieces in turned[2:]:
+        for pieces in turned[3:]:
             fill(pieces, *past)
         multiply((0, 3), *[(g, t) for g in others for t in range(2, 4)])
     else:

time: 236 us -> 231 us (0.979)
  waiting for transfers between devices: 96 us -> 92.7 us
  transfers between devices with their start and end apart: 36 -> 36, of which waited for: 16 -> 14; matrix products, arithmetic and copies ran while one was open for 5% -> 5% of each run, Pallas kernels for 33% -> 33%
where the time goes in v12:
time: 231 us; the launch traced here: 227 us
  waiting for transfers between devices  92.7 us (40%)
  Pallas kernels  79.5 us (34%)
  starting transfers between devices  40.6 us (18%)
  local copies, waits for them, and re-layouts  8.53 us (4%)
  other arithmetic  5.05 us (2%)
    ppermute x26, waiting for transfers between devices, swap(): return lax.ppermute(value, axis, [(i, i ^ bit) for i in range(size)])  55.7 us
    pallas_call x2, Pallas kernels, base(): pl.pallas_call(functools.partial(base_kernel, n_dp, tiles, len(chunks), [...  39.9 us
    ppermute x4, waiting for transfers between devices, turn(): turned[j].append({top: lax.ppermute(piece, 'groups', ring)})  22.8 us
    ppermute x26, starting transfers between devices, swap(): return lax.ppermute(value, axis, [(i, i ^ bit) for i in range(size)])  20.5 us
    ppermute x6, starting transfers between devices, hop(): sent.append(lax.ppermute(piece, 'fsdp', pairs))  15.9 us
    ppermute x6, waiting for transfers between devices, hop(): sent.append(lax.ppermute(piece, 'fsdp', pairs))  14.2 us
    pallas_call x1, Pallas kernels, early_sums(): pl.pallas_call(functools.partial(early_kernel, n_dp, tiles, len(chunks),...  12.9 us
    pallas_call x1, Pallas kernels, project(): pl.pallas_call(functools.partial(project_kernel, pieces), grid_spec=pltpu...  11.2 us
  transfers between devices with their start and end apart: 36, of which 14 were waited for; matrix products, arithmetic and copies ran while one was open for 5% of the time, Pallas kernels for 33%

profile of v12, /device:TPU:11, one launch (start us, length us, event | category | flops | bytes accessed | tf_op | source)
XLA Modules:
  0.0 227.5 jit_solution(17041552240396702586)
XLA Ops:
  0.6 0.7 collective-permute-start.3
  1.4 3.2 %collective-permute-start = (bf16[768,1024]{1,0:T(8,128)(2,1)}, bf16[768,1024]{1,0:T(8,128)(2,1)S(1)}, u32[]{:S(2)}, u32[]{:S(2)}) collective-permute-start(bf16[768,1024]{1,0:T(8,128)(2,1)} %refs_0_.5), channel_id=1, source_target_pairs={{0,4},{4,8},{8,12},{1,5},{5,9},{9,13},{2,6},{6,10},{10,14},{3,7},{... | collective-permute-start | bytes 4718600 | tf_op jit(solution)/shard_map/ppermute | solution.py:643
  4.6 2.2 collective-permute-start.1
  6.8 0.9 select_reduce_fusion
  7.6 0.3 collective-permute-start.2
  7.9 0.9 collective-permute-start.4
  8.8 4.3 %constant_dynamic-slice_fusion = (bf16[512,1024]{1,0:T(8,128)(2,1)}, bf16[512,1024]{1,0:T(8,128)(2,1)}, bf16[512,1024]{1,0:T(8,128)(2,1)}, bf16[512,1024]{1,0:T(8,128)(2,1)}) fusion(bf16[4096,1024]{1,0:T(8,128)(2,1)} %refs_7_.2, s32[]{:T(128)S(6)} %select_n.94, s32[]{:T(128)S(6)} %select_n.89, s32[]{:T(128)S(6)} %select_n.88, s32[]{:T(128)S(6)} %select_n.93), kind=kLoop, calls=%fused_computation.13 | loop fusion | bytes 8388624 | tf_op jit(solution)/shard_map/dynamic_slice | solution.py:673
  13.1 1.2 collective-permute-start.6
  14.3 0.6 compare_select_fusion.1
  14.9 0.7 pad_add_fusion.index_ref
  15.7 4.8 %shard_map.103 = bf16[3,64,5120]{2,1,0:T(8,128)(2,1)} custom-call(s32[6]{0:T(128)} %pad_add_fusion.index_ref, s32[3]{0:T(128)} %get-tuple-element.99.source_ref, bf16[8,64,4096]{2,1,0:T(8,128)(2,1)} %bitcast.22, bf16[8,64,4096]{2,1,0:T(8,128)(2,1)} %collective-permute-done.3.refs_1_, bf16[8,64,1024]{2,1,0:T(8,128)(2,1)} %refs_2_.3, ...), custom_call_target="tpu_custom_call" | custom-call | bytes 5898240 | tf_op jit(solution)/shard_map/pallas_call | solution.py:54
  20.4 0.3 collective-permute-start.5
  20.7 17.5 %collective-permute-done.6.refs_9_ = bf16[512,1024]{1,0:T(8,128)(2,1)} collective-permute-done((bf16[512,1024]{1,0:T(8,128)(2,1)}, bf16[512,1024]{1,0:T(8,128)(2,1)}, u32[]{:S(2)}, u32[]{:S(2)}) %collective-permute-start.6) | collective-permute-done | bytes 1048608 | tf_op jit(solution)/shard_map/ppermute | solution.py:611
  38.2 1.2 collective-permute-done.refs_1_
  39.5 2.9 %collective-permute-done.1.refs_2_ = bf16[768,1024]{1,0:T(8,128)(2,1)S(1)} collective-permute-done((bf16[768,1024]{1,0:T(8,128)(2,1)}, bf16[768,1024]{1,0:T(8,128)(2,1)S(1)}, u32[]{:S(2)}, u32[]{:S(2)}) %collective-permute-start.1) | collective-permute-done | bytes 1572896 | tf_op jit(solution)/shard_map/ppermute | solution.py:643
  42.4 1.1 collective-permute-start.13
  43.8 2.2 collective-permute-start.8
  45.9 3.1 %collective-permute-start.7 = (bf16[768,1024]{1,0:T(8,128)(2,1)S(1)}, bf16[768,1024]{1,0:T(8,128)(2,1)}, u32[]{:S(2)}, u32[]{:S(2)}) collective-permute-start(bf16[768,1024]{1,0:T(8,128)(2,1)S(1)} %collective-permute-done.refs_1_), channel_id=1, source_target_pairs={{0,4},{4,8},{8,12},{1,5},{5,9},{9,13},{2,6},{6,10},{10,14},{3,7},{... | collective-permute-start | bytes 4718600 | tf_op jit(solution)/shard_map/ppermute | solution.py:643
  49.0 1.3 collective-permute-start.10
  50.3 22.8 %collective-permute-done.10.refs_15_ = bf16[512,1024]{1,0:T(8,128)(2,1)S(1)} collective-permute-done((bf16[512,1024]{1,0:T(8,128)(2,1)}, bf16[512,1024]{1,0:T(8,128)(2,1)S(1)}, u32[]{:S(2)}, u32[]{:S(2)}) %collective-permute-start.10) | collective-permute-done | bytes 1048608 | tf_op jit(solution)/shard_map/ppermute | solution.py:685
  73.2 8.2 %collective-permute-done.8.refs_4_ = bf16[768,1024]{1,0:T(8,128)(2,1)} collective-permute-done((bf16[768,1024]{1,0:T(8,128)(2,1)S(1)}, bf16[768,1024]{1,0:T(8,128)(2,1)}, u32[]{:S(2)}, u32[]{:S(2)}) %collective-permute-start.8) | collective-permute-done | bytes 1572896 | tf_op jit(solution)/shard_map/ppermute | solution.py:643
  81.4 1.9 collective-permute-done.7.refs_3_
  83.2 5.0 %collective-permute-done.9.refs_4_ = bf16[3,64,5120]{2,1,0:T(8,128)(2,1)} collective-permute-done((bf16[3,64,5120]{2,1,0:T(8,128)(2,1)}, bf16[3,64,5120]{2,1,0:T(8,128)(2,1)}, u32[]{:S(2)}, u32[]{:S(2)}) %collective-permute-start.9) | collective-permute-done | bytes 1966112 | tf_op jit(solution)/shard_map/ppermute | solution.py:611
  88.4 2.2 collective-permute-start.12
  90.6 3.1 %collective-permute-start.11 = (bf16[768,1024]{1,0:T(8,128)(2,1)}, bf16[768,1024]{1,0:T(8,128)(2,1)}, u32[]{:S(2)}, u32[]{:S(2)}) collective-permute-start(bf16[768,1024]{1,0:T(8,128)(2,1)} %collective-permute-done.7.refs_3_), channel_id=1, source_target_pairs={{0,4},{4,8},{8,12},{1,5},{5,9},{9,13},{2,6},{6,10},{10,14},{3,7},{... | collective-permute-start | bytes 4718600 | tf_op jit(solution)/shard_map/ppermute | solution.py:643
  93.7 1.3 collective-permute-start.16
  95.0 0.5 compare_select_fusion
  95.5 0.6 pad_add_fusion.2.index_ref
  96.2 11.2 %shard_map.104 = (f32[3,256,128]{2,1,0:T(8,128)}, bf16[3,64,4096]{2,1,0:T(8,128)(2,1)}, f32[8,64,4096]{2,1,0:T(8,128)}, f32[8,64,1024]{2,1,0:T(8,128)}) custom-call(s32[6]{0:T(128)} %pad_add_fusion.2.index_ref, s32[3]{0:T(128)} %get-tuple-element.97.source_ref, bf16[8,64,4096]{2,1,0:T(8,128)(2,1)} %bitcast.23, ...), custom_call_target="tpu_custom_call" | custom-call | flops 503316480 | bytes 15728640 | tf_op jit(solution)/shard_map/pallas_call | solution.py:121
  107.4 4.9 %collective-permute-done.15.refs_11_ = bf16[512,1024]{1,0:T(8,128)(2,1)} collective-permute-done((bf16[512,1024]{1,0:T(8,128)(2,1)}, bf16[512,1024]{1,0:T(8,128)(2,1)}, u32[]{:S(2)}, u32[]{:S(2)}) %collective-permute-start.15) | collective-permute-done | bytes 1048608 | tf_op jit(solution)/shard_map/ppermute | solution.py:611
  112.3 1.2 collective-permute-start.17
  113.6 0.3 collective-permute-start.14
  113.8 21.9 %collective-permute-done.14 = f32[3,256,128]{2,1,0:T(8,128)S(1)} collective-permute-done((f32[3,256,128]{2,1,0:T(8,128)}, f32[3,256,128]{2,1,0:T(8,128)S(1)}, u32[]{:S(2)}, u32[]{:S(2)}) %collective-permute-start.14) | collective-permute-done | bytes 393248 | tf_op jit(solution)/shard_map/ppermute | solution.py:611
  135.7 1.0 add.113.here_ref
  136.8 2.3 %collective-permute-start.20 = (bf16[512,1024]{1,0:T(8,128)(2,1)}, bf16[512,1024]{1,0:T(8,128)(2,1)S(1)}, u32[]{:S(2)}, u32[]{:S(2)}) collective-permute-start(bf16[512,1024]{1,0:T(8,128)(2,1)} %collective-permute-done.15.refs_11_), channel_id=1, source_target_pairs={{0,1},{1,0},{2,3},{3,2},{4,5},{5,4},{6,7},{7,6},{8,9},{9,8},{10,11... | collective-permute-start | bytes 3145736 | tf_op jit(solution)/shard_map/ppermute | solution.py:611
  139.2 1.2 collective-permute-start.23
  140.5 0.7 collective-permute-start.22
  141.2 1.2 collective-permute-start.18
  142.4 3.4 %collective-permute-start.21 = (f32[3,256,128]{2,1,0:T(8,128)S(1)}, f32[3,256,128]{2,1,0:T(8,128)}, u32[]{:S(2)}, u32[]{:S(2)}) collective-permute-start(f32[3,256,128]{2,1,0:T(8,128)S(1)} %add.113.here_ref), channel_id=1, source_target_pairs={{0,8},{4,12},{8,0},{12,4},{1,9},{5,13},{9,1},{13,5},{2,10},{6,14},... | collective-permute-start | bytes 1179656 | tf_op jit(solution)/shard_map/ppermute | solution.py:611
  145.8 0.6 concatenate.30.scalars_ref
  146.5 1.0 copy-done.3
  147.5 12.9 %shard_map.105 = (f32[768,512]{1,0:T(8,128)}, f32[768,512]{1,0:T(8,128)}) custom-call(s32[13]{0:T(128)} %concatenate.30.scalars_ref, bf16[768,1024]{1,0:T(8,128)(2,1)} %refs_0_.5, bf16[768,1024]{1,0:T(8,128)(2,1)} %copy-done, bf16[768,1024]{1,0:T(8,128)(2,1)} %copy-done.1, bf16[768,1024]{1,0:T(8,128)(2,1)} %collective-permute-done.7.refs_3_, ...), custom_call_target="tpu_custom_call" | custom-call | flops 1 | bytes 1 | tf_op jit(solution)/shard_map/pallas_call | solution.py:438
  160.4 1.8 collective-permute-done.21.there_ref
  162.2 6.8 %shard_map.106 = (bf16[3,64,2560]{2,1,0:T(8,128)(2,1)}, bf16[3,64,2560]{2,1,0:T(8,128)(2,1)}, bf16[3,256,64]{2,1,0:T(8,128)(2,1)}) custom-call(s32[3]{0:T(128)} %live_ref, f32[3,256,128]{2,1,0:T(8,128)} %copy-done.4, f32[3,256,128]{2,1,0:T(8,128)} %collective-permute-done.21.there_ref, bf16[768,4096]{1,0:T(8,128)(2,1)} %hid_ref.1, bf16[768,1024]{1,0:T(8,128)(2,1)} %refs_0_.5), custom_call_target="tpu_custom_call" | custom-call | flops 503316480 | bytes 9830400 | tf_op jit(solution)/shard_map/pallas_call | solution.py:186
  169.1 0.5 collective-permute-start.28
  169.7 0.4 collective-permute-start.26
  170.1 1.2 collective-permute-start.29
  171.3 0.6 concatenate.31.scalars_ref
  172.0 1.0 collective-permute-start.24
  173.1 0.6 collective-permute-done.27.refs_14_
  173.7 20.5 %shard_map.107 = (bf16[768,4096]{1,0:T(8,128)(2,1)}, f32[8,128]{1,0:T(8,128)}) custom-call(s32[19]{0:T(128)} %concatenate.31.scalars_ref, bf16[768,1024]{1,0:T(8,128)(2,1)} %refs_0_.5, bf16[768,1024]{1,0:T(8,128)(2,1)} %copy-done, bf16[768,1024]{1,0:T(8,128)(2,1)} %copy-done.1, bf16[768,1024]{1,0:T(8,128)(2,1)} %collective-permute-done.7.refs_3_, ...), custom_call_target="tpu_custom_call" | custom-call | flops 1 | bytes 1 | tf_op jit(solution)/shard_map/pallas_call | solution.py:473
  194.2 1.2 collective-permute-start.30
  195.5 0.4 collective-permute-start.33
  195.9 0.7 concatenate.26.scalars_ref
  196.6 0.3 collective-permute-start.35
  197.1 0.3 collective-permute-start.31
  197.4 0.5 collective-permute-done.30.refs_14_
  197.9 19.4 %shard_map.108 = (bf16[768,4096]{1,0:T(8,128)(2,1)}, f32[8,128]{1,0:T(8,128)}) custom-call(s32[17]{0:T(128)} %concatenate.26.scalars_ref, bf16[768,1024]{1,0:T(8,128)(2,1)} %refs_0_.5, bf16[768,1024]{1,0:T(8,128)(2,1)} %copy-done, bf16[768,1024]{1,0:T(8,128)(2,1)} %copy-done.1, ...), custom_call_target="tpu_custom_call", output_to_operand_aliasing={{0}: (19, {})} | custom-call | flops 1 | bytes 1 | tf_op jit(solution)/shard_map/pallas_call | solution.py:473
  217.3 1.8 collective-permute-done.33.refs_4_
  219.2 0.8 collective-permute-start.34
  220.1 0.7 add_subtract_fusion.slots_ref
  220.8 1.6 collective-permute-done.34.refs_6_
  222.4 1.0 copy-done.12
  223.4 4.0 %shard_map.109 = (f32[8,64,4096]{2,1,0:T(8,128)}, f32[8,64,1024]{2,1,0:T(8,128)}) custom-call(s32[12]{0:T(128)} %add_subtract_fusion.slots_ref, bf16[3,64,2560]{2,1,0:T(8,128)(2,1)} %get-tuple-element.80.refs_0_, bf16[3,64,2560]{2,1,0:T(8,128)(2,1)} %get-tuple-element.81.refs_1_, ...), custom_call_target="tpu_custom_call", output_to_operand_aliasing={{0}: (10, {}), {1}: (11, {})} | custom-call | flops 1 | bytes 1 | tf_op jit(solution)/shard_map/pallas_call | solution.py:563
  (57 shorter events, 1.3 us)
Async XLA Ops:
  0.6 15.0 %collective-permute-start.3 = (bf16[8,64,4096]{2,1,0:T(8,128)(2,1)}, bf16[8,64,4096]{2,1,0:T(8,128)(2,1)}, u32[]{:S(2)}, u32[]{:S(2)}) collective-permute-start(bf16[8,64,4096]{2,1,0:T(8,128)(2,1)} %bitcast.21), channel_id=1, source_target_pairs={{0,1},{1,0},{2,3},{3,2},{4,5},{5,4},{6,7},{7,6},{8,9},{9,8},{10,11... | collective-permute-start | bytes 12582920 | tf_op jit(solution)/shard_map/ppermute | solution.py:611
  1.4 38.1 %collective-permute-start = (bf16[768,1024]{1,0:T(8,128)(2,1)}, bf16[768,1024]{1,0:T(8,128)(2,1)S(1)}, u32[]{:S(2)}, u32[]{:S(2)}) collective-permute-start(bf16[768,1024]{1,0:T(8,128)(2,1)} %refs_0_.5), channel_id=1, source_target_pairs={{0,4},{4,8},{8,12},{1,5},{5,9},{9,13},{2,6},{6,10},{10,14},{3,7},{... | collective-permute-start | bytes 4718600 | tf_op jit(solution)/shard_map/ppermute | solution.py:643
  4.6 37.8 %collective-permute-start.1 = (bf16[768,1024]{1,0:T(8,128)(2,1)}, bf16[768,1024]{1,0:T(8,128)(2,1)S(1)}, u32[]{:S(2)}, u32[]{:S(2)}) collective-permute-start(bf16[768,1024]{1,0:T(8,128)(2,1)} %refs_0_.5), channel_id=1, source_target_pairs={{4,0},{8,4},{12,8},{5,1},{9,5},{13,9},{6,2},{10,6},{14,10},{7,3},{... | collective-permute-start | bytes 4718600 | tf_op jit(solution)/shard_map/ppermute | solution.py:643
  7.6 5.5 %collective-permute-start.2 = (s32[3]{0:T(128)S(1)}, s32[3]{0:T(128)S(1)}, u32[]{:S(2)}, u32[]{:S(2)}) collective-permute-start(s32[3]{0:T(128)S(1)} %select_reduce_fusion), channel_id=1, source_target_pairs={{0,2},{1,3},{2,0},{3,1},{4,6},{5,7},{6,4},{7,5},{8,10},{9,11},{10,... | collective-permute-start | bytes 44 | tf_op jit(solution)/shard_map/ppermute | solution.py:611
  7.9 7.7 %collective-permute-start.4 = (bf16[8,64,1024]{2,1,0:T(8,128)(2,1)}, bf16[8,64,1024]{2,1,0:T(8,128)(2,1)}, u32[]{:S(2)}, u32[]{:S(2)}) collective-permute-start(bf16[8,64,1024]{2,1,0:T(8,128)(2,1)} %refs_2_.3), channel_id=1, source_target_pairs={{0,1},{1,0},{2,3},{3,2},{4,5},{5,4},{6,7},{7,6},{8,9},{9,8},{10,11... | collective-permute-start | bytes 3145736 | tf_op jit(solution)/shard_map/ppermute | solution.py:611
  13.1 25.1 %collective-permute-start.6 = (bf16[512,1024]{1,0:T(8,128)(2,1)}, bf16[512,1024]{1,0:T(8,128)(2,1)}, u32[]{:S(2)}, u32[]{:S(2)}) collective-permute-start(bf16[512,1024]{1,0:T(8,128)(2,1)} %get-tuple-element.47), channel_id=1, source_target_pairs={{0,2},{1,3},{2,0},{3,1},{4,6},{5,7},{6,4},{7,5},{8,10},{9,11},{10,... | collective-permute-start | bytes 3145736 | tf_op jit(solution)/shard_map/ppermute | solution.py:611
  20.4 21.9 %collective-permute-start.5 = (s32[6]{0:T(128)S(1)}, s32[6]{0:T(128)S(1)}, u32[]{:S(2)}, u32[]{:S(2)}) collective-permute-start(s32[6]{0:T(128)S(1)} %pad_add_fusion.1), channel_id=1, source_target_pairs={{0,1},{1,0},{2,3},{3,2},{4,5},{5,4},{6,7},{7,6},{8,9},{9,8},{10,11... | collective-permute-start | bytes 80 | tf_op jit(solution)/shard_map/ppermute | solution.py:611
  39.5 67.9 %copy-start = (bf16[768,1024]{1,0:T(8,128)(2,1)}, bf16[768,1024]{1,0:T(8,128)(2,1)S(1)}, u32[]{:S(2)}) copy-start(bf16[768,1024]{1,0:T(8,128)(2,1)S(1)} %collective-permute-done.refs_1_) | copy-start | bytes 4718596
  42.4 65.0 %copy-start.1 = (bf16[768,1024]{1,0:T(8,128)(2,1)}, bf16[768,1024]{1,0:T(8,128)(2,1)S(1)}, u32[]{:S(2)}) copy-start(bf16[768,1024]{1,0:T(8,128)(2,1)S(1)} %collective-permute-done.1.refs_2_) | copy-start | bytes 4718596
  42.4 52.7 %collective-permute-start.13 = (bf16[4096,1024]{1,0:T(8,128)(2,1)}, bf16[4096,1024]{1,0:T(8,128)(2,1)}, u32[]{:S(2)}, u32[]{:S(2)}) collective-permute-start(bf16[4096,1024]{1,0:T(8,128)(2,1)} %refs_7_.2), channel_id=1, source_target_pairs={{0,1},{1,0},{2,3},{3,2},{4,5},{5,4},{6,7},{7,6},{8,9},{9,8},{10,11... | collective-permute-start | bytes 25165832 | tf_op jit(solution)/shard_map/ppermute | solution.py:611
  43.5 44.7 %collective-permute-start.9 = (bf16[3,64,5120]{2,1,0:T(8,128)(2,1)}, bf16[3,64,5120]{2,1,0:T(8,128)(2,1)}, u32[]{:S(2)}, u32[]{:S(2)}) collective-permute-start(bf16[3,64,5120]{2,1,0:T(8,128)(2,1)} %shard_map.103), channel_id=1, source_target_pairs={{0,2},{1,3},{2,0},{3,1},{4,6},{5,7},{6,4},{7,5},{8,10},{9,11},{10,... | collective-permute-start | bytes 5898248 | tf_op jit(solution)/shard_map/ppermute | solution.py:611
  43.8 37.6 %collective-permute-start.8 = (bf16[768,1024]{1,0:T(8,128)(2,1)S(1)}, bf16[768,1024]{1,0:T(8,128)(2,1)}, u32[]{:S(2)}, u32[]{:S(2)}) collective-permute-start(bf16[768,1024]{1,0:T(8,128)(2,1)S(1)} %collective-permute-done.1.refs_2_), channel_id=1, source_target_pairs={{4,0},{8,4},{12,8},{5,1},{9,5},{13,9},{6,2},{10,6},{14,10},{7,3},{... | collective-permute-start | bytes 4718600 | tf_op jit(solution)/shard_map/ppermute | solution.py:643
  45.9 37.3 %collective-permute-start.7 = (bf16[768,1024]{1,0:T(8,128)(2,1)S(1)}, bf16[768,1024]{1,0:T(8,128)(2,1)}, u32[]{:S(2)}, u32[]{:S(2)}) collective-permute-start(bf16[768,1024]{1,0:T(8,128)(2,1)S(1)} %collective-permute-done.refs_1_), channel_id=1, source_target_pairs={{0,4},{4,8},{8,12},{1,5},{5,9},{9,13},{2,6},{6,10},{10,14},{3,7},{... | collective-permute-start | bytes 4718600 | tf_op jit(solution)/shard_map/ppermute | solution.py:643
  49.0 24.1 %collective-permute-start.10 = (bf16[512,1024]{1,0:T(8,128)(2,1)}, bf16[512,1024]{1,0:T(8,128)(2,1)S(1)}, u32[]{:S(2)}, u32[]{:S(2)}) collective-permute-start(bf16[512,1024]{1,0:T(8,128)(2,1)} %collective-permute-done.6.refs_9_), channel_id=1, source_target_pairs={{0,16},{16,0},{1,17},{17,1},{2,18},{18,2},{3,19},{19,3},{4,20},{20... | collective-permute-start | bytes 3145736 | tf_op jit(solution)/shard_map/ppermute | solution.py:685
  73.2 10.1 %copy-start.5 = (bf16[512,1024]{1,0:T(8,128)(2,1)}, bf16[512,1024]{1,0:T(8,128)(2,1)S(1)}, u32[]{:S(2)}) copy-start(bf16[512,1024]{1,0:T(8,128)(2,1)S(1)} %collective-permute-done.10.refs_15_) | copy-start | bytes 3145732
  88.2 24.1 %collective-permute-start.15 = (bf16[512,1024]{1,0:T(8,128)(2,1)}, bf16[512,1024]{1,0:T(8,128)(2,1)}, u32[]{:S(2)}, u32[]{:S(2)}) collective-permute-start(bf16[512,1024]{1,0:T(8,128)(2,1)} %get-tuple-element.57), channel_id=1, source_target_pairs={{0,2},{1,3},{2,0},{3,1},{4,6},{5,7},{6,4},{7,5},{8,10},{9,11},{10,... | collective-permute-start | bytes 3145736 | tf_op jit(solution)/shard_map/ppermute | solution.py:611
  88.4 48.3 %collective-permute-start.12 = (bf16[768,1024]{1,0:T(8,128)(2,1)}, bf16[768,1024]{1,0:T(8,128)(2,1)}, u32[]{:S(2)}, u32[]{:S(2)}) collective-permute-start(bf16[768,1024]{1,0:T(8,128)(2,1)} %collective-permute-done.8.refs_4_), channel_id=1, source_target_pairs={{4,0},{8,4},{12,8},{5,1},{9,5},{13,9},{6,2},{10,6},{14,10},{7,3},{... | collective-permute-start | bytes 4718600 | tf_op jit(solution)/shard_map/ppermute | solution.py:643
  90.6 46.2 %collective-permute-start.11 = (bf16[768,1024]{1,0:T(8,128)(2,1)}, bf16[768,1024]{1,0:T(8,128)(2,1)}, u32[]{:S(2)}, u32[]{:S(2)}) collective-permute-start(bf16[768,1024]{1,0:T(8,128)(2,1)} %collective-permute-done.7.refs_3_), channel_id=1, source_target_pairs={{0,4},{4,8},{8,12},{1,5},{5,9},{9,13},{2,6},{6,10},{10,14},{3,7},{... | collective-permute-start | bytes 4718600 | tf_op jit(solution)/shard_map/ppermute | solution.py:643
  93.7 43.0 %collective-permute-start.16 = (bf16[512,1024]{1,0:T(8,128)(2,1)}, bf16[512,1024]{1,0:T(8,128)(2,1)}, u32[]{:S(2)}, u32[]{:S(2)}) collective-permute-start(bf16[512,1024]{1,0:T(8,128)(2,1)} %get-tuple-element.58), channel_id=1, source_target_pairs={{0,2},{1,3},{2,0},{3,1},{4,6},{5,7},{6,4},{7,5},{8,10},{9,11},{10,... | collective-permute-start | bytes 3145736 | tf_op jit(solution)/shard_map/ppermute | solution.py:611
  112.3 24.5 %collective-permute-start.17 = (bf16[512,1024]{1,0:T(8,128)(2,1)}, bf16[512,1024]{1,0:T(8,128)(2,1)S(1)}, u32[]{:S(2)}, u32[]{:S(2)}) collective-permute-start(bf16[512,1024]{1,0:T(8,128)(2,1)} %collective-permute-done.15.refs_11_), channel_id=1, source_target_pairs={{0,16},{16,0},{1,17},{17,1},{2,18},{18,2},{3,19},{19,3},{4,20},{20... | collective-permute-start | bytes 3145736 | tf_op jit(solution)/shard_map/ppermute | solution.py:685
  113.6 22.2 %collective-permute-start.14 = (f32[3,256,128]{2,1,0:T(8,128)}, f32[3,256,128]{2,1,0:T(8,128)S(1)}, u32[]{:S(2)}, u32[]{:S(2)}) collective-permute-start(f32[3,256,128]{2,1,0:T(8,128)} %get-tuple-element.56), channel_id=1, source_target_pairs={{0,4},{4,0},{8,12},{12,8},{1,5},{5,1},{9,13},{13,9},{2,6},{6,2},{1... | collective-permute-start | bytes 1179656 | tf_op jit(solution)/shard_map/ppermute | solution.py:611
  136.8 23.6 %copy-start.4 = (f32[3,256,128]{2,1,0:T(8,128)}, f32[3,256,128]{2,1,0:T(8,128)S(1)}, u32[]{:S(2)}) copy-start(f32[3,256,128]{2,1,0:T(8,128)S(1)} %add.113.here_ref) | copy-start | bytes 1179652
  136.8 5.6 %copy-start.7 = (bf16[512,1024]{1,0:T(8,128)(2,1)}, bf16[512,1024]{1,0:T(8,128)(2,1)S(1)}, u32[]{:S(2)}) copy-start(bf16[512,1024]{1,0:T(8,128)(2,1)S(1)} %collective-permute-done.17.refs_17_) | copy-start | bytes 3145732
  136.8 5.5 %collective-permute-start.20 = (bf16[512,1024]{1,0:T(8,128)(2,1)}, bf16[512,1024]{1,0:T(8,128)(2,1)S(1)}, u32[]{:S(2)}, u32[]{:S(2)}) collective-permute-start(bf16[512,1024]{1,0:T(8,128)(2,1)} %collective-permute-done.15.refs_11_), channel_id=1, source_target_pairs={{0,1},{1,0},{2,3},{3,2},{4,5},{5,4},{6,7},{7,6},{8,9},{9,8},{10,11... | collective-permute-start | bytes 3145736 | tf_op jit(solution)/shard_map/ppermute | solution.py:611
  139.1 7.3 %collective-permute-start.19 = (bf16[512,1024]{1,0:T(8,128)(2,1)}, bf16[512,1024]{1,0:T(8,128)(2,1)S(1)}, u32[]{:S(2)}, u32[]{:S(2)}) collective-permute-start(bf16[512,1024]{1,0:T(8,128)(2,1)} %collective-permute-done.6.refs_9_), channel_id=1, source_target_pairs={{0,1},{1,0},{2,3},{3,2},{4,5},{5,4},{6,7},{7,6},{8,9},{9,8},{10,11... | collective-permute-start | bytes 3145736 | tf_op jit(solution)/shard_map/ppermute | solution.py:611
  139.2 29.8 %collective-permute-start.23 = (bf16[512,1024]{1,0:T(8,128)(2,1)}, bf16[512,1024]{1,0:T(8,128)(2,1)S(1)}, u32[]{:S(2)}, u32[]{:S(2)}) collective-permute-start(bf16[512,1024]{1,0:T(8,128)(2,1)} %collective-permute-done.16.refs_13_), channel_id=1, source_target_pairs={{0,16},{16,0},{1,17},{17,1},{2,18},{18,2},{3,19},{19,3},{4,20},{20... | collective-permute-start | bytes 3145736 | tf_op jit(solution)/shard_map/ppermute | solution.py:685
  140.5 28.6 %collective-permute-start.22 = (bf16[512,1024]{1,0:T(8,128)(2,1)}, bf16[512,1024]{1,0:T(8,128)(2,1)}, u32[]{:S(2)}, u32[]{:S(2)}) collective-permute-start(bf16[512,1024]{1,0:T(8,128)(2,1)} %copy-done.5), channel_id=1, source_target_pairs={{0,1},{1,0},{2,3},{3,2},{4,5},{5,4},{6,7},{7,6},{8,9},{9,8},{10,11... | collective-permute-start | bytes 3145736 | tf_op jit(solution)/shard_map/ppermute | solution.py:611
  141.2 27.9 %collective-permute-start.18 = (bf16[512,1024]{1,0:T(8,128)(2,1)}, bf16[512,1024]{1,0:T(8,128)(2,1)}, u32[]{:S(2)}, u32[]{:S(2)}) collective-permute-start(bf16[512,1024]{1,0:T(8,128)(2,1)} %get-tuple-element.60), channel_id=1, source_target_pairs={{0,2},{1,3},{2,0},{3,1},{4,6},{5,7},{6,4},{7,5},{8,10},{9,11},{10,... | collective-permute-start | bytes 3145736 | tf_op jit(solution)/shard_map/ppermute | solution.py:611
  142.4 4.1 %copy-start.2 = (bf16[512,1024]{1,0:T(8,128)(2,1)}, bf16[512,1024]{1,0:T(8,128)(2,1)S(1)}, u32[]{:S(2)}) copy-start(bf16[512,1024]{1,0:T(8,128)(2,1)S(1)} %collective-permute-done.20.refs_12_) | copy-start | bytes 3145732
  142.4 19.8 %collective-permute-start.21 = (f32[3,256,128]{2,1,0:T(8,128)S(1)}, f32[3,256,128]{2,1,0:T(8,128)}, u32[]{:S(2)}, u32[]{:S(2)}) collective-permute-start(f32[3,256,128]{2,1,0:T(8,128)S(1)} %add.113.here_ref), channel_id=1, source_target_pairs={{0,8},{4,12},{8,0},{12,4},{1,9},{5,13},{9,1},{13,5},{2,10},{6,14},... | collective-permute-start | bytes 1179656 | tf_op jit(solution)/shard_map/ppermute | solution.py:611
  146.5 1.0 copy-start.3
  160.3 8.7 %copy-start.8 = (bf16[512,1024]{1,0:T(8,128)(2,1)S(1)}, bf16[512,1024]{1,0:T(8,128)(2,1)}, u32[]{:S(2)}) copy-start(bf16[512,1024]{1,0:T(8,128)(2,1)} %copy-done.7) | copy-start | bytes 3145732
  160.4 11.0 %copy-start.13 = (s32[3]{0:T(128)S(1)}, s32[3]{0:T(128)}, u32[]{:S(2)}) copy-start(s32[3]{0:T(128)} %live_ref) | copy-start | bytes 40
  169.0 25.2 %copy-start.6 = (bf16[512,1024]{1,0:T(8,128)(2,1)}, bf16[512,1024]{1,0:T(8,128)(2,1)S(1)}, u32[]{:S(2)}) copy-start(bf16[512,1024]{1,0:T(8,128)(2,1)S(1)} %collective-permute-done.23.refs_11_) | copy-start | bytes 3145732
  169.1 3.9 %collective-permute-start.28 = (bf16[512,1024]{1,0:T(8,128)(2,1)S(1)}, bf16[512,1024]{1,0:T(8,128)(2,1)}, u32[]{:S(2)}, u32[]{:S(2)}) collective-permute-start(bf16[512,1024]{1,0:T(8,128)(2,1)S(1)} %copy-done.8), channel_id=1, source_target_pairs={{0,1},{1,0},{2,3},{3,2},{4,5},{5,4},{6,7},{7,6},{8,9},{9,8},{10,11... | collective-permute-start | bytes 3145736 | tf_op jit(solution)/shard_map/ppermute | solution.py:611
  169.6 4.1 %collective-permute-start.27 = (bf16[512,1024]{1,0:T(8,128)(2,1)}, bf16[512,1024]{1,0:T(8,128)(2,1)}, u32[]{:S(2)}, u32[]{:S(2)}) collective-permute-start(bf16[512,1024]{1,0:T(8,128)(2,1)} %collective-permute-done.16.refs_13_), channel_id=1, source_target_pairs={{0,1},{1,0},{2,3},{3,2},{4,5},{5,4},{6,7},{7,6},{8,9},{9,8},{10,11... | collective-permute-start | bytes 3145736 | tf_op jit(solution)/shard_map/ppermute | solution.py:611
  169.7 24.5 %collective-permute-start.26 = (bf16[512,1024]{1,0:T(8,128)(2,1)}, bf16[512,1024]{1,0:T(8,128)(2,1)S(1)}, u32[]{:S(2)}, u32[]{:S(2)}) collective-permute-start(bf16[512,1024]{1,0:T(8,128)(2,1)} %collective-permute-done.18.refs_9_), channel_id=1, source_target_pairs={{0,16},{16,0},{1,17},{17,1},{2,18},{18,2},{3,19},{19,3},{4,20},{20... | collective-permute-start | bytes 3145736 | tf_op jit(solution)/shard_map/ppermute | solution.py:685
  170.1 24.1 %collective-permute-start.29 = (bf16[3,64,2560]{2,1,0:T(8,128)(2,1)}, bf16[3,64,2560]{2,1,0:T(8,128)(2,1)}, u32[]{:S(2)}, u32[]{:S(2)}) collective-permute-start(bf16[3,64,2560]{2,1,0:T(8,128)(2,1)} %get-tuple-element.81.refs_1_), channel_id=1, source_target_pairs={{0,2},{1,3},{2,0},{3,1},{4,6},{5,7},{6,4},{7,5},{8,10},{9,11},{10,... | collective-permute-start | bytes 2949128 | tf_op jit(solution)/shard_map/ppermute | solution.py:611
  172.0 25.1 %collective-permute-start.24 = (bf16[512,1024]{1,0:T(8,128)(2,1)}, bf16[512,1024]{1,0:T(8,128)(2,1)}, u32[]{:S(2)}, u32[]{:S(2)}) collective-permute-start(bf16[512,1024]{1,0:T(8,128)(2,1)} %collective-permute-done.18.refs_9_), channel_id=1, source_target_pairs={{0,1},{1,0},{2,3},{3,2},{4,5},{5,4},{6,7},{7,6},{8,9},{9,8},{10,11... | collective-permute-start | bytes 3145736 | tf_op jit(solution)/shard_map/ppermute | solution.py:611
  173.0 23.9 %collective-permute-start.25 = (bf16[512,1024]{1,0:T(8,128)(2,1)S(1)}, bf16[512,1024]{1,0:T(8,128)(2,1)S(1)}, u32[]{:S(2)}, u32[]{:S(2)}) collective-permute-start(bf16[512,1024]{1,0:T(8,128)(2,1)S(1)} %collective-permute-done.23.refs_11_), channel_id=1, source_target_pairs={{0,1},{1,0},{2,3},{3,2},{4,5},{5,4},{6,7},{7,6},{8,9},{9,8},{10,11... | collective-permute-start | bytes 3145736 | tf_op jit(solution)/shard_map/ppermute | solution.py:611
  194.2 3.7 %copy-start.9 = (bf16[512,1024]{1,0:T(8,128)(2,1)}, bf16[512,1024]{1,0:T(8,128)(2,1)S(1)}, u32[]{:S(2)}) copy-start(bf16[512,1024]{1,0:T(8,128)(2,1)S(1)} %collective-permute-done.26.refs_13_) | copy-start | bytes 3145732
  194.2 3.6 %collective-permute-start.30 = (bf16[512,1024]{1,0:T(8,128)(2,1)S(1)}, bf16[512,1024]{1,0:T(8,128)(2,1)}, u32[]{:S(2)}, u32[]{:S(2)}) collective-permute-start(bf16[512,1024]{1,0:T(8,128)(2,1)S(1)} %collective-permute-done.26.refs_13_), channel_id=1, source_target_pairs={{0,1},{1,0},{2,3},{3,2},{4,5},{5,4},{6,7},{7,6},{8,9},{9,8},{10,11... | collective-permute-start | bytes 3145736 | tf_op jit(solution)/shard_map/ppermute | solution.py:611
  195.5 23.7 %collective-permute-start.33 = (bf16[3,64,2560]{2,1,0:T(8,128)(2,1)}, bf16[3,64,2560]{2,1,0:T(8,128)(2,1)}, u32[]{:S(2)}, u32[]{:S(2)}) collective-permute-start(bf16[3,64,2560]{2,1,0:T(8,128)(2,1)} %get-tuple-element.80.refs_0_), channel_id=1, source_target_pairs={{0,2},{1,3},{2,0},{3,1},{4,6},{5,7},{6,4},{7,5},{8,10},{9,11},{10,... | collective-permute-start | bytes 2949128 | tf_op jit(solution)/shard_map/ppermute | solution.py:611
  196.6 24.2 %collective-permute-start.35 = (bf16[3,64,2560]{2,1,0:T(8,128)(2,1)}, bf16[3,64,2560]{2,1,0:T(8,128)(2,1)}, u32[]{:S(2)}, u32[]{:S(2)}) collective-permute-start(bf16[3,64,2560]{2,1,0:T(8,128)(2,1)} %collective-permute-done.29.refs_5_), channel_id=1, source_target_pairs={{0,1},{1,0},{2,3},{3,2},{4,5},{5,4},{6,7},{7,6},{8,9},{9,8},{10,11... | collective-permute-start | bytes 2949128 | tf_op jit(solution)/shard_map/ppermute | solution.py:611
  196.9 1.0 copy-start.10
  196.9 23.9 %collective-permute-start.32 = (bf16[3,64,2560]{2,1,0:T(8,128)(2,1)}, bf16[3,64,2560]{2,1,0:T(8,128)(2,1)S(1)}, u32[]{:S(2)}, u32[]{:S(2)}) collective-permute-start(bf16[3,64,2560]{2,1,0:T(8,128)(2,1)} %get-tuple-element.81.refs_1_), channel_id=1, source_target_pairs={{0,1},{1,0},{2,3},{3,2},{4,5},{5,4},{6,7},{7,6},{8,9},{9,8},{10,11... | collective-permute-start | bytes 2949128 | tf_op jit(solution)/shard_map/ppermute | solution.py:611
  197.1 23.7 %collective-permute-start.31 = (bf16[3,64,2560]{2,1,0:T(8,128)(2,1)}, bf16[3,64,2560]{2,1,0:T(8,128)(2,1)}, u32[]{:S(2)}, u32[]{:S(2)}) collective-permute-start(bf16[3,64,2560]{2,1,0:T(8,128)(2,1)} %get-tuple-element.80.refs_0_), channel_id=1, source_target_pairs={{0,1},{1,0},{2,3},{3,2},{4,5},{5,4},{6,7},{7,6},{8,9},{9,8},{10,11... | collective-permute-start | bytes 2949128 | tf_op jit(solution)/shard_map/ppermute | solution.py:611
  219.2 3.2 %collective-permute-start.34 = (bf16[3,64,2560]{2,1,0:T(8,128)(2,1)}, bf16[3,64,2560]{2,1,0:T(8,128)(2,1)S(1)}, u32[]{:S(2)}, u32[]{:S(2)}) collective-permute-start(bf16[3,64,2560]{2,1,0:T(8,128)(2,1)} %collective-permute-done.33.refs_4_), channel_id=1, source_target_pairs={{0,1},{1,0},{2,3},{3,2},{4,5},{5,4},{6,7},{7,6},{8,9},{9,8},{10,11... | collective-permute-start | bytes 2949128 | tf_op jit(solution)/shard_map/ppermute | solution.py:611
  220.8 1.6 copy-start.11
  222.3 1.0 copy-start.12

commit v13 on v12

--- a/solution.py
+++ b/solution.py
@@ -729,7 +729,6 @@
     cross(*past)
     turn(*past)
     fill(crossed[:2], *past)
-    fill(turned[0], *past)
 
     order = [me ^ r for r in range(n_dp)]
     order = jnp.stack(order).astype(i32)
@@ -769,7 +768,7 @@
     far_low = swap(low_terms, top)
     turn(*past)
     fill(crossed[2:], *past)
-    for pieces in turned[1:3]:
+    for pieces in turned[:3]:
         fill(pieces, *past)
     if line:
         at = jnp.stack(where).astype(i32)

time: 231 us -> 230 us (level)
  transfers between devices with their start and end apart: 36 -> 36, of which waited for: 14 -> 15; matrix products, arithmetic and copies ran while one was open for 5% -> 5% of each run, Pallas kernels for 33% -> 33%
where the time goes in v13:
time: 230 us; the launch traced here: 228 us
  waiting for transfers between devices  94.1 us (41%)
  Pallas kernels  80.5 us (35%)
  starting transfers between devices  38.4 us (17%)
  local copies, waits for them, and re-layouts  9.35 us (4%)
  other arithmetic  5.01 us (2%)
    ppermute x26, waiting for transfers between devices, swap(): return lax.ppermute(value, axis, [(i, i ^ bit) for i in range(size)])  57.1 us
    pallas_call x2, Pallas kernels, base(): pl.pallas_call(functools.partial(base_kernel, n_dp, tiles, len(chunks), [...  39.9 us
    ppermute x4, waiting for transfers between devices, turn(): turned[j].append({top: lax.ppermute(piece, 'groups', ring)})  22.8 us
    ppermute x26, starting transfers between devices, swap(): return lax.ppermute(value, axis, [(i, i ^ bit) for i in range(size)])  18.5 us
    ppermute x6, starting transfers between devices, hop(): sent.append(lax.ppermute(piece, 'fsdp', pairs))  15.9 us
    ppermute x6, waiting for transfers between devices, hop(): sent.append(lax.ppermute(piece, 'fsdp', pairs))  14.2 us
    pallas_call x1, Pallas kernels, early_sums(): pl.pallas_call(functools.partial(early_kernel, n_dp, tiles, len(chunks),...  12.9 us
    pallas_call x1, Pallas kernels, project(): pl.pallas_call(functools.partial(project_kernel, pieces), grid_spec=pltpu...  11.2 us
  transfers between devices with their start and end apart: 36, of which 15 were waited for; matrix products, arithmetic and copies ran while one was open for 5% of the time, Pallas kernels for 33%

profile of v13, /device:TPU:11, one launch (start us, length us, event | category | flops | bytes accessed | tf_op | source)
XLA Modules:
  0.0 228.5 jit_solution(13673952561369593964)
XLA Ops:
  0.6 0.7 collective-permute-start.3
  1.4 3.2 %collective-permute-start = (bf16[768,1024]{1,0:T(8,128)(2,1)}, bf16[768,1024]{1,0:T(8,128)(2,1)S(1)}, u32[]{:S(2)}, u32[]{:S(2)}) collective-permute-start(bf16[768,1024]{1,0:T(8,128)(2,1)} %refs_0_.5), channel_id=1, source_target_pairs={{0,4},{4,8},{8,12},{1,5},{5,9},{9,13},{2,6},{6,10},{10,14},{3,7},{... | collective-permute-start | bytes 4718600 | tf_op jit(solution)/shard_map/ppermute | solution.py:643
  4.6 2.2 collective-permute-start.1
  6.8 0.9 select_reduce_fusion
  7.6 0.3 collective-permute-start.2
  7.9 0.9 collective-permute-start.4
  8.8 4.3 %constant_dynamic-slice_fusion = (bf16[512,1024]{1,0:T(8,128)(2,1)}, bf16[512,1024]{1,0:T(8,128)(2,1)}, bf16[512,1024]{1,0:T(8,128)(2,1)}, bf16[512,1024]{1,0:T(8,128)(2,1)}) fusion(bf16[4096,1024]{1,0:T(8,128)(2,1)} %refs_7_.2, s32[]{:T(128)S(6)} %select_n.94, s32[]{:T(128)S(6)} %select_n.89, s32[]{:T(128)S(6)} %select_n.88, s32[]{:T(128)S(6)} %select_n.93), kind=kLoop, calls=%fused_computation.13 | loop fusion | bytes 8388624 | tf_op jit(solution)/shard_map/dynamic_slice | solution.py:673
  13.1 1.2 collective-permute-start.6
  14.3 0.6 compare_select_fusion.1
  14.9 0.6 pad_add_fusion.index_ref
  15.6 4.8 %shard_map.103 = bf16[3,64,5120]{2,1,0:T(8,128)(2,1)} custom-call(s32[6]{0:T(128)} %pad_add_fusion.index_ref, s32[3]{0:T(128)} %get-tuple-element.99.source_ref, bf16[8,64,4096]{2,1,0:T(8,128)(2,1)} %bitcast.22, bf16[8,64,4096]{2,1,0:T(8,128)(2,1)} %collective-permute-done.3.refs_1_, bf16[8,64,1024]{2,1,0:T(8,128)(2,1)} %refs_2_.3, ...), custom_call_target="tpu_custom_call" | custom-call | bytes 5898240 | tf_op jit(solution)/shard_map/pallas_call | solution.py:54
  20.4 0.3 collective-permute-start.5
  20.7 17.6 %collective-permute-done.6.refs_9_ = bf16[512,1024]{1,0:T(8,128)(2,1)} collective-permute-done((bf16[512,1024]{1,0:T(8,128)(2,1)}, bf16[512,1024]{1,0:T(8,128)(2,1)}, u32[]{:S(2)}, u32[]{:S(2)}) %collective-permute-start.6) | collective-permute-done | bytes 1048608 | tf_op jit(solution)/shard_map/ppermute | solution.py:611
  38.2 1.2 collective-permute-done.refs_1_
  39.5 2.9 %collective-permute-done.1.refs_2_ = bf16[768,1024]{1,0:T(8,128)(2,1)S(1)} collective-permute-done((bf16[768,1024]{1,0:T(8,128)(2,1)}, bf16[768,1024]{1,0:T(8,128)(2,1)S(1)}, u32[]{:S(2)}, u32[]{:S(2)}) %collective-permute-start.1) | collective-permute-done | bytes 1572896 | tf_op jit(solution)/shard_map/ppermute | solution.py:643
  42.4 1.1 collective-permute-start.13
  43.8 2.2 collective-permute-start.8
  45.9 3.1 %collective-permute-start.7 = (bf16[768,1024]{1,0:T(8,128)(2,1)S(1)}, bf16[768,1024]{1,0:T(8,128)(2,1)}, u32[]{:S(2)}, u32[]{:S(2)}) collective-permute-start(bf16[768,1024]{1,0:T(8,128)(2,1)S(1)} %collective-permute-done.refs_1_), channel_id=1, source_target_pairs={{0,4},{4,8},{8,12},{1,5},{5,9},{9,13},{2,6},{6,10},{10,14},{3,7},{... | collective-permute-start | bytes 4718600 | tf_op jit(solution)/shard_map/ppermute | solution.py:643
  49.0 1.3 collective-permute-start.10
  50.3 22.8 %collective-permute-done.10.refs_15_ = bf16[512,1024]{1,0:T(8,128)(2,1)S(1)} collective-permute-done((bf16[512,1024]{1,0:T(8,128)(2,1)}, bf16[512,1024]{1,0:T(8,128)(2,1)S(1)}, u32[]{:S(2)}, u32[]{:S(2)}) %collective-permute-start.10) | collective-permute-done | bytes 1048608 | tf_op jit(solution)/shard_map/ppermute | solution.py:685
  73.2 8.2 %collective-permute-done.8.refs_4_ = bf16[768,1024]{1,0:T(8,128)(2,1)} collective-permute-done((bf16[768,1024]{1,0:T(8,128)(2,1)S(1)}, bf16[768,1024]{1,0:T(8,128)(2,1)}, u32[]{:S(2)}, u32[]{:S(2)}) %collective-permute-start.8) | collective-permute-done | bytes 1572896 | tf_op jit(solution)/shard_map/ppermute | solution.py:643
  81.4 1.9 collective-permute-done.7.refs_3_
  83.2 5.0 %collective-permute-done.9.refs_4_ = bf16[3,64,5120]{2,1,0:T(8,128)(2,1)} collective-permute-done((bf16[3,64,5120]{2,1,0:T(8,128)(2,1)}, bf16[3,64,5120]{2,1,0:T(8,128)(2,1)}, u32[]{:S(2)}, u32[]{:S(2)}) %collective-permute-start.9) | collective-permute-done | bytes 1966112 | tf_op jit(solution)/shard_map/ppermute | solution.py:611
  88.4 2.2 collective-permute-start.12
  90.6 3.1 %collective-permute-start.11 = (bf16[768,1024]{1,0:T(8,128)(2,1)}, bf16[768,1024]{1,0:T(8,128)(2,1)}, u32[]{:S(2)}, u32[]{:S(2)}) collective-permute-start(bf16[768,1024]{1,0:T(8,128)(2,1)} %collective-permute-done.7.refs_3_), channel_id=1, source_target_pairs={{0,4},{4,8},{8,12},{1,5},{5,9},{9,13},{2,6},{6,10},{10,14},{3,7},{... | collective-permute-start | bytes 4718600 | tf_op jit(solution)/shard_map/ppermute | solution.py:643
  93.7 1.3 collective-permute-start.16
  95.0 0.6 compare_select_fusion
  95.6 0.6 pad_add_fusion.2.index_ref
  96.2 11.2 %shard_map.104 = (f32[3,256,128]{2,1,0:T(8,128)}, bf16[3,64,4096]{2,1,0:T(8,128)(2,1)}, f32[8,64,4096]{2,1,0:T(8,128)}, f32[8,64,1024]{2,1,0:T(8,128)}) custom-call(s32[6]{0:T(128)} %pad_add_fusion.2.index_ref, s32[3]{0:T(128)} %get-tuple-element.97.source_ref, bf16[8,64,4096]{2,1,0:T(8,128)(2,1)} %bitcast.23, ...), custom_call_target="tpu_custom_call" | custom-call | flops 503316480 | bytes 15728640 | tf_op jit(solution)/shard_map/pallas_call | solution.py:121
  107.4 4.9 %collective-permute-done.15.refs_11_ = bf16[512,1024]{1,0:T(8,128)(2,1)} collective-permute-done((bf16[512,1024]{1,0:T(8,128)(2,1)}, bf16[512,1024]{1,0:T(8,128)(2,1)}, u32[]{:S(2)}, u32[]{:S(2)}) %collective-permute-start.15) | collective-permute-done | bytes 1048608 | tf_op jit(solution)/shard_map/ppermute | solution.py:611
  112.3 1.2 collective-permute-start.17
  113.6 0.3 collective-permute-start.14
  113.8 21.9 %collective-permute-done.14 = f32[3,256,128]{2,1,0:T(8,128)S(1)} collective-permute-done((f32[3,256,128]{2,1,0:T(8,128)}, f32[3,256,128]{2,1,0:T(8,128)S(1)}, u32[]{:S(2)}, u32[]{:S(2)}) %collective-permute-start.14) | collective-permute-done | bytes 393248 | tf_op jit(solution)/shard_map/ppermute | solution.py:611
  135.7 1.0 add.113.here_ref
  136.8 2.3 %collective-permute-start.20 = (bf16[512,1024]{1,0:T(8,128)(2,1)}, bf16[512,1024]{1,0:T(8,128)(2,1)S(1)}, u32[]{:S(2)}, u32[]{:S(2)}) collective-permute-start(bf16[512,1024]{1,0:T(8,128)(2,1)} %collective-permute-done.15.refs_11_), channel_id=1, source_target_pairs={{0,1},{1,0},{2,3},{3,2},{4,5},{5,4},{6,7},{7,6},{8,9},{9,8},{10,11... | collective-permute-start | bytes 3145736 | tf_op jit(solution)/shard_map/ppermute | solution.py:611
  139.2 1.2 collective-permute-start.22
  140.5 1.2 collective-permute-start.18
  141.7 3.4 %collective-permute-start.21 = (f32[3,256,128]{2,1,0:T(8,128)S(1)}, f32[3,256,128]{2,1,0:T(8,128)}, u32[]{:S(2)}, u32[]{:S(2)}) collective-permute-start(f32[3,256,128]{2,1,0:T(8,128)S(1)} %add.113.here_ref), channel_id=1, source_target_pairs={{0,8},{4,12},{8,0},{12,4},{1,9},{5,13},{9,1},{13,5},{2,10},{6,14},... | collective-permute-start | bytes 1179656 | tf_op jit(solution)/shard_map/ppermute | solution.py:611
  145.0 0.7 concatenate.30.scalars_ref
  145.7 1.0 copy-done.2
  146.7 1.0 copy-done.3
  147.7 12.9 %shard_map.105 = (f32[768,512]{1,0:T(8,128)}, f32[768,512]{1,0:T(8,128)}) custom-call(s32[13]{0:T(128)} %concatenate.30.scalars_ref, bf16[768,1024]{1,0:T(8,128)(2,1)} %refs_0_.5, bf16[768,1024]{1,0:T(8,128)(2,1)} %copy-done, bf16[768,1024]{1,0:T(8,128)(2,1)} %copy-done.1, bf16[768,1024]{1,0:T(8,128)(2,1)} %collective-permute-done.7.refs_3_, ...), custom_call_target="tpu_custom_call" | custom-call | flops 1 | bytes 1 | tf_op jit(solution)/shard_map/pallas_call | solution.py:438
  160.6 0.8 collective-permute-done.21.there_ref
  161.4 6.8 %shard_map.106 = (bf16[3,64,2560]{2,1,0:T(8,128)(2,1)}, bf16[3,64,2560]{2,1,0:T(8,128)(2,1)}, bf16[3,256,64]{2,1,0:T(8,128)(2,1)}) custom-call(s32[3]{0:T(128)} %live_ref, f32[3,256,128]{2,1,0:T(8,128)} %copy-done.4, f32[3,256,128]{2,1,0:T(8,128)} %collective-permute-done.21.there_ref, bf16[768,4096]{1,0:T(8,128)(2,1)} %hid_ref.1, bf16[768,1024]{1,0:T(8,128)(2,1)} %refs_0_.5), custom_call_target="tpu_custom_call" | custom-call | flops 503316480 | bytes 9830400 | tf_op jit(solution)/shard_map/pallas_call | solution.py:186
  168.2 0.7 collective-permute-start.28
  169.0 0.4 collective-permute-start.26
  169.9 0.6 concatenate.31.scalars_ref
  170.6 0.8 collective-permute-done.28.refs_18_
  171.3 0.4 collective-permute-start.23
  171.7 2.6 %collective-permute-done.27.refs_16_ = bf16[512,1024]{1,0:T(8,128)(2,1)} collective-permute-done((bf16[512,1024]{1,0:T(8,128)(2,1)S(1)}, bf16[512,1024]{1,0:T(8,128)(2,1)}, u32[]{:S(2)}, u32[]{:S(2)}) %collective-permute-start.27) | collective-permute-done | bytes 1048608 | tf_op jit(solution)/shard_map/ppermute | solution.py:611
  174.3 0.4 collective-permute-start.24
  174.7 20.5 %shard_map.107 = (bf16[768,4096]{1,0:T(8,128)(2,1)}, f32[8,128]{1,0:T(8,128)}) custom-call(s32[19]{0:T(128)} %concatenate.31.scalars_ref, bf16[768,1024]{1,0:T(8,128)(2,1)} %refs_0_.5, bf16[768,1024]{1,0:T(8,128)(2,1)} %copy-done, bf16[768,1024]{1,0:T(8,128)(2,1)} %copy-done.1, bf16[768,1024]{1,0:T(8,128)(2,1)} %collective-permute-done.7.refs_3_, ...), custom_call_target="tpu_custom_call" | custom-call | flops 1 | bytes 1 | tf_op jit(solution)/shard_map/pallas_call | solution.py:473
  195.2 0.3 collective-permute-start.30
  195.8 0.6 concatenate.26.scalars_ref
  196.4 0.6 collective-permute-start.35
  197.0 0.4 collective-permute-start.31
  197.5 0.8 collective-permute-done.30.refs_14_
  198.3 19.5 %shard_map.108 = (bf16[768,4096]{1,0:T(8,128)(2,1)}, f32[8,128]{1,0:T(8,128)}) custom-call(s32[17]{0:T(128)} %concatenate.26.scalars_ref, bf16[768,1024]{1,0:T(8,128)(2,1)} %refs_0_.5, bf16[768,1024]{1,0:T(8,128)(2,1)} %copy-done, bf16[768,1024]{1,0:T(8,128)(2,1)} %copy-done.1, ...), custom_call_target="tpu_custom_call", output_to_operand_aliasing={{0}: (19, {})} | custom-call | flops 1 | bytes 1 | tf_op jit(solution)/shard_map/pallas_call | solution.py:473
  217.8 1.1 collective-permute-done.33.refs_4_
  218.9 1.1 collective-permute-start.34
  220.1 0.6 add_subtract_fusion.slots_ref
  220.8 1.6 collective-permute-done.34.refs_6_
  222.4 1.0 copy-done.13
  223.4 4.9 %shard_map.109 = (f32[8,64,4096]{2,1,0:T(8,128)}, f32[8,64,1024]{2,1,0:T(8,128)}) custom-call(s32[12]{0:T(128)} %add_subtract_fusion.slots_ref, bf16[3,64,2560]{2,1,0:T(8,128)(2,1)} %get-tuple-element.80.refs_0_, bf16[3,64,2560]{2,1,0:T(8,128)(2,1)} %get-tuple-element.81.refs_1_, ...), custom_call_target="tpu_custom_call", output_to_operand_aliasing={{0}: (10, {}), {1}: (11, {})} | custom-call | flops 1 | bytes 1 | tf_op jit(solution)/shard_map/pallas_call | solution.py:563
  (59 shorter events, 1.8 us)
Async XLA Ops:
  0.6 15.0 %collective-permute-start.3 = (bf16[8,64,4096]{2,1,0:T(8,128)(2,1)}, bf16[8,64,4096]{2,1,0:T(8,128)(2,1)}, u32[]{:S(2)}, u32[]{:S(2)}) collective-permute-start(bf16[8,64,4096]{2,1,0:T(8,128)(2,1)} %bitcast.21), channel_id=1, source_target_pairs={{0,1},{1,0},{2,3},{3,2},{4,5},{5,4},{6,7},{7,6},{8,9},{9,8},{10,11... | collective-permute-start | bytes 12582920 | tf_op jit(solution)/shard_map/ppermute | solution.py:611
  1.4 38.1 %collective-permute-start = (bf16[768,1024]{1,0:T(8,128)(2,1)}, bf16[768,1024]{1,0:T(8,128)(2,1)S(1)}, u32[]{:S(2)}, u32[]{:S(2)}) collective-permute-start(bf16[768,1024]{1,0:T(8,128)(2,1)} %refs_0_.5), channel_id=1, source_target_pairs={{0,4},{4,8},{8,12},{1,5},{5,9},{9,13},{2,6},{6,10},{10,14},{3,7},{... | collective-permute-start | bytes 4718600 | tf_op jit(solution)/shard_map/ppermute | solution.py:643
  4.6 37.8 %collective-permute-start.1 = (bf16[768,1024]{1,0:T(8,128)(2,1)}, bf16[768,1024]{1,0:T(8,128)(2,1)S(1)}, u32[]{:S(2)}, u32[]{:S(2)}) collective-permute-start(bf16[768,1024]{1,0:T(8,128)(2,1)} %refs_0_.5), channel_id=1, source_target_pairs={{4,0},{8,4},{12,8},{5,1},{9,5},{13,9},{6,2},{10,6},{14,10},{7,3},{... | collective-permute-start | bytes 4718600 | tf_op jit(solution)/shard_map/ppermute | solution.py:643
  7.6 5.5 %collective-permute-start.2 = (s32[3]{0:T(128)S(1)}, s32[3]{0:T(128)S(1)}, u32[]{:S(2)}, u32[]{:S(2)}) collective-permute-start(s32[3]{0:T(128)S(1)} %select_reduce_fusion), channel_id=1, source_target_pairs={{0,2},{1,3},{2,0},{3,1},{4,6},{5,7},{6,4},{7,5},{8,10},{9,11},{10,... | collective-permute-start | bytes 44 | tf_op jit(solution)/shard_map/ppermute | solution.py:611
  7.9 7.7 %collective-permute-start.4 = (bf16[8,64,1024]{2,1,0:T(8,128)(2,1)}, bf16[8,64,1024]{2,1,0:T(8,128)(2,1)}, u32[]{:S(2)}, u32[]{:S(2)}) collective-permute-start(bf16[8,64,1024]{2,1,0:T(8,128)(2,1)} %refs_2_.3), channel_id=1, source_target_pairs={{0,1},{1,0},{2,3},{3,2},{4,5},{5,4},{6,7},{7,6},{8,9},{9,8},{10,11... | collective-permute-start | bytes 3145736 | tf_op jit(solution)/shard_map/ppermute | solution.py:611
  13.1 25.1 %collective-permute-start.6 = (bf16[512,1024]{1,0:T(8,128)(2,1)}, bf16[512,1024]{1,0:T(8,128)(2,1)}, u32[]{:S(2)}, u32[]{:S(2)}) collective-permute-start(bf16[512,1024]{1,0:T(8,128)(2,1)} %get-tuple-element.47), channel_id=1, source_target_pairs={{0,2},{1,3},{2,0},{3,1},{4,6},{5,7},{6,4},{7,5},{8,10},{9,11},{10,... | collective-permute-start | bytes 3145736 | tf_op jit(solution)/shard_map/ppermute | solution.py:611
  20.4 22.0 %collective-permute-start.5 = (s32[6]{0:T(128)S(1)}, s32[6]{0:T(128)S(1)}, u32[]{:S(2)}, u32[]{:S(2)}) collective-permute-start(s32[6]{0:T(128)S(1)} %pad_add_fusion.1), channel_id=1, source_target_pairs={{0,1},{1,0},{2,3},{3,2},{4,5},{5,4},{6,7},{7,6},{8,9},{9,8},{10,11... | collective-permute-start | bytes 80 | tf_op jit(solution)/shard_map/ppermute | solution.py:611
  39.5 68.0 %copy-start = (bf16[768,1024]{1,0:T(8,128)(2,1)}, bf16[768,1024]{1,0:T(8,128)(2,1)S(1)}, u32[]{:S(2)}) copy-start(bf16[768,1024]{1,0:T(8,128)(2,1)S(1)} %collective-permute-done.refs_1_) | copy-start | bytes 4718596
  42.4 65.1 %copy-start.1 = (bf16[768,1024]{1,0:T(8,128)(2,1)}, bf16[768,1024]{1,0:T(8,128)(2,1)S(1)}, u32[]{:S(2)}) copy-start(bf16[768,1024]{1,0:T(8,128)(2,1)S(1)} %collective-permute-done.1.refs_2_) | copy-start | bytes 4718596
  42.4 52.7 %collective-permute-start.13 = (bf16[4096,1024]{1,0:T(8,128)(2,1)}, bf16[4096,1024]{1,0:T(8,128)(2,1)}, u32[]{:S(2)}, u32[]{:S(2)}) collective-permute-start(bf16[4096,1024]{1,0:T(8,128)(2,1)} %refs_7_.2), channel_id=1, source_target_pairs={{0,1},{1,0},{2,3},{3,2},{4,5},{5,4},{6,7},{7,6},{8,9},{9,8},{10,11... | collective-permute-start | bytes 25165832 | tf_op jit(solution)/shard_map/ppermute | solution.py:611
  43.5 44.7 %collective-permute-start.9 = (bf16[3,64,5120]{2,1,0:T(8,128)(2,1)}, bf16[3,64,5120]{2,1,0:T(8,128)(2,1)}, u32[]{:S(2)}, u32[]{:S(2)}) collective-permute-start(bf16[3,64,5120]{2,1,0:T(8,128)(2,1)} %shard_map.103), channel_id=1, source_target_pairs={{0,2},{1,3},{2,0},{3,1},{4,6},{5,7},{6,4},{7,5},{8,10},{9,11},{10,... | collective-permute-start | bytes 5898248 | tf_op jit(solution)/shard_map/ppermute | solution.py:611
  43.8 37.6 %collective-permute-start.8 = (bf16[768,1024]{1,0:T(8,128)(2,1)S(1)}, bf16[768,1024]{1,0:T(8,128)(2,1)}, u32[]{:S(2)}, u32[]{:S(2)}) collective-permute-start(bf16[768,1024]{1,0:T(8,128)(2,1)S(1)} %collective-permute-done.1.refs_2_), channel_id=1, source_target_pairs={{4,0},{8,4},{12,8},{5,1},{9,5},{13,9},{6,2},{10,6},{14,10},{7,3},{... | collective-permute-start | bytes 4718600 | tf_op jit(solution)/shard_map/ppermute | solution.py:643
  45.9 37.3 %collective-permute-start.7 = (bf16[768,1024]{1,0:T(8,128)(2,1)S(1)}, bf16[768,1024]{1,0:T(8,128)(2,1)}, u32[]{:S(2)}, u32[]{:S(2)}) collective-permute-start(bf16[768,1024]{1,0:T(8,128)(2,1)S(1)} %collective-permute-done.refs_1_), channel_id=1, source_target_pairs={{0,4},{4,8},{8,12},{1,5},{5,9},{9,13},{2,6},{6,10},{10,14},{3,7},{... | collective-permute-start | bytes 4718600 | tf_op jit(solution)/shard_map/ppermute | solution.py:643
  49.0 24.1 %collective-permute-start.10 = (bf16[512,1024]{1,0:T(8,128)(2,1)}, bf16[512,1024]{1,0:T(8,128)(2,1)S(1)}, u32[]{:S(2)}, u32[]{:S(2)}) collective-permute-start(bf16[512,1024]{1,0:T(8,128)(2,1)} %collective-permute-done.6.refs_9_), channel_id=1, source_target_pairs={{0,16},{16,0},{1,17},{17,1},{2,18},{18,2},{3,19},{19,3},{4,20},{20... | collective-permute-start | bytes 3145736 | tf_op jit(solution)/shard_map/ppermute | solution.py:685
  73.2 10.1 %copy-start.5 = (bf16[512,1024]{1,0:T(8,128)(2,1)}, bf16[512,1024]{1,0:T(8,128)(2,1)S(1)}, u32[]{:S(2)}) copy-start(bf16[512,1024]{1,0:T(8,128)(2,1)S(1)} %collective-permute-done.10.refs_15_) | copy-start | bytes 3145732
  88.2 24.1 %collective-permute-start.15 = (bf16[512,1024]{1,0:T(8,128)(2,1)}, bf16[512,1024]{1,0:T(8,128)(2,1)}, u32[]{:S(2)}, u32[]{:S(2)}) collective-permute-start(bf16[512,1024]{1,0:T(8,128)(2,1)} %get-tuple-element.57), channel_id=1, source_target_pairs={{0,2},{1,3},{2,0},{3,1},{4,6},{5,7},{6,4},{7,5},{8,10},{9,11},{10,... | collective-permute-start | bytes 3145736 | tf_op jit(solution)/shard_map/ppermute | solution.py:611
  88.4 48.3 %collective-permute-start.12 = (bf16[768,1024]{1,0:T(8,128)(2,1)}, bf16[768,1024]{1,0:T(8,128)(2,1)}, u32[]{:S(2)}, u32[]{:S(2)}) collective-permute-start(bf16[768,1024]{1,0:T(8,128)(2,1)} %collective-permute-done.8.refs_4_), channel_id=1, source_target_pairs={{4,0},{8,4},{12,8},{5,1},{9,5},{13,9},{6,2},{10,6},{14,10},{7,3},{... | collective-permute-start | bytes 4718600 | tf_op jit(solution)/shard_map/ppermute | solution.py:643
  90.6 46.2 %collective-permute-start.11 = (bf16[768,1024]{1,0:T(8,128)(2,1)}, bf16[768,1024]{1,0:T(8,128)(2,1)}, u32[]{:S(2)}, u32[]{:S(2)}) collective-permute-start(bf16[768,1024]{1,0:T(8,128)(2,1)} %collective-permute-done.7.refs_3_), channel_id=1, source_target_pairs={{0,4},{4,8},{8,12},{1,5},{5,9},{9,13},{2,6},{6,10},{10,14},{3,7},{... | collective-permute-start | bytes 4718600 | tf_op jit(solution)/shard_map/ppermute | solution.py:643
  93.7 43.0 %collective-permute-start.16 = (bf16[512,1024]{1,0:T(8,128)(2,1)}, bf16[512,1024]{1,0:T(8,128)(2,1)}, u32[]{:S(2)}, u32[]{:S(2)}) collective-permute-start(bf16[512,1024]{1,0:T(8,128)(2,1)} %get-tuple-element.58), channel_id=1, source_target_pairs={{0,2},{1,3},{2,0},{3,1},{4,6},{5,7},{6,4},{7,5},{8,10},{9,11},{10,... | collective-permute-start | bytes 3145736 | tf_op jit(solution)/shard_map/ppermute | solution.py:611
  112.3 24.5 %collective-permute-start.17 = (bf16[512,1024]{1,0:T(8,128)(2,1)}, bf16[512,1024]{1,0:T(8,128)(2,1)S(1)}, u32[]{:S(2)}, u32[]{:S(2)}) collective-permute-start(bf16[512,1024]{1,0:T(8,128)(2,1)} %collective-permute-done.15.refs_11_), channel_id=1, source_target_pairs={{0,16},{16,0},{1,17},{17,1},{2,18},{18,2},{3,19},{19,3},{4,20},{20... | collective-permute-start | bytes 3145736 | tf_op jit(solution)/shard_map/ppermute | solution.py:685
  113.6 22.2 %collective-permute-start.14 = (f32[3,256,128]{2,1,0:T(8,128)}, f32[3,256,128]{2,1,0:T(8,128)S(1)}, u32[]{:S(2)}, u32[]{:S(2)}) collective-permute-start(f32[3,256,128]{2,1,0:T(8,128)} %get-tuple-element.56), channel_id=1, source_target_pairs={{0,4},{4,0},{8,12},{12,8},{1,5},{5,1},{9,13},{13,9},{2,6},{6,2},{1... | collective-permute-start | bytes 1179656 | tf_op jit(solution)/shard_map/ppermute | solution.py:611
  136.8 23.8 %copy-start.4 = (f32[3,256,128]{2,1,0:T(8,128)}, f32[3,256,128]{2,1,0:T(8,128)S(1)}, u32[]{:S(2)}) copy-start(f32[3,256,128]{2,1,0:T(8,128)S(1)} %add.113.here_ref) | copy-start | bytes 1179652
  136.8 3.6 %copy-start.8 = (bf16[512,1024]{1,0:T(8,128)(2,1)}, bf16[512,1024]{1,0:T(8,128)(2,1)S(1)}, u32[]{:S(2)}) copy-start(bf16[512,1024]{1,0:T(8,128)(2,1)S(1)} %collective-permute-done.17.refs_17_) | copy-start | bytes 3145732
  136.8 8.9 %collective-permute-start.20 = (bf16[512,1024]{1,0:T(8,128)(2,1)}, bf16[512,1024]{1,0:T(8,128)(2,1)S(1)}, u32[]{:S(2)}, u32[]{:S(2)}) collective-permute-start(bf16[512,1024]{1,0:T(8,128)(2,1)} %collective-permute-done.15.refs_11_), channel_id=1, source_target_pairs={{0,1},{1,0},{2,3},{3,2},{4,5},{5,4},{6,7},{7,6},{8,9},{9,8},{10,11... | collective-permute-start | bytes 3145736 | tf_op jit(solution)/shard_map/ppermute | solution.py:611
  139.1 6.6 %collective-permute-start.19 = (bf16[512,1024]{1,0:T(8,128)(2,1)}, bf16[512,1024]{1,0:T(8,128)(2,1)S(1)}, u32[]{:S(2)}, u32[]{:S(2)}) collective-permute-start(bf16[512,1024]{1,0:T(8,128)(2,1)} %collective-permute-done.6.refs_9_), channel_id=1, source_target_pairs={{0,1},{1,0},{2,3},{3,2},{4,5},{5,4},{6,7},{7,6},{8,9},{9,8},{10,11... | collective-permute-start | bytes 3145736 | tf_op jit(solution)/shard_map/ppermute | solution.py:611
  139.2 29.0 %collective-permute-start.22 = (bf16[512,1024]{1,0:T(8,128)(2,1)}, bf16[512,1024]{1,0:T(8,128)(2,1)S(1)}, u32[]{:S(2)}, u32[]{:S(2)}) collective-permute-start(bf16[512,1024]{1,0:T(8,128)(2,1)} %collective-permute-done.16.refs_13_), channel_id=1, source_target_pairs={{0,16},{16,0},{1,17},{17,1},{2,18},{18,2},{3,19},{19,3},{4,20},{20... | collective-permute-start | bytes 3145736 | tf_op jit(solution)/shard_map/ppermute | solution.py:685
  140.5 27.8 %collective-permute-start.18 = (bf16[512,1024]{1,0:T(8,128)(2,1)}, bf16[512,1024]{1,0:T(8,128)(2,1)}, u32[]{:S(2)}, u32[]{:S(2)}) collective-permute-start(bf16[512,1024]{1,0:T(8,128)(2,1)} %get-tuple-element.60), channel_id=1, source_target_pairs={{0,2},{1,3},{2,0},{3,1},{4,6},{5,7},{6,4},{7,5},{8,10},{9,11},{10,... | collective-permute-start | bytes 3145736 | tf_op jit(solution)/shard_map/ppermute | solution.py:611
  141.7 19.7 %collective-permute-start.21 = (f32[3,256,128]{2,1,0:T(8,128)S(1)}, f32[3,256,128]{2,1,0:T(8,128)}, u32[]{:S(2)}, u32[]{:S(2)}) collective-permute-start(f32[3,256,128]{2,1,0:T(8,128)S(1)} %add.113.here_ref), channel_id=1, source_target_pairs={{0,8},{4,12},{8,0},{12,4},{1,9},{5,13},{9,1},{13,5},{2,10},{6,14},... | collective-permute-start | bytes 1179656 | tf_op jit(solution)/shard_map/ppermute | solution.py:611
  145.7 1.0 copy-start.2
  146.7 1.0 copy-start.3
  160.5 7.7 %copy-start.9 = (bf16[512,1024]{1,0:T(8,128)(2,1)S(1)}, bf16[512,1024]{1,0:T(8,128)(2,1)}, u32[]{:S(2)}) copy-start(bf16[512,1024]{1,0:T(8,128)(2,1)} %copy-done.8) | copy-start | bytes 3145732
  160.5 8.4 %copy-start.6 = (bf16[512,1024]{1,0:T(8,128)(2,1)S(1)}, bf16[512,1024]{1,0:T(8,128)(2,1)}, u32[]{:S(2)}) copy-start(bf16[512,1024]{1,0:T(8,128)(2,1)} %copy-done.5) | copy-start | bytes 3145732
  160.5 9.4 %copy-start.14 = (s32[3]{0:T(128)S(1)}, s32[3]{0:T(128)}, u32[]{:S(2)}) copy-start(s32[3]{0:T(128)} %live_ref) | copy-start | bytes 40
  168.2 27.0 %copy-start.7 = (bf16[512,1024]{1,0:T(8,128)(2,1)}, bf16[512,1024]{1,0:T(8,128)(2,1)S(1)}, u32[]{:S(2)}) copy-start(bf16[512,1024]{1,0:T(8,128)(2,1)S(1)} %collective-permute-done.22.refs_11_) | copy-start | bytes 3145732
  168.2 3.1 %collective-permute-start.28 = (bf16[512,1024]{1,0:T(8,128)(2,1)S(1)}, bf16[512,1024]{1,0:T(8,128)(2,1)}, u32[]{:S(2)}, u32[]{:S(2)}) collective-permute-start(bf16[512,1024]{1,0:T(8,128)(2,1)S(1)} %copy-done.9), channel_id=1, source_target_pairs={{0,1},{1,0},{2,3},{3,2},{4,5},{5,4},{6,7},{7,6},{8,9},{9,8},{10,11... | collective-permute-start | bytes 3145736 | tf_op jit(solution)/shard_map/ppermute | solution.py:611
  168.9 5.4 %collective-permute-start.27 = (bf16[512,1024]{1,0:T(8,128)(2,1)S(1)}, bf16[512,1024]{1,0:T(8,128)(2,1)}, u32[]{:S(2)}, u32[]{:S(2)}) collective-permute-start(bf16[512,1024]{1,0:T(8,128)(2,1)S(1)} %copy-done.6), channel_id=1, source_target_pairs={{0,1},{1,0},{2,3},{3,2},{4,5},{5,4},{6,7},{7,6},{8,9},{9,8},{10,11... | collective-permute-start | bytes 3145736 | tf_op jit(solution)/shard_map/ppermute | solution.py:611
  169.0 5.7 %collective-permute-start.26 = (bf16[512,1024]{1,0:T(8,128)(2,1)}, bf16[512,1024]{1,0:T(8,128)(2,1)}, u32[]{:S(2)}, u32[]{:S(2)}) collective-permute-start(bf16[512,1024]{1,0:T(8,128)(2,1)} %collective-permute-done.16.refs_13_), channel_id=1, source_target_pairs={{0,1},{1,0},{2,3},{3,2},{4,5},{5,4},{6,7},{7,6},{8,9},{9,8},{10,11... | collective-permute-start | bytes 3145736 | tf_op jit(solution)/shard_map/ppermute | solution.py:611
  169.4 25.8 %collective-permute-start.25 = (bf16[512,1024]{1,0:T(8,128)(2,1)}, bf16[512,1024]{1,0:T(8,128)(2,1)}, u32[]{:S(2)}, u32[]{:S(2)}) collective-permute-start(bf16[512,1024]{1,0:T(8,128)(2,1)} %collective-permute-done.18.refs_9_), channel_id=1, source_target_pairs={{0,16},{16,0},{1,17},{17,1},{2,18},{18,2},{3,19},{19,3},{4,20},{20... | collective-permute-start | bytes 3145736 | tf_op jit(solution)/shard_map/ppermute | solution.py:685
  169.7 25.5 %collective-permute-start.29 = (bf16[3,64,2560]{2,1,0:T(8,128)(2,1)}, bf16[3,64,2560]{2,1,0:T(8,128)(2,1)}, u32[]{:S(2)}, u32[]{:S(2)}) collective-permute-start(bf16[3,64,2560]{2,1,0:T(8,128)(2,1)} %get-tuple-element.81.refs_1_), channel_id=1, source_target_pairs={{0,2},{1,3},{2,0},{3,1},{4,6},{5,7},{6,4},{7,5},{8,10},{9,11},{10,... | collective-permute-start | bytes 2949128 | tf_op jit(solution)/shard_map/ppermute | solution.py:611
  171.3 25.7 %collective-permute-start.23 = (bf16[512,1024]{1,0:T(8,128)(2,1)}, bf16[512,1024]{1,0:T(8,128)(2,1)S(1)}, u32[]{:S(2)}, u32[]{:S(2)}) collective-permute-start(bf16[512,1024]{1,0:T(8,128)(2,1)} %collective-permute-done.18.refs_9_), channel_id=1, source_target_pairs={{0,1},{1,0},{2,3},{3,2},{4,5},{5,4},{6,7},{7,6},{8,9},{9,8},{10,11... | collective-permute-start | bytes 3145736 | tf_op jit(solution)/shard_map/ppermute | solution.py:611
  174.3 22.6 %collective-permute-start.24 = (bf16[512,1024]{1,0:T(8,128)(2,1)S(1)}, bf16[512,1024]{1,0:T(8,128)(2,1)S(1)}, u32[]{:S(2)}, u32[]{:S(2)}) collective-permute-start(bf16[512,1024]{1,0:T(8,128)(2,1)S(1)} %collective-permute-done.22.refs_11_), channel_id=1, source_target_pairs={{0,1},{1,0},{2,3},{3,2},{4,5},{5,4},{6,7},{7,6},{8,9},{9,8},{10,11... | collective-permute-start | bytes 3145736 | tf_op jit(solution)/shard_map/ppermute | solution.py:611
  195.2 3.1 %collective-permute-start.30 = (bf16[512,1024]{1,0:T(8,128)(2,1)}, bf16[512,1024]{1,0:T(8,128)(2,1)}, u32[]{:S(2)}, u32[]{:S(2)}) collective-permute-start(bf16[512,1024]{1,0:T(8,128)(2,1)} %collective-permute-done.25.refs_13_), channel_id=1, source_target_pairs={{0,1},{1,0},{2,3},{3,2},{4,5},{5,4},{6,7},{7,6},{8,9},{9,8},{10,11... | collective-permute-start | bytes 3145736 | tf_op jit(solution)/shard_map/ppermute | solution.py:611
  195.5 23.4 %collective-permute-start.33 = (bf16[3,64,2560]{2,1,0:T(8,128)(2,1)}, bf16[3,64,2560]{2,1,0:T(8,128)(2,1)}, u32[]{:S(2)}, u32[]{:S(2)}) collective-permute-start(bf16[3,64,2560]{2,1,0:T(8,128)(2,1)} %get-tuple-element.80.refs_0_), channel_id=1, source_target_pairs={{0,2},{1,3},{2,0},{3,1},{4,6},{5,7},{6,4},{7,5},{8,10},{9,11},{10,... | collective-permute-start | bytes 2949128 | tf_op jit(solution)/shard_map/ppermute | solution.py:611
  196.4 24.4 %collective-permute-start.35 = (bf16[3,64,2560]{2,1,0:T(8,128)(2,1)}, bf16[3,64,2560]{2,1,0:T(8,128)(2,1)}, u32[]{:S(2)}, u32[]{:S(2)}) collective-permute-start(bf16[3,64,2560]{2,1,0:T(8,128)(2,1)} %collective-permute-done.29.refs_5_), channel_id=1, source_target_pairs={{0,1},{1,0},{2,3},{3,2},{4,5},{5,4},{6,7},{7,6},{8,9},{9,8},{10,11... | collective-permute-start | bytes 2949128 | tf_op jit(solution)/shard_map/ppermute | solution.py:611
  196.9 1.3 copy-start.11
  196.9 23.8 %collective-permute-start.32 = (bf16[3,64,2560]{2,1,0:T(8,128)(2,1)}, bf16[3,64,2560]{2,1,0:T(8,128)(2,1)S(1)}, u32[]{:S(2)}, u32[]{:S(2)}) collective-permute-start(bf16[3,64,2560]{2,1,0:T(8,128)(2,1)} %get-tuple-element.81.refs_1_), channel_id=1, source_target_pairs={{0,1},{1,0},{2,3},{3,2},{4,5},{5,4},{6,7},{7,6},{8,9},{9,8},{10,11... | collective-permute-start | bytes 2949128 | tf_op jit(solution)/shard_map/ppermute | solution.py:611
  197.0 1.3 copy-start.10
  197.0 23.8 %collective-permute-start.31 = (bf16[3,64,2560]{2,1,0:T(8,128)(2,1)}, bf16[3,64,2560]{2,1,0:T(8,128)(2,1)}, u32[]{:S(2)}, u32[]{:S(2)}) collective-permute-start(bf16[3,64,2560]{2,1,0:T(8,128)(2,1)} %get-tuple-element.80.refs_0_), channel_id=1, source_target_pairs={{0,1},{1,0},{2,3},{3,2},{4,5},{5,4},{6,7},{7,6},{8,9},{9,8},{10,11... | collective-permute-start | bytes 2949128 | tf_op jit(solution)/shard_map/ppermute | solution.py:611
  218.9 3.5 %collective-permute-start.34 = (bf16[3,64,2560]{2,1,0:T(8,128)(2,1)}, bf16[3,64,2560]{2,1,0:T(8,128)(2,1)S(1)}, u32[]{:S(2)}, u32[]{:S(2)}) collective-permute-start(bf16[3,64,2560]{2,1,0:T(8,128)(2,1)} %collective-permute-done.33.refs_4_), channel_id=1, source_target_pairs={{0,1},{1,0},{2,3},{3,2},{4,5},{5,4},{6,7},{7,6},{8,9},{9,8},{10,11... | collective-permute-start | bytes 2949128 | tf_op jit(solution)/shard_map/ppermute | solution.py:611
  220.8 1.6 copy-start.12
  222.4 1.0 copy-start.13
